TPU v7x, 32 devices: a whole 2x2x4 slice. The times are simulated.
32 devices in a mesh: lat: 4 (over z), lon: 8 (over y, x, core).
Axes of the slice: x: 2, y: 2, z: 4, core: 2. Of those that a mesh axis runs over, the one named last changes fastest.
Arguments:
- tokens: bfloat16 [2, 64, 192, 1024], P(None, 'lat', 'lon'), may hold values from -6 to 6
- qkv_weight: bfloat16 [1024, 3072], replicated, may hold values from -0.1875 to 0.1875
- out_weight: bfloat16 [1024, 1024], replicated, may hold values from -0.1875 to 0.1875
- merge_weight: bfloat16 [4096, 1024], replicated, may hold values from -0.09375 to 0.09375
- merged_grad: bfloat16 [2, 32, 96, 1024], P(None, 'lat', 'lon'), may hold values from -6 to 6
Outputs:
- merged: bfloat16 [2, 32, 96, 1024], P(None, 'lat', 'lon')
- tokens_grad: bfloat16 [2, 64, 192, 1024], P(None, 'lat', 'lon')
- qkv_weight_grad: float32 [1024, 3072], P(('lat', 'lon'))
- out_weight_grad: float32 [1024, 1024], P(('lat', 'lon'))
All inputs are finite; a program needn't handle non-finite values.
Results may differ from a plain program's by a relative error of at most 0.02.
Values may be sent and summed in bfloat16 or wider, within the bound.
No kernel may reach another device: no remote copies, remote signals or barrier semaphores. Data moves between devices by JAX's collectives and lax.ppermute only.
A program may use at most 192 MiB of HBM per device.

v0:
```python
import jax
import jax.numpy as jnp
from jax import lax
from jax.sharding import PartitionSpec as P

HEADS = 32
WIN = 8
SHIFT = 4


epsilon = 1e-05


def shifted(block, axis, distance):
    devices = range(lax.axis_size(axis))
    route = [((i - distance) % len(devices), i) for i in devices]
    return lax.ppermute(block, axis, route)


def normalize(grid_field):
    values = grid_field.astype(jnp.float32)
    center = jnp.mean(values, axis=-1, keepdims=True)
    spread = jnp.mean(jnp.square(values - center), axis=-1, keepdims=True)
    return ((values - center) * lax.rsqrt(spread + epsilon)).astype(jnp.bfloat16)


def window_attention(window_values, region_marks):
    windows = window_values.shape[0]
    places = window_values.shape[1]
    channels = window_values.shape[2] // 3
    head_dim = channels // HEADS
    pieces = window_values.reshape(windows, places, 3, HEADS, head_dim)
    queries = pieces[:, :, 0]
    keys_part = pieces[:, :, 1]
    values_part = pieces[:, :, 2]
    scores = jnp.einsum(
        "bqhd,bkhd->bhqk", queries, keys_part, preferred_element_type=jnp.float32
    ) * head_dim ** (-0.5)
    same_region = region_marks[:, None, :, None] == region_marks[:, None, None, :]
    weights = jnp.where(same_region, jnp.exp(scores), 0.0)
    attention = (weights / jnp.sum(weights, axis=-1, keepdims=True)).astype(jnp.bfloat16)
    mixture = jnp.einsum(
        "bhqk,bkhd->bqhd", attention, values_part, preferred_element_type=jnp.float32
    )
    return mixture.astype(jnp.bfloat16).reshape(windows, places, channels)


def to_windows(grid_field):
    lev_count, lat_rows, lon_cols, channels = grid_field.shape
    blocks = grid_field.reshape(lev_count, lat_rows // WIN, WIN, lon_cols // WIN, WIN, channels)
    blocks = blocks.transpose(1, 3, 0, 2, 4, 5)
    return blocks.reshape(lat_rows // WIN * (lon_cols // WIN), lev_count * WIN * WIN, channels)


def from_windows(blocks, lev_count, lat_rows, lon_cols):
    channels = blocks.shape[-1]
    grid_field = blocks.reshape(lat_rows // WIN, lon_cols // WIN, lev_count, WIN, WIN, channels)
    return grid_field.transpose(2, 0, 3, 1, 4, 5).reshape(lev_count, lat_rows, lon_cols, channels)


def attend_local(projected, region):
    lev_count, lat_rows, lon_cols, channels = projected.shape
    blocks = to_windows(projected)
    region_blocks = to_windows(region[..., None])[..., 0]
    mixture = window_attention(blocks, region_blocks)
    return from_windows(mixture, lev_count, lat_rows, lon_cols)


def merge(grid_field, merge_weight):
    lev_count, lat_rows, lon_cols, channels = grid_field.shape
    groups = grid_field.reshape(lev_count, lat_rows // 2, 2, lon_cols // 2, 2, channels)
    groups = groups.transpose(0, 1, 3, 4, 2, 5).reshape(
        lev_count, lat_rows // 2, lon_cols // 2, 4 * channels
    )
    normed = normalize(groups)
    result = jnp.dot(
        normed.reshape(-1, 4 * channels), merge_weight, preferred_element_type=jnp.float32
    )
    return result.astype(jnp.bfloat16).reshape(
        lev_count, lat_rows // 2, lon_cols // 2, merge_weight.shape[1]
    )


def move_strips(grid_field, strip_width, offset):
    if offset == 1:
        outgoing = grid_field[:, :, -strip_width:]
    else:
        outgoing = grid_field[:, :, :strip_width]
    arrived = shifted(outgoing, "lon", offset)
    if offset == 1:
        middle = jnp.concatenate([arrived, grid_field[:, :, :-strip_width]], axis=2)
        outgoing_rows = middle[:, -strip_width:]
    else:
        middle = jnp.concatenate([grid_field[:, :, strip_width:], arrived], axis=2)
        outgoing_rows = middle[:, :strip_width]
    arrived_rows = shifted(outgoing_rows, "lat", offset)
    if offset == 1:
        return jnp.concatenate([arrived_rows, middle[:, :-strip_width]], axis=1)
    return jnp.concatenate([middle[:, strip_width:], arrived_rows], axis=1)


def shards(tokens, qkv_weight, out_weight, merge_weight, merged_grad):
    lev_count, lat_rows, lon_cols, channels = tokens.shape
    framed = move_strips(tokens, SHIFT, 1)
    normed, norm_back = jax.vjp(normalize, framed)
    flat_norm = normed.reshape(-1, channels)
    projected = jnp.dot(flat_norm, qkv_weight, preferred_element_type=jnp.float32).astype(
        jnp.bfloat16
    )
    projected = projected.reshape(lev_count, lat_rows, lon_cols, 3 * channels)
    edge_rows = (lax.axis_index("lat") == 0) & (jnp.arange(lat_rows) < SHIFT)
    region = jnp.broadcast_to(
        edge_rows.astype(jnp.int32)[None, :, None], (lev_count, lat_rows, lon_cols)
    )
    mixture, attend_back = jax.vjp(lambda grid_values: attend_local(grid_values, region), projected)
    mixture_flat = mixture.reshape(-1, channels)
    branch = jnp.dot(mixture_flat, out_weight, preferred_element_type=jnp.float32)
    shifted_out = (framed.reshape(-1, channels).astype(jnp.float32) + branch).astype(jnp.bfloat16)
    shifted_out = shifted_out.reshape(framed.shape)
    block_out = move_strips(shifted_out, SHIFT, -1)
    merged, merge_back = jax.vjp(lambda grid_values: merge(grid_values, merge_weight), block_out)
    block_grad = merge_back(merged_grad)[0]
    framed_grad_out = move_strips(block_grad, SHIFT, 1)
    grad_rolled = framed_grad_out.reshape(-1, channels)
    mixture_grad = lax.dot_general(
        grad_rolled, out_weight, (((1,), (1,)), ((), ())), preferred_element_type=jnp.float32
    ).astype(jnp.bfloat16)
    out_terms = lax.dot_general(
        mixture_flat, grad_rolled, (((0,), (0,)), ((), ())), preferred_element_type=jnp.float32
    )
    projected_grad = attend_back(mixture_grad.reshape(mixture.shape))[0].reshape(-1, 3 * channels)
    qkv_terms = lax.dot_general(
        flat_norm, projected_grad, (((0,), (0,)), ((), ())), preferred_element_type=jnp.float32
    )
    normed_grad = lax.dot_general(
        projected_grad, qkv_weight, (((1,), (1,)), ((), ())), preferred_element_type=jnp.float32
    ).astype(jnp.bfloat16)
    input_part = norm_back(normed_grad.reshape(normed.shape))[0].reshape(-1, channels)
    framed_grad = (grad_rolled.astype(jnp.float32) + input_part.astype(jnp.float32)).astype(
        jnp.bfloat16
    )
    tokens_grad = move_strips(framed_grad.reshape(framed.shape), SHIFT, -1)
    qkv_weight_grad, out_weight_grad = (
        lax.psum_scatter(qkv_terms, ("lat", "lon"), scatter_dimension=0, tiled=True),
        lax.psum_scatter(out_terms, ("lat", "lon"), scatter_dimension=0, tiled=True),
    )
    return (merged, tokens_grad, qkv_weight_grad, out_weight_grad)


def solution(mesh):
    in_specs = (P(None, "lat", "lon", None), P(), P(), P(), P(None, "lat", "lon", None))
    out_specs = (
        P(None, "lat", "lon", None),
        P(None, "lat", "lon", None),
        P(("lat", "lon"), None),
        P(("lat", "lon"), None),
    )
    return jax.shard_map(shards, mesh=mesh, in_specs=in_specs, out_specs=out_specs, check_vma=False)
```

profile of v0, /device:TPU:0, one launch (start us, length us, event | category | flops | bytes accessed | tf_op | source)
XLA Modules:
  0.0 542.0 jit_solution(8315116063583145523)
XLA Ops:
  9.1 6.9 %collective-permute-done = bf16[2,16,4,1024]{3,2,1,0:T(4,128)(2,1)S(1)} collective-permute-done((bf16[2,16,4,1024]{3,2,1,0:T(4,128)(2,1)S(1)}, bf16[2,16,4,1024]{3,2,1,0:T(4,128)(2,1)S(1)}, u32[]{:S(2)}, u32[]{:S(2)}) %collective-permute-start) | collective-permute-done | bytes 262176 | tf_op jit(solution)/shard_map/ppermute | solution.py:17
  19.9 9.2 %collective-permute-done.1 = bf16[2,4,24,1024]{3,2,1,0:T(8,128)(2,1)S(1)} collective-permute-done((bf16[2,4,24,1024]{3,2,1,0:T(8,128)(2,1)S(1)}, bf16[2,4,24,1024]{3,2,1,0:T(8,128)(2,1)S(1)}, u32[]{:S(2)}, u32[]{:S(2)}) %collective-permute-start.1) | collective-permute-done | bytes 393248 | tf_op jit(solution)/shard_map/ppermute | solution.py:17
  36.0 8.2 %convolution_convert_fusion = bf16[768,3072]{1,0:T(8,128)(2,1)S(1)} fusion(bf16[768,1024]{1,0:T(8,128)(2,1)S(1)} %fusion.19, bf16[1024,3072]{1,0:T(8,128)(2,1)} %param.6), kind=kOutput, calls=%fused_computation.12 | convolution fusion | flops 4834197504 | bytes 12582912 | tf_op jit(solution)/shard_map/dot_general | solution.py:107
  46.9 21.3 %reshape.250 = bf16[6,128,3,32,32]{4,3,2,1,0:T(8,128)(2,1)} reshape(bf16[2,3,2,8,8,3072]{5,4,3,2,1,0:T(8,128)(2,1)} %bitcast.127) | data formatting | bytes 9437184 | tf_op jit(solution)/shard_map/jvp()/reshape;jvp()/reshape | solution.py:32
  68.2 14.3 %fusion.56 = (bf16[6,128,1,32,32]{4,3,2,1,0:T(8,128)(2,1)}, bf16[6,128,1,32,32]{4,3,2,1,0:T(8,128)(2,1)}, bf16[6,128,1,32,32]{4,3,2,1,0:T(8,128)(2,1)}) fusion(bf16[6,128,3,32,32]{4,3,2,1,0:T(8,128)(2,1)} %reshape.250), kind=kLoop, calls=%fused_computation.102 | loop fusion | bytes 9437184 | tf_op jit(solution)/shard_map/jvp()/slice | solution.py:35
  82.5 8.6 %copy.41 = bf16[6,128,1,32,32]{1,4,3,0,2:T(8,128)(2,1)} copy(bf16[6,128,1,32,32]{4,3,2,1,0:T(8,128)(2,1)} %get-tuple-element.19) | data formatting | bytes 3145728
  91.1 8.6 %copy.42 = bf16[6,128,1,32,32]{1,4,3,0,2:T(8,128)(2,1)} copy(bf16[6,128,1,32,32]{4,3,2,1,0:T(8,128)(2,1)} %get-tuple-element.20) | data formatting | bytes 3145728
  99.7 8.6 %copy.40 = bf16[6,128,1,32,32]{1,4,3,0,2:T(8,128)(2,1)} copy(bf16[6,128,1,32,32]{4,3,2,1,0:T(8,128)(2,1)} %get-tuple-element.18) | data formatting | bytes 3145728
  108.3 5.0 fusion.7
  123.7 9.9 %copy.22 = bf16[6,128,32,32]{3,2,1,0:T(8,128)(2,1)} copy(bf16[6,128,32,32]{1,3,2,0:T(8,128)(2,1)} %fusion.43) | data formatting | bytes 3145728 | tf_op jit(solution)/shard_map/jvp()/convert_element_type | solution.py:45
  133.6 9.6 %reshape.251 = bf16[2,3,2,8,8,1024]{5,4,3,2,1,0:T(8,128)(2,1)} reshape(bf16[6,128,32,32]{3,2,1,0:T(8,128)(2,1)} %copy.22) | data formatting | bytes 3145728 | tf_op jit(solution)/shard_map/jvp()/reshape;jvp()/reshape | solution.py:57
  155.7 8.0 %fusion.8 = f32[192,4096]{1,0:T(8,128)} fusion(bf16[192,1024]{1,0:T(8,128)(2,1)S(1)} %reshape.255, bf16[4096,1024]{1,0:T(8,128)(2,1)} %param.8), kind=kOutput, calls=%fused_computation.14 | convolution fusion | flops 1612185600 | bytes 11927552 | tf_op jit(solution)/shard_map/transpose(jvp())/dot_general | solution.py:76
  163.6 6.1 %reshape.264 = f32[2,8,12,2,2,1024]{5,4,3,2,1,0:T(2,128)} reshape(f32[192,4096]{1,0:T(8,128)} %fusion.8) | data formatting | bytes 6291456 | tf_op jit(solution)/shard_map/transpose(jvp())/convert_element_type | solution.py:24
  173.1 5.2 reshape.266
  178.3 4.5 fusion.54
  182.8 5.6 %multiply_reduce_fusion.1 = (f32[2,8,12]{2,1,0:T(8,128)S(1)}, f32[2,8,12]{2,1,0:T(8,128)S(1)}) fusion(f32[2,8,12,2,2,1024]{5,4,3,2,1,0:T(2,128)} %reshape.264, f32[2,8,12]{2,1,0:T(8,128)S(1)} %broadcast_multiply_fusion.1, f32[2,8,2,12,2,1024]{5,4,3,2,1,0:T(2,128)S(1)} %copy-done.2), kind=kLoop, calls=%fused_computation.43 | loop fusion | flops 3931776 | bytes 6293760 | tf_op jit(solution)/shard_map/transpose(jvp())/reduce_sum | solution.py:24
  194.2 7.2 %fusion.36 = bf16[2,8,2,12,2,1024]{5,2,4,3,1,0:T(2,128)(2,1)S(1)} fusion(f32[2,8,12]{2,1,0:T(8,128)S(1)} %add_multiply_fusion, f32[2,8,12]{2,1,0:T(8,128)S(1)} %get-tuple-element.25, f32[2,8,12,2,2,1024]{5,4,3,2,1,0:T(2,128)} %reshape.264, f32[2,8,12]{2,1,0:T(8,128)S(1)} %get-tuple-element.26, f32[2,8,12]{2,1,0:T(8,128)S(1)} %broadcast_multiply_fusion.1, ...), kind=kLoop, calls=%fused_computation.75 | loop fusion | flops 4718592 | bytes 7867392 | tf_op jit(solution)/shard_map/transpose(jvp())/transpose | solution.py:72
  210.7 5.3 collective-permute-done.4
  217.7 10.7 %collective-permute-done.5 = bf16[2,4,24,1024]{3,2,1,0:T(8,128)(2,1)S(1)} collective-permute-done((bf16[2,4,24,1024]{3,2,1,0:T(8,128)(2,1)S(1)}, bf16[2,4,24,1024]{3,2,1,0:T(8,128)(2,1)S(1)}, u32[]{:S(2)}, u32[]{:S(2)}) %collective-permute-start.5) | collective-permute-done | bytes 393248 | tf_op jit(solution)/shard_map/ppermute | solution.py:17
  240.0 6.2 %reshape.258 = bf16[6,128,32,32]{3,2,1,0:T(8,128)(2,1)} reshape(bf16[2,3,2,8,8,1024]{5,4,3,2,1,0:T(8,128)(2,1)S(1)} %bitcast.140) | data formatting | bytes 3145728 | tf_op jit(solution)/shard_map/transpose(jvp())/reshape;transpose(jvp())/reshape | solution.py:45
  246.2 8.6 %copy.28 = bf16[6,32,32,128]{3,2,1,0:T(8,128)(2,1)} copy(bf16[6,32,32,128]{2,1,3,0:T(8,128)(2,1)} %bitcast.124) | data formatting | bytes 3145728 | tf_op jit(solution)/shard_map/transpose(jvp(bhqk,bkhd->bqhd))/transpose | solution.py:42
  254.8 8.0 %fusion.46 = bf16[6,128,1,32,32]{1,4,3,0,2:T(8,128)(2,1)} fusion(bf16[6,32,32,128]{3,2,1,0:T(8,128)(2,1)} %copy.28, bf16[6,32,128,128]{2,3,1,0:T(8,128)(2,1)} %copy-done.4), kind=kOutput, calls=%fused_computation.79 | convolution fusion | flops 202113024 | bytes 9437184 | tf_op jit(solution)/shard_map/transpose(jvp(bhqk,bkhd->bqhd))/dot_general | solution.py:42
  262.8 9.1 %fusion.5 = (f32[6,32,128]{2,1,0:T(8,128)S(1)}, bf16[6,32,128,128]{2,3,1,0:T(8,128)(2,1)}) fusion(f32[6,32,128,128]{2,3,1,0:T(8,128)} %copy-done.11, f32[6,32,128]{2,1,0:T(8,128)S(1)} %multiply_divide_fusion, pred[6,128,128]{1,2,0:T(8,128)(4,1)S(1)} %broadcast_compare_fusion, bf16[6,32,32,128]{3,2,1,0:T(8,128)(2,1)S(1)} %copy-done.17, ...), kind=kOutput, calls=%fused_computation.7 | convolution fusion | flops 223322112 | bytes 22315008 | tf_op jit(solution)/shard_map/transpose(jvp(bhqk,bkhd->bqhd))/dot_general | solution.py:42
  271.9 12.3 %fusion.40 = bf16[6,128,1,32,32]{1,4,3,0,2:T(8,128)(2,1)} fusion(bf16[6,128,1,32,32]{1,4,3,0,2:T(8,128)(2,1)} %copy.42, bf16[6,32,128,128]{2,3,1,0:T(8,128)(2,1)} %get-tuple-element.30, f32[6,32,128,128]{2,3,1,0:T(8,128)} %copy-done.11, f32[6,32,128]{2,1,0:T(8,128)S(1)} %neg.25, f32[6,32,128]{2,1,0:T(8,128)S(1)} %get-tuple-element.27, ...), kind=kOutput, calls=%fused_computation.77 | convolution fusion | flops 224133120 | bytes 22315008 | tf_op jit(solution)/shard_map/transpose(jvp(bqhd,bkhd->bhqk))/dot_general | solution.py:36
  284.2 12.2 %fusion.37 = bf16[6,128,1,32,32]{1,4,3,0,2:T(8,128)(2,1)} fusion(bf16[6,128,1,32,32]{1,4,3,0,2:T(8,128)(2,1)} %copy.41, bf16[6,32,128,128]{2,3,1,0:T(8,128)(2,1)} %get-tuple-element.30, f32[6,32,128,128]{2,3,1,0:T(8,128)} %copy-done.11, f32[6,32,128]{2,1,0:T(8,128)S(1)} %neg.25, f32[6,32,128]{2,1,0:T(8,128)S(1)} %get-tuple-element.27, ...), kind=kOutput, calls=%fused_computation.76 | convolution fusion | flops 224133120 | bytes 22315008 | tf_op jit(solution)/shard_map/transpose(jvp(bqhd,bkhd->bhqk))/dot_general | solution.py:36
  300.2 25.8 %copy.33 = bf16[6,128,3,32,32]{4,3,2,1,0:T(8,128)(2,1)} copy(bf16[6,128,3,32,32]{1,4,3,0,2:T(8,128)(2,1)} %pad_add_fusion) | data formatting | bytes 9437184 | tf_op jit(solution)/shard_map/transpose(jvp())/add_any | solution.py:33
  326.0 24.5 %reshape.259 = bf16[2,3,2,8,8,3072]{5,4,3,2,1,0:T(8,128)(2,1)} reshape(bf16[6,128,3,32,32]{4,3,2,1,0:T(8,128)(2,1)} %copy.33) | data formatting | bytes 9437184 | tf_op jit(solution)/shard_map/transpose(jvp())/reshape;transpose(jvp())/reshape | solution.py:52
  353.5 11.3 %fusion.9 = (f32[768]{0:T(1024)S(1)}, f32[768]{0:T(1024)S(1)}, bf16[768,1024]{1,0:T(8,128)(2,1)}) fusion(f32[768]{0:T(1024)S(1)} %copy-done.30, f32[768]{0:T(1024)S(1)} %copy-done.28, bf16[2,16,24,1024]{3,2,1,0:T(8,128)(2,1)S(1)} %copy-done.6, bf16[768,3072]{1,0:T(8,128)(2,1)S(1)} %bitcast.125, bf16[1024,3072]{1,0:T(8,128)(2,1)} %param.6), kind=kOutput, calls=%fused_computation.19 | convolution fusion | flops 4838127616 | bytes 14168064 | tf_op jit(solution)/shard_map/dot_general | solution.py:135
  365.7 10.4 %fusion.57 = f32[1024,3072]{1,0:T(8,128)} fusion(bf16[768,1024]{1,0:T(8,128)(2,1)S(1)} %bitcast.136, bf16[768,3072]{1,0:T(8,128)(2,1)} %bitcast.126), kind=kOutput, calls=%fused_computation.103 | convolution fusion | flops 4831838208 | bytes 18874368 | tf_op jit(solution)/shard_map/dot_general | solution.py:132
  385.4 5.7 %reshape.263 = f32[192,4096]{1,0:T(8,128)} reshape(f32[2,8,12,2,2,1024]{5,4,3,2,1,0:T(2,128)} %bitcast.131) | data formatting | bytes 6291456 | tf_op jit(solution)/shard_map/jvp()/convert_element_type | solution.py:21
  394.4 5.7 %fusion.47 = bf16[192,1024]{1,0:T(8,128)(2,1)S(1)} fusion(bf16[4096,1024]{1,0:T(8,128)(2,1)} %param.8, f32[192,4096]{1,0:T(8,128)S(1)} %copy-done.18, f32[192]{0:T(256)S(1)} %rsqrt.30, f32[192]{0:T(256)S(1)} %div.67), kind=kOutput, calls=%fused_computation.80 | convolution fusion | flops 1613168640 | bytes 11929088 | tf_op jit(solution)/shard_map/jvp()/dot_general | solution.py:76
  407.4 127.3 %reduce-scatter.3.cloned.1.call-done = f32[32,3072]{1,0:T(8,128)} async-done(((f32[1024,3072]{1,0:T(8,128)}), f32[32,3072]{1,0:T(8,128)}) %reduce-scatter.3.cloned.1.call-update) | async-done | bytes 393232 | tf_op jit(solution)/shard_map/reduce_scatter | solution.py:144
  (145 shorter events, 97.0 us)
Async XLA Ops:
  7.2 137.7 %copy-start = (bf16[1024,1024]{1,0:T(8,128)(2,1)S(1)}, bf16[1024,1024]{1,0:T(8,128)(2,1)}, u32[]{:S(2)}) copy-start(bf16[1024,1024]{1,0:T(8,128)(2,1)} %param.7) | copy-start | bytes 6291460
  7.2 400.3 %reduce-scatter.5.cloned.1.call-start = ((), (), s32[]{:S(2)}) async-start(), calls=%async_computation.3 | async-start | bytes 4325376 | tf_op jit(solution)/shard_map/reduce_scatter | solution.py:145
  8.6 7.4 %collective-permute-start = (bf16[2,16,4,1024]{3,2,1,0:T(4,128)(2,1)S(1)}, bf16[2,16,4,1024]{3,2,1,0:T(4,128)(2,1)S(1)}, u32[]{:S(2)}, u32[]{:S(2)}) collective-permute-start(bf16[2,16,4,1024]{3,2,1,0:T(4,128)(2,1)S(1)} %slice.57), channel_id=1, source_target_pairs={{7,0},{0,1},{1,2},{2,3},{3,4},{4,5},{5,6},{6,7},{15,8},{8,9},{9,10... | collective-permute-start | bytes 786440 | tf_op jit(solution)/shard_map/ppermute | solution.py:17
  17.1 11.9 %collective-permute-start.1 = (bf16[2,4,24,1024]{3,2,1,0:T(8,128)(2,1)S(1)}, bf16[2,4,24,1024]{3,2,1,0:T(8,128)(2,1)S(1)}, u32[]{:S(2)}, u32[]{:S(2)}) collective-permute-start(bf16[2,4,24,1024]{3,2,1,0:T(8,128)(2,1)S(1)} %pad_maximum_fusion.6), channel_id=1, source_target_pairs={{24,0},{0,8},{8,16},{16,24},{25,1},{1,9},{9,17},{17,25},{26,2},{2,... | collective-permute-start | bytes 1179656 | tf_op jit(solution)/shard_map/ppermute | solution.py:17
  32.0 12.3 %copy-start.23 = (f32[2,16,24]{2,1,0:T(8,128)}, f32[2,16,24]{2,1,0:T(8,128)S(1)}, u32[]{:S(2)}) copy-start(f32[2,16,24]{2,1,0:T(8,128)S(1)} %broadcast_multiply_fusion) | copy-start | bytes 9220
  32.1 12.2 %copy-start.27 = (f32[768]{0:T(1024)}, f32[768]{0:T(1024)S(1)}, u32[]{:S(2)}) copy-start(f32[768]{0:T(1024)S(1)} %div.62) | copy-start | bytes 9220
  34.1 10.3 %copy-start.25 = (f32[2,16,24]{2,1,0:T(8,128)}, f32[2,16,24]{2,1,0:T(8,128)S(1)}, u32[]{:S(2)}) copy-start(f32[2,16,24]{2,1,0:T(8,128)S(1)} %fusion.20) | copy-start | bytes 9220
  34.2 10.2 %copy-start.31 = (f32[768]{0:T(1024)}, f32[768]{0:T(1024)S(1)}, u32[]{:S(2)}) copy-start(f32[768]{0:T(1024)S(1)} %add.52) | copy-start | bytes 9220
  34.2 10.1 %copy-start.29 = (f32[768]{0:T(1024)}, f32[768]{0:T(1024)S(1)}, u32[]{:S(2)}) copy-start(f32[768]{0:T(1024)S(1)} %rsqrt.28) | copy-start | bytes 9220
  113.4 4.7 copy-start.11
  113.4 7.3 %copy-start.12 = (bf16[6,128,1,32,32]{1,4,3,0,2:T(8,128)(2,1)S(1)}, bf16[6,128,1,32,32]{1,4,3,0,2:T(8,128)(2,1)}, u32[]{:S(2)}) copy-start(bf16[6,128,1,32,32]{1,4,3,0,2:T(8,128)(2,1)} %copy.40) | copy-start | bytes 4718596
  145.1 3.8 copy-start.22
  148.9 4.2 collective-permute-start.2
  153.9 17.3 %collective-permute-start.3 = (bf16[2,4,24,1024]{3,2,1,0:T(8,128)(2,1)}, bf16[2,4,24,1024]{3,2,1,0:T(8,128)(2,1)S(1)}, u32[]{:S(2)}, u32[]{:S(2)}) collective-permute-start(bf16[2,4,24,1024]{3,2,1,0:T(8,128)(2,1)} %pad_maximum_fusion.5), channel_id=1, source_target_pairs={{8,0},{16,8},{24,16},{0,24},{9,1},{17,9},{25,17},{1,25},{10,2},{18... | collective-permute-start | bytes 1179656 | tf_op jit(solution)/shard_map/ppermute | solution.py:17
  178.3 4.5 copy-start.2
  208.0 20.5 %copy-start.8 = (bf16[2,16,24,1024]{3,2,1,0:T(8,128)(2,1)S(1)}, bf16[2,16,24,1024]{3,2,1,0:T(8,128)(2,1)}, u32[]{:S(2)}) copy-start(bf16[2,16,24,1024]{3,2,1,0:T(8,128)(2,1)} %reshape.256) | copy-start | bytes 4718596
  209.3 20.9 %copy-start.21 = (bf16[2,2,8,3,8,1024]{5,4,3,2,1,0:T(8,128)(2,1)S(1)}, bf16[2,2,8,3,8,1024]{5,4,3,2,1,0:T(8,128)(2,1)}, u32[]{:S(2)}) copy-start(bf16[2,2,8,3,8,1024]{5,4,3,2,1,0:T(8,128)(2,1)} %copy-done.20) | copy-start | bytes 4718596
  209.3 6.7 %collective-permute-start.4 = (bf16[2,16,4,1024]{3,2,1,0:T(4,128)(2,1)S(1)}, bf16[2,16,4,1024]{3,2,1,0:T(4,128)(2,1)S(1)}, u32[]{:S(2)}, u32[]{:S(2)}) collective-permute-start(bf16[2,16,4,1024]{3,2,1,0:T(4,128)(2,1)S(1)} %slice.83), channel_id=1, source_target_pairs={{7,0},{0,1},{1,2},{2,3},{3,4},{4,5},{5,6},{6,7},{15,8},{8,9},{9,10... | collective-permute-start | bytes 786440 | tf_op jit(solution)/shard_map/ppermute | solution.py:17
  217.2 11.3 %collective-permute-start.5 = (bf16[2,4,24,1024]{3,2,1,0:T(8,128)(2,1)S(1)}, bf16[2,4,24,1024]{3,2,1,0:T(8,128)(2,1)S(1)}, u32[]{:S(2)}, u32[]{:S(2)}) collective-permute-start(bf16[2,4,24,1024]{3,2,1,0:T(8,128)(2,1)S(1)} %pad_maximum_fusion.4), channel_id=1, source_target_pairs={{24,0},{0,8},{8,16},{16,24},{25,1},{1,9},{9,17},{17,25},{26,2},{2,... | collective-permute-start | bytes 1179656 | tf_op jit(solution)/shard_map/ppermute | solution.py:17
  238.4 296.3 %reduce-scatter.3.cloned.1.call-start = ((), (), s32[]{:S(2)}) async-start(), calls=%async_computation.2 | async-start | bytes 12976128 | tf_op jit(solution)/shard_map/reduce_scatter | solution.py:144
  254.8 8.0 %copy-start.13 = (bf16[6,128,1,32,32]{1,4,3,0,2:T(8,128)(2,1)S(1)}, bf16[6,128,1,32,32]{1,4,3,0,2:T(8,128)(2,1)}, u32[]{:S(2)}) copy-start(bf16[6,128,1,32,32]{1,4,3,0,2:T(8,128)(2,1)} %copy.40) | copy-start | bytes 4718596
  254.8 8.0 %copy-start.17 = (bf16[6,32,32,128]{3,2,1,0:T(8,128)(2,1)S(1)}, bf16[6,32,32,128]{3,2,1,0:T(8,128)(2,1)}, u32[]{:S(2)}) copy-start(bf16[6,32,32,128]{3,2,1,0:T(8,128)(2,1)} %copy.28) | copy-start | bytes 4718596
  284.2 12.2 %copy-start.15 = (bf16[6,128,1,32,32]{1,4,3,0,2:T(8,128)(2,1)S(1)}, bf16[6,128,1,32,32]{1,4,3,0,2:T(8,128)(2,1)}, u32[]{:S(2)}) copy-start(bf16[6,128,1,32,32]{1,4,3,0,2:T(8,128)(2,1)} %fusion.46) | copy-start | bytes 4718596
  353.5 11.4 %copy-start.7 = (bf16[2,2,8,3,8,3072]{5,4,3,2,1,0:T(8,128)(2,1)}, bf16[2,2,8,3,8,3072]{5,4,3,2,1,0:T(8,128)(2,1)S(1)}, u32[]{:S(2)}) copy-start(bf16[2,2,8,3,8,3072]{5,4,3,2,1,0:T(8,128)(2,1)S(1)} %copy.34) | copy-start | bytes 14155780
  353.5 11.4 %copy-start.26 = (f32[2,16,24]{2,1,0:T(8,128)S(1)}, f32[2,16,24]{2,1,0:T(8,128)}, u32[]{:S(2)}) copy-start(f32[2,16,24]{2,1,0:T(8,128)} %copy-done.25) | copy-start | bytes 9220
  353.5 11.4 %copy-start.24 = (f32[2,16,24]{2,1,0:T(8,128)S(1)}, f32[2,16,24]{2,1,0:T(8,128)}, u32[]{:S(2)}) copy-start(f32[2,16,24]{2,1,0:T(8,128)} %copy-done.23) | copy-start | bytes 9220
  376.8 4.1 copy-start.3
  380.8 12.7 %collective-permute-start.6 = (bf16[2,16,4,1024]{3,2,1,0:T(4,128)(2,1)S(1)}, bf16[2,16,4,1024]{3,2,1,0:T(4,128)(2,1)S(1)}, u32[]{:S(2)}, u32[]{:S(2)}) collective-permute-start(bf16[2,16,4,1024]{3,2,1,0:T(4,128)(2,1)S(1)} %slice.86), channel_id=1, source_target_pairs={{1,0},{2,1},{3,2},{4,3},{5,4},{6,5},{7,6},{0,7},{9,8},{10,9},{11,1... | collective-permute-start | bytes 786440 | tf_op jit(solution)/shard_map/ppermute | solution.py:17
  391.1 3.3 copy-start.18
  393.5 6.6 %copy-start.9 = (bf16[2,16,20,1024]{3,2,1,0:T(8,128)(2,1)}, bf16[2,16,20,1024]{3,2,1,0:T(8,128)(2,1)S(1)}, u32[]{:S(2)}) copy-start(bf16[2,16,20,1024]{3,2,1,0:T(8,128)(2,1)S(1)} %slice.85) | copy-start | bytes 3932164
  394.4 11.7 %collective-permute-start.7 = (bf16[2,4,24,1024]{3,2,1,0:T(8,128)(2,1)}, bf16[2,4,24,1024]{3,2,1,0:T(8,128)(2,1)S(1)}, u32[]{:S(2)}, u32[]{:S(2)}) collective-permute-start(bf16[2,4,24,1024]{3,2,1,0:T(8,128)(2,1)} %pad_maximum_fusion.3), channel_id=1, source_target_pairs={{8,0},{16,8},{24,16},{0,24},{9,1},{17,9},{25,17},{1,25},{10,2},{18... | collective-permute-start | bytes 1179656 | tf_op jit(solution)/shard_map/ppermute | solution.py:17
  400.2 134.5 %copy-start.1 = (bf16[1024,1024]{1,0:T(8,128)(2,1)S(1)}, bf16[1024,1024]{1,0:T(8,128)(2,1)}, u32[]{:S(2)}) copy-start(bf16[1024,1024]{1,0:T(8,128)(2,1)} %param.7) | copy-start | bytes 6291460
  (11 other events, 21.3 us)
Sparse Core Ops, SparseCore 0:
  238.5 138.1 reduce-scatter.4
  383.3 151.3 reduce-scatter.2
where the time goes:
time: 547 us; the launch traced here: 542 us
  local copies, waits for them, and re-layouts  202 us (37%)
  waiting for transfers between devices  165 us (30%)
  matrix products  103 us (19%)
  other arithmetic  50.9 us (9%)
  between operations  15.1 us (3%)
  starting transfers between devices  6.72 us (1%)
    reduce_scatter x1, waiting for transfers between devices, shards(): lax.psum_scatter(qkv_terms, ('lat', 'lon'), scatter_dimension=0, tiled=True)  127 us
    ppermute x8, waiting for transfers between devices, shifted(): return lax.ppermute(block, axis, route)  37.3 us
    unnamed x71, local copies, waits for them, and re-layouts  35.7 us
    dot_general x3, matrix products, window_attention(): jnp.einsum('bqhd,bkhd->bhqk', queries, keys_part, preferred_element_type=...  29.5 us
    add_any x1, local copies, waits for them, and re-layouts, window_attention(): queries = pieces[:, :, 0]  25.8 us
    reshape x1, local copies, waits for them, and re-layouts, to_windows(): blocks.reshape(lat_rows // WIN * (lon_cols // WIN), lev_count * WIN * WIN...  24.5 us
    reshape x1, local copies, waits for them, and re-layouts, window_attention(): pieces = window_values.reshape(windows, places, 3, HEADS, head_dim)  21.3 us
    dot_general x3, matrix products, window_attention(): jnp.einsum('bhqk,bkhd->bqhd', attention, values_part, preferred_element_t...  20.1 us
  transfers between devices with their start and end apart: 10, of which 7 were waited for; matrix products, arithmetic and copies ran while one was open for 34% of the time, Pallas kernels for 0%

commit v1 on v0

v1 whole, which is shorter than its diff:
```python
import functools

import jax
import jax.numpy as jnp
import numpy as np
from jax import lax
from jax.experimental import pallas as pl
from jax.experimental.pallas import tpu as pltpu
from jax.sharding import PartitionSpec as P

HEADS = 32
WIN = 8
SHIFT = 4
LANES = 128
HALF = SHIFT // 2
EPSILON = 1e-05
MIB = 1 << 20

NN = (((1,), (0,)), ((), ()))
NT = (((1,), (1,)), ((), ()))
TN = (((0,), (0,)), ((), ()))
BF16 = jnp.bfloat16
F32 = jnp.float32


def dot(a, b, dims=NN):
    return lax.dot_general(a, b, dims, preferred_element_type=F32)


def window_order(levels, columns):
    windows, half = columns // WIN, WIN // 2
    order = []
    for window in range(windows):
        for sub in range(4):
            for level in range(levels):
                for row in range(half):
                    for column in range(half):
                        order.append(
                            (level * WIN + 2 * row + sub % 2) * columns
                            + window * WIN + 2 * column + sub // 2
                        )
    return np.eye(len(order), dtype=np.float32)[np.array(order)]


def group_order(levels, rows, columns):
    half = WIN // 2
    order = []
    for window_row in range(rows // half):
        for window in range(columns // half):
            for level in range(levels):
                for row in range(half):
                    for column in range(half):
                        order.append(
                            (level * rows + window_row * half + row) * columns
                            + window * half + column
                        )
    return np.eye(len(order), dtype=np.float32)[np.array(order)]


def head_masks():
    head = lax.broadcasted_iota(jnp.int32, (LANES, LANES), 1) // (LANES // 4)
    return [jnp.where(head == h, 1.0, 0.0).astype(BF16) for h in range(4)]


def region_bias(places, active):
    step = 2 * (WIN // 2)
    one = (lax.broadcasted_iota(jnp.int32, (places, places), 0) // step) % 2
    other = (lax.broadcasted_iota(jnp.int32, (places, places), 1) // step) % 2
    return jnp.where((one != other) & active, -1e30, 0.0)


def score_scale(channels):
    return float((channels // HEADS) ** -0.5 * np.log2(np.e))


def forward_kernel(
    edge, framed, merged_grad, order, group, rowmap, wqkv_h, wout_h, wm_h,
    normed_h, normt_h, proj_h, dmr_h, dmm_h, grad_h, rstd, merged, out_mine, out_theirs,
    wqkv, wout, wm, xw, normed, normt, proj, mixture, inverse, subs, dsubs, grad, dmr, dmm,
    in_sem, out_sem,
):
    tokens, channels = xw.shape
    places = 2 * WIN * WIN
    windows = tokens // places
    per_row = order.shape[0] // places
    quarter = places // 4
    groups = tokens // 4
    tile = 256

    loads = [
        pltpu.make_async_copy(src, dst, in_sem.at[i])
        for i, (src, dst) in enumerate([(wqkv_h, wqkv), (wout_h, wout), (wm_h, wm)])
    ]
    for load in loads:
        load.start()
    stores = [
        pltpu.make_async_copy(src, dst, out_sem.at[i])
        for i, (src, dst) in enumerate(
            [(normed, normed_h), (proj, proj_h), (normt, normt_h),
             (grad, grad_h), (dmr, dmr_h), (dmm, dmm_h)]
        )
    ]

    span = order.shape[0] // 2

    @pl.loop(0, windows)
    def _(w):
        wi, wj = w // per_row, w % per_row
        first = framed[pl.ds(pl.multiple_of(wi * span, 64), span)]
        second = framed[pl.ds(pl.multiple_of(tokens // 2 + wi * span, 64), span)]
        source = jnp.concatenate([first, second], axis=0)
        x = dot(order[pl.ds(pl.multiple_of(wj * places, places), places)], source)
        rows = pl.ds(pl.multiple_of(w * places, places), places)
        xw[rows] = x.astype(BF16)
        center = jnp.mean(x, axis=1, keepdims=True)
        moved = x - center
        scale = lax.rsqrt(jnp.mean(moved * moved, axis=1, keepdims=True) + EPSILON)
        rstd[rows] = jnp.broadcast_to(scale, (places, LANES))
        normed[rows] = (moved * scale).astype(BF16)

    stores[0].start()
    loads[0].wait()

    @pl.loop(0, wqkv.shape[1] // tile)
    def _(n):
        columns = pl.ds(pl.multiple_of(n * tile, tile), tile)
        proj[:, columns] = dot(normed[...], wqkv[:, columns]).astype(BF16)

    stores[1].start()

    masks = head_masks()
    factor = score_scale(channels)

    @pl.loop(0, windows)
    def _(w):
        rows = pl.ds(pl.multiple_of(w * places, places), places)
        bias = region_bias(places, (edge[0] == 1) & (w < per_row))
        for g in range(channels // LANES):
            lanes = pl.ds(g * LANES, LANES)
            q = proj[rows, lanes]
            k = proj[rows, pl.ds(channels + g * LANES, LANES)]
            v = proj[rows, pl.ds(2 * channels + g * LANES, LANES)]
            scores = dot(q, jnp.concatenate([k * m for m in masks], axis=0), NT)
            parts = []
            for h in range(4):
                part = scores[:, h * places:(h + 1) * places] * factor + bias
                part = part - jnp.max(part, axis=1, keepdims=True)
                parts.append(jnp.exp2(part).astype(BF16))
            values = jnp.concatenate(
                [jnp.concatenate([v * m, m], axis=1) for m in masks], axis=0
            )
            summed = dot(jnp.concatenate(parts, axis=1), values)
            inv = 1.0 / summed[:, LANES:]
            inverse[rows, lanes] = inv
            mixture[rows, lanes] = (summed[:, :LANES] * inv).astype(BF16)

    loads[1].wait()

    @pl.loop(0, channels // tile)
    def _(n):
        columns = pl.ds(pl.multiple_of(n * tile, tile), tile)
        out = dot(mixture[...], wout[:, columns]) + xw[:, columns].astype(F32)
        out = out.astype(BF16)
        for w in range(windows):
            for s in range(4):
                at = w * places + s * quarter
                subs[s, w * quarter:(w + 1) * quarter, columns] = out[at:at + quarter]

    total = jnp.zeros((groups, 1), F32)
    for s in range(4):
        total += jnp.sum(subs[s].astype(F32), axis=1, keepdims=True)
    center = total / (4 * channels)
    total = jnp.zeros((groups, 1), F32)
    for s in range(4):
        moved = subs[s].astype(F32) - center
        total += jnp.sum(moved * moved, axis=1, keepdims=True)
    scale = lax.rsqrt(total / (4 * channels) + EPSILON)
    loads[2].wait()
    result = jnp.zeros((groups, wm.shape[1]), F32)
    for s in range(4):
        unit = ((subs[s].astype(F32) - center) * scale).astype(BF16)
        result += dot(unit, wm[s * channels:(s + 1) * channels])
    merged[...] = dot(group[...], result.astype(BF16), TN).astype(BF16)

    cotangent = dot(group[...], merged_grad[...]).astype(BF16)
    mean_g = jnp.zeros((groups, 1), F32)
    mean_gx = jnp.zeros((groups, 1), F32)
    for s in range(4):
        d = dot(cotangent, wm[s * channels:(s + 1) * channels], NT).astype(BF16)
        dsubs[s] = d
        d = d.astype(F32)
        mean_g += jnp.sum(d, axis=1, keepdims=True)
        mean_gx += jnp.sum(d * ((subs[s].astype(F32) - center) * scale), axis=1, keepdims=True)
    mean_g = mean_g / (4 * channels)
    mean_gx = mean_gx / (4 * channels)
    for s in range(4):
        unit = (subs[s].astype(F32) - center) * scale
        d = (scale * (dsubs[s].astype(F32) - mean_g - unit * mean_gx)).astype(BF16)
        for w in range(windows):
            at = w * places + s * quarter
            grad[at:at + quarter] = d[w * quarter:(w + 1) * quarter]
    stores[3].start()

    @pl.loop(0, channels // tile)
    def _(n):
        columns = pl.ds(pl.multiple_of(n * tile, tile), tile)
        d = dot(grad[...], wout[columns], NT).astype(BF16).astype(F32)
        d = d * inverse[:, columns]
        dmr[:, columns] = d.astype(BF16)
        dmm[:, columns] = (-d * mixture[:, columns].astype(F32)).astype(BF16)

    stores[4].start()
    stores[5].start()

    @pl.loop(0, channels // tile)
    def _(n):
        rows = pl.ds(pl.multiple_of(n * tile, tile), tile)
        spot = lax.broadcasted_iota(jnp.int32, (tile, channels), 1)
        pick = jnp.where(spot == rowmap[rows], 1.0, 0.0).astype(BF16)
        normt[rows] = dot(pick, normed[...], NT).astype(BF16)
        turned = dot(pick, mixture[...], NT).astype(BF16)
        part = dot(turned, grad[...]).astype(BF16)

        @pl.when(n < channels // tile // 2)
        def _():
            out_mine[rows] = part

        @pl.when(n >= channels // tile // 2)
        def _():
            out_theirs[pl.ds(pl.multiple_of(n * tile - channels // 2, tile), tile)] = part

    stores[2].start()
    for store in stores:
        store.wait()


def backward_kernel(
    edge, q_ref, k_ref, v_ref, dmr, dmm, normt, pgrad, mine, theirs
):
    tokens, width = q_ref.shape
    channels = normt.shape[0]
    places = 2 * WIN * WIN
    windows = tokens // places
    per_row = windows // 2
    masks = head_masks()
    factor = score_scale(channels)
    plain = (channels // HEADS) ** -0.5

    @pl.loop(0, windows)
    def _(w):
        rows = pl.ds(pl.multiple_of(w * places, places), places)
        bias = region_bias(places, (edge[0] == 1) & (w < per_row))
        for g in range(width // LANES):
            lanes = pl.ds(g * LANES, LANES)
            q, k, v = q_ref[rows, lanes], k_ref[rows, lanes], v_ref[rows, lanes]
            dm, dd = dmr[rows, lanes], dmm[rows, lanes]
            keys = jnp.concatenate([k * m for m in masks], axis=0)
            scores = dot(keys, q, NT)
            values = jnp.concatenate(
                [jnp.concatenate([v * m, m], axis=1) for m in masks], axis=0
            )
            slope = dot(values, jnp.concatenate([dm, dd], axis=1), NT)
            weights, slopes = [], []
            for h in range(4):
                block = slice(h * places, (h + 1) * places)
                part = scores[block] * factor + bias
                part = jnp.exp2(part - jnp.max(part, axis=0, keepdims=True))
                weights.append(part.astype(BF16))
                slopes.append((part * slope[block]).astype(BF16))
            dv = dot(
                jnp.concatenate(weights, axis=1),
                jnp.concatenate([dm * m for m in masks], axis=0),
            )
            dk = dot(
                jnp.concatenate(slopes, axis=1),
                jnp.concatenate([q * m for m in masks], axis=0),
            )
            dq = dot(jnp.concatenate(slopes, axis=0), keys, TN)
            pgrad[rows, lanes] = (dq * plain).astype(BF16)
            pgrad[rows, pl.ds(width + g * LANES, LANES)] = (dk * plain).astype(BF16)
            pgrad[rows, pl.ds(2 * width + g * LANES, LANES)] = dv.astype(BF16)

    tile = 256

    @pl.loop(0, 3 * width // tile)
    def _(n):
        columns = pl.ds(pl.multiple_of(n * tile, tile), tile)
        half = channels // 2
        mine[:, columns] = dot(normt[:half], pgrad[:, columns]).astype(BF16)
        theirs[:, columns] = dot(normt[half:], pgrad[:, columns]).astype(BF16)


def input_kernel(chunks, *refs):
    pgrads = refs[:chunks]
    wqkv, normed, rstd, grad, order, out, ngrad, full = refs[chunks:]
    tokens, channels = normed.shape
    places = 2 * WIN * WIN
    windows = tokens // places
    width = channels // chunks
    tile = 256

    @pl.loop(0, channels // tile)
    def _(n):
        rows = pl.ds(pl.multiple_of(n * tile, tile), tile)
        total = jnp.zeros((tokens, tile), F32)
        for c in range(chunks):
            for part in range(3):
                total += dot(
                    pgrads[c][:, part * width:(part + 1) * width],
                    wqkv[rows, pl.ds(part * channels + c * width, width)],
                    NT,
                )
        ngrad[:, rows] = total.astype(BF16)

    @pl.loop(0, windows)
    def _(w):
        rows = pl.ds(pl.multiple_of(w * places, places), places)
        d = ngrad[rows].astype(F32)
        unit = normed[rows].astype(F32)
        mean_d = jnp.mean(d, axis=1, keepdims=True)
        mean_dx = jnp.mean(d * unit, axis=1, keepdims=True)
        part = rstd[rows, :1] * (d - mean_d - unit * mean_dx)
        full[rows] = (part.astype(BF16).astype(F32) + grad[rows].astype(F32)).astype(BF16)

    count = order.shape[0]
    for wi in range(tokens // count):
        moved = dot(order[...], full[wi * count:(wi + 1) * count], TN).astype(BF16)
        for level in range(2):
            at = level * (tokens // 2) + wi * (count // 2)
            out[at:at + count // 2] = moved[level * (count // 2):(level + 1) * (count // 2)]


def linear_route(sizes, lat_step, lon_step):
    n_lat, n_lon = sizes
    return [
        (a * n_lon + b, (a + lat_step) % n_lat * n_lon + (b + lon_step) % n_lon)
        for a in range(n_lat) for b in range(n_lon)
    ]


def sent(block, sizes, lat_step, lon_step):
    return lax.ppermute(block, ("lat", "lon"), linear_route(sizes, lat_step, lon_step))


def forward_move(field, width, sizes):
    kept_rows = field[:, :-width]
    last_rows = field[:, -width:]
    side = sent(kept_rows[:, :, -width:], sizes, 0, 1)
    above = sent(last_rows[:, :, :-width], sizes, 1, 0)
    corner = sent(last_rows[:, :, -width:], sizes, 1, 1)
    top = jnp.concatenate([corner, above], axis=2)
    rest = jnp.concatenate([side, kept_rows[:, :, :-width]], axis=2)
    return jnp.concatenate([top, rest], axis=1)


def backward_move(field, width, sizes):
    first_rows = field[:, :width]
    kept_rows = field[:, width:]
    side = sent(kept_rows[:, :, :width], sizes, 0, -1)
    below = sent(first_rows[:, :, width:], sizes, -1, 0)
    corner = sent(first_rows[:, :, :width], sizes, -1, -1)
    rest = jnp.concatenate([kept_rows[:, :, width:], side], axis=2)
    bottom = jnp.concatenate([below, corner], axis=2)
    return jnp.concatenate([rest, bottom], axis=1)


def bit_list(count):
    return [1 << i for i in range(count.bit_length() - 1)]


def device_rows(channels, sizes):
    n_lat, n_lon = sizes
    devices = n_lat * n_lon
    bits = bit_list(devices)
    rows = channels // devices
    place = np.arange(channels) // rows
    partner = np.zeros_like(place)
    for i, bit in enumerate(bits):
        partner |= np.where(place & (devices >> (i + 1)), bit, 0)
    me = lax.axis_index("lat") * n_lon + lax.axis_index("lon")
    owner = jnp.bitwise_xor(jnp.asarray(partner, jnp.int32), me.astype(jnp.int32))
    return (owner * rows + jnp.asarray(np.arange(channels) % rows, jnp.int32))[:, None]


def exchange(block, sizes, bit):
    devices = sizes[0] * sizes[1]
    return lax.ppermute(block, ("lat", "lon"), [(i, i ^ bit) for i in range(devices)])


def added(a, b, dtype=BF16):
    return (a.astype(F32) + b.astype(F32)).astype(dtype)


def halved(block, bits, bit, sizes, dtype=BF16):
    axis = bits.index(bit)
    kept = lax.index_in_dim(block, 0, axis, keepdims=False)
    given = lax.index_in_dim(block, 1, axis, keepdims=False)
    return added(kept, exchange(given, sizes, bit), dtype), [b for b in bits if b != bit]


def scattered_sum(mine, theirs, sizes):
    n_lat, n_lon = sizes
    lon_bits = bit_list(n_lon)
    lat_bits = [n_lon * b for b in bit_list(n_lat)]
    columns = mine.shape[1]
    rows = 2 * mine.shape[0] // (n_lat * n_lon)
    half = added(mine, exchange(theirs, sizes, lon_bits[0]))
    left = lon_bits[1:] + lat_bits
    parts = []
    for i, turn in enumerate((lon_bits[1:], lon_bits[:0:-1])):
        part = half[:, i * (columns // 2):(i + 1) * (columns // 2)]
        part = part.reshape([2] * len(left) + [rows, columns // 2])
        bits = left
        for bit in turn:
            part, bits = halved(part, bits, bit, sizes)
        parts.append(part)
    part = jnp.concatenate(parts, axis=-1)
    for bit in lat_bits:
        part, bits = halved(part, bits, bit, sizes, F32 if bit == lat_bits[-1] else BF16)
    return part


def shards(sizes, tokens, qkv_weight, out_weight, merge_weight, merged_grad):
    levels, lat_rows, lon_cols, channels = tokens.shape
    merged_width = merge_weight.shape[1]
    count = levels * lat_rows * lon_cols
    groups = count // 4
    half = channels // 2
    vmem = pl.BlockSpec(memory_space=pltpu.VMEM)
    smem = pl.BlockSpec(memory_space=pltpu.SMEM)
    hbm = pl.BlockSpec(memory_space=pl.ANY)

    order = jnp.asarray(window_order(levels, lon_cols), BF16)
    group = jnp.asarray(group_order(levels, lat_rows // 2, lon_cols // 2), BF16)
    edge = (lax.axis_index("lat") == 0).astype(jnp.int32).reshape(1)
    rowmap = device_rows(channels, sizes)

    framed = forward_move(tokens, SHIFT, sizes).reshape(count, channels)
    framed_grad = forward_move(merged_grad, HALF, sizes).reshape(groups, merged_width)

    wide = jax.ShapeDtypeStruct((count, channels), BF16)
    normed, normt, proj, dmr, dmm, grad, rstd, merged, out_mine, out_theirs = pl.pallas_call(
        forward_kernel,
        out_shape=[
            wide,
            jax.ShapeDtypeStruct((channels, count), BF16),
            jax.ShapeDtypeStruct((count, 3 * channels), BF16),
            wide, wide, wide,
            jax.ShapeDtypeStruct((count, LANES), F32),
            jax.ShapeDtypeStruct((groups, merged_width), BF16),
            jax.ShapeDtypeStruct((half, channels), BF16),
            jax.ShapeDtypeStruct((half, channels), BF16),
        ],
        in_specs=[smem] + [vmem] * 5 + [hbm] * 3,
        out_specs=[hbm] * 6 + [vmem] * 4,
        scratch_shapes=[
            pltpu.VMEM(qkv_weight.shape, BF16),
            pltpu.VMEM(out_weight.shape, BF16),
            pltpu.VMEM(merge_weight.shape, BF16),
            pltpu.VMEM((count, channels), BF16),
            pltpu.VMEM((count, channels), BF16),
            pltpu.VMEM((channels, count), BF16),
            pltpu.VMEM((count, 3 * channels), BF16),
            pltpu.VMEM((count, channels), BF16),
            pltpu.VMEM((count, channels), F32),
            pltpu.VMEM((4, groups, channels), BF16),
            pltpu.VMEM((4, groups, channels), BF16),
            pltpu.VMEM((count, channels), BF16),
            pltpu.VMEM((count, channels), BF16),
            pltpu.VMEM((count, channels), BF16),
            pltpu.SemaphoreType.DMA((3,)),
            pltpu.SemaphoreType.DMA((6,)),
        ],
        compiler_params=pltpu.CompilerParams(vmem_limit_bytes=58 * MIB),
        cost_estimate=pl.CostEstimate(
            flops=24 * count * channels * channels, bytes_accessed=34 * MIB, transcendentals=0
        ),
        name="block_forward",
    )(edge, framed, framed_grad, order, group, rowmap, qkv_weight, out_weight, merge_weight)

    merged = backward_move(
        merged.reshape(levels, lat_rows // 2, lon_cols // 2, merged_width), HALF, sizes
    )
    out_weight_grad = scattered_sum(out_mine, out_theirs, sizes)

    chunks = 2
    width = channels // chunks
    pgrads, qkv_parts = [], []
    for c in range(chunks):
        def columns(part, c=c):
            return pl.BlockSpec((count, width), lambda i: (0, part * chunks + c))

        pgrad, mine, theirs = pl.pallas_call(
            backward_kernel,
            grid=(1,),
            out_shape=[
                jax.ShapeDtypeStruct((count, 3 * width), BF16),
                jax.ShapeDtypeStruct((half, 3 * width), BF16),
                jax.ShapeDtypeStruct((half, 3 * width), BF16),
            ],
            in_specs=[smem, columns(0), columns(1), columns(2), columns(0), columns(0),
                      pl.BlockSpec((channels, count), lambda i: (0, 0))],
            out_specs=[
                pl.BlockSpec((count, 3 * width), lambda i: (0, 0)),
                pl.BlockSpec((half, 3 * width), lambda i: (0, 0)),
                pl.BlockSpec((half, 3 * width), lambda i: (0, 0)),
            ],
            compiler_params=pltpu.CompilerParams(vmem_limit_bytes=48 * MIB),
            cost_estimate=pl.CostEstimate(
                flops=8 * count * channels * channels, bytes_accessed=12 * MIB, transcendentals=0
            ),
            name="attention_backward",
        )(edge, proj, proj, proj, dmr, dmm, normt)
        pgrads.append(pgrad)
        qkv_parts.append(scattered_sum(mine, theirs, sizes))

    framed_out = pl.pallas_call(
        functools.partial(input_kernel, chunks),
        out_shape=wide,
        in_specs=[vmem] * (chunks + 5),
        out_specs=vmem,
        scratch_shapes=[pltpu.VMEM((count, channels), BF16)] * 2,
        compiler_params=pltpu.CompilerParams(vmem_limit_bytes=48 * MIB),
        cost_estimate=pl.CostEstimate(
            flops=7 * count * channels * channels, bytes_accessed=18 * MIB, transcendentals=0
        ),
        name="input_backward",
    )(*pgrads, qkv_weight, normed, rstd, grad, order)
    tokens_grad = backward_move(framed_out.reshape(tokens.shape), SHIFT, sizes)

    qkv_weight_grad = jnp.concatenate(
        [part[:, i * width:(i + 1) * width] for i in range(3) for part in qkv_parts], axis=1
    )
    return merged, tokens_grad, qkv_weight_grad, out_weight_grad


def solution(mesh):
    sizes = (mesh.shape["lat"], mesh.shape["lon"])
    in_specs = (P(None, "lat", "lon", None), P(), P(), P(), P(None, "lat", "lon", None))
    out_specs = (
        P(None, "lat", "lon", None),
        P(None, "lat", "lon", None),
        P(("lat", "lon"), None),
        P(("lat", "lon"), None),
    )
    return jax.shard_map(
        functools.partial(shards, sizes),
        mesh=mesh, in_specs=in_specs, out_specs=out_specs, check_vma=False,
    )
```

time: 547 us -> 202 us (0.37)
  local copies, waits for them, and re-layouts: 202 us -> 15.6 us
  waiting for transfers between devices: 165 us -> 56.8 us
  matrix products: 103 us -> 0 us
  Pallas kernels: 0 us -> 83.3 us
  other arithmetic: 50.9 us -> 8.64 us
  starting transfers between devices: 6.72 us -> 36.2 us
  between operations: 15.1 us -> 1.22 us
    reduce_scatter x2 -> x0, waiting for transfers between devices: 127 us -> none  [the longest x1 127 us: shards(): lax.psum_scatter(qkv_terms, ('lat', 'lon'), scatter_dimension=0, tiled=True)]
    dot_general x14 -> x0, matrix products: 103 us -> none  [the longest x3 29.5 us: window_attention(): jnp.einsum('bqhd,bkhd->bhqk', queries, keys_part, preferred_element_type=...]
    pallas_call x0 -> x4, Pallas kernels: none -> 83.3 us  [the longest x1 38.4 us: shards(): pl.pallas_call(forward_kernel, out_shape=[wide, jax.ShapeDtypeStruct((cha...]
    reshape x7 -> x2, local copies, waits for them, and re-layouts: 65.5 us -> 1.92 us  [the longest x1 1.09 us: shards(): merged.reshape(levels, lat_rows // 2, lon_cols // 2, merged_width)]
    convert_element_type x5 -> x0, local copies, waits for them, and re-layouts: 31.2 us -> none  [the longest x3 15.3 us: normalize(): values = grid_field.astype(jnp.float32)]
    unnamed x71 -> x32, local copies, waits for them, and re-layouts: 35.7 us -> 4.49 us
    ppermute x8 -> x33, starting transfers between devices: 6.64 us -> 36.2 us  [the longest x21 21.9 us: exchange(): lax.ppermute(block, ('lat', 'lon'), [(i, i ^ bit) for i in range(devices)])]
    add_any x1 -> x0, local copies, waits for them, and re-layouts: 25.8 us -> none  [window_attention(): queries = pieces[:, :, 0]]
  transfers between devices with their start and end apart: 10 -> 33, of which waited for: 7 -> 18; matrix products, arithmetic and copies ran while one was open for 34% -> 8% of each run, Pallas kernels for 0% -> 22%
where the time goes in v1:
time: 202 us
  Pallas kernels  83.3 us (41%)
  waiting for transfers between devices  56.8 us (28%)
  starting transfers between devices  36.2 us (18%)
  local copies, waits for them, and re-layouts  15.6 us (8%)
  other arithmetic  8.64 us (4%)
    ppermute x21, waiting for transfers between devices, exchange(): lax.ppermute(block, ('lat', 'lon'), [(i, i ^ bit) for i in range(devices)])  42.8 us
    pallas_call x1, Pallas kernels, shards(): pl.pallas_call(forward_kernel, out_shape=[wide, jax.ShapeDtypeStruct((cha...  38.4 us
    pallas_call x2, Pallas kernels, shards(): pl.pallas_call(backward_kernel, grid=(1,), out_shape=[jax.ShapeDtypeStruc...  32.2 us
    ppermute x21, starting transfers between devices, exchange(): lax.ppermute(block, ('lat', 'lon'), [(i, i ^ bit) for i in range(devices)])  21.9 us
    ppermute x12, starting transfers between devices, sent(): lax.ppermute(block, ('lat', 'lon'), linear_route(sizes, lat_step, lon_step))  14.3 us
    ppermute x12, waiting for transfers between devices, sent(): lax.ppermute(block, ('lat', 'lon'), linear_route(sizes, lat_step, lon_step))  14 us
    pallas_call x1, Pallas kernels, shards(): pl.pallas_call(functools.partial(input_kernel, chunks), out_shape=wide, i...  12.8 us
    unnamed x32, local copies, waits for them, and re-layouts  4.49 us
  transfers between devices with their start and end apart: 33, of which 18 were waited for; matrix products, arithmetic and copies ran while one was open for 8% of the time, Pallas kernels for 22%

profile of v1, /device:TPU:0, one launch (start us, length us, event | category | flops | bytes accessed | tf_op | source)
XLA Modules:
  0.0 201.8 jit_solution(4500459132481182597)
XLA Ops:
  1.8 3.1 %collective-permute-start.1 = (bf16[2,4,20,1024]{3,2,1,0:T(8,128)(2,1)S(1)}, bf16[2,4,20,1024]{3,2,1,0:T(8,128)(2,1)}, u32[]{:S(2)}, u32[]{:S(2)}) collective-permute-start(bf16[2,4,20,1024]{3,2,1,0:T(8,128)(2,1)S(1)} %slice.223), channel_id=1, source_target_pairs={{0,8},{1,9},{2,10},{3,11},{4,12},{5,13},{6,14},{7,15},{8,16},{9,17... | collective-permute-start | bytes 983048 | tf_op jit(solution)/shard_map/ppermute | solution.py:342
  4.9 1.8 slice.224
  8.3 2.7 %collective-permute-start = (bf16[2,4,4,1024]{3,2,1,0:T(4,128)(2,1)}, bf16[2,4,4,1024]{3,2,1,0:T(4,128)(2,1)}, u32[]{:S(2)}, u32[]{:S(2)}) collective-permute-start(bf16[2,4,4,1024]{3,2,1,0:T(4,128)(2,1)} %slice.222), channel_id=1, source_target_pairs={{0,9},{1,10},{2,11},{3,12},{4,13},{5,14},{6,15},{7,8},{8,17},{9,18... | collective-permute-start | bytes 196616 | tf_op jit(solution)/shard_map/ppermute | solution.py:342
  17.1 5.9 %collective-permute-done.3 = bf16[2,2,2,1024]{3,2,1,0:T(2,128)(2,1)} collective-permute-done((bf16[2,2,2,1024]{3,2,1,0:T(2,128)(2,1)}, bf16[2,2,2,1024]{3,2,1,0:T(2,128)(2,1)}, u32[]{:S(2)}, u32[]{:S(2)}) %collective-permute-start.3) | collective-permute-done | bytes 16416 | tf_op jit(solution)/shard_map/ppermute | solution.py:342
  24.0 3.5 %collective-permute-done.5 = bf16[2,6,2,1024]{3,1,2,0:T(8,128)(2,1)S(1)} collective-permute-done((bf16[2,6,2,1024]{3,1,2,0:T(8,128)(2,1)S(1)}, bf16[2,6,2,1024]{3,1,2,0:T(8,128)(2,1)S(1)}, u32[]{:S(2)}, u32[]{:S(2)}) %collective-permute-start.5) | collective-permute-done | bytes 49184 | tf_op jit(solution)/shard_map/ppermute | solution.py:342
  28.8 3.0 %maximum_maximum_fusion = bf16[2,16,24,1024]{3,2,1,0:T(8,128)(2,1)} fusion(bf16[2,12,20,1024]{3,2,1,0:T(8,128)(2,1)S(1)} %slice.225, bf16[2,12,4,1024]{3,2,1,0:T(4,128)(2,1)} %collective-permute-done.2, bf16[2,4,20,1024]{3,2,1,0:T(8,128)(2,1)} %collective-permute-done.1, bf16[2,4,4,1024]{3,2,1,0:T(4,128)(2,1)} %collective-permute-done), kind=kLoop, calls=%fused_computation.3 | loop fusion | flops 6291456 | bytes 3145728 | tf_op jit(solution)/shard_map/concatenate | solution.py:353
  31.8 38.4 %block_forward.1 = (bf16[768,1024]{1,0:T(8,128)(2,1)}, bf16[1024,768]{1,0:T(8,128)(2,1)}, bf16[768,3072]{1,0:T(8,128)(2,1)}, bf16[768,1024]{1,0:T(8,128)(2,1)}, ...) custom-call(s32[1]{0:T(128)} %bitcast.edge, ...), custom_call_target="tpu_custom_call" | custom-call | flops 19327352832 | bytes 35651584 | tf_op jit(solution)/shard_map/block_forward/pallas_call | solution.py:442
  73.6 16.0 %attention_backward.3 = (bf16[768,1536]{1,0:T(8,128)(2,1)}, bf16[512,1536]{1,0:T(8,128)(2,1)S(1)}, bf16[512,1536]{1,0:T(8,128)(2,1)S(1)}) custom-call(s32[1]{0:T(128)} %bitcast.edge, bf16[768,3072]{1,0:T(8,128)(2,1)} %get-tuple-element.21.q_ref.k_ref.v_ref, bf16[768,3072]{1,0:T(8,128)(2,1)} %get-tuple-element.21.q_ref.k_ref.v_ref, ...), custom_call_target="tpu_custom_call" | custom-call | flops 6442450944 | bytes 12582912 | tf_op jit(solution)/shard_map/attention_backward/pallas_call | solution.py:493
  89.7 16.1 %attention_backward.2 = (bf16[768,1536]{1,0:T(8,128)(2,1)}, bf16[512,1536]{1,0:T(8,128)(2,1)S(1)}, bf16[512,1536]{1,0:T(8,128)(2,1)S(1)}) custom-call(s32[1]{0:T(128)} %bitcast.edge, bf16[768,3072]{1,0:T(8,128)(2,1)} %get-tuple-element.21.q_ref.k_ref.v_ref, bf16[768,3072]{1,0:T(8,128)(2,1)} %get-tuple-element.21.q_ref.k_ref.v_ref, ...), custom_call_target="tpu_custom_call" | custom-call | flops 6442450944 | bytes 12582912 | tf_op jit(solution)/shard_map/attention_backward/pallas_call | solution.py:493
  105.9 12.8 %input_backward.1 = bf16[768,1024]{1,0:T(8,128)(2,1)S(1)} custom-call(bf16[768,1536]{1,0:T(8,128)(2,1)} %get-tuple-element.25.refs_0_, bf16[768,1536]{1,0:T(8,128)(2,1)} %get-tuple-element.26.refs_1_, bf16[1024,3072]{1,0:T(8,128)(2,1)} %refs_2_.1, bf16[768,1024]{1,0:T(8,128)(2,1)S(1)} %copy-done.1, f32[768,128]{1,0:T(8,128)S(1)} %copy-done.5, ...), custom_call_target="tpu_custom_call" | custom-call | flops 5637144576 | bytes 18874368 | tf_op jit(solution)/shard_map/input_backward/pallas_call | solution.py:517
  120.6 2.2 %collective-permute-start.9 = (bf16[2,12,4,1024]{3,2,1,0:T(4,128)(2,1)S(1)}, bf16[2,12,4,1024]{3,2,1,0:T(4,128)(2,1)S(1)}, u32[]{:S(2)}, u32[]{:S(2)}) collective-permute-start(bf16[2,12,4,1024]{3,2,1,0:T(4,128)(2,1)S(1)} %slice.288), channel_id=1, source_target_pairs={{0,7},{1,0},{2,1},{3,2},{4,3},{5,4},{6,5},{7,6},{8,15},{9,8},{10,9... | collective-permute-start | bytes 589832 | tf_op jit(solution)/shard_map/ppermute | solution.py:342
  123.9 3.5 %collective-permute-start.11 = (bf16[2,4,4,1024]{3,2,1,0:T(4,128)(2,1)S(1)}, bf16[2,4,4,1024]{3,2,1,0:T(4,128)(2,1)S(1)}, u32[]{:S(2)}, u32[]{:S(2)}) collective-permute-start(bf16[2,4,4,1024]{3,2,1,0:T(4,128)(2,1)S(1)} %slice.290), channel_id=1, source_target_pairs={{0,31},{1,24},{2,25},{3,26},{4,27},{5,28},{6,29},{7,30},{8,7},{9,0... | collective-permute-start | bytes 196616 | tf_op jit(solution)/shard_map/ppermute | solution.py:342
  127.8 4.7 %collective-permute-done.11 = bf16[2,4,4,1024]{3,2,1,0:T(4,128)(2,1)S(1)} collective-permute-done((bf16[2,4,4,1024]{3,2,1,0:T(4,128)(2,1)S(1)}, bf16[2,4,4,1024]{3,2,1,0:T(4,128)(2,1)S(1)}, u32[]{:S(2)}, u32[]{:S(2)}) %collective-permute-start.11) | collective-permute-done | bytes 65568 | tf_op jit(solution)/shard_map/ppermute | solution.py:342
  132.5 1.7 collective-permute-start.27
  137.0 4.2 %collective-permute-done.27 = bf16[2,2,2,32,512]{4,3,2,1,0:T(8,128)(2,1)S(1)} collective-permute-done((bf16[2,2,2,32,512]{4,3,2,1,0:T(8,128)(2,1)S(1)}, bf16[2,2,2,32,512]{4,3,2,1,0:T(8,128)(2,1)S(1)}, u32[]{:S(2)}, u32[]{:S(2)}) %collective-permute-start.27) | collective-permute-done | bytes 262176 | tf_op jit(solution)/shard_map/ppermute | solution.py:387
  142.6 1.9 collective-permute-done.29
  145.2 2.1 %collective-permute-done.28 = bf16[2,2,32,512]{3,2,1,0:T(8,128)(2,1)S(1)} collective-permute-done((bf16[2,2,32,512]{3,2,1,0:T(8,128)(2,1)S(1)}, bf16[2,2,32,512]{3,2,1,0:T(8,128)(2,1)S(1)}, u32[]{:S(2)}, u32[]{:S(2)}) %collective-permute-start.28) | collective-permute-done | bytes 131104 | tf_op jit(solution)/shard_map/ppermute | solution.py:387
  147.4 2.4 %collective-permute-done.30 = bf16[2,2,32,512]{3,2,1,0:T(8,128)(2,1)S(1)} collective-permute-done((bf16[2,2,32,512]{3,2,1,0:T(8,128)(2,1)S(1)}, bf16[2,2,32,512]{3,2,1,0:T(8,128)(2,1)S(1)}, u32[]{:S(2)}, u32[]{:S(2)}) %collective-permute-start.30) | collective-permute-done | bytes 131104 | tf_op jit(solution)/shard_map/ppermute | solution.py:387
  149.8 1.6 collective-permute-start.31
  152.5 2.3 %collective-permute-done.31 = bf16[2,32,1024]{2,1,0:T(8,128)(2,1)S(1)} collective-permute-done((bf16[2,32,1024]{2,1,0:T(8,128)(2,1)S(1)}, bf16[2,32,1024]{2,1,0:T(8,128)(2,1)S(1)}, u32[]{:S(2)}, u32[]{:S(2)}) %collective-permute-start.31) | collective-permute-done | bytes 131104 | tf_op jit(solution)/shard_map/ppermute | solution.py:387
  154.9 2.8 %collective-permute-start.32 = (bf16[32,1024]{1,0:T(8,128)(2,1)S(1)}, bf16[32,1024]{1,0:T(8,128)(2,1)S(1)}, u32[]{:S(2)}, u32[]{:S(2)}) collective-permute-start(bf16[32,1024]{1,0:T(8,128)(2,1)S(1)} %slice_bitcast_fusion.22), channel_id=1, source_target_pairs={{0,16},{1,17},{2,18},{3,19},{4,20},{5,21},{6,22},{7,23},{8,24},{9,... | collective-permute-start | bytes 196616 | tf_op jit(solution)/shard_map/ppermute | solution.py:387
  160.2 1.8 collective-permute-start.15
  162.6 7.1 %collective-permute-done.20 = bf16[2,2,2,32,768]{4,3,2,1,0:T(8,128)(2,1)S(1)} collective-permute-done((bf16[2,2,2,32,768]{4,3,2,1,0:T(8,128)(2,1)S(1)}, bf16[2,2,2,32,768]{4,3,2,1,0:T(8,128)(2,1)S(1)}, u32[]{:S(2)}, u32[]{:S(2)}) %collective-permute-start.20) | collective-permute-done | bytes 393248 | tf_op jit(solution)/shard_map/ppermute | solution.py:387
  170.6 1.7 collective-permute-start.23
  172.2 6.0 %collective-permute-done.13 = bf16[2,2,2,32,768]{4,3,2,1,0:T(8,128)(2,1)S(1)} collective-permute-done((bf16[2,2,2,32,768]{4,3,2,1,0:T(8,128)(2,1)S(1)}, bf16[2,2,2,32,768]{4,3,2,1,0:T(8,128)(2,1)S(1)}, u32[]{:S(2)}, u32[]{:S(2)}) %collective-permute-start.13) | collective-permute-done | bytes 393248 | tf_op jit(solution)/shard_map/ppermute | solution.py:387
  179.0 1.7 collective-permute-start.16
  180.7 3.4 %collective-permute-done.14 = bf16[2,2,32,768]{3,2,1,0:T(8,128)(2,1)S(1)} collective-permute-done((bf16[2,2,32,768]{3,2,1,0:T(8,128)(2,1)S(1)}, bf16[2,2,32,768]{3,2,1,0:T(8,128)(2,1)S(1)}, u32[]{:S(2)}, u32[]{:S(2)}) %collective-permute-start.14) | collective-permute-done | bytes 196640 | tf_op jit(solution)/shard_map/ppermute | solution.py:387
  185.5 1.6 collective-permute-start.24
  187.1 5.1 %collective-permute-done.17 = bf16[2,32,1536]{2,1,0:T(8,128)(2,1)S(1)} collective-permute-done((bf16[2,32,1536]{2,1,0:T(8,128)(2,1)S(1)}, bf16[2,32,1536]{2,1,0:T(8,128)(2,1)S(1)}, u32[]{:S(2)}, u32[]{:S(2)}) %collective-permute-start.17) | collective-permute-done | bytes 196640 | tf_op jit(solution)/shard_map/ppermute | solution.py:387
  193.0 1.8 collective-permute-done.24
  195.4 3.2 %collective-permute-done.18 = bf16[32,1536]{1,0:T(8,128)(2,1)S(1)} collective-permute-done((bf16[32,1536]{1,0:T(8,128)(2,1)S(1)}, bf16[32,1536]{1,0:T(8,128)(2,1)S(1)}, u32[]{:S(2)}, u32[]{:S(2)}) %collective-permute-start.18) | collective-permute-done | bytes 98336 | tf_op jit(solution)/shard_map/ppermute | solution.py:387
  198.7 2.3 %collective-permute-done.25 = bf16[32,1536]{1,0:T(8,128)(2,1)S(1)} collective-permute-done((bf16[32,1536]{1,0:T(8,128)(2,1)S(1)}, bf16[32,1536]{1,0:T(8,128)(2,1)S(1)}, u32[]{:S(2)}, u32[]{:S(2)}) %collective-permute-start.25) | collective-permute-done | bytes 98336 | tf_op jit(solution)/shard_map/ppermute | solution.py:387
  (140 shorter events, 32.3 us)
Async XLA Ops:
  1.8 27.0 %collective-permute-start.1 = (bf16[2,4,20,1024]{3,2,1,0:T(8,128)(2,1)S(1)}, bf16[2,4,20,1024]{3,2,1,0:T(8,128)(2,1)}, u32[]{:S(2)}, u32[]{:S(2)}) collective-permute-start(bf16[2,4,20,1024]{3,2,1,0:T(8,128)(2,1)S(1)} %slice.223), channel_id=1, source_target_pairs={{0,8},{1,9},{2,10},{3,11},{4,12},{5,13},{6,14},{7,15},{8,16},{9,17... | collective-permute-start | bytes 983048 | tf_op jit(solution)/shard_map/ppermute | solution.py:342
  6.7 22.1 %collective-permute-start.2 = (bf16[2,12,4,1024]{3,2,1,0:T(4,128)(2,1)}, bf16[2,12,4,1024]{3,2,1,0:T(4,128)(2,1)}, u32[]{:S(2)}, u32[]{:S(2)}) collective-permute-start(bf16[2,12,4,1024]{3,2,1,0:T(4,128)(2,1)} %slice.224), channel_id=1, source_target_pairs={{0,1},{1,2},{2,3},{3,4},{4,5},{5,6},{6,7},{7,0},{8,9},{9,10},{10,1... | collective-permute-start | bytes 589832 | tf_op jit(solution)/shard_map/ppermute | solution.py:342
  8.3 20.5 %collective-permute-start = (bf16[2,4,4,1024]{3,2,1,0:T(4,128)(2,1)}, bf16[2,4,4,1024]{3,2,1,0:T(4,128)(2,1)}, u32[]{:S(2)}, u32[]{:S(2)}) collective-permute-start(bf16[2,4,4,1024]{3,2,1,0:T(4,128)(2,1)} %slice.222), channel_id=1, source_target_pairs={{0,9},{1,10},{2,11},{3,12},{4,13},{5,14},{6,15},{7,8},{8,17},{9,18... | collective-permute-start | bytes 196616 | tf_op jit(solution)/shard_map/ppermute | solution.py:342
  12.8 10.1 %collective-permute-start.4 = (bf16[2,2,10,1024]{3,2,1,0:T(8,128)(2,1)}, bf16[2,2,10,1024]{3,2,1,0:T(8,128)(2,1)}, u32[]{:S(2)}, u32[]{:S(2)}) collective-permute-start(bf16[2,2,10,1024]{3,2,1,0:T(8,128)(2,1)} %copy.46), channel_id=1, source_target_pairs={{0,8},{1,9},{2,10},{3,11},{4,12},{5,13},{6,14},{7,15},{8,16},{9,17... | collective-permute-start | bytes 245768 | tf_op jit(solution)/shard_map/ppermute | solution.py:342
  15.8 7.1 %collective-permute-start.3 = (bf16[2,2,2,1024]{3,2,1,0:T(2,128)(2,1)}, bf16[2,2,2,1024]{3,2,1,0:T(2,128)(2,1)}, u32[]{:S(2)}, u32[]{:S(2)}) collective-permute-start(bf16[2,2,2,1024]{3,2,1,0:T(2,128)(2,1)} %copy.45), channel_id=1, source_target_pairs={{0,9},{1,10},{2,11},{3,12},{4,13},{5,14},{6,15},{7,8},{8,17},{9,18... | collective-permute-start | bytes 49160 | tf_op jit(solution)/shard_map/ppermute | solution.py:342
  71.4 52.5 %collective-permute-start.26 = (bf16[512,1024]{1,0:T(8,128)(2,1)}, bf16[512,1024]{1,0:T(8,128)(2,1)S(1)}, u32[]{:S(2)}, u32[]{:S(2)}) collective-permute-start(bf16[512,1024]{1,0:T(8,128)(2,1)} %get-tuple-element.35), channel_id=1, source_target_pairs={{0,1},{1,0},{2,3},{3,2},{4,5},{5,4},{6,7},{7,6},{8,9},{9,8},{10,11... | collective-permute-start | bytes 3145736 | tf_op jit(solution)/shard_map/ppermute | solution.py:387
  71.4 49.1 %collective-permute-start.7 = (bf16[2,2,10,1024]{3,2,1,0:T(8,128)(2,1)S(1)}, bf16[2,2,10,1024]{3,2,1,0:T(8,128)(2,1)S(1)}, u32[]{:S(2)}, u32[]{:S(2)}) collective-permute-start(bf16[2,2,10,1024]{3,2,1,0:T(8,128)(2,1)S(1)} %slice.285), channel_id=1, source_target_pairs={{0,24},{1,25},{2,26},{3,27},{4,28},{5,29},{6,30},{7,31},{8,0},{9,1... | collective-permute-start | bytes 245768 | tf_op jit(solution)/shard_map/ppermute | solution.py:342
  72.2 47.9 %collective-permute-start.6 = (bf16[2,6,2,1024]{3,2,1,0:T(2,128)(2,1)S(1)}, bf16[2,6,2,1024]{3,2,1,0:T(2,128)(2,1)S(1)}, u32[]{:S(2)}, u32[]{:S(2)}) collective-permute-start(bf16[2,6,2,1024]{3,2,1,0:T(2,128)(2,1)S(1)} %slice.284), channel_id=1, source_target_pairs={{0,7},{1,0},{2,1},{3,2},{4,3},{5,4},{6,5},{7,6},{8,15},{9,8},{10,9... | collective-permute-start | bytes 147464 | tf_op jit(solution)/shard_map/ppermute | solution.py:342
  72.2 47.8 %collective-permute-start.8 = (bf16[2,2,2,1024]{3,2,1,0:T(2,128)(2,1)S(1)}, bf16[2,2,2,1024]{3,2,1,0:T(2,128)(2,1)S(1)}, u32[]{:S(2)}, u32[]{:S(2)}) collective-permute-start(bf16[2,2,2,1024]{3,2,1,0:T(2,128)(2,1)S(1)} %slice.286), channel_id=1, source_target_pairs={{0,31},{1,24},{2,25},{3,26},{4,27},{5,28},{6,29},{7,30},{8,7},{9,0... | collective-permute-start | bytes 49160 | tf_op jit(solution)/shard_map/ppermute | solution.py:342
  119.4 32.1 %collective-permute-start.19 = (bf16[512,1536]{1,0:T(8,128)(2,1)S(1)}, bf16[512,1536]{1,0:T(8,128)(2,1)S(1)}, u32[]{:S(2)}, u32[]{:S(2)}) collective-permute-start(bf16[512,1536]{1,0:T(8,128)(2,1)S(1)} %get-tuple-element.33), channel_id=1, source_target_pairs={{0,1},{1,0},{2,3},{3,2},{4,5},{5,4},{6,7},{7,6},{8,9},{9,8},{10,11... | collective-permute-start | bytes 4718600 | tf_op jit(solution)/shard_map/ppermute | solution.py:387
  120.0 32.0 %collective-permute-start.12 = (bf16[512,1536]{1,0:T(8,128)(2,1)S(1)}, bf16[512,1536]{1,0:T(8,128)(2,1)S(1)}, u32[]{:S(2)}, u32[]{:S(2)}) collective-permute-start(bf16[512,1536]{1,0:T(8,128)(2,1)S(1)} %get-tuple-element.31), channel_id=1, source_target_pairs={{0,1},{1,0},{2,3},{3,2},{4,5},{5,4},{6,7},{7,6},{8,9},{9,8},{10,11... | collective-permute-start | bytes 4718600 | tf_op jit(solution)/shard_map/ppermute | solution.py:387
  120.1 14.1 %collective-permute-start.10 = (bf16[2,4,20,1024]{3,2,1,0:T(8,128)(2,1)S(1)}, bf16[2,4,20,1024]{3,2,1,0:T(8,128)(2,1)S(1)}, u32[]{:S(2)}, u32[]{:S(2)}) collective-permute-start(bf16[2,4,20,1024]{3,2,1,0:T(8,128)(2,1)S(1)} %slice.289), channel_id=1, source_target_pairs={{0,24},{1,25},{2,26},{3,27},{4,28},{5,29},{6,30},{7,31},{8,0},{9,1... | collective-permute-start | bytes 983048 | tf_op jit(solution)/shard_map/ppermute | solution.py:342
  120.6 13.6 %collective-permute-start.9 = (bf16[2,12,4,1024]{3,2,1,0:T(4,128)(2,1)S(1)}, bf16[2,12,4,1024]{3,2,1,0:T(4,128)(2,1)S(1)}, u32[]{:S(2)}, u32[]{:S(2)}) collective-permute-start(bf16[2,12,4,1024]{3,2,1,0:T(4,128)(2,1)S(1)} %slice.288), channel_id=1, source_target_pairs={{0,7},{1,0},{2,1},{3,2},{4,3},{5,4},{6,5},{7,6},{8,15},{9,8},{10,9... | collective-permute-start | bytes 589832 | tf_op jit(solution)/shard_map/ppermute | solution.py:342
  123.9 8.6 %collective-permute-start.11 = (bf16[2,4,4,1024]{3,2,1,0:T(4,128)(2,1)S(1)}, bf16[2,4,4,1024]{3,2,1,0:T(4,128)(2,1)S(1)}, u32[]{:S(2)}, u32[]{:S(2)}) collective-permute-start(bf16[2,4,4,1024]{3,2,1,0:T(4,128)(2,1)S(1)} %slice.290), channel_id=1, source_target_pairs={{0,31},{1,24},{2,25},{3,26},{4,27},{5,28},{6,29},{7,30},{8,7},{9,0... | collective-permute-start | bytes 196616 | tf_op jit(solution)/shard_map/ppermute | solution.py:342
  132.5 8.7 %collective-permute-start.27 = (bf16[2,2,2,32,512]{4,3,2,1,0:T(8,128)(2,1)S(1)}, bf16[2,2,2,32,512]{4,3,2,1,0:T(8,128)(2,1)S(1)}, u32[]{:S(2)}, u32[]{:S(2)}) collective-permute-start(bf16[2,2,2,32,512]{4,3,2,1,0:T(8,128)(2,1)S(1)} %bitcast.149), channel_id=1, source_target_pairs={{0,2},{1,3},{2,0},{3,1},{4,6},{5,7},{6,4},{7,5},{8,10},{9,11},{10,... | collective-permute-start | bytes 786440 | tf_op jit(solution)/shard_map/ppermute | solution.py:387
  135.7 8.8 %collective-permute-start.29 = (bf16[2,2,2,32,512]{4,3,2,1,0:T(8,128)(2,1)S(1)}, bf16[2,2,2,32,512]{4,3,2,1,0:T(8,128)(2,1)S(1)}, u32[]{:S(2)}, u32[]{:S(2)}) collective-permute-start(bf16[2,2,2,32,512]{4,3,2,1,0:T(8,128)(2,1)S(1)} %slice_bitcast_fusion.4), channel_id=1, source_target_pairs={{0,4},{1,5},{2,6},{3,7},{4,0},{5,1},{6,2},{7,3},{8,12},{9,13},{10,... | collective-permute-start | bytes 786440 | tf_op jit(solution)/shard_map/ppermute | solution.py:387
  141.3 6.1 %collective-permute-start.28 = (bf16[2,2,32,512]{3,2,1,0:T(8,128)(2,1)S(1)}, bf16[2,2,32,512]{3,2,1,0:T(8,128)(2,1)S(1)}, u32[]{:S(2)}, u32[]{:S(2)}) collective-permute-start(bf16[2,2,32,512]{3,2,1,0:T(8,128)(2,1)S(1)} %slice_bitcast_fusion.16), channel_id=1, source_target_pairs={{0,4},{1,5},{2,6},{3,7},{4,0},{5,1},{6,2},{7,3},{8,12},{9,13},{10,... | collective-permute-start | bytes 393224 | tf_op jit(solution)/shard_map/ppermute | solution.py:387
  144.6 5.2 %collective-permute-start.30 = (bf16[2,2,32,512]{3,2,1,0:T(8,128)(2,1)S(1)}, bf16[2,2,32,512]{3,2,1,0:T(8,128)(2,1)S(1)}, u32[]{:S(2)}, u32[]{:S(2)}) collective-permute-start(bf16[2,2,32,512]{3,2,1,0:T(8,128)(2,1)S(1)} %slice_bitcast_fusion.14), channel_id=1, source_target_pairs={{0,2},{1,3},{2,0},{3,1},{4,6},{5,7},{6,4},{7,5},{8,10},{9,11},{10,... | collective-permute-start | bytes 393224 | tf_op jit(solution)/shard_map/ppermute | solution.py:387
  149.8 5.0 %collective-permute-start.31 = (bf16[2,32,1024]{2,1,0:T(8,128)(2,1)S(1)}, bf16[2,32,1024]{2,1,0:T(8,128)(2,1)S(1)}, u32[]{:S(2)}, u32[]{:S(2)}) collective-permute-start(bf16[2,32,1024]{2,1,0:T(8,128)(2,1)S(1)} %fusion.23), channel_id=1, source_target_pairs={{0,8},{1,9},{2,10},{3,11},{4,12},{5,13},{6,14},{7,15},{8,0},{9,1},... | collective-permute-start | bytes 393224 | tf_op jit(solution)/shard_map/ppermute | solution.py:387
  154.9 7.1 %collective-permute-start.32 = (bf16[32,1024]{1,0:T(8,128)(2,1)S(1)}, bf16[32,1024]{1,0:T(8,128)(2,1)S(1)}, u32[]{:S(2)}, u32[]{:S(2)}) collective-permute-start(bf16[32,1024]{1,0:T(8,128)(2,1)S(1)} %slice_bitcast_fusion.22), channel_id=1, source_target_pairs={{0,16},{1,17},{2,18},{3,19},{4,20},{5,21},{6,22},{7,23},{8,24},{9,... | collective-permute-start | bytes 196616 | tf_op jit(solution)/shard_map/ppermute | solution.py:387
  157.7 12.1 %collective-permute-start.20 = (bf16[2,2,2,32,768]{4,3,2,1,0:T(8,128)(2,1)S(1)}, bf16[2,2,2,32,768]{4,3,2,1,0:T(8,128)(2,1)S(1)}, u32[]{:S(2)}, u32[]{:S(2)}) collective-permute-start(bf16[2,2,2,32,768]{4,3,2,1,0:T(8,128)(2,1)S(1)} %bitcast.148), channel_id=1, source_target_pairs={{0,2},{1,3},{2,0},{3,1},{4,6},{5,7},{6,4},{7,5},{8,10},{9,11},{10,... | collective-permute-start | bytes 1179656 | tf_op jit(solution)/shard_map/ppermute | solution.py:387
  158.3 12.1 %collective-permute-start.22 = (bf16[2,2,2,32,768]{4,3,2,1,0:T(8,128)(2,1)S(1)}, bf16[2,2,2,32,768]{4,3,2,1,0:T(8,128)(2,1)S(1)}, u32[]{:S(2)}, u32[]{:S(2)}) collective-permute-start(bf16[2,2,2,32,768]{4,3,2,1,0:T(8,128)(2,1)S(1)} %slice_bitcast_fusion), channel_id=1, source_target_pairs={{0,4},{1,5},{2,6},{3,7},{4,0},{5,1},{6,2},{7,3},{8,12},{9,13},{10,... | collective-permute-start | bytes 1179656 | tf_op jit(solution)/shard_map/ppermute | solution.py:387
  159.9 18.3 %collective-permute-start.13 = (bf16[2,2,2,32,768]{4,3,2,1,0:T(8,128)(2,1)S(1)}, bf16[2,2,2,32,768]{4,3,2,1,0:T(8,128)(2,1)S(1)}, u32[]{:S(2)}, u32[]{:S(2)}) collective-permute-start(bf16[2,2,2,32,768]{4,3,2,1,0:T(8,128)(2,1)S(1)} %bitcast.147), channel_id=1, source_target_pairs={{0,2},{1,3},{2,0},{3,1},{4,6},{5,7},{6,4},{7,5},{8,10},{9,11},{10,... | collective-permute-start | bytes 1179656 | tf_op jit(solution)/shard_map/ppermute | solution.py:387
  160.2 18.7 %collective-permute-start.15 = (bf16[2,2,2,32,768]{4,3,2,1,0:T(8,128)(2,1)S(1)}, bf16[2,2,2,32,768]{4,3,2,1,0:T(8,128)(2,1)S(1)}, u32[]{:S(2)}, u32[]{:S(2)}) collective-permute-start(bf16[2,2,2,32,768]{4,3,2,1,0:T(8,128)(2,1)S(1)} %slice_bitcast_fusion.2), channel_id=1, source_target_pairs={{0,4},{1,5},{2,6},{3,7},{4,0},{5,1},{6,2},{7,3},{8,12},{9,13},{10,... | collective-permute-start | bytes 1179656 | tf_op jit(solution)/shard_map/ppermute | solution.py:387
  169.9 15.4 %collective-permute-start.21 = (bf16[2,2,32,768]{3,2,1,0:T(8,128)(2,1)S(1)}, bf16[2,2,32,768]{3,2,1,0:T(8,128)(2,1)S(1)}, u32[]{:S(2)}, u32[]{:S(2)}) collective-permute-start(bf16[2,2,32,768]{3,2,1,0:T(8,128)(2,1)S(1)} %slice_bitcast_fusion.8), channel_id=1, source_target_pairs={{0,4},{1,5},{2,6},{3,7},{4,0},{5,1},{6,2},{7,3},{8,12},{9,13},{10,... | collective-permute-start | bytes 589832 | tf_op jit(solution)/shard_map/ppermute | solution.py:387
  170.6 14.8 %collective-permute-start.23 = (bf16[2,2,32,768]{3,2,1,0:T(8,128)(2,1)S(1)}, bf16[2,2,32,768]{3,2,1,0:T(8,128)(2,1)S(1)}, u32[]{:S(2)}, u32[]{:S(2)}) collective-permute-start(bf16[2,2,32,768]{3,2,1,0:T(8,128)(2,1)S(1)} %slice_bitcast_fusion.6), channel_id=1, source_target_pairs={{0,2},{1,3},{2,0},{3,1},{4,6},{5,7},{6,4},{7,5},{8,10},{9,11},{10,... | collective-permute-start | bytes 589832 | tf_op jit(solution)/shard_map/ppermute | solution.py:387
  178.3 5.7 %collective-permute-start.14 = (bf16[2,2,32,768]{3,2,1,0:T(8,128)(2,1)S(1)}, bf16[2,2,32,768]{3,2,1,0:T(8,128)(2,1)S(1)}, u32[]{:S(2)}, u32[]{:S(2)}) collective-permute-start(bf16[2,2,32,768]{3,2,1,0:T(8,128)(2,1)S(1)} %slice_bitcast_fusion.12), channel_id=1, source_target_pairs={{0,4},{1,5},{2,6},{3,7},{4,0},{5,1},{6,2},{7,3},{8,12},{9,13},{10,... | collective-permute-start | bytes 589832 | tf_op jit(solution)/shard_map/ppermute | solution.py:387
  179.0 5.7 %collective-permute-start.16 = (bf16[2,2,32,768]{3,2,1,0:T(8,128)(2,1)S(1)}, bf16[2,2,32,768]{3,2,1,0:T(8,128)(2,1)S(1)}, u32[]{:S(2)}, u32[]{:S(2)}) collective-permute-start(bf16[2,2,32,768]{3,2,1,0:T(8,128)(2,1)S(1)} %slice_bitcast_fusion.10), channel_id=1, source_target_pairs={{0,2},{1,3},{2,0},{3,1},{4,6},{5,7},{6,4},{7,5},{8,10},{9,11},{10,... | collective-permute-start | bytes 589832 | tf_op jit(solution)/shard_map/ppermute | solution.py:387
  184.8 7.4 %collective-permute-start.17 = (bf16[2,32,1536]{2,1,0:T(8,128)(2,1)S(1)}, bf16[2,32,1536]{2,1,0:T(8,128)(2,1)S(1)}, u32[]{:S(2)}, u32[]{:S(2)}) collective-permute-start(bf16[2,32,1536]{2,1,0:T(8,128)(2,1)S(1)} %fusion.20), channel_id=1, source_target_pairs={{0,8},{1,9},{2,10},{3,11},{4,12},{5,13},{6,14},{7,15},{8,0},{9,1},... | collective-permute-start | bytes 589832 | tf_op jit(solution)/shard_map/ppermute | solution.py:387
  185.5 9.3 %collective-permute-start.24 = (bf16[2,32,1536]{2,1,0:T(8,128)(2,1)S(1)}, bf16[2,32,1536]{2,1,0:T(8,128)(2,1)S(1)}, u32[]{:S(2)}, u32[]{:S(2)}) collective-permute-start(bf16[2,32,1536]{2,1,0:T(8,128)(2,1)S(1)} %fusion.19), channel_id=1, source_target_pairs={{0,8},{1,9},{2,10},{3,11},{4,12},{5,13},{6,14},{7,15},{8,0},{9,1},... | collective-permute-start | bytes 589832 | tf_op jit(solution)/shard_map/ppermute | solution.py:387
  192.3 6.4 %collective-permute-start.18 = (bf16[32,1536]{1,0:T(8,128)(2,1)S(1)}, bf16[32,1536]{1,0:T(8,128)(2,1)S(1)}, u32[]{:S(2)}, u32[]{:S(2)}) collective-permute-start(bf16[32,1536]{1,0:T(8,128)(2,1)S(1)} %slice_bitcast_fusion.20), channel_id=1, source_target_pairs={{0,16},{1,17},{2,18},{3,19},{4,20},{5,21},{6,22},{7,23},{8,24},{9,... | collective-permute-start | bytes 294920 | tf_op jit(solution)/shard_map/ppermute | solution.py:387
  194.8 6.1 %collective-permute-start.25 = (bf16[32,1536]{1,0:T(8,128)(2,1)S(1)}, bf16[32,1536]{1,0:T(8,128)(2,1)S(1)}, u32[]{:S(2)}, u32[]{:S(2)}) collective-permute-start(bf16[32,1536]{1,0:T(8,128)(2,1)S(1)} %slice_bitcast_fusion.18), channel_id=1, source_target_pairs={{0,16},{1,17},{2,18},{3,19},{4,20},{5,21},{6,22},{7,23},{8,24},{9,... | collective-permute-start | bytes 294920 | tf_op jit(solution)/shard_map/ppermute | solution.py:387
  (13 other events, 150.5 us)

commit v2 on v1

v2 whole, which is shorter than its diff:
```python
import functools

import jax
import jax.numpy as jnp
import numpy as np
from jax import lax
from jax.experimental import pallas as pl
from jax.experimental.pallas import tpu as pltpu
from jax.sharding import PartitionSpec as P

HEADS = 32
WIN = 8
SHIFT = 4
LANES = 128
HALF = SHIFT // 2
TILE = 256
EPSILON = 1e-05
MIB = 1 << 20
PARTS = 4

NN = (((1,), (0,)), ((), ()))
NT = (((1,), (1,)), ((), ()))
TN = (((0,), (0,)), ((), ()))
BF16 = jnp.bfloat16
F32 = jnp.float32


def dot(a, b, dims=NN):
    return lax.dot_general(a, b, dims, preferred_element_type=F32)


def window_cells(levels, rows, columns):
    half = WIN // 2
    return [
        (level, wi * WIN + 2 * row + sub % 2, wj * WIN + 2 * column + sub // 2)
        for wi in range(rows // WIN) for wj in range(columns // WIN) for sub in range(4)
        for level in range(levels) for row in range(half) for column in range(half)
    ]


def window_groups(levels, rows, columns):
    half = WIN // 2
    return [
        (level, wi * half + row, wj * half + column)
        for wi in range(rows // half) for wj in range(columns // half)
        for level in range(levels) for row in range(half) for column in range(half)
    ]


def box(levels, rows, columns):
    return [(l, r, c) for l in range(levels) for r in rows for c in columns]


def turned_box(levels, rows, columns):
    return [(l, r, c) for l in range(levels) for c in columns for r in rows]


def padded(cells, step=16):
    return cells + [None] * (-len(cells) % step)


def picks(wanted, held):
    spot = {cell: i for i, cell in enumerate(held) if cell is not None}
    table = np.zeros((len(wanted), len(held)), np.float32)
    for i, cell in enumerate(wanted):
        if cell is not None:
            table[i, spot[cell]] = 1.0
    return jnp.asarray(table, BF16)


class Strips:
    def __init__(self, levels, rows, columns, width, cut):
        self.side = (box(levels, range(width, 2 * width), range(width))
                     + box(levels, range(2 * width, rows), range(width)))
        self.above = box(levels, range(width), range(width, columns))
        self.corner = box(levels, range(width), range(width))
        if not cut:
            self.side = box(levels, range(width, rows), range(width))

    @staticmethod
    def sent(cells, down, across):
        return [None if c is None else (c[0], c[1] + down, c[2] + across) for c in cells]


def head_masks():
    head = lax.broadcasted_iota(jnp.int32, (LANES, LANES), 1) // (LANES // 4)
    return [jnp.where(head == h, 1.0, 0.0).astype(BF16) for h in range(4)]


def region_bias(places, active):
    step = 2 * (WIN // 2)
    one = (lax.broadcasted_iota(jnp.int32, (places, places), 0) // step) % 2
    other = (lax.broadcasted_iota(jnp.int32, (places, places), 1) // step) % 2
    return jnp.where((one != other) & active, -1e30, 0.0)


def score_scale(channels):
    return float((channels // HEADS) ** -0.5 * np.log2(np.e))


def aligned(start, size, step=None):
    return pl.ds(pl.multiple_of(start, step or size), size)


def pack_kernel(tokens, merged_grad, pick_cells, pick_groups, side, above, corner):
    cells = dot(pick_cells[...], tokens[...]).astype(BF16)
    groups = dot(pick_groups[...], merged_grad[...]).astype(BF16)
    at, at_group = 0, 0
    for out, (count, extra) in zip((side, above, corner), strip_rows(pick_cells, pick_groups)):
        out[:count] = cells[at:at + count]
        out[count:] = groups[at_group:at_group + extra]
        at, at_group = at + count, at_group + extra


def strip_rows(pick_cells, pick_groups):
    levels = 2
    rows, columns = strip_rows.extent
    cells = [levels * (rows - SHIFT) * SHIFT, levels * SHIFT * (columns - SHIFT), levels * SHIFT * SHIFT]
    groups = [n // 4 + (-(n // 4)) % 16 for n in cells]
    return list(zip(cells, groups))


def forward_kernel(
    edge, owner, tokens, merged_grad, side, above, corner, order, group, rowmap,
    wqkv_h, wout_h, wm_h,
    normed_h, normt_h, proj_h, dmr_h, dmm_h, grad_h, rstd, merged, out_mine, out_theirs,
    wqkv, wout, wm, source, xw, normed, normt, proj, mixture, inverse, subs, dsubs, grad,
    dmr, dmm, turned, in_sem, out_sem,
):
    count, channels = xw.shape
    places = 2 * WIN * WIN
    windows = count // places
    per_row = windows // 2
    quarter = places // 4
    groups = count // 4
    devices = owner.shape[0]
    block = channels // devices

    loads = [
        pltpu.make_async_copy(src, dst, in_sem.at[i])
        for i, (src, dst) in enumerate([(wqkv_h, wqkv), (wout_h, wout), (wm_h, wm)])
    ]
    for load in loads:
        load.start()
    stores = [
        pltpu.make_async_copy(src, dst, out_sem.at[i])
        for i, (src, dst) in enumerate(
            [(normed, normed_h), (proj, proj_h), (normt, normt_h),
             (grad, grad_h), (dmr, dmr_h), (dmm, dmm_h)]
        )
    ]

    (n_side, g_side), (n_above, g_above), (n_corner, g_corner) = strip_rows(None, None)
    half = count // 2
    line = half // (2 * WIN)
    cut = SHIFT * line
    side_cut = 2 * SHIFT * SHIFT
    blocks = [
        [tokens[:cut], tokens[half:half + cut], side[:side_cut], above[:n_above], corner[:n_corner]],
        [tokens[cut:cut + WIN * line], tokens[half + cut:half + cut + WIN * line], side[side_cut:n_side]],
    ]
    for wi in range(2):
        at = 0
        for piece in blocks[wi]:
            source[wi, at:at + piece.shape[0]] = piece
            at += piece.shape[0]
        if at < source.shape[1]:
            source[wi, at:] = jnp.zeros((source.shape[1] - at, channels), BF16)

    @pl.loop(0, windows)
    def _(w):
        rows = aligned(w * places, places)
        x = dot(order[rows], source[w // per_row])
        xw[rows] = x.astype(BF16)
        center = jnp.mean(x, axis=1, keepdims=True)
        moved = x - center
        scale = lax.rsqrt(jnp.mean(moved * moved, axis=1, keepdims=True) + EPSILON)
        rstd[rows] = jnp.broadcast_to(scale, (places, LANES))
        normed[rows] = (moved * scale).astype(BF16)

    stores[0].start()
    loads[0].wait()

    @pl.loop(0, wqkv.shape[1] // TILE)
    def _(n):
        columns = aligned(n * TILE, TILE)
        proj[:, columns] = dot(normed[...], wqkv[:, columns]).astype(BF16)

    stores[1].start()

    masks = head_masks()
    factor = score_scale(channels)

    @pl.loop(0, windows)
    def _(w):
        rows = aligned(w * places, places)
        bias = region_bias(places, (edge[0] == 1) & (w < per_row))
        for g in range(channels // LANES):
            lanes = pl.ds(g * LANES, LANES)
            q = proj[rows, lanes]
            k = proj[rows, pl.ds(channels + g * LANES, LANES)]
            v = proj[rows, pl.ds(2 * channels + g * LANES, LANES)]
            scores = dot(q, jnp.concatenate([k * m for m in masks], axis=0), NT)
            parts = []
            for h in range(4):
                part = scores[:, h * places:(h + 1) * places] * factor + bias
                part = part - jnp.max(part, axis=1, keepdims=True)
                parts.append(jnp.exp2(part).astype(BF16))
            values = jnp.concatenate(
                [jnp.concatenate([v * m, m], axis=1) for m in masks], axis=0
            )
            summed = dot(jnp.concatenate(parts, axis=1), values)
            inv = 1.0 / summed[:, LANES:]
            inverse[rows, lanes] = inv
            mixture[rows, lanes] = (summed[:, :LANES] * inv).astype(BF16)

    loads[1].wait()

    @pl.loop(0, channels // TILE)
    def _(n):
        columns = aligned(n * TILE, TILE)
        out = dot(mixture[...], wout[:, columns]) + xw[:, columns].astype(F32)
        out = out.astype(BF16)
        for w in range(windows):
            for s in range(4):
                at = w * places + s * quarter
                subs[s, w * quarter:(w + 1) * quarter, columns] = out[at:at + quarter]

    total = jnp.zeros((groups, 1), F32)
    for s in range(4):
        total += jnp.sum(subs[s].astype(F32), axis=1, keepdims=True)
    center = total / (4 * channels)
    total = jnp.zeros((groups, 1), F32)
    for s in range(4):
        moved = subs[s].astype(F32) - center
        total += jnp.sum(moved * moved, axis=1, keepdims=True)
    scale = lax.rsqrt(total / (4 * channels) + EPSILON)
    loads[2].wait()
    result = jnp.zeros((groups, wm.shape[1]), F32)
    for s in range(4):
        unit = ((subs[s].astype(F32) - center) * scale).astype(BF16)
        result += dot(unit, wm[s * channels:(s + 1) * channels])
    merged[...] = result.astype(BF16)

    held = jnp.concatenate(
        [merged_grad[...], side[n_side:], above[n_above:], corner[n_corner:]], axis=0
    )
    cotangent = dot(group[...], held).astype(BF16)
    mean_g = jnp.zeros((groups, 1), F32)
    mean_gx = jnp.zeros((groups, 1), F32)
    for s in range(4):
        d = dot(cotangent, wm[s * channels:(s + 1) * channels], NT).astype(BF16)
        dsubs[s] = d
        d = d.astype(F32)
        mean_g += jnp.sum(d, axis=1, keepdims=True)
        mean_gx += jnp.sum(d * ((subs[s].astype(F32) - center) * scale), axis=1, keepdims=True)
    mean_g = mean_g / (4 * channels)
    mean_gx = mean_gx / (4 * channels)
    for s in range(4):
        unit = (subs[s].astype(F32) - center) * scale
        d = (scale * (dsubs[s].astype(F32) - mean_g - unit * mean_gx)).astype(BF16)
        for w in range(windows):
            at = w * places + s * quarter
            grad[at:at + quarter] = d[w * quarter:(w + 1) * quarter]
    stores[3].start()

    @pl.loop(0, channels // TILE)
    def _(n):
        columns = aligned(n * TILE, TILE)
        d = dot(grad[...], wout[columns], NT).astype(BF16).astype(F32)
        d = d * inverse[:, columns]
        dmr[:, columns] = d.astype(BF16)
        dmm[:, columns] = (-d * mixture[:, columns].astype(F32)).astype(BF16)

    stores[4].start()
    stores[5].start()

    def turn(field, out):
        if block % 16:
            @pl.loop(0, channels // TILE)
            def _(n):
                rows = aligned(n * TILE, TILE)
                spot = lax.broadcasted_iota(jnp.int32, (TILE, channels), 1)
                pick = jnp.where(spot == rowmap[rows], 1.0, 0.0).astype(BF16)
                out[rows] = dot(pick, field[...], NT).astype(BF16)
        else:
            @pl.loop(0, channels // TILE)
            def _(n):
                rows = aligned(n * TILE, TILE)
                turned[rows] = field[:, rows].T

            for d in range(devices):
                out[d * block:(d + 1) * block] = turned[aligned(owner[d] * block, block)]

    turn(normed, normt)
    stores[2].start()
    mixt = wqkv.at[:, :count]
    turn(mixture, mixt)
    part = channels // 2

    @pl.loop(0, channels // TILE)
    def _(n):
        columns = aligned(n * TILE, TILE)
        out_mine[:, columns] = dot(mixt[:part], grad[:, columns]).astype(BF16)
        out_theirs[:, columns] = dot(mixt[part:], grad[:, columns]).astype(BF16)

    for store in stores:
        store.wait()


def backward_kernel(index, waits, summing, *refs):
    refs = refs[waits:]
    edge, proj_h, dmr_h, dmm_h, normt_h = refs[:5]
    if summing:
        before_h, pgrad_h, mine_h, theirs_h, held, pgrad, normt, mine, theirs = refs[5:14]
        in_sem, sem, out_sem = refs[14:]
    else:
        pgrad_h, held, pgrad, in_sem, sem, out_sem = refs[5:]
    _, count, width = held.shape
    channels = dmr_h.shape[1]
    places = 2 * WIN * WIN
    windows = count // places
    per_row = windows // 2
    masks = head_masks()
    factor = score_scale(channels)
    plain = (channels // HEADS) ** -0.5
    first = 3 * width if summing else 0

    def loads(w):
        rows = aligned(w * places, places)
        for i in range(5):
            field, start = (proj_h, i * channels) if i < 3 else ((dmr_h, dmm_h)[i - 3], 0)
            columns = pl.ds(start + index * width, width)
            yield pltpu.make_async_copy(field.at[rows, columns], held.at[i, rows], in_sem.at[w, i])

    for w in range(windows):
        for load in loads(w):
            load.start()
    if summing:
        extra = [
            pltpu.make_async_copy(normt_h, normt, sem.at[0]),
            pltpu.make_async_copy(before_h, pgrad.at[:, pl.ds(0, first)], sem.at[1]),
        ]
        for load in extra:
            load.start()

    @pl.loop(0, windows)
    def _(w):
        for load in loads(w):
            load.wait()
        rows = aligned(w * places, places)
        bias = region_bias(places, (edge[0] == 1) & (w < per_row))
        for g in range(width // LANES):
            lanes = pl.ds(g * LANES, LANES)
            q, k, v, dm, dd = (held[i, rows, lanes] for i in range(5))
            keys = jnp.concatenate([k * m for m in masks], axis=0)
            scores = dot(keys, q, NT)
            values = jnp.concatenate(
                [jnp.concatenate([v * m, m], axis=1) for m in masks], axis=0
            )
            slope = dot(values, jnp.concatenate([dm, dd], axis=1), NT)
            weights, slopes = [], []
            for h in range(4):
                block = slice(h * places, (h + 1) * places)
                part = scores[block] * factor + bias
                part = jnp.exp2(part - jnp.max(part, axis=0, keepdims=True))
                weights.append(part.astype(BF16))
                slopes.append((part * slope[block]).astype(BF16))
            dv = dot(
                jnp.concatenate(weights, axis=1),
                jnp.concatenate([dm * m for m in masks], axis=0),
            )
            dk = dot(
                jnp.concatenate(slopes, axis=1),
                jnp.concatenate([q * m for m in masks], axis=0),
            )
            dq = dot(jnp.concatenate(slopes, axis=0), keys, TN)
            at = first + g * LANES
            pgrad[rows, pl.ds(at, LANES)] = (dq * plain).astype(BF16)
            pgrad[rows, pl.ds(at + width, LANES)] = (dk * plain).astype(BF16)
            pgrad[rows, pl.ds(at + 2 * width, LANES)] = dv.astype(BF16)

    stores = [pltpu.make_async_copy(pgrad.at[:, pl.ds(first, 3 * width)], pgrad_h, out_sem.at[0])]
    stores[0].start()
    if summing:
        for load in extra:
            load.wait()
        half = channels // 2
        for n in range(2 * first // TILE):
            columns = pl.ds(n * TILE, TILE)
            right = pgrad[:, columns]
            mine[:, columns] = dot(normt[:half], right).astype(BF16)
            theirs[:, columns] = dot(normt[half:], right).astype(BF16)
        stores += [
            pltpu.make_async_copy(mine, mine_h, out_sem.at[1]),
            pltpu.make_async_copy(theirs, theirs_h, out_sem.at[2]),
        ]
        stores[1].start()
        stores[2].start()
    for store in stores:
        store.wait()


def projection_back(pgrads, wqkv_h, pgrad, wqkv, sem, start):
    width = pgrads[0].shape[1] // 3
    channels = wqkv_h.shape[1] // 3
    rows = pl.ds(start, wqkv.shape[0])
    loads = []
    for c, field in enumerate(pgrads):
        at = 3 * width * c
        loads.append(pltpu.make_async_copy(field, pgrad.at[:, pl.ds(at, 3 * width)], sem.at[c, 3]))
        for i in range(3):
            loads.append(pltpu.make_async_copy(
                wqkv_h.at[rows, pl.ds(i * channels + c * width, width)],
                wqkv.at[:, pl.ds(at + i * width, width)], sem.at[c, i],
            ))
    for load in loads:
        load.start()
    return loads


def input_first_kernel(waits, *refs):
    pgrads = refs[waits:waits + PARTS]
    wqkv_h, ngrad, pgrad, wqkv, sem = refs[waits + PARTS:]
    for load in projection_back(pgrads, wqkv_h, pgrad, wqkv, sem, 0):
        load.wait()
    for n in range(wqkv.shape[0] // TILE):
        rows = slice(n * TILE, (n + 1) * TILE)
        ngrad[:, rows] = dot(pgrad[...], wqkv[rows], NT).astype(BF16)


def input_last_kernel(waits, *refs):
    pgrads = refs[waits:waits + PARTS]
    (wqkv_h, nfirst_h, normed_h, rstd_h, grad_h, merged, pick_first, pick_last, pick_groups,
     full, side, below, corner,
     pgrad, wqkv, ngrad, normed, rstd, grad, sem, more_sem) = refs[waits + PARTS:]
    count, channels = ngrad.shape
    half = channels // 2
    loads = projection_back(pgrads, wqkv_h, pgrad, wqkv, sem, half)
    more = [
        pltpu.make_async_copy(src, dst, more_sem.at[i])
        for i, (src, dst) in enumerate(
            [(nfirst_h, ngrad.at[:, pl.ds(0, half)]), (normed_h, normed), (rstd_h, rstd), (grad_h, grad)]
        )
    ]
    for load in more:
        load.start()
    for load in loads:
        load.wait()
    for n in range(half // TILE):
        rows = slice(n * TILE, (n + 1) * TILE)
        ngrad[:, half + n * TILE:half + (n + 1) * TILE] = dot(
            pgrad[...], wqkv[rows], NT
        ).astype(BF16)
    for load in more:
        load.wait()
    places = 2 * WIN * WIN

    @pl.loop(0, count // places)
    def _(w):
        rows = aligned(w * places, places)
        d = ngrad[rows].astype(F32)
        unit = normed[rows].astype(F32)
        mean_d = jnp.mean(d, axis=1, keepdims=True)
        mean_dx = jnp.mean(d * unit, axis=1, keepdims=True)
        part = rstd[rows, :1] * (d - mean_d - unit * mean_dx)
        full[rows] = (part.astype(BF16).astype(F32) + grad[rows].astype(F32)).astype(BF16)

    (n_side, g_side), (n_above, g_above), (n_corner, g_corner) = strip_rows(None, None)
    side_cut = 2 * SHIFT * SHIFT
    first = dot(pick_first[...], full[:count // 2]).astype(BF16)
    last = dot(pick_last[...], full[count // 2:]).astype(BF16)
    groups = dot(pick_groups[...], merged[...]).astype(BF16)
    side[:side_cut] = first[:side_cut]
    side[side_cut:n_side] = last
    below[:n_above] = first[side_cut:side_cut + n_above]
    corner[:n_corner] = first[side_cut + n_above:]
    side[n_side:] = groups[:g_side]
    below[n_above:] = groups[g_side:g_side + g_above]
    corner[n_corner:] = groups[g_side + g_above:]


def unpack_kernel(full, merged, side, below, corner, pick_top, pick_middle, pick_bottom,
                  pick_groups, tokens_out, merged_out):
    count = full.shape[0]
    half = count // 2
    (n_side, _), (n_above, _), (n_corner, _) = strip_rows(None, None)
    side_cut = 2 * SHIFT * SHIFT
    line = half // (2 * WIN)
    pieces = [
        (pick_top, [full[:half], side[:side_cut]]),
        (pick_middle, [full[half:], side[side_cut:n_side]]),
        (pick_bottom, [below[:n_above], corner[:n_corner]]),
    ]
    at = 0
    for pick, held in pieces:
        rows = pick.shape[0] // 2
        out = dot(pick[...], jnp.concatenate(held, axis=0)).astype(BF16)
        for level in range(2):
            start = level * half + at
            tokens_out[start:start + rows] = out[level * rows:(level + 1) * rows]
        at += rows
    held = [merged[...], side[n_side:], below[n_above:], corner[n_corner:]]
    merged_out[...] = dot(pick_groups[...], jnp.concatenate(held, axis=0)).astype(BF16)


def sent(block, sizes, lat_step, lon_step):
    n_lat, n_lon = sizes
    route = [
        (a * n_lon + b, (a + lat_step) % n_lat * n_lon + (b + lon_step) % n_lon)
        for a in range(n_lat) for b in range(n_lon)
    ]
    return lax.ppermute(block, ("lat", "lon"), route)


def sent_strips(strips, sizes, step):
    side, lines, corner = strips
    return [sent(side, sizes, 0, step), sent(lines, sizes, step, 0), sent(corner, sizes, step, step)]


def device_rows(channels, sizes):
    n_lat, n_lon = sizes
    devices = n_lat * n_lon
    rows = channels // devices
    place = np.arange(devices)
    lon = 2 * (place // n_lat % (n_lon // 2)) + place // (devices // 2)
    lat = place % n_lat
    owner = (
        jnp.bitwise_xor(lax.axis_index("lat").astype(jnp.int32), jnp.asarray(lat, jnp.int32)) * n_lon
        + jnp.bitwise_xor(lax.axis_index("lon").astype(jnp.int32), jnp.asarray(lon, jnp.int32))
    )
    rowmap = owner[:, None] * rows + jnp.arange(rows, dtype=jnp.int32)[None, :]
    return owner, rowmap.reshape(channels, 1)


def exchange(block, sizes, lat_bits, lon_bits):
    n_lat, n_lon = sizes
    route = [
        (a * n_lon + b, (a ^ lat_bits) * n_lon + (b ^ lon_bits))
        for a in range(n_lat) for b in range(n_lon)
    ]
    return lax.ppermute(block, ("lat", "lon"), route)


def core_step(theirs, sizes):
    return exchange(theirs, sizes, 0, 1)


def layer_blocks(mine, arrived, sizes):
    blocks = sizes[1] // 2
    rows = mine.shape[0] // blocks
    total = [
        (mine[i * rows:(i + 1) * rows].astype(F32) + arrived[i * rows:(i + 1) * rows].astype(F32))
        for i in range(blocks)
    ]
    return [total[0]] + [t.astype(BF16) for t in total[1:]]


def layer_step(blocks, sizes):
    return [exchange(b, sizes, 0, 2 * i) for i, b in enumerate(blocks) if i]


def column_blocks(kept, arrived, sizes):
    total = kept
    for block in arrived:
        total = total + block.astype(F32)
    rows = total.shape[0] // sizes[0]
    blocks = [total[i * rows:(i + 1) * rows] for i in range(sizes[0])]
    return [blocks[0]] + [b.astype(BF16) for b in blocks[1:]]


def column_step(blocks, sizes):
    return [exchange(b, sizes, i, 0) for i, b in enumerate(blocks) if i]


def finished(kept, arrived):
    for block in arrived:
        kept = kept + block.astype(F32)
    return kept


def shards(sizes, tokens, qkv_weight, out_weight, merge_weight, merged_grad):
    levels, lat_rows, lon_cols, channels = tokens.shape
    merged_width = merge_weight.shape[1]
    count = levels * lat_rows * lon_cols
    groups = count // 4
    half = channels // 2
    strip_rows.extent = (lat_rows, lon_cols)
    vmem = pl.BlockSpec(memory_space=pltpu.VMEM)
    smem = pl.BlockSpec(memory_space=pltpu.SMEM)
    hbm = pl.BlockSpec(memory_space=pl.ANY)

    def shape(*extent, dtype=BF16):
        return jax.ShapeDtypeStruct(extent, dtype)

    def settings(limit, flops, moved):
        return dict(
            compiler_params=pltpu.CompilerParams(vmem_limit_bytes=limit * MIB),
            cost_estimate=pl.CostEstimate(
                flops=int(flops * count * channels * channels), bytes_accessed=int(moved * MIB),
                transcendentals=0,
            ),
        )

    g_rows, g_cols = lat_rows // 2, lon_cols // 2
    cells = window_cells(levels, lat_rows, lon_cols)
    grps = window_groups(levels, g_rows, g_cols)
    cs = Strips(levels, lat_rows, lon_cols, SHIFT, True)
    gs = Strips(levels, g_rows, g_cols, HALF, False)
    g_strips = [padded(gs.side), padded(gs.above), padded(gs.corner)]
    to = ((0, lon_cols), (lat_rows, 0), (lat_rows, lon_cols))
    g_to = ((0, g_cols), (g_rows, 0), (g_rows, g_cols))
    own_rows = range(SHIFT, SHIFT + lat_rows)
    own_cols = range(SHIFT, SHIFT + lon_cols)
    own = box(levels, own_rows, own_cols)
    g_own = turned_box(levels, range(HALF, HALF + g_rows), range(HALF, HALF + g_cols))
    half_cells = count // 2
    side_cut = levels * SHIFT * SHIFT
    sent_cells = sum((Strips.sent(s, *t) for s, t in zip((cs.side, cs.above, cs.corner), to)), [])
    sent_groups = sum((Strips.sent(s, *t) for s, t in zip(g_strips, g_to)), [])
    held_top = box(levels, range(SHIFT, 2 * SHIFT), own_cols) + cs.side[:side_cut] + cs.above + cs.corner
    held_low = box(levels, range(2 * SHIFT, lat_rows), own_cols) + cs.side[side_cut:]
    depth = max(len(held_top), len(held_low))
    depth += -depth % 16
    held_top += [None] * (depth - len(held_top))
    held_low += [None] * (depth - len(held_low))

    tokens_flat = tokens.reshape(count, channels)
    merged_grad_flat = merged_grad.transpose(0, 2, 1, 3).reshape(groups, merged_width)
    extents = [(n + g, channels) for n, g in strip_rows(None, None)]
    strips = pl.pallas_call(
        pack_kernel,
        out_shape=[shape(*e) for e in extents],
        in_specs=[vmem] * 4, out_specs=[vmem] * 3,
        name="pack_strips", **settings(24, 1, 3),
    )(tokens_flat, merged_grad_flat, picks(sent_cells, own), picks(sent_groups, g_own))
    strips = sent_strips(strips, sizes, 1)

    order = jnp.concatenate([picks(cells[:half_cells], held_top), picks(cells[half_cells:], held_low)])
    group = picks(grps, g_own + sum(g_strips, []))
    edge = (lax.axis_index("lat") == 0).astype(jnp.int32).reshape(1)
    owner, rowmap = device_rows(channels, sizes)

    wide = shape(count, channels)
    normed, normt, proj, dmr, dmm, grad, rstd, merged, out_mine, out_theirs = pl.pallas_call(
        forward_kernel,
        out_shape=[
            wide, shape(channels, count), shape(count, 3 * channels), wide, wide, wide,
            shape(count, LANES, dtype=F32), shape(groups, merged_width),
            shape(half, channels), shape(half, channels),
        ],
        in_specs=[smem, smem] + [vmem] * 8 + [hbm] * 3,
        out_specs=[hbm] * 6 + [vmem] * 4,
        scratch_shapes=[
            pltpu.VMEM(qkv_weight.shape, BF16),
            pltpu.VMEM(out_weight.shape, BF16),
            pltpu.VMEM(merge_weight.shape, BF16),
            pltpu.VMEM((2, depth, channels), BF16),
            pltpu.VMEM((count, channels), BF16),
            pltpu.VMEM((count, channels), BF16),
            pltpu.VMEM((channels, count), BF16),
            pltpu.VMEM((count, 3 * channels), BF16),
            pltpu.VMEM((count, channels), BF16),
            pltpu.VMEM((count, channels), F32),
            pltpu.VMEM((4, groups, channels), BF16),
            pltpu.VMEM((4, groups, channels), BF16),
            pltpu.VMEM((count, channels), BF16),
            pltpu.VMEM((count, channels), BF16),
            pltpu.VMEM((count, channels), BF16),
            pltpu.VMEM((channels, count), BF16),
            pltpu.SemaphoreType.DMA((3,)),
            pltpu.SemaphoreType.DMA((6,)),
        ],
        name="block_forward", **settings(58, 24, 34),
    )(edge, owner, tokens_flat, merged_grad_flat, *strips, order, group, rowmap,
      qkv_weight, out_weight, merge_weight)

    width = channels // PARTS

    def backward(index, before, after):
        summing = before is not None
        outs = [shape(count, 3 * width)]
        scratch = [
            pltpu.VMEM((5, count, width), BF16),
            pltpu.VMEM((count, (6 if summing else 3) * width), BF16),
        ]
        if summing:
            outs += [shape(half, 6 * width)] * 2
            scratch += [
                pltpu.VMEM((channels, count), BF16),
                pltpu.VMEM((half, 6 * width), BF16),
                pltpu.VMEM((half, 6 * width), BF16),
            ]
        scratch += [
            pltpu.SemaphoreType.DMA((count // (2 * WIN * WIN), 5)),
            pltpu.SemaphoreType.DMA((2,)),
            pltpu.SemaphoreType.DMA((3,)),
        ]
        operands = [edge, proj, dmr, dmm, normt] + ([before] if summing else [])
        return pl.pallas_call(
            functools.partial(backward_kernel, index, len(after), summing),
            out_shape=outs,
            in_specs=[hbm] * len(after) + [smem] + [hbm] * (len(operands) - 1),
            out_specs=[hbm] * len(outs),
            scratch_shapes=scratch,
            name="attention_backward", **settings(40, 6 if summing else 3, 6),
        )(*after, *operands)

    arrived = core_step(out_theirs, sizes)
    (pg0,) = backward(0, None, [])
    out_layer = layer_blocks(out_mine, arrived, sizes)
    arrived = layer_step(out_layer, sizes)
    pg1, mine1, theirs1 = backward(1, pg0, out_layer[1:])
    out_column = column_blocks(out_layer[0], arrived, sizes)
    out_arrived = column_step(out_column, sizes)
    arrived = core_step(theirs1, sizes)
    (pg2,) = backward(2, None, out_column[1:])
    layer1 = layer_blocks(mine1, arrived, sizes)
    arrived1 = layer_step(layer1, sizes)
    pg3, mine2, theirs2 = backward(3, pg2, layer1[1:])
    arrived2 = core_step(theirs2, sizes)
    pgrads = [pg0, pg1, pg2, pg3]

    in_scratch = [
        pltpu.VMEM((count, 3 * channels), BF16),
        pltpu.VMEM((half, 3 * channels), BF16),
    ]
    in_sems = pltpu.SemaphoreType.DMA((PARTS, 4))
    nfirst = pl.pallas_call(
        functools.partial(input_first_kernel, 0),
        out_shape=shape(count, half),
        in_specs=[hbm] * (PARTS + 1), out_specs=vmem,
        scratch_shapes=in_scratch + [in_sems],
        name="input_first", **settings(40, 3, 8),
    )(*pgrads, qkv_weight)
    column1 = column_blocks(layer1[0], arrived1, sizes)
    column_arrived1 = column_step(column1, sizes)
    layer2 = layer_blocks(mine2, arrived2, sizes)
    arrived2 = layer_step(layer2, sizes)
    after = layer2[1:] + column1[1:]

    first_picks = picks(cs.side[:side_cut] + cs.above + cs.corner, cells[:half_cells])
    last_picks = picks(cs.side[side_cut:], cells[half_cells:])
    full, *strips = pl.pallas_call(
        functools.partial(input_last_kernel, len(after)),
        out_shape=[wide] + [shape(*e) for e in extents],
        in_specs=[hbm] * (len(after) + PARTS + 5) + [vmem] * 4, out_specs=[vmem] * 4,
        scratch_shapes=in_scratch + [
            pltpu.VMEM((count, channels), BF16),
            pltpu.VMEM((count, channels), BF16),
            pltpu.VMEM((count, LANES), F32),
            pltpu.VMEM((count, channels), BF16),
            in_sems,
            pltpu.SemaphoreType.DMA((4,)),
        ],
        name="input_last", **settings(48, 4, 12),
    )(*after, *pgrads, qkv_weight, nfirst, normed, rstd, grad, merged,
      first_picks, last_picks, picks(sum(g_strips, []), grps))
    strips = sent_strips(strips, sizes, -1)

    column2 = column_blocks(layer2[0], arrived2, sizes)
    column_arrived2 = column_step(column2, sizes)

    got = [Strips.sent(s, *t) for s, t in zip((cs.side, cs.above, cs.corner), to)]
    g_got = sum((Strips.sent(s, *t) for s, t in zip(g_strips, g_to)), [])
    tokens_grad, merged = pl.pallas_call(
        unpack_kernel,
        out_shape=[wide, shape(groups, merged_width)],
        in_specs=[vmem] * 9, out_specs=[vmem] * 2,
        name="unpack_strips", **settings(24, 1, 5),
    )(
        full, merged, *strips,
        picks(box(levels, range(SHIFT, 2 * SHIFT), own_cols), cells[:half_cells] + got[0][:side_cut]),
        picks(box(levels, range(2 * SHIFT, lat_rows), own_cols), cells[half_cells:] + got[0][side_cut:]),
        picks(box(levels, range(lat_rows, lat_rows + SHIFT), own_cols), got[1] + got[2]),
        picks(g_own, grps + g_got),
    )
    merged = merged.reshape(levels, g_cols, g_rows, merged_width).transpose(0, 2, 1, 3)

    out_weight_grad = finished(out_column[0], out_arrived)
    parts = [finished(column1[0], column_arrived1), finished(column2[0], column_arrived2)]
    pieces = [
        part[:, (3 * i + kind) * width:(3 * i + kind + 1) * width]
        for kind in range(3) for part in parts for i in range(2)
    ]
    qkv_weight_grad = jnp.concatenate(pieces, axis=1)
    return merged, tokens_grad.reshape(tokens.shape), qkv_weight_grad, out_weight_grad


def solution(mesh):
    sizes = (mesh.shape["lat"], mesh.shape["lon"])
    in_specs = (P(None, "lat", "lon", None), P(), P(), P(), P(None, "lat", "lon", None))
    out_specs = (
        P(None, "lat", "lon", None),
        P(None, "lat", "lon", None),
        P(("lat", "lon"), None),
        P(("lat", "lon"), None),
    )
    return jax.shard_map(
        functools.partial(shards, sizes),
        mesh=mesh, in_specs=in_specs, out_specs=out_specs, check_vma=False,
    )
```

time: 202 us -> 179 us (0.89)
  waiting for transfers between devices: 56.8 us -> 40.4 us
  other arithmetic: 8.64 us -> 4.19 us
  starting transfers between devices: 36.2 us -> 32.8 us
    ppermute x33 -> x27, waiting for transfers between devices: 56.8 us -> 40.4 us  [the longest x21 27.4 us: exchange(): return lax.ppermute(block, ('lat', 'lon'), route)]
    unnamed x32 -> x89, local copies, waits for them, and re-layouts: 4.49 us -> 14.7 us
    slice x22 -> x3, local copies, waits for them, and re-layouts: 7.66 us -> 0.06 us  [column_blocks(): blocks = [total[i * rows:(i + 1) * rows] for i in range(sizes[0])]]
    concatenate x5 -> x0, other arithmetic: 5.78 us -> none  [the longest x2 3.21 us: forward_move(): return jnp.concatenate([top, rest], axis=1)]
    ppermute x33 -> x27, starting transfers between devices: 36.2 us -> 32.8 us  [the longest x21 23.7 us: exchange(): return lax.ppermute(block, ('lat', 'lon'), route)]
    pallas_call x4 -> x9, Pallas kernels: 83.3 us -> 83.9 us  [the longest x1 35.2 us: shards(): pl.pallas_call(forward_kernel, out_shape=[wide, shape(channels, count), s...]
  transfers between devices with their start and end apart: 33 -> 27, of which waited for: 18 -> 14; matrix products, arithmetic and copies ran while one was open for 8% -> 3% of each run, Pallas kernels for 22% -> 21%
where the time goes in v2:
time: 179 us
  Pallas kernels  83.9 us (47%)
  waiting for transfers between devices  40.4 us (23%)
  starting transfers between devices  32.8 us (18%)
  local copies, waits for them, and re-layouts  16.1 us (9%)
  other arithmetic  4.19 us (2%)
    pallas_call x1, Pallas kernels, shards(): pl.pallas_call(forward_kernel, out_shape=[wide, shape(channels, count), s...  35.2 us
    pallas_call x4, Pallas kernels, backward(): pl.pallas_call(functools.partial(backward_kernel, index, len(after), summ...  32.9 us
    ppermute x21, waiting for transfers between devices, exchange(): return lax.ppermute(block, ('lat', 'lon'), route)  27.4 us
    ppermute x21, starting transfers between devices, exchange(): return lax.ppermute(block, ('lat', 'lon'), route)  23.7 us
    unnamed x89, local copies, waits for them, and re-layouts  14.7 us
    ppermute x6, waiting for transfers between devices, sent(): return lax.ppermute(block, ('lat', 'lon'), route)  13 us
    pallas_call x1, Pallas kernels, shards(): pl.pallas_call(functools.partial(input_last_kernel, len(after)), out_shap...  9.14 us
    ppermute x6, starting transfers between devices, sent(): return lax.ppermute(block, ('lat', 'lon'), route)  9.13 us
  transfers between devices with their start and end apart: 27, of which 14 were waited for; matrix products, arithmetic and copies ran while one was open for 3% of the time, Pallas kernels for 21%

profile of v2, /device:TPU:0, one launch (start us, length us, event | category | flops | bytes accessed | tf_op | source)
XLA Modules:
  0.0 178.7 jit_solution(5270901052576978162)
XLA Ops:
  0.7 1.4 copy-done.23
  5.6 2.5 %collective-permute-start.2 = (bf16[48,1024]{1,0:T(8,128)(2,1)S(1)}, bf16[48,1024]{1,0:T(8,128)(2,1)S(1)}, u32[]{:S(2)}, u32[]{:S(2)}) collective-permute-start(bf16[48,1024]{1,0:T(8,128)(2,1)S(1)} %get-tuple-element.31), channel_id=1, source_target_pairs={{0,9},{1,10},{2,11},{3,12},{4,13},{5,14},{6,15},{7,8},{8,17},{9,18... | collective-permute-start | bytes 294920 | tf_op jit(solution)/shard_map/ppermute | solution.py:513
  8.1 1.6 collective-permute-start
  9.7 1.6 collective-permute-start.1
  15.8 7.6 %collective-permute-done.1.above = bf16[208,1024]{1,0:T(8,128)(2,1)S(1)} collective-permute-done((bf16[208,1024]{1,0:T(8,128)(2,1)S(1)}, bf16[208,1024]{1,0:T(8,128)(2,1)S(1)}, u32[]{:S(2)}, u32[]{:S(2)}) %collective-permute-start.1) | collective-permute-done | bytes 426016 | tf_op jit(solution)/shard_map/ppermute | solution.py:513
  24.2 35.2 %block_forward.1 = (bf16[768,1024]{1,0:T(8,128)(2,1)}, bf16[1024,768]{1,0:T(8,128)(2,1)}, bf16[768,3072]{1,0:T(8,128)(2,1)}, bf16[768,1024]{1,0:T(8,128)(2,1)}, ...) custom-call(s32[1]{0:T(128)} %bitcast.edge.refs_0_.refs_3_, ...), custom_call_target="tpu_custom_call" | custom-call | flops 19327352832 | bytes 35651584 | tf_op jit(solution)/shard_map/block_forward/pallas_call | solution.py:645
  59.5 2.3 %copy-done = bf16[768,3072]{1,0:T(8,128)(2,1)S(1)} copy-done((bf16[768,3072]{1,0:T(8,128)(2,1)S(1)}, bf16[768,3072]{1,0:T(8,128)(2,1)}, u32[]{:S(2)}) %copy-start) | copy-done | bytes 4718616
  61.8 1.4 copy-done.4
  63.2 1.4 copy-done.5
  66.0 6.1 %attention_backward.4.refs_8_.refs_0_.refs_6_ = bf16[768,768]{1,0:T(8,128)(2,1)S(1)} custom-call(s32[1]{0:T(128)} %bitcast.edge.refs_0_.refs_3_, bf16[768,3072]{1,0:T(8,128)(2,1)S(1)} %copy-done, bf16[768,1024]{1,0:T(8,128)(2,1)S(1)} %copy-done.5, bf16[768,1024]{1,0:T(8,128)(2,1)S(1)} %copy-done.7, bf16[1024,768]{1,0:T(8,128)(2,1)S(1)} %copy-done.4), custom_call_target="tpu_custom_call" | custom-call | flops 2415919104 | bytes 6291456 | tf_op jit(solution)/shard_map/attention_backward/pallas_call | solution.py:700
  72.5 1.5 copy-done.6
  74.0 9.9 %attention_backward.5 = (bf16[768,768]{1,0:T(8,128)(2,1)S(1)}, bf16[512,1536]{1,0:T(8,128)(2,1)S(1)}, bf16[512,1536]{1,0:T(8,128)(2,1)S(1)}) custom-call(bf16[128,1024]{1,0:T(8,128)(2,1)S(1)} %get-tuple-element.70.refs_0_, bf16[128,1024]{1,0:T(8,128)(2,1)S(1)} %get-tuple-element.69.refs_1_, bf16[128,1024]{1,0:T(8,128)(2,1)S(1)} %get-tuple-element.68.refs_2_, ...), custom_call_target="tpu_custom_call" | custom-call | flops 4831838208 | bytes 6291456 | tf_op jit(solution)/shard_map/attention_backward/pallas_call | solution.py:700
  84.5 1.6 collective-permute-start.7
  87.9 6.6 %collective-permute-done.7 = bf16[128,1024]{1,0:T(8,128)(2,1)S(1)} collective-permute-done((bf16[128,1024]{1,0:T(8,128)(2,1)S(1)}, bf16[128,1024]{1,0:T(8,128)(2,1)S(1)}, u32[]{:S(2)}, u32[]{:S(2)}) %collective-permute-start.7) | collective-permute-done | bytes 262176 | tf_op jit(solution)/shard_map/ppermute | solution.py:542
  94.6 4.7 %collective-permute-done.6 = bf16[128,1024]{1,0:T(8,128)(2,1)S(1)} collective-permute-done((bf16[128,1024]{1,0:T(8,128)(2,1)S(1)}, bf16[128,1024]{1,0:T(8,128)(2,1)S(1)}, u32[]{:S(2)}, u32[]{:S(2)}) %collective-permute-start.6) | collective-permute-done | bytes 262176 | tf_op jit(solution)/shard_map/ppermute | solution.py:542
  100.9 3.2 %collective-permute-start.24 = (bf16[32,1024]{1,0:T(8,128)(2,1)S(1)}, bf16[32,1024]{1,0:T(8,128)(2,1)S(1)}, u32[]{:S(2)}, u32[]{:S(2)}) collective-permute-start(bf16[32,1024]{1,0:T(8,128)(2,1)S(1)} %get-tuple-element.79.refs_0_), channel_id=1, source_target_pairs={{0,8},{1,9},{2,10},{3,11},{4,12},{5,13},{6,14},{7,15},{8,0},{9,1},... | collective-permute-start | bytes 196616 | tf_op jit(solution)/shard_map/ppermute | solution.py:542
  104.1 6.1 %attention_backward.6.refs_8_.refs_2_ = bf16[768,768]{1,0:T(8,128)(2,1)S(1)} custom-call(bf16[32,1024]{1,0:T(8,128)(2,1)S(1)} %get-tuple-element.79.refs_0_, bf16[32,1024]{1,0:T(8,128)(2,1)S(1)} %get-tuple-element.78.refs_1_, bf16[32,1024]{1,0:T(8,128)(2,1)S(1)} %get-tuple-element.77.refs_2_, s32[1]{0:T(128)} %bitcast.edge.refs_0_.refs_3_, ...), custom_call_target="tpu_custom_call" | custom-call | flops 2415919104 | bytes 6291456 | tf_op jit(solution)/shard_map/attention_backward/pallas_call | solution.py:700
  111.4 1.5 collective-permute-start.11
  114.9 10.8 %attention_backward.7 = (bf16[768,768]{1,0:T(8,128)(2,1)S(1)}, bf16[512,1536]{1,0:T(8,128)(2,1)S(1)}, bf16[512,1536]{1,0:T(8,128)(2,1)}) custom-call(bf16[128,1536]{1,0:T(8,128)(2,1)S(1)} %get-tuple-element.67.refs_0_, bf16[128,1536]{1,0:T(8,128)(2,1)S(1)} %get-tuple-element.66.refs_1_, bf16[128,1536]{1,0:T(8,128)(2,1)S(1)} %get-tuple-element.65.refs_2_, ...), custom_call_target="tpu_custom_call" | custom-call | flops 4831838208 | bytes 6291456 | tf_op jit(solution)/shard_map/attention_backward/pallas_call | solution.py:700
  125.9 5.0 %collective-permute-done.10 = bf16[128,1536]{1,0:T(8,128)(2,1)S(1)} collective-permute-done((bf16[128,1536]{1,0:T(8,128)(2,1)S(1)}, bf16[128,1536]{1,0:T(8,128)(2,1)S(1)}, u32[]{:S(2)}, u32[]{:S(2)}) %collective-permute-start.10) | collective-permute-done | bytes 393248 | tf_op jit(solution)/shard_map/ppermute | solution.py:542
  133.1 2.6 %collective-permute-start.15 = (bf16[32,1536]{1,0:T(8,128)(2,1)S(1)}, bf16[32,1536]{1,0:T(8,128)(2,1)S(1)}, u32[]{:S(2)}, u32[]{:S(2)}) collective-permute-start(bf16[32,1536]{1,0:T(8,128)(2,1)S(1)} %get-tuple-element.76.refs_3_), channel_id=1, source_target_pairs={{0,8},{1,9},{2,10},{3,11},{4,12},{5,13},{6,14},{7,15},{8,0},{9,1},... | collective-permute-start | bytes 294920 | tf_op jit(solution)/shard_map/ppermute | solution.py:542
  135.7 3.9 %input_first.1.refs_11_ = bf16[768,512]{1,0:T(8,128)(2,1)S(1)} custom-call(bf16[768,768]{1,0:T(8,128)(2,1)S(1)} %attention_backward.4.refs_8_.refs_0_.refs_6_, bf16[768,768]{1,0:T(8,128)(2,1)S(1)} %copy-done.11, bf16[768,768]{1,0:T(8,128)(2,1)S(1)} %attention_backward.6.refs_8_.refs_2_, bf16[768,768]{1,0:T(8,128)(2,1)S(1)} %get-tuple-element.43.refs_3_.refs_9_, ...), custom_call_target="tpu_custom_call" | custom-call | flops 2415919104 | bytes 8388608 | tf_op jit(solution)/shard_map/input_first/pallas_call | solution.py:729
  139.6 2.3 %collective-permute-done.16 = bf16[32,1536]{1,0:T(8,128)(2,1)S(1)} collective-permute-done((bf16[32,1536]{1,0:T(8,128)(2,1)S(1)}, bf16[32,1536]{1,0:T(8,128)(2,1)S(1)}, u32[]{:S(2)}, u32[]{:S(2)}) %collective-permute-start.16) | collective-permute-done | bytes 98336 | tf_op jit(solution)/shard_map/ppermute | solution.py:542
  143.2 1.6 collective-permute-start.20
  146.7 9.1 %input_last.1 = (bf16[768,1024]{1,0:T(8,128)(2,1)}, bf16[128,1024]{1,0:T(8,128)(2,1)S(1)}, bf16[208,1024]{1,0:T(8,128)(2,1)S(1)}, bf16[48,1024]{1,0:T(8,128)(2,1)S(1)}) custom-call(bf16[128,1536]{1,0:T(8,128)(2,1)S(1)} %get-tuple-element.64.refs_0_, bf16[128,1536]{1,0:T(8,128)(2,1)S(1)} %get-tuple-element.63.refs_1_, ...), custom_call_target="tpu_custom_call" | custom-call | flops 3221225472 | bytes 12582912 | tf_op jit(solution)/shard_map/input_last/pallas_call | solution.py:744
  156.8 1.9 %collective-permute-start.12 = (bf16[128,1024]{1,0:T(8,128)(2,1)S(1)}, bf16[128,1024]{1,0:T(8,128)(2,1)S(1)}, u32[]{:S(2)}, u32[]{:S(2)}) collective-permute-start(bf16[128,1024]{1,0:T(8,128)(2,1)S(1)} %get-tuple-element.49), channel_id=1, source_target_pairs={{0,7},{1,0},{2,1},{3,2},{4,3},{5,4},{6,5},{7,6},{8,15},{9,8},{10,9... | collective-permute-start | bytes 786440 | tf_op jit(solution)/shard_map/ppermute | solution.py:513
  159.3 4.2 %collective-permute-done.19 = bf16[128,1536]{1,0:T(8,128)(2,1)S(1)} collective-permute-done((bf16[128,1536]{1,0:T(8,128)(2,1)S(1)}, bf16[128,1536]{1,0:T(8,128)(2,1)S(1)}, u32[]{:S(2)}, u32[]{:S(2)}) %collective-permute-start.19) | collective-permute-done | bytes 393248 | tf_op jit(solution)/shard_map/ppermute | solution.py:542
  166.1 1.4 collective-permute-start.23
  167.6 2.0 %collective-permute-start.22 = (bf16[32,1536]{1,0:T(8,128)(2,1)S(1)}, bf16[32,1536]{1,0:T(8,128)(2,1)S(1)}, u32[]{:S(2)}, u32[]{:S(2)}) collective-permute-start(bf16[32,1536]{1,0:T(8,128)(2,1)S(1)} %get-tuple-element.73), channel_id=1, source_target_pairs={{0,16},{1,17},{2,18},{3,19},{4,20},{5,21},{6,22},{7,23},{8,24},{9,... | collective-permute-start | bytes 294920 | tf_op jit(solution)/shard_map/ppermute | solution.py:542
  169.6 2.8 %collective-permute-done.13.below = bf16[208,1024]{1,0:T(8,128)(2,1)S(1)} collective-permute-done((bf16[208,1024]{1,0:T(8,128)(2,1)S(1)}, bf16[208,1024]{1,0:T(8,128)(2,1)S(1)}, u32[]{:S(2)}, u32[]{:S(2)}) %collective-permute-start.13) | collective-permute-done | bytes 426016 | tf_op jit(solution)/shard_map/ppermute | solution.py:513
  172.5 2.1 %unpack_strips.1 = (bf16[768,1024]{1,0:T(8,128)(2,1)}, bf16[192,1024]{1,0:T(8,128)(2,1)}) custom-call(bf16[768,1024]{1,0:T(8,128)(2,1)S(1)} %copy-done.13, bf16[192,1024]{1,0:T(8,128)(2,1)S(1)} %copy-done.14, bf16[128,1024]{1,0:T(8,128)(2,1)S(1)} %collective-permute-done.12.side, bf16[208,1024]{1,0:T(8,128)(2,1)S(1)} %collective-permute-done.13.below, ...), custom_call_target="tpu_custom_call" | custom-call | flops 805306368 | bytes 5242880 | tf_op jit(solution)/shard_map/unpack_strips/pallas_call | solution.py:766
  175.4 2.3 %collective-permute-done.22 = bf16[32,1536]{1,0:T(8,128)(2,1)S(1)} collective-permute-done((bf16[32,1536]{1,0:T(8,128)(2,1)S(1)}, bf16[32,1536]{1,0:T(8,128)(2,1)S(1)}, u32[]{:S(2)}, u32[]{:S(2)}) %collective-permute-start.22) | collective-permute-done | bytes 98336 | tf_op jit(solution)/shard_map/ppermute | solution.py:542
  (138 shorter events, 28.9 us)
Async XLA Ops:
  5.6 8.9 %collective-permute-start.2 = (bf16[48,1024]{1,0:T(8,128)(2,1)S(1)}, bf16[48,1024]{1,0:T(8,128)(2,1)S(1)}, u32[]{:S(2)}, u32[]{:S(2)}) collective-permute-start(bf16[48,1024]{1,0:T(8,128)(2,1)S(1)} %get-tuple-element.31), channel_id=1, source_target_pairs={{0,9},{1,10},{2,11},{3,12},{4,13},{5,14},{6,15},{7,8},{8,17},{9,18... | collective-permute-start | bytes 294920 | tf_op jit(solution)/shard_map/ppermute | solution.py:513
  8.1 7.8 %collective-permute-start = (bf16[128,1024]{1,0:T(8,128)(2,1)S(1)}, bf16[128,1024]{1,0:T(8,128)(2,1)S(1)}, u32[]{:S(2)}, u32[]{:S(2)}) collective-permute-start(bf16[128,1024]{1,0:T(8,128)(2,1)S(1)} %get-tuple-element.29), channel_id=1, source_target_pairs={{0,1},{1,2},{2,3},{3,4},{4,5},{5,6},{6,7},{7,0},{8,9},{9,10},{10,1... | collective-permute-start | bytes 786440 | tf_op jit(solution)/shard_map/ppermute | solution.py:513
  9.7 13.8 %collective-permute-start.1 = (bf16[208,1024]{1,0:T(8,128)(2,1)S(1)}, bf16[208,1024]{1,0:T(8,128)(2,1)S(1)}, u32[]{:S(2)}, u32[]{:S(2)}) collective-permute-start(bf16[208,1024]{1,0:T(8,128)(2,1)S(1)} %get-tuple-element.30), channel_id=1, source_target_pairs={{0,8},{1,9},{2,10},{3,11},{4,12},{5,13},{6,14},{7,15},{8,16},{9,17... | collective-permute-start | bytes 1277960 | tf_op jit(solution)/shard_map/ppermute | solution.py:513
  59.4 12.8 %collective-permute-start.3 = (bf16[512,1024]{1,0:T(8,128)(2,1)}, bf16[512,1024]{1,0:T(8,128)(2,1)S(1)}, u32[]{:S(2)}, u32[]{:S(2)}) collective-permute-start(bf16[512,1024]{1,0:T(8,128)(2,1)} %get-tuple-element.33), channel_id=1, source_target_pairs={{0,1},{1,0},{2,3},{3,2},{4,5},{5,4},{6,7},{7,6},{8,9},{9,8},{10,11... | collective-permute-start | bytes 3145736 | tf_op jit(solution)/shard_map/ppermute | solution.py:542
  72.2 63.5 %copy-start.1 = (bf16[768,768]{1,0:T(8,128)(2,1)}, bf16[768,768]{1,0:T(8,128)(2,1)S(1)}, u32[]{:S(2)}) copy-start(bf16[768,768]{1,0:T(8,128)(2,1)S(1)} %attention_backward.4.refs_8_.refs_0_.refs_6_) | copy-start | bytes 3538948
  72.5 31.6 %slice-start.2 = ((s8[4718592]{0:T(1024)(128)(4,1)}), s8[4194304]{0:T(1024)(128)(4,1)S(1)}, s32[]{:S(2)}) async-start(s8[4718592]{0:T(1024)(128)(4,1)} %bitcast.11), calls=%async_computation.2 | async-start | bytes 8388608
  74.0 30.1 %slice-start.3 = ((s8[4718592]{0:T(1024)(128)(4,1)}), s8[524288]{0:T(1024)(128)(4,1)S(1)}, s32[]{:S(2)}) async-start(s8[4718592]{0:T(1024)(128)(4,1)} %bitcast.11), calls=%async_computation.3 | async-start | bytes 1048576
  83.9 26.3 %copy-start.10 = (bf16[768,768]{1,0:T(8,128)(2,1)}, bf16[768,768]{1,0:T(8,128)(2,1)S(1)}, u32[]{:S(2)}) copy-start(bf16[768,768]{1,0:T(8,128)(2,1)S(1)} %get-tuple-element.42.refs_1_.refs_7_) | copy-start | bytes 3538948
  83.9 27.2 %collective-permute-start.4 = (bf16[512,1536]{1,0:T(8,128)(2,1)S(1)}, bf16[512,1536]{1,0:T(8,128)(2,1)S(1)}, u32[]{:S(2)}, u32[]{:S(2)}) collective-permute-start(bf16[512,1536]{1,0:T(8,128)(2,1)S(1)} %get-tuple-element.39), channel_id=1, source_target_pairs={{0,1},{1,0},{2,3},{3,2},{4,5},{5,4},{6,7},{7,6},{8,9},{9,8},{10,11... | collective-permute-start | bytes 4718600 | tf_op jit(solution)/shard_map/ppermute | solution.py:542
  84.5 10.1 %collective-permute-start.7 = (bf16[128,1024]{1,0:T(8,128)(2,1)S(1)}, bf16[128,1024]{1,0:T(8,128)(2,1)S(1)}, u32[]{:S(2)}, u32[]{:S(2)}) collective-permute-start(bf16[128,1024]{1,0:T(8,128)(2,1)S(1)} %get-tuple-element.68.refs_2_), channel_id=1, source_target_pairs={{0,6},{1,7},{2,4},{3,5},{4,2},{5,3},{6,0},{7,1},{8,14},{9,15},{10,... | collective-permute-start | bytes 786440 | tf_op jit(solution)/shard_map/ppermute | solution.py:542
  86.0 13.2 %collective-permute-start.6 = (bf16[128,1024]{1,0:T(8,128)(2,1)S(1)}, bf16[128,1024]{1,0:T(8,128)(2,1)S(1)}, u32[]{:S(2)}, u32[]{:S(2)}) collective-permute-start(bf16[128,1024]{1,0:T(8,128)(2,1)S(1)} %get-tuple-element.69.refs_1_), channel_id=1, source_target_pairs={{0,4},{1,5},{2,6},{3,7},{4,0},{5,1},{6,2},{7,3},{8,12},{9,13},{10,... | collective-permute-start | bytes 786440 | tf_op jit(solution)/shard_map/ppermute | solution.py:542
  87.4 12.0 %collective-permute-start.5 = (bf16[128,1024]{1,0:T(8,128)(2,1)S(1)}, bf16[128,1024]{1,0:T(8,128)(2,1)S(1)}, u32[]{:S(2)}, u32[]{:S(2)}) collective-permute-start(bf16[128,1024]{1,0:T(8,128)(2,1)S(1)} %get-tuple-element.70.refs_0_), channel_id=1, source_target_pairs={{0,2},{1,3},{2,0},{3,1},{4,6},{5,7},{6,4},{7,5},{8,10},{9,11},{10,... | collective-permute-start | bytes 786440 | tf_op jit(solution)/shard_map/ppermute | solution.py:542
  99.6 10.6 %collective-permute-start.26 = (bf16[32,1024]{1,0:T(8,128)(2,1)S(1)}, bf16[32,1024]{1,0:T(8,128)(2,1)S(1)}, u32[]{:S(2)}, u32[]{:S(2)}) collective-permute-start(bf16[32,1024]{1,0:T(8,128)(2,1)S(1)} %get-tuple-element.77.refs_2_), channel_id=1, source_target_pairs={{0,24},{1,25},{2,26},{3,27},{4,28},{5,29},{6,30},{7,31},{8,16},{9,... | collective-permute-start | bytes 196616 | tf_op jit(solution)/shard_map/ppermute | solution.py:542
  100.9 9.4 %collective-permute-start.25 = (bf16[32,1024]{1,0:T(8,128)(2,1)S(1)}, bf16[32,1024]{1,0:T(8,128)(2,1)S(1)}, u32[]{:S(2)}, u32[]{:S(2)}) collective-permute-start(bf16[32,1024]{1,0:T(8,128)(2,1)S(1)} %get-tuple-element.78.refs_1_), channel_id=1, source_target_pairs={{0,16},{1,17},{2,18},{3,19},{4,20},{5,21},{6,22},{7,23},{8,24},{9,... | collective-permute-start | bytes 196616 | tf_op jit(solution)/shard_map/ppermute | solution.py:542
  100.9 9.4 %collective-permute-start.24 = (bf16[32,1024]{1,0:T(8,128)(2,1)S(1)}, bf16[32,1024]{1,0:T(8,128)(2,1)S(1)}, u32[]{:S(2)}, u32[]{:S(2)}) collective-permute-start(bf16[32,1024]{1,0:T(8,128)(2,1)S(1)} %get-tuple-element.79.refs_0_), channel_id=1, source_target_pairs={{0,8},{1,9},{2,10},{3,11},{4,12},{5,13},{6,14},{7,15},{8,0},{9,1},... | collective-permute-start | bytes 196616 | tf_op jit(solution)/shard_map/ppermute | solution.py:542
  110.2 25.5 %copy-start.3 = (bf16[768,768]{1,0:T(8,128)(2,1)}, bf16[768,768]{1,0:T(8,128)(2,1)S(1)}, u32[]{:S(2)}) copy-start(bf16[768,768]{1,0:T(8,128)(2,1)S(1)} %attention_backward.6.refs_8_.refs_2_) | copy-start | bytes 3538948
  111.4 14.5 %collective-permute-start.11 = (bf16[128,1536]{1,0:T(8,128)(2,1)S(1)}, bf16[128,1536]{1,0:T(8,128)(2,1)S(1)}, u32[]{:S(2)}, u32[]{:S(2)}) collective-permute-start(bf16[128,1536]{1,0:T(8,128)(2,1)S(1)} %get-tuple-element.65.refs_2_), channel_id=1, source_target_pairs={{0,6},{1,7},{2,4},{3,5},{4,2},{5,3},{6,0},{7,1},{8,14},{9,15},{10,... | collective-permute-start | bytes 1179656 | tf_op jit(solution)/shard_map/ppermute | solution.py:542
  112.9 17.9 %collective-permute-start.10 = (bf16[128,1536]{1,0:T(8,128)(2,1)S(1)}, bf16[128,1536]{1,0:T(8,128)(2,1)S(1)}, u32[]{:S(2)}, u32[]{:S(2)}) collective-permute-start(bf16[128,1536]{1,0:T(8,128)(2,1)S(1)} %get-tuple-element.66.refs_1_), channel_id=1, source_target_pairs={{0,4},{1,5},{2,6},{3,7},{4,0},{5,1},{6,2},{7,3},{8,12},{9,13},{10,... | collective-permute-start | bytes 1179656 | tf_op jit(solution)/shard_map/ppermute | solution.py:542
  114.3 16.7 %collective-permute-start.9 = (bf16[128,1536]{1,0:T(8,128)(2,1)S(1)}, bf16[128,1536]{1,0:T(8,128)(2,1)S(1)}, u32[]{:S(2)}, u32[]{:S(2)}) collective-permute-start(bf16[128,1536]{1,0:T(8,128)(2,1)S(1)} %get-tuple-element.67.refs_0_), channel_id=1, source_target_pairs={{0,2},{1,3},{2,0},{3,1},{4,6},{5,7},{6,4},{7,5},{8,10},{9,11},{10,... | collective-permute-start | bytes 1179656 | tf_op jit(solution)/shard_map/ppermute | solution.py:542
  125.8 16.2 %collective-permute-start.8 = (bf16[512,1536]{1,0:T(8,128)(2,1)}, bf16[512,1536]{1,0:T(8,128)(2,1)S(1)}, u32[]{:S(2)}, u32[]{:S(2)}) collective-permute-start(bf16[512,1536]{1,0:T(8,128)(2,1)} %get-tuple-element.41), channel_id=1, source_target_pairs={{0,1},{1,0},{2,3},{3,2},{4,5},{5,4},{6,7},{7,6},{8,9},{9,8},{10,11... | collective-permute-start | bytes 4718600 | tf_op jit(solution)/shard_map/ppermute | solution.py:542
  131.2 8.4 %collective-permute-start.17 = (bf16[32,1536]{1,0:T(8,128)(2,1)S(1)}, bf16[32,1536]{1,0:T(8,128)(2,1)S(1)}, u32[]{:S(2)}, u32[]{:S(2)}) collective-permute-start(bf16[32,1536]{1,0:T(8,128)(2,1)S(1)} %get-tuple-element.74.refs_5_), channel_id=1, source_target_pairs={{0,24},{1,25},{2,26},{3,27},{4,28},{5,29},{6,30},{7,31},{8,16},{9,... | collective-permute-start | bytes 294920 | tf_op jit(solution)/shard_map/ppermute | solution.py:542
  132.5 9.5 %collective-permute-start.16 = (bf16[32,1536]{1,0:T(8,128)(2,1)S(1)}, bf16[32,1536]{1,0:T(8,128)(2,1)S(1)}, u32[]{:S(2)}, u32[]{:S(2)}) collective-permute-start(bf16[32,1536]{1,0:T(8,128)(2,1)S(1)} %get-tuple-element.75.refs_4_), channel_id=1, source_target_pairs={{0,16},{1,17},{2,18},{3,19},{4,20},{5,21},{6,22},{7,23},{8,24},{9,... | collective-permute-start | bytes 294920 | tf_op jit(solution)/shard_map/ppermute | solution.py:542
  133.1 8.9 %collective-permute-start.15 = (bf16[32,1536]{1,0:T(8,128)(2,1)S(1)}, bf16[32,1536]{1,0:T(8,128)(2,1)S(1)}, u32[]{:S(2)}, u32[]{:S(2)}) collective-permute-start(bf16[32,1536]{1,0:T(8,128)(2,1)S(1)} %get-tuple-element.76.refs_3_), channel_id=1, source_target_pairs={{0,8},{1,9},{2,10},{3,11},{4,12},{5,13},{6,14},{7,15},{8,0},{9,1},... | collective-permute-start | bytes 294920 | tf_op jit(solution)/shard_map/ppermute | solution.py:542
  143.2 15.5 %collective-permute-start.20 = (bf16[128,1536]{1,0:T(8,128)(2,1)S(1)}, bf16[128,1536]{1,0:T(8,128)(2,1)S(1)}, u32[]{:S(2)}, u32[]{:S(2)}) collective-permute-start(bf16[128,1536]{1,0:T(8,128)(2,1)S(1)} %get-tuple-element.62.refs_2_), channel_id=1, source_target_pairs={{0,6},{1,7},{2,4},{3,5},{4,2},{5,3},{6,0},{7,1},{8,14},{9,15},{10,... | collective-permute-start | bytes 1179656 | tf_op jit(solution)/shard_map/ppermute | solution.py:542
  144.8 18.8 %collective-permute-start.19 = (bf16[128,1536]{1,0:T(8,128)(2,1)S(1)}, bf16[128,1536]{1,0:T(8,128)(2,1)S(1)}, u32[]{:S(2)}, u32[]{:S(2)}) collective-permute-start(bf16[128,1536]{1,0:T(8,128)(2,1)S(1)} %get-tuple-element.63.refs_1_), channel_id=1, source_target_pairs={{0,4},{1,5},{2,6},{3,7},{4,0},{5,1},{6,2},{7,3},{8,12},{9,13},{10,... | collective-permute-start | bytes 1179656 | tf_op jit(solution)/shard_map/ppermute | solution.py:542
  146.1 18.6 %collective-permute-start.18 = (bf16[128,1536]{1,0:T(8,128)(2,1)S(1)}, bf16[128,1536]{1,0:T(8,128)(2,1)S(1)}, u32[]{:S(2)}, u32[]{:S(2)}) collective-permute-start(bf16[128,1536]{1,0:T(8,128)(2,1)S(1)} %get-tuple-element.64.refs_0_), channel_id=1, source_target_pairs={{0,2},{1,3},{2,0},{3,1},{4,6},{5,7},{6,4},{7,5},{8,10},{9,11},{10,... | collective-permute-start | bytes 1179656 | tf_op jit(solution)/shard_map/ppermute | solution.py:542
  155.9 11.7 %collective-permute-start.14 = (bf16[48,1024]{1,0:T(8,128)(2,1)S(1)}, bf16[48,1024]{1,0:T(8,128)(2,1)S(1)}, u32[]{:S(2)}, u32[]{:S(2)}) collective-permute-start(bf16[48,1024]{1,0:T(8,128)(2,1)S(1)} %get-tuple-element.51), channel_id=1, source_target_pairs={{0,31},{1,24},{2,25},{3,26},{4,27},{5,28},{6,29},{7,30},{8,7},{9,0... | collective-permute-start | bytes 294920 | tf_op jit(solution)/shard_map/ppermute | solution.py:513
  156.8 12.8 %collective-permute-start.12 = (bf16[128,1024]{1,0:T(8,128)(2,1)S(1)}, bf16[128,1024]{1,0:T(8,128)(2,1)S(1)}, u32[]{:S(2)}, u32[]{:S(2)}) collective-permute-start(bf16[128,1024]{1,0:T(8,128)(2,1)S(1)} %get-tuple-element.49), channel_id=1, source_target_pairs={{0,7},{1,0},{2,1},{3,2},{4,3},{5,4},{6,5},{7,6},{8,15},{9,8},{10,9... | collective-permute-start | bytes 786440 | tf_op jit(solution)/shard_map/ppermute | solution.py:513
  158.7 13.8 %collective-permute-start.13 = (bf16[208,1024]{1,0:T(8,128)(2,1)S(1)}, bf16[208,1024]{1,0:T(8,128)(2,1)S(1)}, u32[]{:S(2)}, u32[]{:S(2)}) collective-permute-start(bf16[208,1024]{1,0:T(8,128)(2,1)S(1)} %get-tuple-element.50), channel_id=1, source_target_pairs={{0,24},{1,25},{2,26},{3,27},{4,28},{5,29},{6,30},{7,31},{8,0},{9,1... | collective-permute-start | bytes 1277960 | tf_op jit(solution)/shard_map/ppermute | solution.py:513
  166.1 9.3 %collective-permute-start.21 = (bf16[32,1536]{1,0:T(8,128)(2,1)S(1)}, bf16[32,1536]{1,0:T(8,128)(2,1)S(1)}, u32[]{:S(2)}, u32[]{:S(2)}) collective-permute-start(bf16[32,1536]{1,0:T(8,128)(2,1)S(1)} %get-tuple-element.71), channel_id=1, source_target_pairs={{0,8},{1,9},{2,10},{3,11},{4,12},{5,13},{6,14},{7,15},{8,0},{9,1},... | collective-permute-start | bytes 294920 | tf_op jit(solution)/shard_map/ppermute | solution.py:542
  166.1 9.3 %collective-permute-start.23 = (bf16[32,1536]{1,0:T(8,128)(2,1)S(1)}, bf16[32,1536]{1,0:T(8,128)(2,1)S(1)}, u32[]{:S(2)}, u32[]{:S(2)}) collective-permute-start(bf16[32,1536]{1,0:T(8,128)(2,1)S(1)} %get-tuple-element.72), channel_id=1, source_target_pairs={{0,24},{1,25},{2,26},{3,27},{4,28},{5,29},{6,30},{7,31},{8,16},{9,... | collective-permute-start | bytes 294920 | tf_op jit(solution)/shard_map/ppermute | solution.py:542
  167.6 10.2 %collective-permute-start.22 = (bf16[32,1536]{1,0:T(8,128)(2,1)S(1)}, bf16[32,1536]{1,0:T(8,128)(2,1)S(1)}, u32[]{:S(2)}, u32[]{:S(2)}) collective-permute-start(bf16[32,1536]{1,0:T(8,128)(2,1)S(1)} %get-tuple-element.73), channel_id=1, source_target_pairs={{0,16},{1,17},{2,18},{3,19},{4,20},{5,21},{6,22},{7,23},{8,24},{9,... | collective-permute-start | bytes 294920 | tf_op jit(solution)/shard_map/ppermute | solution.py:542
  (34 other events, 229.0 us)

commit v3 on v2

--- a/solution.py
+++ b/solution.py
@@ -124,8 +124,8 @@
     edge, owner, tokens, merged_grad, side, above, corner, order, group, rowmap,
     wqkv_h, wout_h, wm_h,
     normed_h, normt_h, proj_h, dmr_h, dmm_h, grad_h, rstd, merged, out_mine, out_theirs,
-    wqkv, wout, wm, source, xw, normed, normt, proj, mixture, inverse, subs, dsubs, grad,
-    dmr, dmm, turned, in_sem, out_sem,
+    wqkv, wout, wm, source, xw, normed, normt, proj, mixture, inverse, subs, dsubs, cotangent,
+    grad, dmr, dmm, turned, in_sem, out_sem,
 ):
     count, channels = xw.shape
     places = 2 * WIN * WIN
@@ -191,19 +191,29 @@
     masks = head_masks()
     factor = score_scale(channels)
 
-    @pl.loop(0, windows)
-    def _(w):
-        rows = aligned(w * places, places)
-        bias = region_bias(places, (edge[0] == 1) & (w < per_row))
-        for g in range(channels // LANES):
-            lanes = pl.ds(g * LANES, LANES)
-            q = proj[rows, lanes]
-            k = proj[rows, pl.ds(channels + g * LANES, LANES)]
-            v = proj[rows, pl.ds(2 * channels + g * LANES, LANES)]
+    edge_bias = region_bias(places, edge[0] == 1)
+    held = jnp.concatenate(
+        [merged_grad[...], side[n_side:], above[n_above:], corner[n_corner:]], axis=0
+    )
+    cotangent[...] = dot(group[...], held).astype(BF16)
+    loads[2].wait()
+    steps = channels // LANES
+    per_step = 4 * channels // TILE // steps
+
+    @pl.loop(0, steps)
+    def _(g):
+        lanes = aligned(g * LANES, LANES)
+        key_lanes = aligned(channels + g * LANES, LANES)
+        value_lanes = aligned(2 * channels + g * LANES, LANES)
+        for w in range(windows):
+            rows = slice(w * places, (w + 1) * places)
+            q, k, v = proj[rows, lanes], proj[rows, key_lanes], proj[rows, value_lanes]
             scores = dot(q, jnp.concatenate([k * m for m in masks], axis=0), NT)
             parts = []
             for h in range(4):
-                part = scores[:, h * places:(h + 1) * places] * factor + bias
+                part = scores[:, h * places:(h + 1) * places] * factor
+                if w < per_row:
+                    part = part + edge_bias
                 part = part - jnp.max(part, axis=1, keepdims=True)
                 parts.append(jnp.exp2(part).astype(BF16))
             values = jnp.concatenate(
@@ -213,6 +223,9 @@
             inv = 1.0 / summed[:, LANES:]
             inverse[rows, lanes] = inv
             mixture[rows, lanes] = (summed[:, :LANES] * inv).astype(BF16)
+        for i in range(per_step):
+            at = aligned((g * per_step + i) * TILE, TILE)
+            dsubs[:, at] = dot(cotangent[...], wm[at], NT).astype(BF16)
 
     loads[1].wait()
 
@@ -235,30 +248,24 @@
         moved = subs[s].astype(F32) - center
         total += jnp.sum(moved * moved, axis=1, keepdims=True)
     scale = lax.rsqrt(total / (4 * channels) + EPSILON)
-    loads[2].wait()
     result = jnp.zeros((groups, wm.shape[1]), F32)
     for s in range(4):
         unit = ((subs[s].astype(F32) - center) * scale).astype(BF16)
         result += dot(unit, wm[s * channels:(s + 1) * channels])
     merged[...] = result.astype(BF16)
 
-    held = jnp.concatenate(
-        [merged_grad[...], side[n_side:], above[n_above:], corner[n_corner:]], axis=0
-    )
-    cotangent = dot(group[...], held).astype(BF16)
     mean_g = jnp.zeros((groups, 1), F32)
     mean_gx = jnp.zeros((groups, 1), F32)
     for s in range(4):
-        d = dot(cotangent, wm[s * channels:(s + 1) * channels], NT).astype(BF16)
-        dsubs[s] = d
-        d = d.astype(F32)
+        d = dsubs[:, s * channels:(s + 1) * channels].astype(F32)
         mean_g += jnp.sum(d, axis=1, keepdims=True)
         mean_gx += jnp.sum(d * ((subs[s].astype(F32) - center) * scale), axis=1, keepdims=True)
     mean_g = mean_g / (4 * channels)
     mean_gx = mean_gx / (4 * channels)
     for s in range(4):
         unit = (subs[s].astype(F32) - center) * scale
-        d = (scale * (dsubs[s].astype(F32) - mean_g - unit * mean_gx)).astype(BF16)
+        d = dsubs[:, s * channels:(s + 1) * channels].astype(F32)
+        d = (scale * (d - mean_g - unit * mean_gx)).astype(BF16)
         for w in range(windows):
             at = w * places + s * quarter
             grad[at:at + quarter] = d[w * quarter:(w + 1) * quarter]
@@ -593,12 +600,11 @@
     def shape(*extent, dtype=BF16):
         return jax.ShapeDtypeStruct(extent, dtype)
 
-    def settings(limit, flops, moved):
+    def settings(weight):
         return dict(
-            compiler_params=pltpu.CompilerParams(vmem_limit_bytes=limit * MIB),
+            compiler_params=pltpu.CompilerParams(vmem_limit_bytes=60 * MIB),
             cost_estimate=pl.CostEstimate(
-                flops=int(flops * count * channels * channels), bytes_accessed=int(moved * MIB),
-                transcendentals=0,
+                flops=int(weight * 1e10), bytes_accessed=16 * MIB, transcendentals=0
             ),
         )
 
@@ -632,7 +638,7 @@
         pack_kernel,
         out_shape=[shape(*e) for e in extents],
         in_specs=[vmem] * 4, out_specs=[vmem] * 3,
-        name="pack_strips", **settings(24, 1, 3),
+        name="pack_strips", **settings(1),
     )(tokens_flat, merged_grad_flat, picks(sent_cells, own), picks(sent_groups, g_own))
     strips = sent_strips(strips, sizes, 1)
 
@@ -663,7 +669,8 @@
             pltpu.VMEM((count, channels), BF16),
             pltpu.VMEM((count, channels), F32),
             pltpu.VMEM((4, groups, channels), BF16),
-            pltpu.VMEM((4, groups, channels), BF16),
+            pltpu.VMEM((groups, 4 * channels), BF16),
+            pltpu.VMEM((groups, merged_width), BF16),
             pltpu.VMEM((count, channels), BF16),
             pltpu.VMEM((count, channels), BF16),
             pltpu.VMEM((count, channels), BF16),
@@ -671,7 +678,7 @@
             pltpu.SemaphoreType.DMA((3,)),
             pltpu.SemaphoreType.DMA((6,)),
         ],
-        name="block_forward", **settings(58, 24, 34),
+        name="block_forward", **settings(30),
     )(edge, owner, tokens_flat, merged_grad_flat, *strips, order, group, rowmap,
       qkv_weight, out_weight, merge_weight)
 
@@ -703,7 +710,7 @@
             in_specs=[hbm] * len(after) + [smem] + [hbm] * (len(operands) - 1),
             out_specs=[hbm] * len(outs),
             scratch_shapes=scratch,
-            name="attention_backward", **settings(40, 6 if summing else 3, 6),
+            name="attention_backward", **settings(10 if summing else 6),
         )(*after, *operands)
 
     arrived = core_step(out_theirs, sizes)
@@ -731,7 +738,7 @@
         out_shape=shape(count, half),
         in_specs=[hbm] * (PARTS + 1), out_specs=vmem,
         scratch_shapes=in_scratch + [in_sems],
-        name="input_first", **settings(40, 3, 8),
+        name="input_first", **settings(5),
     )(*pgrads, qkv_weight)
     column1 = column_blocks(layer1[0], arrived1, sizes)
     column_arrived1 = column_step(column1, sizes)
@@ -753,7 +760,7 @@
             in_sems,
             pltpu.SemaphoreType.DMA((4,)),
         ],
-        name="input_last", **settings(48, 4, 12),
+        name="input_last", **settings(9),
     )(*after, *pgrads, qkv_weight, nfirst, normed, rstd, grad, merged,
       first_picks, last_picks, picks(sum(g_strips, []), grps))
     strips = sent_strips(strips, sizes, -1)
@@ -767,7 +774,7 @@
         unpack_kernel,
         out_shape=[wide, shape(groups, merged_width)],
         in_specs=[vmem] * 9, out_specs=[vmem] * 2,
-        name="unpack_strips", **settings(24, 1, 5),
+        name="unpack_strips", **settings(2),
     )(
         full, merged, *strips,
         picks(box(levels, range(SHIFT, 2 * SHIFT), own_cols), cells[:half_cells] + got[0][:side_cut]),

time: 179 us -> 182 us (1.017)
  Pallas kernels: 83.9 us -> 99 us
  waiting for transfers between devices: 40.4 us -> 26.1 us
  other arithmetic: 4.19 us -> 12.3 us
  local copies, waits for them, and re-layouts: 16.1 us -> 11.9 us
    ppermute x21, waiting for transfers between devices: 27.4 us -> 10 us  [exchange(): return lax.ppermute(block, ('lat', 'lon'), route)]
    unnamed x89 -> x51, local copies, waits for them, and re-layouts: 14.7 us -> 9.23 us
    pallas_call x4, Pallas kernels: 32.9 us -> 37.1 us  [backward(): pl.pallas_call(functools.partial(backward_kernel, index, len(after), summ...]
    another operation x3, other arithmetic: 1.76 us -> 5.22 us
    pallas_call x1, Pallas kernels: 3.88 us -> 7.03 us  [shards(): pl.pallas_call(functools.partial(input_first_kernel, 0), out_shape=shape(...]
    ppermute x6, waiting for transfers between devices: 13 us -> 16.1 us  [sent(): return lax.ppermute(block, ('lat', 'lon'), route)]
    convert_element_type x3, other arithmetic: 0.9 us -> 3.74 us  [layer_blocks(): return [total[0]] + [t.astype(BF16) for t in total[1:]]]
    pallas_call x1, Pallas kernels: 0.67 us -> 3.14 us  [shards(): pl.pallas_call(pack_kernel, out_shape=[shape(*e) for e in extents], in_sp...]
  transfers between devices with their start and end apart: 27 -> 27, of which waited for: 14 -> 10; matrix products, arithmetic and copies ran while one was open for 3% -> 6% of each run, Pallas kernels for 21% -> 33%
where the time goes in v3:
time: 182 us
  Pallas kernels  99 us (54%)
  starting transfers between devices  31.6 us (17%)
  waiting for transfers between devices  26.1 us (14%)
  other arithmetic  12.3 us (7%)
  local copies, waits for them, and re-layouts  11.9 us (7%)
    pallas_call x4, Pallas kernels, backward(): pl.pallas_call(functools.partial(backward_kernel, index, len(after), summ...  37.1 us
    pallas_call x1, Pallas kernels, shards(): pl.pallas_call(forward_kernel, out_shape=[wide, shape(channels, count), s...  36.5 us
    ppermute x21, starting transfers between devices, exchange(): return lax.ppermute(block, ('lat', 'lon'), route)  23.1 us
    ppermute x6, waiting for transfers between devices, sent(): return lax.ppermute(block, ('lat', 'lon'), route)  16.1 us
    pallas_call x1, Pallas kernels, shards(): pl.pallas_call(functools.partial(input_last_kernel, len(after)), out_shap...  11.2 us
    ppermute x21, waiting for transfers between devices, exchange(): return lax.ppermute(block, ('lat', 'lon'), route)  10 us
    unnamed x51, local copies, waits for them, and re-layouts  9.23 us
    ppermute x6, starting transfers between devices, sent(): return lax.ppermute(block, ('lat', 'lon'), route)  8.5 us
  transfers between devices with their start and end apart: 27, of which 10 were waited for; matrix products, arithmetic and copies ran while one was open for 6% of the time, Pallas kernels for 33%

profile of v3, /device:TPU:0, one launch (start us, length us, event | category | flops | bytes accessed | tf_op | source)
XLA Modules:
  0.0 181.8 jit_solution(12525666046304417950)
XLA Ops:
  0.7 3.1 %pack_strips.1 = (bf16[128,1024]{1,0:T(8,128)(2,1)}, bf16[208,1024]{1,0:T(8,128)(2,1)}, bf16[48,1024]{1,0:T(8,128)(2,1)}) custom-call(bf16[768,1024]{1,0:T(8,128)(2,1)} %bitcast.9, bf16[192,1024]{1,0:T(8,128)(2,1)} %bitcast.11, bf16[288,768]{1,0:T(8,128)(2,1)} %constant.42.clone.pick_cells, bf16[96,192]{1,0:T(8,128)(2,1)} %constant.43.clone.pick_groups), custom_call_target="tpu_custom_call" | custom-call | flops 10000000000 | bytes 16777216 | tf_op jit(solution)/shard_map/pack_strips/pallas_call | solution.py:637
  3.8 2.5 %collective-permute-start.2 = (bf16[48,1024]{1,0:T(8,128)(2,1)}, bf16[48,1024]{1,0:T(8,128)(2,1)S(1)}, u32[]{:S(2)}, u32[]{:S(2)}) collective-permute-start(bf16[48,1024]{1,0:T(8,128)(2,1)} %get-tuple-element.31), channel_id=1, source_target_pairs={{0,9},{1,10},{2,11},{3,12},{4,13},{5,14},{6,15},{7,8},{8,17},{9,18... | collective-permute-start | bytes 294920 | tf_op jit(solution)/shard_map/ppermute | solution.py:520
  6.3 1.6 collective-permute-start
  7.9 1.6 collective-permute-start.1
  11.4 1.5 collective-permute-done.2.corner
  14.2 7.6 %collective-permute-done.1.above = bf16[208,1024]{1,0:T(8,128)(2,1)S(1)} collective-permute-done((bf16[208,1024]{1,0:T(8,128)(2,1)}, bf16[208,1024]{1,0:T(8,128)(2,1)S(1)}, u32[]{:S(2)}, u32[]{:S(2)}) %collective-permute-start.1) | collective-permute-done | bytes 426016 | tf_op jit(solution)/shard_map/ppermute | solution.py:520
  22.6 36.5 %block_forward.1 = (bf16[768,1024]{1,0:T(8,128)(2,1)}, bf16[1024,768]{1,0:T(8,128)(2,1)}, bf16[768,3072]{1,0:T(8,128)(2,1)}, bf16[768,1024]{1,0:T(8,128)(2,1)}, ...) custom-call(s32[1]{0:T(128)} %bitcast.edge.refs_0_.refs_3_, ...), custom_call_target="tpu_custom_call" | custom-call | flops 299999985664 | bytes 16777216 | tf_op jit(solution)/shard_map/block_forward/pallas_call | solution.py:651
  59.2 7.6 %attention_backward.4.refs_8_.refs_0_.refs_6_ = bf16[768,768]{1,0:T(8,128)(2,1)} custom-call(s32[1]{0:T(128)} %bitcast.edge.refs_0_.refs_3_, bf16[768,3072]{1,0:T(8,128)(2,1)} %get-tuple-element.34.refs_1_.refs_4_, bf16[768,1024]{1,0:T(8,128)(2,1)} %get-tuple-element.35.refs_2_.refs_5_, bf16[768,1024]{1,0:T(8,128)(2,1)} %get-tuple-element.36.refs_3_.refs_6_, ...), custom_call_target="tpu_custom_call" | custom-call | flops 60000002048 | bytes 16777216 | tf_op jit(solution)/shard_map/attention_backward/pallas_call | solution.py:707
  68.0 1.6 collective-permute-start.7
  69.6 1.4 collective-permute-start.6
  71.5 11.0 %attention_backward.5 = (bf16[768,768]{1,0:T(8,128)(2,1)}, bf16[512,1536]{1,0:T(8,128)(2,1)}, bf16[512,1536]{1,0:T(8,128)(2,1)}) custom-call(bf16[128,1024]{1,0:T(8,128)(2,1)} %copy-done.8, bf16[128,1024]{1,0:T(8,128)(2,1)} %get-tuple-element.69.refs_1_, bf16[128,1024]{1,0:T(8,128)(2,1)} %get-tuple-element.68.refs_2_, s32[1]{0:T(128)} %bitcast.edge.refs_0_.refs_3_, ...), custom_call_target="tpu_custom_call" | custom-call | flops 99999997952 | bytes 16777216 | tf_op jit(solution)/shard_map/attention_backward/pallas_call | solution.py:707
  83.6 2.1 %fusion.8 = (bf16[128,1024]{1,0:T(8,128)(2,1)S(1)}, f32[128,1024]{1,0:T(8,128)}) fusion(bf16[128,1024]{1,0:T(8,128)(2,1)} %collective-permute-done.7, bf16[128,1024]{1,0:T(8,128)(2,1)} %collective-permute-done.6, bf16[128,1024]{1,0:T(8,128)(2,1)} %collective-permute-done.5, bf16[512,1024]{1,0:T(8,128)(2,1)S(1)} %collective-permute-done.3, ...), kind=kLoop, calls=%fused_computation.38 | loop fusion | flops 1310720 | bytes 2097152 | tf_op jit(solution)/shard_map/convert.9
  87.0 3.2 %collective-permute-start.24 = (bf16[32,1024]{1,0:T(8,128)(2,1)S(1)}, bf16[32,1024]{1,0:T(8,128)(2,1)S(1)}, u32[]{:S(2)}, u32[]{:S(2)}) collective-permute-start(bf16[32,1024]{1,0:T(8,128)(2,1)S(1)} %get-tuple-element.79.refs_0_), channel_id=1, source_target_pairs={{0,8},{1,9},{2,10},{3,11},{4,12},{5,13},{6,14},{7,15},{8,0},{9,1},... | collective-permute-start | bytes 196616 | tf_op jit(solution)/shard_map/ppermute | solution.py:549
  90.3 7.6 %attention_backward.6.refs_8_.refs_2_ = bf16[768,768]{1,0:T(8,128)(2,1)} custom-call(bf16[32,1024]{1,0:T(8,128)(2,1)} %copy-done.11, bf16[32,1024]{1,0:T(8,128)(2,1)} %copy-done.12, bf16[32,1024]{1,0:T(8,128)(2,1)} %copy-done.13, s32[1]{0:T(128)} %bitcast.edge.refs_0_.refs_3_, bf16[768,3072]{1,0:T(8,128)(2,1)} %get-tuple-element.34.refs_1_.refs_4_, ...), custom_call_target="tpu_custom_call" | custom-call | flops 60000002048 | bytes 16777216 | tf_op jit(solution)/shard_map/attention_backward/pallas_call | solution.py:707
  97.9 1.6 fusion.5
  99.5 1.5 add_convert_fusion.3
  101.0 1.5 collective-permute-start.11
  102.5 1.4 collective-permute-start.10
  104.5 10.8 %attention_backward.7 = (bf16[768,768]{1,0:T(8,128)(2,1)}, bf16[512,1536]{1,0:T(8,128)(2,1)}, bf16[512,1536]{1,0:T(8,128)(2,1)}) custom-call(bf16[128,1536]{1,0:T(8,128)(2,1)} %get-tuple-element.67.refs_0_, bf16[128,1536]{1,0:T(8,128)(2,1)} %get-tuple-element.66.refs_1_, bf16[128,1536]{1,0:T(8,128)(2,1)} %get-tuple-element.65.refs_2_, ...), custom_call_target="tpu_custom_call" | custom-call | flops 99999997952 | bytes 16777216 | tf_op jit(solution)/shard_map/attention_backward/pallas_call | solution.py:707
  115.5 5.2 %collective-permute-done.10 = bf16[128,1536]{1,0:T(8,128)(2,1)S(1)} collective-permute-done((bf16[128,1536]{1,0:T(8,128)(2,1)}, bf16[128,1536]{1,0:T(8,128)(2,1)S(1)}, u32[]{:S(2)}, u32[]{:S(2)}) %collective-permute-start.10) | collective-permute-done | bytes 393248 | tf_op jit(solution)/shard_map/ppermute | solution.py:549
  121.5 1.6 fusion.7
  125.6 2.5 %collective-permute-start.15 = (bf16[32,1536]{1,0:T(8,128)(2,1)}, bf16[32,1536]{1,0:T(8,128)(2,1)}, u32[]{:S(2)}, u32[]{:S(2)}) collective-permute-start(bf16[32,1536]{1,0:T(8,128)(2,1)} %get-tuple-element.76.refs_3_), channel_id=1, source_target_pairs={{0,8},{1,9},{2,10},{3,11},{4,12},{5,13},{6,14},{7,15},{8,0},{9,1},... | collective-permute-start | bytes 294920 | tf_op jit(solution)/shard_map/ppermute | solution.py:549
  128.2 7.0 %input_first.1.refs_11_ = bf16[768,512]{1,0:T(8,128)(2,1)} custom-call(bf16[768,768]{1,0:T(8,128)(2,1)} %attention_backward.4.refs_8_.refs_0_.refs_6_, bf16[768,768]{1,0:T(8,128)(2,1)} %get-tuple-element.42.refs_1_.refs_7_, bf16[768,768]{1,0:T(8,128)(2,1)} %attention_backward.6.refs_8_.refs_2_, bf16[768,768]{1,0:T(8,128)(2,1)} %get-tuple-element.43.refs_3_.refs_9_, ...), custom_call_target="tpu_custom_call" | custom-call | flops 49999998976 | bytes 16777216 | tf_op jit(solution)/shard_map/input_first/pallas_call | solution.py:736
  138.7 1.6 collective-permute-start.20
  142.2 11.2 %input_last.1 = (bf16[768,1024]{1,0:T(8,128)(2,1)}, bf16[128,1024]{1,0:T(8,128)(2,1)}, bf16[208,1024]{1,0:T(8,128)(2,1)}, bf16[48,1024]{1,0:T(8,128)(2,1)}) custom-call(bf16[128,1536]{1,0:T(8,128)(2,1)} %get-tuple-element.64.refs_0_, bf16[128,1536]{1,0:T(8,128)(2,1)} %get-tuple-element.63.refs_1_, bf16[128,1536]{1,0:T(8,128)(2,1)} %get-tuple-element.62.refs_2_, ...), custom_call_target="tpu_custom_call" | custom-call | flops 89999998976 | bytes 16777216 | tf_op jit(solution)/shard_map/input_last/pallas_call | solution.py:751
  153.7 2.3 %collective-permute-start.12 = (bf16[128,1024]{1,0:T(8,128)(2,1)}, bf16[128,1024]{1,0:T(8,128)(2,1)}, u32[]{:S(2)}, u32[]{:S(2)}) collective-permute-start(bf16[128,1024]{1,0:T(8,128)(2,1)} %get-tuple-element.49), channel_id=1, source_target_pairs={{0,7},{1,0},{2,1},{3,2},{4,3},{5,4},{6,5},{7,6},{8,15},{9,8},{10,9... | collective-permute-start | bytes 786440 | tf_op jit(solution)/shard_map/ppermute | solution.py:520
  156.2 2.6 %collective-permute-done.19 = bf16[128,1536]{1,0:T(8,128)(2,1)S(1)} collective-permute-done((bf16[128,1536]{1,0:T(8,128)(2,1)}, bf16[128,1536]{1,0:T(8,128)(2,1)S(1)}, u32[]{:S(2)}, u32[]{:S(2)}) %collective-permute-start.19) | collective-permute-done | bytes 393248 | tf_op jit(solution)/shard_map/ppermute | solution.py:549
  159.9 1.5 fusion.6
  161.5 1.4 collective-permute-start.23
  162.9 2.0 %collective-permute-start.22 = (bf16[32,1536]{1,0:T(8,128)(2,1)S(1)}, bf16[32,1536]{1,0:T(8,128)(2,1)S(1)}, u32[]{:S(2)}, u32[]{:S(2)}) collective-permute-start(bf16[32,1536]{1,0:T(8,128)(2,1)S(1)} %get-tuple-element.73), channel_id=1, source_target_pairs={{0,16},{1,17},{2,18},{3,19},{4,20},{5,21},{6,22},{7,23},{8,24},{9,... | collective-permute-start | bytes 294920 | tf_op jit(solution)/shard_map/ppermute | solution.py:549
  165.0 5.7 %collective-permute-done.13.below = bf16[208,1024]{1,0:T(8,128)(2,1)} collective-permute-done((bf16[208,1024]{1,0:T(8,128)(2,1)}, bf16[208,1024]{1,0:T(8,128)(2,1)}, u32[]{:S(2)}, u32[]{:S(2)}) %collective-permute-start.13) | collective-permute-done | bytes 426016 | tf_op jit(solution)/shard_map/ppermute | solution.py:520
  170.7 4.1 %unpack_strips.1 = (bf16[768,1024]{1,0:T(8,128)(2,1)}, bf16[192,1024]{1,0:T(8,128)(2,1)}) custom-call(bf16[768,1024]{1,0:T(8,128)(2,1)} %get-tuple-element.48.full, bf16[192,1024]{1,0:T(8,128)(2,1)} %get-tuple-element.47.refs_15_.merged, bf16[128,1024]{1,0:T(8,128)(2,1)} %collective-permute-done.12.side, bf16[208,1024]{1,0:T(8,128)(2,1)} %collective-permute-done.13.below, ...), custom_call_target="tpu_custom_call" | custom-call | flops 20000000000 | bytes 16777216 | tf_op jit(solution)/shard_map/unpack_strips/pallas_call | solution.py:773
  (98 shorter events, 26.4 us)
Async XLA Ops:
  3.8 9.1 %collective-permute-start.2 = (bf16[48,1024]{1,0:T(8,128)(2,1)}, bf16[48,1024]{1,0:T(8,128)(2,1)S(1)}, u32[]{:S(2)}, u32[]{:S(2)}) collective-permute-start(bf16[48,1024]{1,0:T(8,128)(2,1)} %get-tuple-element.31), channel_id=1, source_target_pairs={{0,9},{1,10},{2,11},{3,12},{4,13},{5,14},{6,15},{7,8},{8,17},{9,18... | collective-permute-start | bytes 294920 | tf_op jit(solution)/shard_map/ppermute | solution.py:520
  6.3 8.0 %collective-permute-start = (bf16[128,1024]{1,0:T(8,128)(2,1)}, bf16[128,1024]{1,0:T(8,128)(2,1)S(1)}, u32[]{:S(2)}, u32[]{:S(2)}) collective-permute-start(bf16[128,1024]{1,0:T(8,128)(2,1)} %get-tuple-element.29), channel_id=1, source_target_pairs={{0,1},{1,2},{2,3},{3,4},{4,5},{5,6},{6,7},{7,0},{8,9},{9,10},{10,1... | collective-permute-start | bytes 786440 | tf_op jit(solution)/shard_map/ppermute | solution.py:520
  7.9 14.0 %collective-permute-start.1 = (bf16[208,1024]{1,0:T(8,128)(2,1)}, bf16[208,1024]{1,0:T(8,128)(2,1)S(1)}, u32[]{:S(2)}, u32[]{:S(2)}) collective-permute-start(bf16[208,1024]{1,0:T(8,128)(2,1)} %get-tuple-element.30), channel_id=1, source_target_pairs={{0,8},{1,9},{2,10},{3,11},{4,12},{5,13},{6,14},{7,15},{8,16},{9,17... | collective-permute-start | bytes 1277960 | tf_op jit(solution)/shard_map/ppermute | solution.py:520
  12.9 8.9 %copy-start.19 = (bf16[48,1024]{1,0:T(8,128)(2,1)}, bf16[48,1024]{1,0:T(8,128)(2,1)S(1)}, u32[]{:S(2)}) copy-start(bf16[48,1024]{1,0:T(8,128)(2,1)S(1)} %collective-permute-done.2.corner) | copy-start | bytes 294916
  59.2 7.7 %collective-permute-start.3 = (bf16[512,1024]{1,0:T(8,128)(2,1)}, bf16[512,1024]{1,0:T(8,128)(2,1)S(1)}, u32[]{:S(2)}, u32[]{:S(2)}) collective-permute-start(bf16[512,1024]{1,0:T(8,128)(2,1)} %get-tuple-element.33), channel_id=1, source_target_pairs={{0,1},{1,0},{2,3},{3,2},{4,5},{5,4},{6,7},{7,6},{8,9},{9,8},{10,11... | collective-permute-start | bytes 3145736 | tf_op jit(solution)/shard_map/ppermute | solution.py:549
  68.0 14.6 %collective-permute-start.7 = (bf16[128,1024]{1,0:T(8,128)(2,1)}, bf16[128,1024]{1,0:T(8,128)(2,1)}, u32[]{:S(2)}, u32[]{:S(2)}) collective-permute-start(bf16[128,1024]{1,0:T(8,128)(2,1)} %get-tuple-element.68.refs_2_), channel_id=1, source_target_pairs={{0,6},{1,7},{2,4},{3,5},{4,2},{5,3},{6,0},{7,1},{8,14},{9,15},{10,... | collective-permute-start | bytes 786440 | tf_op jit(solution)/shard_map/ppermute | solution.py:549
  69.6 14.0 %collective-permute-start.6 = (bf16[128,1024]{1,0:T(8,128)(2,1)}, bf16[128,1024]{1,0:T(8,128)(2,1)}, u32[]{:S(2)}, u32[]{:S(2)}) collective-permute-start(bf16[128,1024]{1,0:T(8,128)(2,1)} %get-tuple-element.69.refs_1_), channel_id=1, source_target_pairs={{0,4},{1,5},{2,6},{3,7},{4,0},{5,1},{6,2},{7,3},{8,12},{9,13},{10,... | collective-permute-start | bytes 786440 | tf_op jit(solution)/shard_map/ppermute | solution.py:549
  71.0 12.7 %collective-permute-start.5 = (bf16[128,1024]{1,0:T(8,128)(2,1)S(1)}, bf16[128,1024]{1,0:T(8,128)(2,1)}, u32[]{:S(2)}, u32[]{:S(2)}) collective-permute-start(bf16[128,1024]{1,0:T(8,128)(2,1)S(1)} %get-tuple-element.70.refs_0_), channel_id=1, source_target_pairs={{0,2},{1,3},{2,0},{3,1},{4,6},{5,7},{6,4},{7,5},{8,10},{9,11},{10,... | collective-permute-start | bytes 786440 | tf_op jit(solution)/shard_map/ppermute | solution.py:549
  82.5 16.9 %collective-permute-start.4 = (bf16[512,1536]{1,0:T(8,128)(2,1)}, bf16[512,1536]{1,0:T(8,128)(2,1)S(1)}, u32[]{:S(2)}, u32[]{:S(2)}) collective-permute-start(bf16[512,1536]{1,0:T(8,128)(2,1)} %get-tuple-element.39), channel_id=1, source_target_pairs={{0,1},{1,0},{2,3},{3,2},{4,5},{5,4},{6,7},{7,6},{8,9},{9,8},{10,11... | collective-permute-start | bytes 4718600 | tf_op jit(solution)/shard_map/ppermute | solution.py:549
  85.8 12.0 %collective-permute-start.26 = (bf16[32,1024]{1,0:T(8,128)(2,1)S(1)}, bf16[32,1024]{1,0:T(8,128)(2,1)S(1)}, u32[]{:S(2)}, u32[]{:S(2)}) collective-permute-start(bf16[32,1024]{1,0:T(8,128)(2,1)S(1)} %get-tuple-element.77.refs_2_), channel_id=1, source_target_pairs={{0,24},{1,25},{2,26},{3,27},{4,28},{5,29},{6,30},{7,31},{8,16},{9,... | collective-permute-start | bytes 196616 | tf_op jit(solution)/shard_map/ppermute | solution.py:549
  87.0 10.8 %collective-permute-start.25 = (bf16[32,1024]{1,0:T(8,128)(2,1)S(1)}, bf16[32,1024]{1,0:T(8,128)(2,1)S(1)}, u32[]{:S(2)}, u32[]{:S(2)}) collective-permute-start(bf16[32,1024]{1,0:T(8,128)(2,1)S(1)} %get-tuple-element.78.refs_1_), channel_id=1, source_target_pairs={{0,16},{1,17},{2,18},{3,19},{4,20},{5,21},{6,22},{7,23},{8,24},{9,... | collective-permute-start | bytes 196616 | tf_op jit(solution)/shard_map/ppermute | solution.py:549
  87.0 12.4 %copy-start.1 = (bf16[512,1536]{1,0:T(8,128)(2,1)S(1)}, bf16[512,1536]{1,0:T(8,128)(2,1)}, u32[]{:S(2)}) copy-start(bf16[512,1536]{1,0:T(8,128)(2,1)} %get-tuple-element.38) | copy-start | bytes 4718596
  87.0 10.8 %collective-permute-start.24 = (bf16[32,1024]{1,0:T(8,128)(2,1)S(1)}, bf16[32,1024]{1,0:T(8,128)(2,1)S(1)}, u32[]{:S(2)}, u32[]{:S(2)}) collective-permute-start(bf16[32,1024]{1,0:T(8,128)(2,1)S(1)} %get-tuple-element.79.refs_0_), channel_id=1, source_target_pairs={{0,8},{1,9},{2,10},{3,11},{4,12},{5,13},{6,14},{7,15},{8,0},{9,1},... | collective-permute-start | bytes 196616 | tf_op jit(solution)/shard_map/ppermute | solution.py:549
  101.0 14.4 %collective-permute-start.11 = (bf16[128,1536]{1,0:T(8,128)(2,1)}, bf16[128,1536]{1,0:T(8,128)(2,1)S(1)}, u32[]{:S(2)}, u32[]{:S(2)}) collective-permute-start(bf16[128,1536]{1,0:T(8,128)(2,1)} %get-tuple-element.65.refs_2_), channel_id=1, source_target_pairs={{0,6},{1,7},{2,4},{3,5},{4,2},{5,3},{6,0},{7,1},{8,14},{9,15},{10,... | collective-permute-start | bytes 1179656 | tf_op jit(solution)/shard_map/ppermute | solution.py:549
  102.5 18.2 %collective-permute-start.10 = (bf16[128,1536]{1,0:T(8,128)(2,1)}, bf16[128,1536]{1,0:T(8,128)(2,1)S(1)}, u32[]{:S(2)}, u32[]{:S(2)}) collective-permute-start(bf16[128,1536]{1,0:T(8,128)(2,1)} %get-tuple-element.66.refs_1_), channel_id=1, source_target_pairs={{0,4},{1,5},{2,6},{3,7},{4,0},{5,1},{6,2},{7,3},{8,12},{9,13},{10,... | collective-permute-start | bytes 1179656 | tf_op jit(solution)/shard_map/ppermute | solution.py:549
  103.9 17.6 %collective-permute-start.9 = (bf16[128,1536]{1,0:T(8,128)(2,1)}, bf16[128,1536]{1,0:T(8,128)(2,1)}, u32[]{:S(2)}, u32[]{:S(2)}) collective-permute-start(bf16[128,1536]{1,0:T(8,128)(2,1)} %get-tuple-element.67.refs_0_), channel_id=1, source_target_pairs={{0,2},{1,3},{2,0},{3,1},{4,6},{5,7},{6,4},{7,5},{8,10},{9,11},{10,... | collective-permute-start | bytes 1179656 | tf_op jit(solution)/shard_map/ppermute | solution.py:549
  115.4 22.1 %collective-permute-start.8 = (bf16[512,1536]{1,0:T(8,128)(2,1)}, bf16[512,1536]{1,0:T(8,128)(2,1)S(1)}, u32[]{:S(2)}, u32[]{:S(2)}) collective-permute-start(bf16[512,1536]{1,0:T(8,128)(2,1)} %get-tuple-element.41), channel_id=1, source_target_pairs={{0,1},{1,0},{2,3},{3,2},{4,5},{5,4},{6,7},{7,6},{8,9},{9,8},{10,11... | collective-permute-start | bytes 4718600 | tf_op jit(solution)/shard_map/ppermute | solution.py:549
  123.8 11.4 %copy-start.9 = (bf16[32,1536]{1,0:T(8,128)(2,1)}, bf16[32,1536]{1,0:T(8,128)(2,1)S(1)}, u32[]{:S(2)}) copy-start(bf16[32,1536]{1,0:T(8,128)(2,1)S(1)} %get-tuple-element.74.refs_5_) | copy-start | bytes 294916
  123.8 11.4 %copy-start.10 = (bf16[32,1536]{1,0:T(8,128)(2,1)}, bf16[32,1536]{1,0:T(8,128)(2,1)S(1)}, u32[]{:S(2)}) copy-start(bf16[32,1536]{1,0:T(8,128)(2,1)S(1)} %get-tuple-element.75.refs_4_) | copy-start | bytes 294916
  123.8 11.5 %collective-permute-start.17 = (bf16[32,1536]{1,0:T(8,128)(2,1)S(1)}, bf16[32,1536]{1,0:T(8,128)(2,1)}, u32[]{:S(2)}, u32[]{:S(2)}) collective-permute-start(bf16[32,1536]{1,0:T(8,128)(2,1)S(1)} %get-tuple-element.74.refs_5_), channel_id=1, source_target_pairs={{0,24},{1,25},{2,26},{3,27},{4,28},{5,29},{6,30},{7,31},{8,16},{9,... | collective-permute-start | bytes 294920 | tf_op jit(solution)/shard_map/ppermute | solution.py:549
  124.9 10.3 %collective-permute-start.16 = (bf16[32,1536]{1,0:T(8,128)(2,1)S(1)}, bf16[32,1536]{1,0:T(8,128)(2,1)}, u32[]{:S(2)}, u32[]{:S(2)}) collective-permute-start(bf16[32,1536]{1,0:T(8,128)(2,1)S(1)} %get-tuple-element.75.refs_4_), channel_id=1, source_target_pairs={{0,16},{1,17},{2,18},{3,19},{4,20},{5,21},{6,22},{7,23},{8,24},{9,... | collective-permute-start | bytes 294920 | tf_op jit(solution)/shard_map/ppermute | solution.py:549
  125.6 9.6 %collective-permute-start.15 = (bf16[32,1536]{1,0:T(8,128)(2,1)}, bf16[32,1536]{1,0:T(8,128)(2,1)}, u32[]{:S(2)}, u32[]{:S(2)}) collective-permute-start(bf16[32,1536]{1,0:T(8,128)(2,1)} %get-tuple-element.76.refs_3_), channel_id=1, source_target_pairs={{0,8},{1,9},{2,10},{3,11},{4,12},{5,13},{6,14},{7,15},{8,0},{9,1},... | collective-permute-start | bytes 294920 | tf_op jit(solution)/shard_map/ppermute | solution.py:549
  128.2 9.4 %copy-start = (bf16[512,1536]{1,0:T(8,128)(2,1)S(1)}, bf16[512,1536]{1,0:T(8,128)(2,1)}, u32[]{:S(2)}) copy-start(bf16[512,1536]{1,0:T(8,128)(2,1)} %get-tuple-element.40) | copy-start | bytes 4718596
  138.7 17.3 %collective-permute-start.20 = (bf16[128,1536]{1,0:T(8,128)(2,1)}, bf16[128,1536]{1,0:T(8,128)(2,1)S(1)}, u32[]{:S(2)}, u32[]{:S(2)}) collective-permute-start(bf16[128,1536]{1,0:T(8,128)(2,1)} %get-tuple-element.62.refs_2_), channel_id=1, source_target_pairs={{0,6},{1,7},{2,4},{3,5},{4,2},{5,3},{6,0},{7,1},{8,14},{9,15},{10,... | collective-permute-start | bytes 1179656 | tf_op jit(solution)/shard_map/ppermute | solution.py:549
  140.2 18.5 %collective-permute-start.19 = (bf16[128,1536]{1,0:T(8,128)(2,1)}, bf16[128,1536]{1,0:T(8,128)(2,1)S(1)}, u32[]{:S(2)}, u32[]{:S(2)}) collective-permute-start(bf16[128,1536]{1,0:T(8,128)(2,1)} %get-tuple-element.63.refs_1_), channel_id=1, source_target_pairs={{0,4},{1,5},{2,6},{3,7},{4,0},{5,1},{6,2},{7,3},{8,12},{9,13},{10,... | collective-permute-start | bytes 1179656 | tf_op jit(solution)/shard_map/ppermute | solution.py:549
  141.6 18.3 %collective-permute-start.18 = (bf16[128,1536]{1,0:T(8,128)(2,1)}, bf16[128,1536]{1,0:T(8,128)(2,1)}, u32[]{:S(2)}, u32[]{:S(2)}) collective-permute-start(bf16[128,1536]{1,0:T(8,128)(2,1)} %get-tuple-element.64.refs_0_), channel_id=1, source_target_pairs={{0,2},{1,3},{2,0},{3,1},{4,6},{5,7},{6,4},{7,5},{8,10},{9,11},{10,... | collective-permute-start | bytes 1179656 | tf_op jit(solution)/shard_map/ppermute | solution.py:549
  153.4 9.6 %collective-permute-start.14 = (bf16[48,1024]{1,0:T(8,128)(2,1)}, bf16[48,1024]{1,0:T(8,128)(2,1)S(1)}, u32[]{:S(2)}, u32[]{:S(2)}) collective-permute-start(bf16[48,1024]{1,0:T(8,128)(2,1)} %get-tuple-element.51), channel_id=1, source_target_pairs={{0,31},{1,24},{2,25},{3,26},{4,27},{5,28},{6,29},{7,30},{8,7},{9,0... | collective-permute-start | bytes 294920 | tf_op jit(solution)/shard_map/ppermute | solution.py:520
  153.7 11.3 %collective-permute-start.12 = (bf16[128,1024]{1,0:T(8,128)(2,1)}, bf16[128,1024]{1,0:T(8,128)(2,1)}, u32[]{:S(2)}, u32[]{:S(2)}) collective-permute-start(bf16[128,1024]{1,0:T(8,128)(2,1)} %get-tuple-element.49), channel_id=1, source_target_pairs={{0,7},{1,0},{2,1},{3,2},{4,3},{5,4},{6,5},{7,6},{8,15},{9,8},{10,9... | collective-permute-start | bytes 786440 | tf_op jit(solution)/shard_map/ppermute | solution.py:520
  156.0 14.7 %collective-permute-start.13 = (bf16[208,1024]{1,0:T(8,128)(2,1)}, bf16[208,1024]{1,0:T(8,128)(2,1)}, u32[]{:S(2)}, u32[]{:S(2)}) collective-permute-start(bf16[208,1024]{1,0:T(8,128)(2,1)} %get-tuple-element.50), channel_id=1, source_target_pairs={{0,24},{1,25},{2,26},{3,27},{4,28},{5,29},{6,30},{7,31},{8,0},{9,1... | collective-permute-start | bytes 1277960 | tf_op jit(solution)/shard_map/ppermute | solution.py:520
  161.4 13.4 %collective-permute-start.21 = (bf16[32,1536]{1,0:T(8,128)(2,1)S(1)}, bf16[32,1536]{1,0:T(8,128)(2,1)S(1)}, u32[]{:S(2)}, u32[]{:S(2)}) collective-permute-start(bf16[32,1536]{1,0:T(8,128)(2,1)S(1)} %get-tuple-element.71), channel_id=1, source_target_pairs={{0,8},{1,9},{2,10},{3,11},{4,12},{5,13},{6,14},{7,15},{8,0},{9,1},... | collective-permute-start | bytes 294920 | tf_op jit(solution)/shard_map/ppermute | solution.py:549
  161.5 13.3 %collective-permute-start.23 = (bf16[32,1536]{1,0:T(8,128)(2,1)S(1)}, bf16[32,1536]{1,0:T(8,128)(2,1)S(1)}, u32[]{:S(2)}, u32[]{:S(2)}) collective-permute-start(bf16[32,1536]{1,0:T(8,128)(2,1)S(1)} %get-tuple-element.72), channel_id=1, source_target_pairs={{0,24},{1,25},{2,26},{3,27},{4,28},{5,29},{6,30},{7,31},{8,16},{9,... | collective-permute-start | bytes 294920 | tf_op jit(solution)/shard_map/ppermute | solution.py:549
  162.9 12.7 %collective-permute-start.22 = (bf16[32,1536]{1,0:T(8,128)(2,1)S(1)}, bf16[32,1536]{1,0:T(8,128)(2,1)S(1)}, u32[]{:S(2)}, u32[]{:S(2)}) collective-permute-start(bf16[32,1536]{1,0:T(8,128)(2,1)S(1)} %get-tuple-element.73), channel_id=1, source_target_pairs={{0,16},{1,17},{2,18},{3,19},{4,20},{5,21},{6,22},{7,23},{8,24},{9,... | collective-permute-start | bytes 294920 | tf_op jit(solution)/shard_map/ppermute | solution.py:549
  (15 other events, 63.8 us)

commit v4 on v3

--- a/solution.py
+++ b/solution.py
@@ -16,7 +16,6 @@
 TILE = 256
 EPSILON = 1e-05
 MIB = 1 << 20
-PARTS = 4
 
 NN = (((1,), (0,)), ((), ()))
 NT = (((1,), (1,)), ((), ()))
@@ -121,9 +120,9 @@
 
 
 def forward_kernel(
-    edge, owner, tokens, merged_grad, side, above, corner, order, group, rowmap,
+    owner, edge, tokens, merged_grad, side, above, corner, order, group,
     wqkv_h, wout_h, wm_h,
-    normed_h, normt_h, proj_h, dmr_h, dmm_h, grad_h, rstd, merged, out_mine, out_theirs,
+    normed_h, normt_h, proj_h, dmr_h, dmm_h, grad_h, rstd, merged, out_terms,
     wqkv, wout, wm, source, xw, normed, normt, proj, mixture, inverse, subs, dsubs, cotangent,
     grad, dmr, dmm, turned, in_sem, out_sem,
 ):
@@ -133,7 +132,7 @@
     per_row = windows // 2
     quarter = places // 4
     groups = count // 4
-    devices = owner.shape[0]
+    devices = len(owner)
     block = channels // devices
 
     loads = [
@@ -283,182 +282,139 @@
     stores[5].start()
 
     def turn(field, out):
-        if block % 16:
-            @pl.loop(0, channels // TILE)
-            def _(n):
-                rows = aligned(n * TILE, TILE)
-                spot = lax.broadcasted_iota(jnp.int32, (TILE, channels), 1)
-                pick = jnp.where(spot == rowmap[rows], 1.0, 0.0).astype(BF16)
-                out[rows] = dot(pick, field[...], NT).astype(BF16)
-        else:
-            @pl.loop(0, channels // TILE)
-            def _(n):
-                rows = aligned(n * TILE, TILE)
-                turned[rows] = field[:, rows].T
-
-            for d in range(devices):
-                out[d * block:(d + 1) * block] = turned[aligned(owner[d] * block, block)]
+        @pl.loop(0, channels // TILE)
+        def _(n):
+            rows = aligned(n * TILE, TILE)
+            turned[rows] = field[:, rows].T
+
+        for d in range(devices):
+            out[d * block:(d + 1) * block] = turned[owner[d] * block:(owner[d] + 1) * block]
 
     turn(normed, normt)
     stores[2].start()
     mixt = wqkv.at[:, :count]
     turn(mixture, mixt)
-    part = channels // 2
 
     @pl.loop(0, channels // TILE)
     def _(n):
         columns = aligned(n * TILE, TILE)
-        out_mine[:, columns] = dot(mixt[:part], grad[:, columns]).astype(BF16)
-        out_theirs[:, columns] = dot(mixt[part:], grad[:, columns]).astype(BF16)
+        out_terms[:, columns] = dot(mixt[...], grad[:, columns]).astype(BF16)
 
     for store in stores:
         store.wait()
 
 
-def backward_kernel(index, waits, summing, *refs):
-    refs = refs[waits:]
-    edge, proj_h, dmr_h, dmm_h, normt_h = refs[:5]
-    if summing:
-        before_h, pgrad_h, mine_h, theirs_h, held, pgrad, normt, mine, theirs = refs[5:14]
-        in_sem, sem, out_sem = refs[14:]
-    else:
-        pgrad_h, held, pgrad, in_sem, sem, out_sem = refs[5:]
-    _, count, width = held.shape
-    channels = dmr_h.shape[1]
+def backward_kernel(
+    edge, proj_h, dmr_h, dmm_h, normt_h, pgrad_h, terms_h,
+    proj, dmr, dmm, normt, pgrad, terms, in_sem, sem, out_sem,
+):
+    count, channels = dmr.shape
     places = 2 * WIN * WIN
     windows = count // places
     per_row = windows // 2
     masks = head_masks()
     factor = score_scale(channels)
     plain = (channels // HEADS) ** -0.5
-    first = 3 * width if summing else 0
-
-    def loads(w):
-        rows = aligned(w * places, places)
+    width = TILE
+    steps = channels // width
+
+    def loads(g):
         for i in range(5):
-            field, start = (proj_h, i * channels) if i < 3 else ((dmr_h, dmm_h)[i - 3], 0)
-            columns = pl.ds(start + index * width, width)
-            yield pltpu.make_async_copy(field.at[rows, columns], held.at[i, rows], in_sem.at[w, i])
-
-    for w in range(windows):
-        for load in loads(w):
+            src, dst = ((proj_h, proj), (dmr_h, dmr), (dmm_h, dmm))[max(i - 2, 0)]
+            columns = aligned((i * channels if i < 3 else 0) + g * width, width)
+            yield pltpu.make_async_copy(src.at[:, columns], dst.at[:, columns], in_sem.at[g, i])
+
+    def stores(g):
+        for i in range(3):
+            columns = aligned(i * channels + g * width, width)
+            yield pltpu.make_async_copy(pgrad.at[:, columns], pgrad_h.at[:, columns], out_sem.at[0, g, i])
+            yield pltpu.make_async_copy(terms.at[:, columns], terms_h.at[:, columns], out_sem.at[1, g, i])
+
+    for g in range(steps):
+        for load in loads(g):
             load.start()
-    if summing:
-        extra = [
-            pltpu.make_async_copy(normt_h, normt, sem.at[0]),
-            pltpu.make_async_copy(before_h, pgrad.at[:, pl.ds(0, first)], sem.at[1]),
-        ]
-        for load in extra:
-            load.start()
-
-    @pl.loop(0, windows)
-    def _(w):
-        for load in loads(w):
+    turned_load = pltpu.make_async_copy(normt_h, normt, sem.at[0])
+    turned_load.start()
+    edge_bias = region_bias(places, edge[0] == 1)
+
+    @pl.loop(0, steps)
+    def _(g):
+        for load in loads(g):
             load.wait()
-        rows = aligned(w * places, places)
-        bias = region_bias(places, (edge[0] == 1) & (w < per_row))
-        for g in range(width // LANES):
-            lanes = pl.ds(g * LANES, LANES)
-            q, k, v, dm, dd = (held[i, rows, lanes] for i in range(5))
-            keys = jnp.concatenate([k * m for m in masks], axis=0)
-            scores = dot(keys, q, NT)
-            values = jnp.concatenate(
-                [jnp.concatenate([v * m, m], axis=1) for m in masks], axis=0
-            )
-            slope = dot(values, jnp.concatenate([dm, dd], axis=1), NT)
-            weights, slopes = [], []
-            for h in range(4):
-                block = slice(h * places, (h + 1) * places)
-                part = scores[block] * factor + bias
-                part = jnp.exp2(part - jnp.max(part, axis=0, keepdims=True))
-                weights.append(part.astype(BF16))
-                slopes.append((part * slope[block]).astype(BF16))
-            dv = dot(
-                jnp.concatenate(weights, axis=1),
-                jnp.concatenate([dm * m for m in masks], axis=0),
-            )
-            dk = dot(
-                jnp.concatenate(slopes, axis=1),
-                jnp.concatenate([q * m for m in masks], axis=0),
-            )
-            dq = dot(jnp.concatenate(slopes, axis=0), keys, TN)
-            at = first + g * LANES
-            pgrad[rows, pl.ds(at, LANES)] = (dq * plain).astype(BF16)
-            pgrad[rows, pl.ds(at + width, LANES)] = (dk * plain).astype(BF16)
-            pgrad[rows, pl.ds(at + 2 * width, LANES)] = dv.astype(BF16)
-
-    stores = [pltpu.make_async_copy(pgrad.at[:, pl.ds(first, 3 * width)], pgrad_h, out_sem.at[0])]
-    stores[0].start()
-    if summing:
-        for load in extra:
-            load.wait()
-        half = channels // 2
-        for n in range(2 * first // TILE):
-            columns = pl.ds(n * TILE, TILE)
-            right = pgrad[:, columns]
-            mine[:, columns] = dot(normt[:half], right).astype(BF16)
-            theirs[:, columns] = dot(normt[half:], right).astype(BF16)
-        stores += [
-            pltpu.make_async_copy(mine, mine_h, out_sem.at[1]),
-            pltpu.make_async_copy(theirs, theirs_h, out_sem.at[2]),
-        ]
-        stores[1].start()
-        stores[2].start()
-    for store in stores:
-        store.wait()
-
-
-def projection_back(pgrads, wqkv_h, pgrad, wqkv, sem, start):
-    width = pgrads[0].shape[1] // 3
-    channels = wqkv_h.shape[1] // 3
-    rows = pl.ds(start, wqkv.shape[0])
-    loads = []
-    for c, field in enumerate(pgrads):
-        at = 3 * width * c
-        loads.append(pltpu.make_async_copy(field, pgrad.at[:, pl.ds(at, 3 * width)], sem.at[c, 3]))
+
+        for half in range(width // LANES):
+            at = [aligned(i * channels + g * width + half * LANES, LANES) for i in range(3)]
+            for w in range(windows):
+                rows = slice(w * places, (w + 1) * places)
+                q, k, v = (proj[rows, at[i]] for i in range(3))
+                dm, dd = dmr[rows, at[0]], dmm[rows, at[0]]
+                keys = jnp.concatenate([k * m for m in masks], axis=0)
+                scores = dot(keys, q, NT)
+                values = jnp.concatenate(
+                    [jnp.concatenate([v * m, m], axis=1) for m in masks], axis=0
+                )
+                slope = dot(values, jnp.concatenate([dm, dd], axis=1), NT)
+                weights, slopes = [], []
+                for h in range(4):
+                    block = slice(h * places, (h + 1) * places)
+                    part = scores[block] * factor
+                    if w < per_row:
+                        part = part + edge_bias
+                    part = jnp.exp2(part - jnp.max(part, axis=0, keepdims=True))
+                    weights.append(part.astype(BF16))
+                    slopes.append((part * slope[block]).astype(BF16))
+                dv = dot(
+                    jnp.concatenate(weights, axis=1),
+                    jnp.concatenate([dm * m for m in masks], axis=0),
+                )
+                dk = dot(
+                    jnp.concatenate(slopes, axis=1),
+                    jnp.concatenate([q * m for m in masks], axis=0),
+                )
+                dq = dot(jnp.concatenate(slopes, axis=0), keys, TN)
+                pgrad[rows, at[0]] = (dq * plain).astype(BF16)
+                pgrad[rows, at[1]] = (dk * plain).astype(BF16)
+                pgrad[rows, at[2]] = dv.astype(BF16)
+
+        @pl.when(g == 0)
+        def _():
+            turned_load.wait()
+
         for i in range(3):
-            loads.append(pltpu.make_async_copy(
-                wqkv_h.at[rows, pl.ds(i * channels + c * width, width)],
-                wqkv.at[:, pl.ds(at + i * width, width)], sem.at[c, i],
-            ))
-    for load in loads:
+            columns = aligned(i * channels + g * width, width)
+            terms[:, columns] = dot(normt[...], pgrad[:, columns]).astype(BF16)
+        for store in stores(g):
+            store.start()
+
+    for g in range(steps):
+        for store in stores(g):
+            store.wait()
+
+
+def input_kernel(
+    pgrad_h, wqkv_h, normed_h, rstd_h, grad_h, merged, pick_first, pick_last, pick_groups,
+    full, side, below, corner, pgrad, wqkv, ngrad, normed, rstd, grad, sem,
+):
+    count, channels = ngrad.shape
+    tiles = channels // TILE
+
+    def rows_of(n):
+        return pl.ds(n * TILE, TILE)
+
+    loads = [pltpu.make_async_copy(pgrad_h, pgrad, sem.at[0])] + [
+        pltpu.make_async_copy(wqkv_h.at[rows_of(n)], wqkv.at[rows_of(n)], sem.at[1 + n])
+        for n in range(tiles)
+    ]
+    more = [
+        pltpu.make_async_copy(src, dst, sem.at[1 + tiles + i])
+        for i, (src, dst) in enumerate([(normed_h, normed), (rstd_h, rstd), (grad_h, grad)])
+    ]
+    for load in loads + more:
         load.start()
-    return loads
-
-
-def input_first_kernel(waits, *refs):
-    pgrads = refs[waits:waits + PARTS]
-    wqkv_h, ngrad, pgrad, wqkv, sem = refs[waits + PARTS:]
-    for load in projection_back(pgrads, wqkv_h, pgrad, wqkv, sem, 0):
-        load.wait()
-    for n in range(wqkv.shape[0] // TILE):
-        rows = slice(n * TILE, (n + 1) * TILE)
-        ngrad[:, rows] = dot(pgrad[...], wqkv[rows], NT).astype(BF16)
-
-
-def input_last_kernel(waits, *refs):
-    pgrads = refs[waits:waits + PARTS]
-    (wqkv_h, nfirst_h, normed_h, rstd_h, grad_h, merged, pick_first, pick_last, pick_groups,
-     full, side, below, corner,
-     pgrad, wqkv, ngrad, normed, rstd, grad, sem, more_sem) = refs[waits + PARTS:]
-    count, channels = ngrad.shape
-    half = channels // 2
-    loads = projection_back(pgrads, wqkv_h, pgrad, wqkv, sem, half)
-    more = [
-        pltpu.make_async_copy(src, dst, more_sem.at[i])
-        for i, (src, dst) in enumerate(
-            [(nfirst_h, ngrad.at[:, pl.ds(0, half)]), (normed_h, normed), (rstd_h, rstd), (grad_h, grad)]
-        )
-    ]
-    for load in more:
-        load.start()
-    for load in loads:
-        load.wait()
-    for n in range(half // TILE):
-        rows = slice(n * TILE, (n + 1) * TILE)
-        ngrad[:, half + n * TILE:half + (n + 1) * TILE] = dot(
-            pgrad[...], wqkv[rows], NT
-        ).astype(BF16)
+    loads[0].wait()
+    for n in range(tiles):
+        loads[1 + n].wait()
+        ngrad[:, rows_of(n)] = dot(pgrad[...], wqkv[rows_of(n)], NT).astype(BF16)
     for load in more:
         load.wait()
     places = 2 * WIN * WIN
@@ -527,63 +483,14 @@
 
 def device_rows(channels, sizes):
     n_lat, n_lon = sizes
-    devices = n_lat * n_lon
-    rows = channels // devices
-    place = np.arange(devices)
-    lon = 2 * (place // n_lat % (n_lon // 2)) + place // (devices // 2)
-    lat = place % n_lat
-    owner = (
-        jnp.bitwise_xor(lax.axis_index("lat").astype(jnp.int32), jnp.asarray(lat, jnp.int32)) * n_lon
-        + jnp.bitwise_xor(lax.axis_index("lon").astype(jnp.int32), jnp.asarray(lon, jnp.int32))
-    )
-    rowmap = owner[:, None] * rows + jnp.arange(rows, dtype=jnp.int32)[None, :]
-    return owner, rowmap.reshape(channels, 1)
-
-
-def exchange(block, sizes, lat_bits, lon_bits):
-    n_lat, n_lon = sizes
-    route = [
-        (a * n_lon + b, (a ^ lat_bits) * n_lon + (b ^ lon_bits))
-        for a in range(n_lat) for b in range(n_lon)
-    ]
-    return lax.ppermute(block, ("lat", "lon"), route)
-
-
-def core_step(theirs, sizes):
-    return exchange(theirs, sizes, 0, 1)
-
-
-def layer_blocks(mine, arrived, sizes):
-    blocks = sizes[1] // 2
-    rows = mine.shape[0] // blocks
-    total = [
-        (mine[i * rows:(i + 1) * rows].astype(F32) + arrived[i * rows:(i + 1) * rows].astype(F32))
-        for i in range(blocks)
-    ]
-    return [total[0]] + [t.astype(BF16) for t in total[1:]]
-
-
-def layer_step(blocks, sizes):
-    return [exchange(b, sizes, 0, 2 * i) for i, b in enumerate(blocks) if i]
-
-
-def column_blocks(kept, arrived, sizes):
-    total = kept
-    for block in arrived:
-        total = total + block.astype(F32)
-    rows = total.shape[0] // sizes[0]
-    blocks = [total[i * rows:(i + 1) * rows] for i in range(sizes[0])]
-    return [blocks[0]] + [b.astype(BF16) for b in blocks[1:]]
-
-
-def column_step(blocks, sizes):
-    return [exchange(b, sizes, i, 0) for i, b in enumerate(blocks) if i]
-
-
-def finished(kept, arrived):
-    for block in arrived:
-        kept = kept + block.astype(F32)
-    return kept
+    place = np.arange(n_lat * n_lon)
+    return place % n_lat * n_lon + place // n_lat
+
+
+def summed(terms):
+    part = lax.psum_scatter(terms, "lon", scatter_dimension=0, tiled=True)
+    part = lax.psum_scatter(part, "lat", scatter_dimension=0, tiled=True)
+    return part.astype(F32)
 
 
 def shards(sizes, tokens, qkv_weight, out_weight, merge_weight, merged_grad):
@@ -591,7 +498,6 @@
     merged_width = merge_weight.shape[1]
     count = levels * lat_rows * lon_cols
     groups = count // 4
-    half = channels // 2
     strip_rows.extent = (lat_rows, lon_cols)
     vmem = pl.BlockSpec(memory_space=pltpu.VMEM)
     smem = pl.BlockSpec(memory_space=pltpu.SMEM)
@@ -645,18 +551,18 @@
     order = jnp.concatenate([picks(cells[:half_cells], held_top), picks(cells[half_cells:], held_low)])
     group = picks(grps, g_own + sum(g_strips, []))
     edge = (lax.axis_index("lat") == 0).astype(jnp.int32).reshape(1)
-    owner, rowmap = device_rows(channels, sizes)
+    owner = tuple(int(d) for d in device_rows(channels, sizes))
 
     wide = shape(count, channels)
-    normed, normt, proj, dmr, dmm, grad, rstd, merged, out_mine, out_theirs = pl.pallas_call(
-        forward_kernel,
+    normed, normt, proj, dmr, dmm, grad, rstd, merged, out_terms = pl.pallas_call(
+        functools.partial(forward_kernel, owner),
         out_shape=[
             wide, shape(channels, count), shape(count, 3 * channels), wide, wide, wide,
             shape(count, LANES, dtype=F32), shape(groups, merged_width),
-            shape(half, channels), shape(half, channels),
+            shape(channels, channels),
         ],
-        in_specs=[smem, smem] + [vmem] * 8 + [hbm] * 3,
-        out_specs=[hbm] * 6 + [vmem] * 4,
+        in_specs=[smem] + [vmem] * 7 + [hbm] * 3,
+        out_specs=[hbm] * 6 + [vmem] * 3,
         scratch_shapes=[
             pltpu.VMEM(qkv_weight.shape, BF16),
             pltpu.VMEM(out_weight.shape, BF16),
@@ -679,94 +585,50 @@
             pltpu.SemaphoreType.DMA((6,)),
         ],
         name="block_forward", **settings(30),
-    )(edge, owner, tokens_flat, merged_grad_flat, *strips, order, group, rowmap,
+    )(edge, tokens_flat, merged_grad_flat, *strips, order, group,
       qkv_weight, out_weight, merge_weight)
 
-    width = channels // PARTS
-
-    def backward(index, before, after):
-        summing = before is not None
-        outs = [shape(count, 3 * width)]
-        scratch = [
-            pltpu.VMEM((5, count, width), BF16),
-            pltpu.VMEM((count, (6 if summing else 3) * width), BF16),
-        ]
-        if summing:
-            outs += [shape(half, 6 * width)] * 2
-            scratch += [
-                pltpu.VMEM((channels, count), BF16),
-                pltpu.VMEM((half, 6 * width), BF16),
-                pltpu.VMEM((half, 6 * width), BF16),
-            ]
-        scratch += [
-            pltpu.SemaphoreType.DMA((count // (2 * WIN * WIN), 5)),
-            pltpu.SemaphoreType.DMA((2,)),
-            pltpu.SemaphoreType.DMA((3,)),
-        ]
-        operands = [edge, proj, dmr, dmm, normt] + ([before] if summing else [])
-        return pl.pallas_call(
-            functools.partial(backward_kernel, index, len(after), summing),
-            out_shape=outs,
-            in_specs=[hbm] * len(after) + [smem] + [hbm] * (len(operands) - 1),
-            out_specs=[hbm] * len(outs),
-            scratch_shapes=scratch,
-            name="attention_backward", **settings(10 if summing else 6),
-        )(*after, *operands)
-
-    arrived = core_step(out_theirs, sizes)
-    (pg0,) = backward(0, None, [])
-    out_layer = layer_blocks(out_mine, arrived, sizes)
-    arrived = layer_step(out_layer, sizes)
-    pg1, mine1, theirs1 = backward(1, pg0, out_layer[1:])
-    out_column = column_blocks(out_layer[0], arrived, sizes)
-    out_arrived = column_step(out_column, sizes)
-    arrived = core_step(theirs1, sizes)
-    (pg2,) = backward(2, None, out_column[1:])
-    layer1 = layer_blocks(mine1, arrived, sizes)
-    arrived1 = layer_step(layer1, sizes)
-    pg3, mine2, theirs2 = backward(3, pg2, layer1[1:])
-    arrived2 = core_step(theirs2, sizes)
-    pgrads = [pg0, pg1, pg2, pg3]
-
-    in_scratch = [
-        pltpu.VMEM((count, 3 * channels), BF16),
-        pltpu.VMEM((half, 3 * channels), BF16),
-    ]
-    in_sems = pltpu.SemaphoreType.DMA((PARTS, 4))
-    nfirst = pl.pallas_call(
-        functools.partial(input_first_kernel, 0),
-        out_shape=shape(count, half),
-        in_specs=[hbm] * (PARTS + 1), out_specs=vmem,
-        scratch_shapes=in_scratch + [in_sems],
-        name="input_first", **settings(5),
-    )(*pgrads, qkv_weight)
-    column1 = column_blocks(layer1[0], arrived1, sizes)
-    column_arrived1 = column_step(column1, sizes)
-    layer2 = layer_blocks(mine2, arrived2, sizes)
-    arrived2 = layer_step(layer2, sizes)
-    after = layer2[1:] + column1[1:]
+    out_weight_grad = summed(out_terms)
+
+    steps = channels // TILE
+    pgrad, terms = pl.pallas_call(
+        backward_kernel,
+        out_shape=[shape(count, 3 * channels), shape(channels, 3 * channels)],
+        in_specs=[smem] + [hbm] * 4, out_specs=[hbm] * 2,
+        scratch_shapes=[
+            pltpu.VMEM((count, 3 * channels), BF16),
+            pltpu.VMEM((count, channels), BF16),
+            pltpu.VMEM((count, channels), BF16),
+            pltpu.VMEM((channels, count), BF16),
+            pltpu.VMEM((count, 3 * channels), BF16),
+            pltpu.VMEM((channels, 3 * channels), BF16),
+            pltpu.SemaphoreType.DMA((steps, 5)),
+            pltpu.SemaphoreType.DMA((1,)),
+            pltpu.SemaphoreType.DMA((2, steps, 3)),
+        ],
+        name="attention_backward", **settings(30),
+    )(edge, proj, dmr, dmm, normt)
+    qkv_weight_grad = summed(terms)
 
     first_picks = picks(cs.side[:side_cut] + cs.above + cs.corner, cells[:half_cells])
     last_picks = picks(cs.side[side_cut:], cells[half_cells:])
     full, *strips = pl.pallas_call(
-        functools.partial(input_last_kernel, len(after)),
+        input_kernel,
         out_shape=[wide] + [shape(*e) for e in extents],
-        in_specs=[hbm] * (len(after) + PARTS + 5) + [vmem] * 4, out_specs=[vmem] * 4,
-        scratch_shapes=in_scratch + [
+        in_specs=[hbm] * 5 + [vmem] * 4, out_specs=[vmem] * 4,
+        scratch_shapes=[
+            pltpu.VMEM((count, 3 * channels), BF16),
+            pltpu.VMEM(qkv_weight.shape, BF16),
             pltpu.VMEM((count, channels), BF16),
             pltpu.VMEM((count, channels), BF16),
             pltpu.VMEM((count, LANES), F32),
             pltpu.VMEM((count, channels), BF16),
-            in_sems,
-            pltpu.SemaphoreType.DMA((4,)),
+            pltpu.SemaphoreType.DMA((4 + steps,)),
         ],
-        name="input_last", **settings(9),
-    )(*after, *pgrads, qkv_weight, nfirst, normed, rstd, grad, merged,
+        name="input_backward", **settings(12),
+    )(pgrad, qkv_weight, normed, rstd, grad, merged,
       first_picks, last_picks, picks(sum(g_strips, []), grps))
     strips = sent_strips(strips, sizes, -1)
-
-    column2 = column_blocks(layer2[0], arrived2, sizes)
-    column_arrived2 = column_step(column2, sizes)
 
     got = [Strips.sent(s, *t) for s, t in zip((cs.side, cs.above, cs.corner), to)]
     g_got = sum((Strips.sent(s, *t) for s, t in zip(g_strips, g_to)), [])
@@ -784,13 +646,6 @@
     )
     merged = merged.reshape(levels, g_cols, g_rows, merged_width).transpose(0, 2, 1, 3)
 
-    out_weight_grad = finished(out_column[0], out_arrived)
-    parts = [finished(column1[0], column_arrived1), finished(column2[0], column_arrived2)]
-    pieces = [
-        part[:, (3 * i + kind) * width:(3 * i + kind + 1) * width]
-        for kind in range(3) for part in parts for i in range(2)
-    ]
-    qkv_weight_grad = jnp.concatenate(pieces, axis=1)
     return merged, tokens_grad.reshape(tokens.shape), qkv_weight_grad, out_weight_grad
 
 

time: 182 us -> 226 us (1.24)
  waiting for transfers between devices: 26.1 us -> 108 us
  starting transfers between devices: 31.6 us -> 11.1 us
  between operations: 0.94 us -> 13.9 us
  Pallas kernels: 99 us -> 87.8 us
  local copies, waits for them, and re-layouts: 11.9 us -> 1.68 us
  other arithmetic: 12.3 us -> 3.2 us
    reduce_scatter x0 -> x4, waiting for transfers between devices: none -> 95.8 us  [the longest x2 56.6 us: summed(): part = lax.psum_scatter(terms, 'lon', scatter_dimension=0, tiled=True)]
    ppermute x21 -> x0, starting transfers between devices: 23.1 us -> none  [exchange(): return lax.ppermute(block, ('lat', 'lon'), route)]
    pallas_call x7 -> x3, Pallas kernels: 91.8 us -> 80.5 us  [the longest x1 36.3 us: shards(): pl.pallas_call(functools.partial(forward_kernel, owner), out_shape=[wide,...]
    ppermute x21 -> x0, waiting for transfers between devices: 10 us -> none  [exchange(): return lax.ppermute(block, ('lat', 'lon'), route)]
    unnamed x51 -> x12, local copies, waits for them, and re-layouts: 9.23 us -> 1.68 us
    another operation x3 -> x0, other arithmetic: 5.22 us -> none
    ppermute x6, waiting for transfers between devices: 16.1 us -> 12.2 us  [sent(): return lax.ppermute(block, ('lat', 'lon'), route)]
    add x4 -> x0, other arithmetic: 2.74 us -> none  [the longest x3 2.67 us: finished(): kept = kept + block.astype(F32)]
  transfers between devices with their start and end apart: 27 -> 10, of which waited for: 10 -> 5; matrix products, arithmetic and copies ran while one was open for 6% -> 1% of each run, Pallas kernels for 33% -> 21%
where the time goes in v4:
time: 226 us
  waiting for transfers between devices  108 us (48%)
  Pallas kernels  87.8 us (39%)
  between operations  13.9 us (6%)
  starting transfers between devices  11.1 us (5%)
  other arithmetic  3.2 us (1%)
    reduce_scatter x2, waiting for transfers between devices, summed(): part = lax.psum_scatter(terms, 'lon', scatter_dimension=0, tiled=True)  56.6 us
    reduce_scatter x2, waiting for transfers between devices, summed(): part = lax.psum_scatter(part, 'lat', scatter_dimension=0, tiled=True)  39.3 us
    pallas_call x1, Pallas kernels, shards(): pl.pallas_call(functools.partial(forward_kernel, owner), out_shape=[wide,...  36.3 us
    pallas_call x1, Pallas kernels, shards(): pl.pallas_call(backward_kernel, out_shape=[shape(count, 3 * channels), sh...  26.5 us
    pallas_call x1, Pallas kernels, shards(): pl.pallas_call(input_kernel, out_shape=[wide] + [shape(*e) for e in exten...  17.7 us
    ppermute x6, waiting for transfers between devices, sent(): return lax.ppermute(block, ('lat', 'lon'), route)  12.2 us
    ppermute x6, starting transfers between devices, sent(): return lax.ppermute(block, ('lat', 'lon'), route)  10.7 us
  transfers between devices with their start and end apart: 10, of which 5 were waited for; matrix products, arithmetic and copies ran while one was open for 1% of the time, Pallas kernels for 21%

profile of v4, /device:TPU:0, one launch (start us, length us, event | category | flops | bytes accessed | tf_op | source)
XLA Modules:
  0.0 225.6 jit_solution(11194607436456583741)
XLA Ops:
  7.2 0.0 reduce-scatter.9.cloned.1.call-start
  7.2 3.1 %pack_strips.1 = (bf16[128,1024]{1,0:T(8,128)(2,1)}, bf16[208,1024]{1,0:T(8,128)(2,1)}, bf16[48,1024]{1,0:T(8,128)(2,1)}) custom-call(bf16[768,1024]{1,0:T(8,128)(2,1)} %bitcast.9, bf16[192,1024]{1,0:T(8,128)(2,1)} %bitcast.11, bf16[288,768]{1,0:T(8,128)(2,1)} %constant.31.clone.pick_cells, bf16[96,192]{1,0:T(8,128)(2,1)} %constant.32.clone.pick_groups), custom_call_target="tpu_custom_call" | custom-call | flops 10000000000 | bytes 16777216 | tf_op jit(solution)/shard_map/pack_strips/pallas_call | solution.py:543
  10.3 3.0 %collective-permute-start.1 = (bf16[208,1024]{1,0:T(8,128)(2,1)}, bf16[208,1024]{1,0:T(8,128)(2,1)S(1)}, u32[]{:S(2)}, u32[]{:S(2)}) collective-permute-start(bf16[208,1024]{1,0:T(8,128)(2,1)} %get-tuple-element.25), channel_id=1, source_target_pairs={{0,8},{1,9},{2,10},{3,11},{4,12},{5,13},{6,14},{7,15},{8,16},{9,17... | collective-permute-start | bytes 1277960 | tf_op jit(solution)/shard_map/ppermute | solution.py:476
  13.4 2.8 %collective-permute-start.2 = (bf16[48,1024]{1,0:T(8,128)(2,1)}, bf16[48,1024]{1,0:T(8,128)(2,1)S(1)}, u32[]{:S(2)}, u32[]{:S(2)}) collective-permute-start(bf16[48,1024]{1,0:T(8,128)(2,1)} %get-tuple-element.26), channel_id=1, source_target_pairs={{0,9},{1,10},{2,11},{3,12},{4,13},{5,14},{6,15},{7,8},{8,17},{9,18... | collective-permute-start | bytes 294920 | tf_op jit(solution)/shard_map/ppermute | solution.py:476
  16.2 12.2 %collective-permute-done.2.corner = bf16[48,1024]{1,0:T(8,128)(2,1)S(1)} collective-permute-done((bf16[48,1024]{1,0:T(8,128)(2,1)}, bf16[48,1024]{1,0:T(8,128)(2,1)S(1)}, u32[]{:S(2)}, u32[]{:S(2)}) %collective-permute-start.2) | collective-permute-done | bytes 98336 | tf_op jit(solution)/shard_map/ppermute | solution.py:476
  28.3 0.6 copy-done.4
  29.0 0.1 copy-done.2
  29.1 0.1 copy-done
  29.2 36.3 %block_forward.1 = (bf16[768,1024]{1,0:T(8,128)(2,1)}, bf16[1024,768]{1,0:T(8,128)(2,1)}, bf16[768,3072]{1,0:T(8,128)(2,1)}, bf16[768,1024]{1,0:T(8,128)(2,1)}, ...) custom-call(s32[1]{0:T(128)} %bitcast.edge, ...), custom_call_target="tpu_custom_call" | custom-call | flops 299999985664 | bytes 16777216 | tf_op jit(solution)/shard_map/block_forward/pallas_call | solution.py:557
  65.5 0.0 reduce-scatter.9.cloned.1.call-update
  65.5 0.2 reduce-scatter.5.cloned.1.call-start
  65.8 26.5 %attention_backward.1 = (bf16[768,3072]{1,0:T(8,128)(2,1)}, bf16[1024,3072]{1,0:T(8,128)(2,1)}) custom-call(s32[1]{0:T(128)} %bitcast.edge, bf16[768,3072]{1,0:T(8,128)(2,1)} %get-tuple-element.27.proj_h, bf16[768,1024]{1,0:T(8,128)(2,1)} %get-tuple-element.28.dmr_h, bf16[768,1024]{1,0:T(8,128)(2,1)} %get-tuple-element.29.dmm_h, ...), custom_call_target="tpu_custom_call" | custom-call | flops 299999985664 | bytes 16777216 | tf_op jit(solution)/shard_map/attention_backward/pallas_call | solution.py:594
  92.3 0.0 reduce-scatter.5.cloned.1.call-update
  92.3 0.0 reduce-scatter.11.cloned.1.call-start
  92.4 12.6 %reduce-scatter.9.cloned.1.call-done = bf16[128,1024]{1,0:T(8,128)(2,1)} async-done(((bf16[1024,1024]{1,0:T(8,128)(2,1)}), bf16[128,1024]{1,0:T(8,128)(2,1)}) %reduce-scatter.9.cloned.1.call-update) | async-done | bytes 262160 | tf_op jit(solution)/shard_map/reduce_scatter | solution.py:491
  105.0 0.0 reduce-scatter.11.cloned.1.call-update
  105.0 0.0 reduce-scatter.7.cloned.1.call-start
  105.1 17.7 %input_backward.1 = (bf16[768,1024]{1,0:T(8,128)(2,1)}, bf16[128,1024]{1,0:T(8,128)(2,1)}, bf16[208,1024]{1,0:T(8,128)(2,1)}, bf16[48,1024]{1,0:T(8,128)(2,1)}) custom-call(bf16[768,3072]{1,0:T(8,128)(2,1)} %get-tuple-element.31.pgrad_h, bf16[1024,3072]{1,0:T(8,128)(2,1)} %wqkv_h.3, bf16[768,1024]{1,0:T(8,128)(2,1)} %get-tuple-element.32.normed_h, ...), custom_call_target="tpu_custom_call" | custom-call | flops 120000004096 | bytes 16777216 | tf_op jit(solution)/shard_map/input_backward/pallas_call | solution.py:615
  122.8 3.4 %collective-permute-start.4 = (bf16[208,1024]{1,0:T(8,128)(2,1)}, bf16[208,1024]{1,0:T(8,128)(2,1)S(1)}, u32[]{:S(2)}, u32[]{:S(2)}) collective-permute-start(bf16[208,1024]{1,0:T(8,128)(2,1)} %get-tuple-element.38), channel_id=1, source_target_pairs={{0,24},{1,25},{2,26},{3,27},{4,28},{5,29},{6,30},{7,31},{8,0},{9,1... | collective-permute-start | bytes 1277960 | tf_op jit(solution)/shard_map/ppermute | solution.py:476
  126.1 0.6 collective-permute-start.3
  126.8 0.9 collective-permute-start.5
  127.7 44.0 %reduce-scatter.5.cloned.1.call-done = bf16[128,3072]{1,0:T(8,128)(2,1)} async-done(((bf16[1024,3072]{1,0:T(8,128)(2,1)}), bf16[128,3072]{1,0:T(8,128)(2,1)}) %reduce-scatter.5.cloned.1.call-update) | async-done | bytes 786448 | tf_op jit(solution)/shard_map/reduce_scatter | solution.py:491
  171.6 0.0 reduce-scatter.7.cloned.1.call-update
  171.7 0.0 copy-start.3
  171.7 0.6 copy-done.5
  172.3 0.1 copy-done.3
  172.4 0.1 copy-done.1
  172.5 4.1 %unpack_strips.1 = (bf16[768,1024]{1,0:T(8,128)(2,1)}, bf16[192,1024]{1,0:T(8,128)(2,1)}) custom-call(bf16[768,1024]{1,0:T(8,128)(2,1)} %get-tuple-element.36.full, bf16[192,1024]{1,0:T(8,128)(2,1)} %get-tuple-element.35.merged, bf16[128,1024]{1,0:T(8,128)(2,1)} %copy-done.3, bf16[208,1024]{1,0:T(8,128)(2,1)} %copy-done.1, bf16[48,1024]{1,0:T(8,128)(2,1)} %copy-done.5, ...), custom_call_target="tpu_custom_call" | custom-call | flops 20000000000 | bytes 16777216 | tf_op jit(solution)/shard_map/unpack_strips/pallas_call | solution.py:635
  176.6 16.9 %reduce-scatter.11.cloned.1.call-done = bf16[32,1024]{1,0:T(8,128)(2,1)} async-done(((bf16[128,1024]{1,0:T(8,128)(2,1)}), bf16[32,1024]{1,0:T(8,128)(2,1)}) %reduce-scatter.11.cloned.1.call-update) | async-done | bytes 65552 | tf_op jit(solution)/shard_map/reduce_scatter | solution.py:492
  193.6 1.5 convert_element_type.8
  195.1 22.3 %reduce-scatter.7.cloned.1.call-done = bf16[32,3072]{1,0:T(8,128)(2,1)} async-done(((bf16[128,3072]{1,0:T(8,128)(2,1)}), bf16[32,3072]{1,0:T(8,128)(2,1)}) %reduce-scatter.7.cloned.1.call-update) | async-done | bytes 196624 | tf_op jit(solution)/shard_map/reduce_scatter | solution.py:492
  217.4 1.7 convert_element_type.7
  (11 shorter events, 0.0 us)
Async XLA Ops:
  7.2 97.8 %reduce-scatter.9.cloned.1.call-start = ((), (), s32[]{:S(2)}) async-start(), calls=%async_computation.6 | async-start | bytes 2359296 | tf_op jit(solution)/shard_map/reduce_scatter | solution.py:491
  10.3 18.0 %collective-permute-start.1 = (bf16[208,1024]{1,0:T(8,128)(2,1)}, bf16[208,1024]{1,0:T(8,128)(2,1)S(1)}, u32[]{:S(2)}, u32[]{:S(2)}) collective-permute-start(bf16[208,1024]{1,0:T(8,128)(2,1)} %get-tuple-element.25), channel_id=1, source_target_pairs={{0,8},{1,9},{2,10},{3,11},{4,12},{5,13},{6,14},{7,15},{8,16},{9,17... | collective-permute-start | bytes 1277960 | tf_op jit(solution)/shard_map/ppermute | solution.py:476
  13.4 15.0 %collective-permute-start = (bf16[128,1024]{1,0:T(8,128)(2,1)}, bf16[128,1024]{1,0:T(8,128)(2,1)S(1)}, u32[]{:S(2)}, u32[]{:S(2)}) collective-permute-start(bf16[128,1024]{1,0:T(8,128)(2,1)} %get-tuple-element.24), channel_id=1, source_target_pairs={{0,1},{1,2},{2,3},{3,4},{4,5},{5,6},{6,7},{7,0},{8,9},{9,10},{10,1... | collective-permute-start | bytes 786440 | tf_op jit(solution)/shard_map/ppermute | solution.py:476
  13.4 14.9 %collective-permute-start.2 = (bf16[48,1024]{1,0:T(8,128)(2,1)}, bf16[48,1024]{1,0:T(8,128)(2,1)S(1)}, u32[]{:S(2)}, u32[]{:S(2)}) collective-permute-start(bf16[48,1024]{1,0:T(8,128)(2,1)} %get-tuple-element.26), channel_id=1, source_target_pairs={{0,9},{1,10},{2,11},{3,12},{4,13},{5,14},{6,15},{7,8},{8,17},{9,18... | collective-permute-start | bytes 294920 | tf_op jit(solution)/shard_map/ppermute | solution.py:476
  28.3 0.6 copy-start.4
  28.3 0.7 copy-start.2
  28.3 0.9 copy-start
  65.5 106.1 %reduce-scatter.5.cloned.1.call-start = ((), (), s32[]{:S(2)}) async-start(), calls=%async_computation.4 | async-start | bytes 7077888 | tf_op jit(solution)/shard_map/reduce_scatter | solution.py:491
  92.3 101.2 %reduce-scatter.11.cloned.1.call-start = ((), (), s32[]{:S(2)}) async-start(), calls=%async_computation.7 | async-start | bytes 327680 | tf_op jit(solution)/shard_map/reduce_scatter | solution.py:492
  105.0 112.4 %reduce-scatter.7.cloned.1.call-start = ((), (), s32[]{:S(2)}) async-start(), calls=%async_computation.5 | async-start | bytes 983040 | tf_op jit(solution)/shard_map/reduce_scatter | solution.py:492
  122.8 48.9 %collective-permute-start.4 = (bf16[208,1024]{1,0:T(8,128)(2,1)}, bf16[208,1024]{1,0:T(8,128)(2,1)S(1)}, u32[]{:S(2)}, u32[]{:S(2)}) collective-permute-start(bf16[208,1024]{1,0:T(8,128)(2,1)} %get-tuple-element.38), channel_id=1, source_target_pairs={{0,24},{1,25},{2,26},{3,27},{4,28},{5,29},{6,30},{7,31},{8,0},{9,1... | collective-permute-start | bytes 1277960 | tf_op jit(solution)/shard_map/ppermute | solution.py:476
  126.1 45.6 %collective-permute-start.3 = (bf16[128,1024]{1,0:T(8,128)(2,1)}, bf16[128,1024]{1,0:T(8,128)(2,1)S(1)}, u32[]{:S(2)}, u32[]{:S(2)}) collective-permute-start(bf16[128,1024]{1,0:T(8,128)(2,1)} %get-tuple-element.37), channel_id=1, source_target_pairs={{0,7},{1,0},{2,1},{3,2},{4,3},{5,4},{6,5},{7,6},{8,15},{9,8},{10,9... | collective-permute-start | bytes 786440 | tf_op jit(solution)/shard_map/ppermute | solution.py:476
  126.8 44.9 %collective-permute-start.5 = (bf16[48,1024]{1,0:T(8,128)(2,1)}, bf16[48,1024]{1,0:T(8,128)(2,1)S(1)}, u32[]{:S(2)}, u32[]{:S(2)}) collective-permute-start(bf16[48,1024]{1,0:T(8,128)(2,1)} %get-tuple-element.39), channel_id=1, source_target_pairs={{0,31},{1,24},{2,25},{3,26},{4,27},{5,28},{6,29},{7,30},{8,7},{9,0... | collective-permute-start | bytes 294920 | tf_op jit(solution)/shard_map/ppermute | solution.py:476
  171.7 0.6 copy-start.5
  171.7 0.7 copy-start.3
  171.7 0.8 copy-start.1
Sparse Core Ops, SparseCore 0:
  65.7 39.2 reduce-scatter.8
  108.8 62.8 reduce-scatter.4
  173.9 19.6 reduce-scatter.10
  195.8 21.5 reduce-scatter.6

commit v5 on v4

--- a/solution.py
+++ b/solution.py
@@ -120,9 +120,9 @@
 
 
 def forward_kernel(
-    owner, edge, tokens, merged_grad, side, above, corner, order, group,
+    owner, edge, core, tokens, merged_grad, side, above, corner, order, group,
     wqkv_h, wout_h, wm_h,
-    normed_h, normt_h, proj_h, dmr_h, dmm_h, grad_h, rstd, merged, out_terms,
+    normed_h, normt_h, proj_h, dmr_h, dmm_h, grad_h, rstd, merged, out_mine, out_theirs,
     wqkv, wout, wm, source, xw, normed, normt, proj, mixture, inverse, subs, dsubs, cotangent,
     grad, dmr, dmm, turned, in_sem, out_sem,
 ):
@@ -294,41 +294,49 @@
     stores[2].start()
     mixt = wqkv.at[:, :count]
     turn(mixture, mixt)
+    own = aligned(core[0] * (channels // 2), channels // 2)
+    other = aligned((1 - core[0]) * (channels // 2), channels // 2)
 
     @pl.loop(0, channels // TILE)
     def _(n):
         columns = aligned(n * TILE, TILE)
-        out_terms[:, columns] = dot(mixt[...], grad[:, columns]).astype(BF16)
+        out_mine[:, columns] = dot(mixt[own], grad[:, columns]).astype(BF16)
+        out_theirs[:, columns] = dot(mixt[other], grad[:, columns]).astype(BF16)
 
     for store in stores:
         store.wait()
 
 
 def backward_kernel(
-    edge, proj_h, dmr_h, dmm_h, normt_h, pgrad_h, terms_h,
-    proj, dmr, dmm, normt, pgrad, terms, in_sem, sem, out_sem,
+    index, waits, *refs,
 ):
-    count, channels = dmr.shape
+    (edge, core, proj_h, dmr_h, dmm_h, normt_h, pgrad_h, mine_h, theirs_h,
+     held, normt, pgrad, mine, theirs, in_sem, sem, out_sem) = refs[waits:]
+    _, count, width = held.shape
+    channels = normt.shape[0]
+    half = channels // 2
     places = 2 * WIN * WIN
     windows = count // places
     per_row = windows // 2
     masks = head_masks()
     factor = score_scale(channels)
     plain = (channels // HEADS) ** -0.5
-    width = TILE
-    steps = channels // width
+    steps = width // TILE
 
     def loads(g):
+        columns = aligned(g * TILE, TILE)
         for i in range(5):
-            src, dst = ((proj_h, proj), (dmr_h, dmr), (dmm_h, dmm))[max(i - 2, 0)]
-            columns = aligned((i * channels if i < 3 else 0) + g * width, width)
-            yield pltpu.make_async_copy(src.at[:, columns], dst.at[:, columns], in_sem.at[g, i])
+            src = (proj_h, proj_h, proj_h, dmr_h, dmm_h)[i]
+            start = (i * channels if i < 3 else 0) + index * width
+            yield pltpu.make_async_copy(
+                src.at[:, aligned(start + g * TILE, TILE)], held.at[i, :, columns], in_sem.at[g, i]
+            )
 
     def stores(g):
         for i in range(3):
-            columns = aligned(i * channels + g * width, width)
-            yield pltpu.make_async_copy(pgrad.at[:, columns], pgrad_h.at[:, columns], out_sem.at[0, g, i])
-            yield pltpu.make_async_copy(terms.at[:, columns], terms_h.at[:, columns], out_sem.at[1, g, i])
+            columns = aligned(i * width + g * TILE, TILE)
+            for j, (src, dst) in enumerate(((pgrad, pgrad_h), (mine, mine_h), (theirs, theirs_h))):
+                yield pltpu.make_async_copy(src.at[:, columns], dst.at[:, columns], out_sem.at[g, i, j])
 
     for g in range(steps):
         for load in loads(g):
@@ -336,18 +344,19 @@
     turned_load = pltpu.make_async_copy(normt_h, normt, sem.at[0])
     turned_load.start()
     edge_bias = region_bias(places, edge[0] == 1)
+    own = aligned(core[0] * half, half)
+    other = aligned((1 - core[0]) * half, half)
 
     @pl.loop(0, steps)
     def _(g):
         for load in loads(g):
             load.wait()
 
-        for half in range(width // LANES):
-            at = [aligned(i * channels + g * width + half * LANES, LANES) for i in range(3)]
+        for part_of in range(TILE // LANES):
+            lanes = aligned(g * TILE + part_of * LANES, LANES)
             for w in range(windows):
                 rows = slice(w * places, (w + 1) * places)
-                q, k, v = (proj[rows, at[i]] for i in range(3))
-                dm, dd = dmr[rows, at[0]], dmm[rows, at[0]]
+                q, k, v, dm, dd = (held[i, rows, lanes] for i in range(5))
                 keys = jnp.concatenate([k * m for m in masks], axis=0)
                 scores = dot(keys, q, NT)
                 values = jnp.concatenate(
@@ -372,17 +381,19 @@
                     jnp.concatenate([q * m for m in masks], axis=0),
                 )
                 dq = dot(jnp.concatenate(slopes, axis=0), keys, TN)
-                pgrad[rows, at[0]] = (dq * plain).astype(BF16)
-                pgrad[rows, at[1]] = (dk * plain).astype(BF16)
-                pgrad[rows, at[2]] = dv.astype(BF16)
+                at = g * TILE + part_of * LANES
+                pgrad[rows, lanes] = (dq * plain).astype(BF16)
+                pgrad[rows, aligned(width + at, LANES)] = (dk * plain).astype(BF16)
+                pgrad[rows, aligned(2 * width + at, LANES)] = dv.astype(BF16)
 
         @pl.when(g == 0)
         def _():
             turned_load.wait()
 
         for i in range(3):
-            columns = aligned(i * channels + g * width, width)
-            terms[:, columns] = dot(normt[...], pgrad[:, columns]).astype(BF16)
+            columns = aligned(i * width + g * TILE, TILE)
+            mine[:, columns] = dot(normt[own], pgrad[:, columns]).astype(BF16)
+            theirs[:, columns] = dot(normt[other], pgrad[:, columns]).astype(BF16)
         for store in stores(g):
             store.start()
 
@@ -391,30 +402,60 @@
             store.wait()
 
 
-def input_kernel(
-    pgrad_h, wqkv_h, normed_h, rstd_h, grad_h, merged, pick_first, pick_last, pick_groups,
-    full, side, below, corner, pgrad, wqkv, ngrad, normed, rstd, grad, sem,
-):
+def projection_loads(pgrads, wqkv_h, pgrad, wqkv, sem, start):
+    width = pgrads[0].shape[1] // 3
+    channels = pgrad.shape[1] // 3
+    loads = [
+        pltpu.make_async_copy(
+            field.at[:, pl.ds(i * width, width)],
+            pgrad.at[:, pl.ds(i * channels + c * width, width)], sem.at[c * 3 + i],
+        )
+        for c, field in enumerate(pgrads) for i in range(3)
+    ]
+    tiles = [
+        pltpu.make_async_copy(
+            wqkv_h.at[pl.ds(start + n * TILE, TILE)], wqkv.at[pl.ds(n * TILE, TILE)],
+            sem.at[3 * len(pgrads) + n],
+        )
+        for n in range(wqkv.shape[0] // TILE)
+    ]
+    for load in loads + tiles:
+        load.start()
+    return loads, tiles
+
+
+def input_first_kernel(pg0, pg1, wqkv_h, ngrad, pgrad, wqkv, sem):
+    loads, tiles = projection_loads([pg0, pg1], wqkv_h, pgrad, wqkv, sem, 0)
+    for load in loads:
+        load.wait()
+    for n, load in enumerate(tiles):
+        load.wait()
+        rows = pl.ds(n * TILE, TILE)
+        ngrad[:, rows] = dot(pgrad[...], wqkv[rows], NT).astype(BF16)
+
+
+def input_last_kernel(waits, *refs):
+    (pg0, pg1, wqkv_h, nfirst_h, normed_h, rstd_h, grad_h, merged,
+     pick_first, pick_last, pick_groups, full, side, below, corner,
+     pgrad, wqkv, ngrad, normed, rstd, grad, sem, more_sem) = refs[waits:]
     count, channels = ngrad.shape
-    tiles = channels // TILE
-
-    def rows_of(n):
-        return pl.ds(n * TILE, TILE)
-
-    loads = [pltpu.make_async_copy(pgrad_h, pgrad, sem.at[0])] + [
-        pltpu.make_async_copy(wqkv_h.at[rows_of(n)], wqkv.at[rows_of(n)], sem.at[1 + n])
-        for n in range(tiles)
-    ]
+    half = channels // 2
+    loads, tiles = projection_loads([pg0, pg1], wqkv_h, pgrad, wqkv, sem, half)
     more = [
-        pltpu.make_async_copy(src, dst, sem.at[1 + tiles + i])
-        for i, (src, dst) in enumerate([(normed_h, normed), (rstd_h, rstd), (grad_h, grad)])
-    ]
-    for load in loads + more:
+        pltpu.make_async_copy(src, dst, more_sem.at[i])
+        for i, (src, dst) in enumerate(
+            [(nfirst_h, ngrad.at[:, pl.ds(0, half)]), (normed_h, normed), (rstd_h, rstd), (grad_h, grad)]
+        )
+    ]
+    for load in more:
         load.start()
-    loads[0].wait()
-    for n in range(tiles):
-        loads[1 + n].wait()
-        ngrad[:, rows_of(n)] = dot(pgrad[...], wqkv[rows_of(n)], NT).astype(BF16)
+    for load in loads:
+        load.wait()
+    for n, load in enumerate(tiles):
+        load.wait()
+        ngrad[:, pl.ds(half + n * TILE, TILE)] = dot(
+            pgrad[...], wqkv[pl.ds(n * TILE, TILE)], NT
+        ).astype(BF16)
     for load in more:
         load.wait()
     places = 2 * WIN * WIN
@@ -484,13 +525,31 @@
 def device_rows(channels, sizes):
     n_lat, n_lon = sizes
     place = np.arange(n_lat * n_lon)
-    return place % n_lat * n_lon + place // n_lat
-
-
-def summed(terms):
-    part = lax.psum_scatter(terms, "lon", scatter_dimension=0, tiled=True)
-    part = lax.psum_scatter(part, "lat", scatter_dimension=0, tiled=True)
-    return part.astype(F32)
+    chips = n_lon // 2
+    return place % n_lat * n_lon + place // n_lat % chips * 2 + place // (n_lat * chips)
+
+
+def core_step(theirs, sizes):
+    n_lat, n_lon = sizes
+    return lax.ppermute(theirs, ("lat", "lon"), [(i, i ^ 1) for i in range(n_lat * n_lon)])
+
+
+def core_sum(mine, arrived):
+    return (mine.astype(F32) + arrived.astype(F32)).astype(BF16)
+
+
+def layer_step(total, sizes):
+    cores = [list(range(c, sizes[1], 2)) for c in range(2)]
+    return lax.all_to_all(total, "lon", 0, 0, axis_index_groups=cores, tiled=True)
+
+
+def column_step(total, sizes):
+    return lax.all_to_all(total, "lat", 0, 0, tiled=True)
+
+
+def block_sum(blocks, count, dtype=BF16):
+    blocks = blocks.reshape(count, blocks.shape[0] // count, blocks.shape[1]).astype(F32)
+    return jnp.sum(blocks, axis=0).astype(dtype)
 
 
 def shards(sizes, tokens, qkv_weight, out_weight, merge_weight, merged_grad):
@@ -498,17 +557,19 @@
     merged_width = merge_weight.shape[1]
     count = levels * lat_rows * lon_cols
     groups = count // 4
+    half = channels // 2
     strip_rows.extent = (lat_rows, lon_cols)
     vmem = pl.BlockSpec(memory_space=pltpu.VMEM)
     smem = pl.BlockSpec(memory_space=pltpu.SMEM)
     hbm = pl.BlockSpec(memory_space=pl.ANY)
+    pinned = pl.BlockSpec(memory_space=pltpu.HBM)
 
     def shape(*extent, dtype=BF16):
         return jax.ShapeDtypeStruct(extent, dtype)
 
-    def settings(weight):
+    def settings(weight, limit=60):
         return dict(
-            compiler_params=pltpu.CompilerParams(vmem_limit_bytes=60 * MIB),
+            compiler_params=pltpu.CompilerParams(vmem_limit_bytes=limit * MIB),
             cost_estimate=pl.CostEstimate(
                 flops=int(weight * 1e10), bytes_accessed=16 * MIB, transcendentals=0
             ),
@@ -551,18 +612,19 @@
     order = jnp.concatenate([picks(cells[:half_cells], held_top), picks(cells[half_cells:], held_low)])
     group = picks(grps, g_own + sum(g_strips, []))
     edge = (lax.axis_index("lat") == 0).astype(jnp.int32).reshape(1)
+    core = (lax.axis_index("lon") % 2).astype(jnp.int32).reshape(1)
     owner = tuple(int(d) for d in device_rows(channels, sizes))
 
     wide = shape(count, channels)
-    normed, normt, proj, dmr, dmm, grad, rstd, merged, out_terms = pl.pallas_call(
+    normed, normt, proj, dmr, dmm, grad, rstd, merged, out_mine, out_theirs = pl.pallas_call(
         functools.partial(forward_kernel, owner),
         out_shape=[
             wide, shape(channels, count), shape(count, 3 * channels), wide, wide, wide,
             shape(count, LANES, dtype=F32), shape(groups, merged_width),
-            shape(channels, channels),
+            shape(half, channels), shape(half, channels),
         ],
-        in_specs=[smem] + [vmem] * 7 + [hbm] * 3,
-        out_specs=[hbm] * 6 + [vmem] * 3,
+        in_specs=[smem] * 2 + [vmem] * 7 + [hbm] * 3,
+        out_specs=[hbm] * 6 + [vmem] * 4,
         scratch_shapes=[
             pltpu.VMEM(qkv_weight.shape, BF16),
             pltpu.VMEM(out_weight.shape, BF16),
@@ -584,51 +646,84 @@
             pltpu.SemaphoreType.DMA((3,)),
             pltpu.SemaphoreType.DMA((6,)),
         ],
-        name="block_forward", **settings(30),
-    )(edge, tokens_flat, merged_grad_flat, *strips, order, group,
+        name="block_forward", **settings(30, 54),
+    )(edge, core, tokens_flat, merged_grad_flat, *strips, order, group,
       qkv_weight, out_weight, merge_weight)
 
-    out_weight_grad = summed(out_terms)
-
-    steps = channels // TILE
-    pgrad, terms = pl.pallas_call(
-        backward_kernel,
-        out_shape=[shape(count, 3 * channels), shape(channels, 3 * channels)],
-        in_specs=[smem] + [hbm] * 4, out_specs=[hbm] * 2,
-        scratch_shapes=[
-            pltpu.VMEM((count, 3 * channels), BF16),
-            pltpu.VMEM((count, channels), BF16),
-            pltpu.VMEM((count, channels), BF16),
-            pltpu.VMEM((channels, count), BF16),
-            pltpu.VMEM((count, 3 * channels), BF16),
-            pltpu.VMEM((channels, 3 * channels), BF16),
-            pltpu.SemaphoreType.DMA((steps, 5)),
-            pltpu.SemaphoreType.DMA((1,)),
-            pltpu.SemaphoreType.DMA((2, steps, 3)),
-        ],
-        name="attention_backward", **settings(30),
-    )(edge, proj, dmr, dmm, normt)
-    qkv_weight_grad = summed(terms)
+    halves = 2
+    width = channels // halves
+    steps = width // TILE
+
+    def backward(index, after):
+        return pl.pallas_call(
+            functools.partial(backward_kernel, index, len(after)),
+            out_shape=[shape(count, 3 * width), shape(half, 3 * width), shape(half, 3 * width)],
+            in_specs=[hbm] * len(after) + [smem] * 2 + [pinned] * 4, out_specs=[hbm] * 3,
+            scratch_shapes=[
+                pltpu.VMEM((5, count, width), BF16),
+                pltpu.VMEM((channels, count), BF16),
+                pltpu.VMEM((count, 3 * width), BF16),
+                pltpu.VMEM((half, 3 * width), BF16),
+                pltpu.VMEM((half, 3 * width), BF16),
+                pltpu.SemaphoreType.DMA((steps, 5)),
+                pltpu.SemaphoreType.DMA((1,)),
+                pltpu.SemaphoreType.DMA((steps, 3, 3)),
+            ],
+            name="attention_backward", **settings(15, 30),
+        )(*after, edge, core, proj, dmr, dmm, normt)
+
+    chips, layers = sizes[1] // 2, sizes[0]
+    arrived = core_step(out_theirs, sizes)
+    pg0, mine1, theirs1 = backward(0, [])
+    total0 = core_sum(out_mine, arrived)
+    blocks0 = layer_step(total0, sizes)
+    arrived = core_step(theirs1, sizes)
+    pg1, mine2, theirs2 = backward(1, [total0])
+    total0 = block_sum(blocks0, chips)
+    blocks0 = column_step(total0, sizes)
+    total1 = core_sum(mine1, arrived)
+    blocks1 = layer_step(total1, sizes)
+    arrived = core_step(theirs2, sizes)
+
+    in_scratch = [
+        pltpu.VMEM((count, 3 * channels), BF16),
+        pltpu.VMEM((half, 3 * channels), BF16),
+    ]
+    in_sems = pltpu.SemaphoreType.DMA((3 * halves + half // TILE,))
+    nfirst = pl.pallas_call(
+        input_first_kernel,
+        out_shape=shape(count, half),
+        in_specs=[hbm] * 3, out_specs=vmem,
+        scratch_shapes=in_scratch + [in_sems],
+        name="input_first", **settings(5, 30),
+    )(pg0, pg1, qkv_weight)
+    total2 = core_sum(mine2, arrived)
+    blocks2 = layer_step(total2, sizes)
+    after = [total1, total2]
 
     first_picks = picks(cs.side[:side_cut] + cs.above + cs.corner, cells[:half_cells])
     last_picks = picks(cs.side[side_cut:], cells[half_cells:])
     full, *strips = pl.pallas_call(
-        input_kernel,
+        functools.partial(input_last_kernel, len(after)),
         out_shape=[wide] + [shape(*e) for e in extents],
-        in_specs=[hbm] * 5 + [vmem] * 4, out_specs=[vmem] * 4,
-        scratch_shapes=[
-            pltpu.VMEM((count, 3 * channels), BF16),
-            pltpu.VMEM(qkv_weight.shape, BF16),
+        in_specs=[hbm] * (len(after) + 7) + [vmem] * 4, out_specs=[vmem] * 4,
+        scratch_shapes=in_scratch + [
             pltpu.VMEM((count, channels), BF16),
             pltpu.VMEM((count, channels), BF16),
             pltpu.VMEM((count, LANES), F32),
             pltpu.VMEM((count, channels), BF16),
-            pltpu.SemaphoreType.DMA((4 + steps,)),
+            in_sems,
+            pltpu.SemaphoreType.DMA((4,)),
         ],
-        name="input_backward", **settings(12),
-    )(pgrad, qkv_weight, normed, rstd, grad, merged,
+        name="input_last", **settings(9, 36),
+    )(*after, pg0, pg1, qkv_weight, nfirst, normed, rstd, grad, merged,
       first_picks, last_picks, picks(sum(g_strips, []), grps))
     strips = sent_strips(strips, sizes, -1)
+
+    total1 = block_sum(blocks1, chips)
+    blocks1 = column_step(total1, sizes)
+    total2 = block_sum(blocks2, chips)
+    blocks2 = column_step(total2, sizes)
 
     got = [Strips.sent(s, *t) for s, t in zip((cs.side, cs.above, cs.corner), to)]
     g_got = sum((Strips.sent(s, *t) for s, t in zip(g_strips, g_to)), [])
@@ -646,6 +741,11 @@
     )
     merged = merged.reshape(levels, g_cols, g_rows, merged_width).transpose(0, 2, 1, 3)
 
+    out_weight_grad = block_sum(blocks0, layers, F32)
+    parts = [block_sum(blocks1, layers, F32), block_sum(blocks2, layers, F32)]
+    qkv_weight_grad = jnp.concatenate(
+        [part[:, i * width:(i + 1) * width] for i in range(3) for part in parts], axis=1
+    )
     return merged, tokens_grad.reshape(tokens.shape), qkv_weight_grad, out_weight_grad
 
 

time: 226 us -> 216 us (0.956)
  waiting for transfers between devices: 108 us -> 45.7 us
  local copies, waits for them, and re-layouts: 1.68 us -> 28.9 us
  starting transfers between devices: 11.1 us -> 36.2 us
  other arithmetic: 3.2 us -> 16.8 us
  between operations: 13.9 us -> 0.97 us
    reduce_scatter x4 -> x0, waiting for transfers between devices: 95.8 us -> none  [the longest x2 56.6 us: summed(): part = lax.psum_scatter(terms, 'lon', scatter_dimension=0, tiled=True)]
    all_to_all x0 -> x6, waiting for transfers between devices: none -> 30 us  [the longest x3 21 us: layer_step(): lax.all_to_all(total, 'lon', 0, 0, axis_index_groups=cores, tiled=True)]
    unnamed x12 -> x67, local copies, waits for them, and re-layouts: 1.68 us -> 28.9 us
    all_to_all x0 -> x6, starting transfers between devices: none -> 23.8 us  [the longest x3 13.3 us: layer_step(): lax.all_to_all(total, 'lon', 0, 0, axis_index_groups=cores, tiled=True)]
    reduce_sum x0 -> x6, other arithmetic: none -> 8.06 us  [block_sum(): return jnp.sum(blocks, axis=0).astype(dtype)]
    convert_element_type x2 -> x3, other arithmetic: 3.2 us -> 8.74 us  [core_sum(): return (mine.astype(F32) + arrived.astype(F32)).astype(BF16)]
    ppermute x6, waiting for transfers between devices: 12.2 us -> 15.7 us  [sent(): return lax.ppermute(block, ('lat', 'lon'), route)]
    pallas_call x2 -> x4, Pallas kernels: 44.2 us -> 42.7 us  [the longest x2 26.6 us: backward(): pl.pallas_call(functools.partial(backward_kernel, index, len(after)), out...]
  transfers between devices with their start and end apart: 10 -> 15, of which waited for: 5 -> 6; matrix products, arithmetic and copies ran while one was open for 1% -> 8% of each run, Pallas kernels for 21% -> 22%
where the time goes in v5:
time: 216 us; the launch traced here: 215 us
  Pallas kernels  86.2 us (40%)
  waiting for transfers between devices  45.7 us (21%)
  starting transfers between devices  36.2 us (17%)
  local copies, waits for them, and re-layouts  28.9 us (13%)
  other arithmetic  16.8 us (8%)
    pallas_call x1, Pallas kernels, shards(): pl.pallas_call(functools.partial(forward_kernel, owner), out_shape=[wide,...  36.3 us
    unnamed x67, local copies, waits for them, and re-layouts  28.9 us
    pallas_call x2, Pallas kernels, backward(): pl.pallas_call(functools.partial(backward_kernel, index, len(after)), out...  26.6 us
    all_to_all x3, waiting for transfers between devices, layer_step(): lax.all_to_all(total, 'lon', 0, 0, axis_index_groups=cores, tiled=True)  21 us
    ppermute x6, waiting for transfers between devices, sent(): return lax.ppermute(block, ('lat', 'lon'), route)  15.7 us
    all_to_all x3, starting transfers between devices, layer_step(): lax.all_to_all(total, 'lon', 0, 0, axis_index_groups=cores, tiled=True)  13.3 us
    ppermute x6, starting transfers between devices, sent(): return lax.ppermute(block, ('lat', 'lon'), route)  11.2 us
    all_to_all x3, starting transfers between devices, column_step(): return lax.all_to_all(total, 'lat', 0, 0, tiled=True)  10.5 us
  transfers between devices with their start and end apart: 15, of which 6 were waited for; matrix products, arithmetic and copies ran while one was open for 8% of the time, Pallas kernels for 22%

profile of v5, /device:TPU:0, one launch (start us, length us, event | category | flops | bytes accessed | tf_op | source)
XLA Modules:
  0.0 214.8 jit_solution(18402050053701082789)
XLA Ops:
  0.6 3.1 %pack_strips.1 = (bf16[128,1024]{1,0:T(8,128)(2,1)}, bf16[208,1024]{1,0:T(8,128)(2,1)}, bf16[48,1024]{1,0:T(8,128)(2,1)}) custom-call(bf16[768,1024]{1,0:T(8,128)(2,1)} %bitcast.16, bf16[192,1024]{1,0:T(8,128)(2,1)} %bitcast.18, bf16[288,768]{1,0:T(8,128)(2,1)} %constant.52.clone.pick_cells, bf16[96,192]{1,0:T(8,128)(2,1)} %constant.53.clone.pick_groups), custom_call_target="tpu_custom_call" | custom-call | flops 10000000000 | bytes 16777216 | tf_op jit(solution)/shard_map/pack_strips/pallas_call | solution.py:604
  3.8 3.0 %collective-permute-start.1 = (bf16[208,1024]{1,0:T(8,128)(2,1)}, bf16[208,1024]{1,0:T(8,128)(2,1)S(1)}, u32[]{:S(2)}, u32[]{:S(2)}) collective-permute-start(bf16[208,1024]{1,0:T(8,128)(2,1)} %get-tuple-element.30), channel_id=1, source_target_pairs={{0,8},{1,9},{2,10},{3,11},{4,12},{5,13},{6,14},{7,15},{8,16},{9,17... | collective-permute-start | bytes 1277960 | tf_op jit(solution)/shard_map/ppermute | solution.py:517
  6.8 2.8 %collective-permute-start.2 = (bf16[48,1024]{1,0:T(8,128)(2,1)}, bf16[48,1024]{1,0:T(8,128)(2,1)S(1)}, u32[]{:S(2)}, u32[]{:S(2)}) collective-permute-start(bf16[48,1024]{1,0:T(8,128)(2,1)} %get-tuple-element.31), channel_id=1, source_target_pairs={{0,9},{1,10},{2,11},{3,12},{4,13},{5,14},{6,15},{7,8},{8,17},{9,18... | collective-permute-start | bytes 294920 | tf_op jit(solution)/shard_map/ppermute | solution.py:517
  9.6 12.2 %collective-permute-done.2.corner = bf16[48,1024]{1,0:T(8,128)(2,1)S(1)} collective-permute-done((bf16[48,1024]{1,0:T(8,128)(2,1)}, bf16[48,1024]{1,0:T(8,128)(2,1)S(1)}, u32[]{:S(2)}, u32[]{:S(2)}) %collective-permute-start.2) | collective-permute-done | bytes 98336 | tf_op jit(solution)/shard_map/ppermute | solution.py:517
  22.7 36.3 %block_forward.1 = (bf16[768,1024]{1,0:T(8,128)(2,1)}, bf16[1024,768]{1,0:T(8,128)(2,1)}, bf16[768,3072]{1,0:T(8,128)(2,1)}, bf16[768,1024]{1,0:T(8,128)(2,1)}, ...) custom-call(s32[1]{0:T(128)} %bitcast.edge.refs_0_.refs_1_, ...), custom_call_target="tpu_custom_call" | custom-call | flops 299999985664 | bytes 16777216 | tf_op jit(solution)/shard_map/block_forward/pallas_call | solution.py:619
  59.0 2.3 %copy-done.14 = bf16[768,3072]{1,0:T(8,128)(2,1)S(1)} copy-done((bf16[768,3072]{1,0:T(8,128)(2,1)S(1)}, bf16[768,3072]{1,0:T(8,128)(2,1)}, u32[]{:S(2)}) %copy-start.14) | copy-done | bytes 4718616
  65.6 13.4 %attention_backward.2 = (bf16[768,1536]{1,0:T(8,128)(2,1)S(1)}, bf16[512,1536]{1,0:T(8,128)(2,1)S(1)}, bf16[512,1536]{1,0:T(8,128)(2,1)}) custom-call(s32[1]{0:T(128)} %bitcast.edge.refs_0_.refs_1_, s32[1]{0:T(128)} %bitcast.1.core.refs_1_.refs_2_, bf16[768,3072]{1,0:T(8,128)(2,1)S(1)} %copy-done.14, bf16[768,1024]{1,0:T(8,128)(2,1)S(1)} %copy-done.18, ...), custom_call_target="tpu_custom_call" | custom-call | flops 149999992832 | bytes 16777216 | tf_op jit(solution)/shard_map/attention_backward/pallas_call | solution.py:658
  79.6 2.9 %add_convert_fusion.2.refs_0_ = bf16[512,1024]{1,0:T(8,128)(2,1)} fusion(bf16[512,1024]{1,0:T(8,128)(2,1)} %collective-permute-done.4, bf16[512,1024]{1,0:T(8,128)(2,1)S(1)} %copy-done.23), kind=kLoop, calls=%fused_computation.2 | loop fusion | flops 2097152 | bytes 3145728 | tf_op jit(solution)/shard_map/convert_element_type | solution.py:538
  82.5 4.2 %all-to-all-start.4 = ((bf16[4,128,1024]{2,1,0:T(8,128)(2,1)}), bf16[4,128,1024]{2,1,0:T(8,128)(2,1)}, u32[]{:S(2)}, u32[]{:S(2)}) async-start(bf16[4,128,1024]{2,1,0:T(8,128)(2,1)} %bitcast.13), calls=%async_computation.4 | async-start | bytes 2097152 | tf_op jit(solution)/shard_map/all_to_all | solution.py:543
  86.7 2.3 %copy-done.15 = bf16[768,3072]{1,0:T(8,128)(2,1)S(1)} copy-done((bf16[768,3072]{1,0:T(8,128)(2,1)S(1)}, bf16[768,3072]{1,0:T(8,128)(2,1)}, u32[]{:S(2)}) %copy-start.15) | copy-done | bytes 4718616
  93.3 13.2 %attention_backward.3 = (bf16[768,1536]{1,0:T(8,128)(2,1)S(1)}, bf16[512,1536]{1,0:T(8,128)(2,1)S(1)}, bf16[512,1536]{1,0:T(8,128)(2,1)}) custom-call(bf16[512,1024]{1,0:T(8,128)(2,1)} %add_convert_fusion.2.refs_0_, s32[1]{0:T(128)} %bitcast.edge.refs_0_.refs_1_, s32[1]{0:T(128)} %bitcast.1.core.refs_1_.refs_2_, bf16[768,3072]{1,0:T(8,128)(2,1)S(1)} %copy-done.15, ...), custom_call_target="tpu_custom_call" | custom-call | flops 149999992832 | bytes 16777216 | tf_op jit(solution)/shard_map/attention_backward/pallas_call | solution.py:658
  108.5 2.2 %reduce_sum.67 = bf16[128,1024]{1,0:T(8,128)(2,1)} reduce(bf16[4,128,1024]{2,1,0:T(8,128)(2,1)} %all-to-all-done.4, bf16[]{:T(256)} %constant.50.clone.1), dimensions={0}, to_apply=%region_4.5 | reduce | flops 393216 | bytes 1310722 | tf_op jit(solution)/shard_map/reduce_sum | solution.py:552
  110.7 3.4 %all-to-all-start.5 = ((bf16[4,32,1024]{2,1,0:T(8,128)(2,1)}), bf16[4,32,1024]{2,1,0:T(8,128)(2,1)S(1)}, u32[]{:S(2)}, u32[]{:S(2)}) async-start(bf16[4,32,1024]{2,1,0:T(8,128)(2,1)} %bitcast.14), calls=%async_computation.5 | async-start | bytes 524288 | tf_op jit(solution)/shard_map/all_to_all | solution.py:547
  114.1 2.9 %add_convert_fusion.1.refs_0_ = bf16[512,1536]{1,0:T(8,128)(2,1)} fusion(bf16[512,1536]{1,0:T(8,128)(2,1)} %collective-permute-done.3, bf16[512,1536]{1,0:T(8,128)(2,1)S(1)} %get-tuple-element.36), kind=kLoop, calls=%fused_computation.1 | loop fusion | flops 3145728 | bytes 4718592 | tf_op jit(solution)/shard_map/convert_element_type | solution.py:538
  117.0 6.3 %all-to-all-done.5 = bf16[4,32,1024]{2,1,0:T(8,128)(2,1)S(1)} async-done(((bf16[4,32,1024]{2,1,0:T(8,128)(2,1)}), bf16[4,32,1024]{2,1,0:T(8,128)(2,1)S(1)}, u32[]{:S(2)}, u32[]{:S(2)}) %all-to-all-start.5) | async-done | bytes 262176 | tf_op jit(solution)/shard_map/all_to_all | solution.py:547
  123.4 4.6 %all-to-all-start = ((bf16[4,128,1536]{2,1,0:T(8,128)(2,1)}), bf16[4,128,1536]{2,1,0:T(8,128)(2,1)}, u32[]{:S(2)}, u32[]{:S(2)}) async-start(bf16[4,128,1536]{2,1,0:T(8,128)(2,1)} %bitcast.9), calls=%async_computation | async-start | bytes 3145728 | tf_op jit(solution)/shard_map/all_to_all | solution.py:543
  128.0 2.9 %add_convert_fusion.refs_1_ = bf16[512,1536]{1,0:T(8,128)(2,1)} fusion(bf16[512,1536]{1,0:T(8,128)(2,1)} %collective-permute-done.5, bf16[512,1536]{1,0:T(8,128)(2,1)S(1)} %get-tuple-element.40), kind=kLoop, calls=%fused_computation | loop fusion | flops 3145728 | bytes 4718592 | tf_op jit(solution)/shard_map/convert_element_type | solution.py:538
  130.9 15.5 %all-to-all-done = bf16[4,128,1536]{2,1,0:T(8,128)(2,1)} async-done(((bf16[4,128,1536]{2,1,0:T(8,128)(2,1)}), bf16[4,128,1536]{2,1,0:T(8,128)(2,1)}, u32[]{:S(2)}, u32[]{:S(2)}) %all-to-all-start) | async-done | bytes 1572896 | tf_op jit(solution)/shard_map/all_to_all | solution.py:543
  146.4 4.5 %all-to-all-start.2 = ((bf16[4,128,1536]{2,1,0:T(8,128)(2,1)}), bf16[4,128,1536]{2,1,0:T(8,128)(2,1)}, u32[]{:S(2)}, u32[]{:S(2)}) async-start(bf16[4,128,1536]{2,1,0:T(8,128)(2,1)} %bitcast.11), calls=%async_computation.2 | async-start | bytes 3145728 | tf_op jit(solution)/shard_map/all_to_all | solution.py:543
  150.9 2.8 %copy-done = bf16[1024,3072]{1,0:T(8,128)(2,1)S(1)} copy-done((bf16[1024,3072]{1,0:T(8,128)(2,1)S(1)}, bf16[1024,3072]{1,0:T(8,128)(2,1)}, u32[]{:S(2)}) %copy-start) | copy-done | bytes 6291480
  153.7 1.7 copy-done.10
  155.4 6.2 %input_first.1.refs_5_ = bf16[768,512]{1,0:T(8,128)(2,1)S(1)} custom-call(bf16[768,1536]{1,0:T(8,128)(2,1)S(1)} %copy-done.7, bf16[768,1536]{1,0:T(8,128)(2,1)S(1)} %copy-done.10, bf16[1024,3072]{1,0:T(8,128)(2,1)S(1)} %copy-done), custom_call_target="tpu_custom_call" | custom-call | flops 49999998976 | bytes 16777216 | tf_op jit(solution)/shard_map/input_first/pallas_call | solution.py:693
  161.7 2.6 %reduce_sum.63 = bf16[128,1536]{1,0:T(8,128)(2,1)} reduce(bf16[4,128,1536]{2,1,0:T(8,128)(2,1)} %all-to-all-done, bf16[]{:T(256)} %constant.50.clone.1), dimensions={0}, to_apply=%region_0.1 | reduce | flops 589824 | bytes 1966082 | tf_op jit(solution)/shard_map/reduce_sum | solution.py:552
  164.3 5.5 %all-to-all-done.2 = bf16[4,128,1536]{2,1,0:T(8,128)(2,1)} async-done(((bf16[4,128,1536]{2,1,0:T(8,128)(2,1)}), bf16[4,128,1536]{2,1,0:T(8,128)(2,1)}, u32[]{:S(2)}, u32[]{:S(2)}) %all-to-all-start.2) | async-done | bytes 1572896 | tf_op jit(solution)/shard_map/all_to_all | solution.py:543
  169.8 3.7 %all-to-all-start.1 = ((bf16[4,32,1536]{2,1,0:T(8,128)(2,1)}), bf16[4,32,1536]{2,1,0:T(8,128)(2,1)S(1)}, u32[]{:S(2)}, u32[]{:S(2)}) async-start(bf16[4,32,1536]{2,1,0:T(8,128)(2,1)} %bitcast.10), calls=%async_computation.1 | async-start | bytes 786432 | tf_op jit(solution)/shard_map/all_to_all | solution.py:547
  179.6 9.8 %input_last.1 = (bf16[768,1024]{1,0:T(8,128)(2,1)S(1)}, bf16[128,1024]{1,0:T(8,128)(2,1)S(1)}, bf16[208,1024]{1,0:T(8,128)(2,1)S(1)}, bf16[48,1024]{1,0:T(8,128)(2,1)S(1)}) custom-call(bf16[512,1536]{1,0:T(8,128)(2,1)} %add_convert_fusion.1.refs_0_, bf16[512,1536]{1,0:T(8,128)(2,1)} %add_convert_fusion.refs_1_, bf16[768,1536]{1,0:T(8,128)(2,1)S(1)} %copy-done.8, ...), custom_call_target="tpu_custom_call" | custom-call | flops 89999998976 | bytes 16777216 | tf_op jit(solution)/shard_map/input_last/pallas_call | solution.py:706
  190.7 3.8 %collective-permute-start.7 = (bf16[208,1024]{1,0:T(8,128)(2,1)S(1)}, bf16[208,1024]{1,0:T(8,128)(2,1)S(1)}, u32[]{:S(2)}, u32[]{:S(2)}) collective-permute-start(bf16[208,1024]{1,0:T(8,128)(2,1)S(1)} %get-tuple-element.50), channel_id=1, source_target_pairs={{0,24},{1,25},{2,26},{3,27},{4,28},{5,29},{6,30},{7,31},{8,0},{9,1... | collective-permute-start | bytes 1277960 | tf_op jit(solution)/shard_map/ppermute | solution.py:517
  196.7 2.5 %reduce_sum.65 = bf16[128,1536]{1,0:T(8,128)(2,1)} reduce(bf16[4,128,1536]{2,1,0:T(8,128)(2,1)} %all-to-all-done.2, bf16[]{:T(256)} %constant.50.clone.1), dimensions={0}, to_apply=%region_2.3 | reduce | flops 589824 | bytes 1966082 | tf_op jit(solution)/shard_map/reduce_sum | solution.py:552
  199.2 3.5 %all-to-all-start.3 = ((bf16[4,32,1536]{2,1,0:T(8,128)(2,1)}), bf16[4,32,1536]{2,1,0:T(8,128)(2,1)S(1)}, u32[]{:S(2)}, u32[]{:S(2)}) async-start(bf16[4,32,1536]{2,1,0:T(8,128)(2,1)} %bitcast.12), calls=%async_computation.3 | async-start | bytes 786432 | tf_op jit(solution)/shard_map/all_to_all | solution.py:547
  202.7 3.5 %collective-permute-done.8.corner = bf16[48,1024]{1,0:T(8,128)(2,1)S(1)} collective-permute-done((bf16[48,1024]{1,0:T(8,128)(2,1)S(1)}, bf16[48,1024]{1,0:T(8,128)(2,1)S(1)}, u32[]{:S(2)}, u32[]{:S(2)}) %collective-permute-start.8) | collective-permute-done | bytes 98336 | tf_op jit(solution)/shard_map/ppermute | solution.py:517
  207.1 4.1 %unpack_strips.1 = (bf16[768,1024]{1,0:T(8,128)(2,1)}, bf16[192,1024]{1,0:T(8,128)(2,1)}) custom-call(bf16[768,1024]{1,0:T(8,128)(2,1)} %copy-done.4, bf16[192,1024]{1,0:T(8,128)(2,1)} %get-tuple-element.47.refs_9_.merged, bf16[128,1024]{1,0:T(8,128)(2,1)} %copy-done.28, bf16[208,1024]{1,0:T(8,128)(2,1)} %copy-done.26, bf16[48,1024]{1,0:T(8,128)(2,1)} %copy-done.30, ...), custom_call_target="tpu_custom_call" | custom-call | flops 20000000000 | bytes 16777216 | tf_op jit(solution)/shard_map/unpack_strips/pallas_call | solution.py:730
  211.3 2.6 %all-to-all-done.3 = bf16[4,32,1536]{2,1,0:T(8,128)(2,1)S(1)} async-done(((bf16[4,32,1536]{2,1,0:T(8,128)(2,1)}), bf16[4,32,1536]{2,1,0:T(8,128)(2,1)S(1)}, u32[]{:S(2)}, u32[]{:S(2)}) %all-to-all-start.3) | async-done | bytes 393248 | tf_op jit(solution)/shard_map/all_to_all | solution.py:547
  (82 shorter events, 23.3 us)
Async XLA Ops:
  3.8 18.0 %collective-permute-start.1 = (bf16[208,1024]{1,0:T(8,128)(2,1)}, bf16[208,1024]{1,0:T(8,128)(2,1)S(1)}, u32[]{:S(2)}, u32[]{:S(2)}) collective-permute-start(bf16[208,1024]{1,0:T(8,128)(2,1)} %get-tuple-element.30), channel_id=1, source_target_pairs={{0,8},{1,9},{2,10},{3,11},{4,12},{5,13},{6,14},{7,15},{8,16},{9,17... | collective-permute-start | bytes 1277960 | tf_op jit(solution)/shard_map/ppermute | solution.py:517
  6.8 15.0 %collective-permute-start = (bf16[128,1024]{1,0:T(8,128)(2,1)}, bf16[128,1024]{1,0:T(8,128)(2,1)S(1)}, u32[]{:S(2)}, u32[]{:S(2)}) collective-permute-start(bf16[128,1024]{1,0:T(8,128)(2,1)} %get-tuple-element.29), channel_id=1, source_target_pairs={{0,1},{1,2},{2,3},{3,4},{4,5},{5,6},{6,7},{7,0},{8,9},{9,10},{10,1... | collective-permute-start | bytes 786440 | tf_op jit(solution)/shard_map/ppermute | solution.py:517
  6.8 14.9 %collective-permute-start.2 = (bf16[48,1024]{1,0:T(8,128)(2,1)}, bf16[48,1024]{1,0:T(8,128)(2,1)S(1)}, u32[]{:S(2)}, u32[]{:S(2)}) collective-permute-start(bf16[48,1024]{1,0:T(8,128)(2,1)} %get-tuple-element.31), channel_id=1, source_target_pairs={{0,9},{1,10},{2,11},{3,12},{4,13},{5,14},{6,15},{7,8},{8,17},{9,18... | collective-permute-start | bytes 294920 | tf_op jit(solution)/shard_map/ppermute | solution.py:517
  58.9 20.6 %collective-permute-start.4 = (bf16[512,1024]{1,0:T(8,128)(2,1)}, bf16[512,1024]{1,0:T(8,128)(2,1)}, u32[]{:S(2)}, u32[]{:S(2)}) collective-permute-start(bf16[512,1024]{1,0:T(8,128)(2,1)} %get-tuple-element.39), channel_id=1, source_target_pairs={{0,1},{1,0},{2,3},{3,2},{4,5},{5,4},{6,7},{7,6},{8,9},{9,8},{10,11... | collective-permute-start | bytes 3145736 | tf_op jit(solution)/shard_map/ppermute | solution.py:534
  59.0 2.3 %copy-start.14 = (bf16[768,3072]{1,0:T(8,128)(2,1)S(1)}, bf16[768,3072]{1,0:T(8,128)(2,1)}, u32[]{:S(2)}) copy-start(bf16[768,3072]{1,0:T(8,128)(2,1)} %get-tuple-element.32.refs_2_.refs_3_) | copy-start | bytes 14155780
  61.4 1.4 copy-start.16
  62.8 1.4 copy-start.18
  65.6 14.0 %copy-start.23 = (bf16[512,1024]{1,0:T(8,128)(2,1)S(1)}, bf16[512,1024]{1,0:T(8,128)(2,1)}, u32[]{:S(2)}) copy-start(bf16[512,1024]{1,0:T(8,128)(2,1)} %get-tuple-element.38) | copy-start | bytes 3145732
  79.0 3.5 %copy-start.6 = (bf16[768,1536]{1,0:T(8,128)(2,1)}, bf16[768,1536]{1,0:T(8,128)(2,1)S(1)}, u32[]{:S(2)}) copy-start(bf16[768,1536]{1,0:T(8,128)(2,1)S(1)} %get-tuple-element.42.pg0.refs_2_) | copy-start | bytes 7077892
  79.0 35.1 %collective-permute-start.3 = (bf16[512,1536]{1,0:T(8,128)(2,1)}, bf16[512,1536]{1,0:T(8,128)(2,1)}, u32[]{:S(2)}, u32[]{:S(2)}) collective-permute-start(bf16[512,1536]{1,0:T(8,128)(2,1)} %get-tuple-element.37), channel_id=1, source_target_pairs={{0,1},{1,0},{2,3},{3,2},{4,5},{5,4},{6,7},{7,6},{8,9},{9,8},{10,11... | collective-permute-start | bytes 4718600 | tf_op jit(solution)/shard_map/ppermute | solution.py:534
  82.5 26.0 %all-to-all-start.4 = ((bf16[4,128,1024]{2,1,0:T(8,128)(2,1)}), bf16[4,128,1024]{2,1,0:T(8,128)(2,1)}, u32[]{:S(2)}, u32[]{:S(2)}) async-start(bf16[4,128,1024]{2,1,0:T(8,128)(2,1)} %bitcast.13), calls=%async_computation.4 | async-start | bytes 2097152 | tf_op jit(solution)/shard_map/all_to_all | solution.py:543
  86.7 2.3 %copy-start.15 = (bf16[768,3072]{1,0:T(8,128)(2,1)S(1)}, bf16[768,3072]{1,0:T(8,128)(2,1)}, u32[]{:S(2)}) copy-start(bf16[768,3072]{1,0:T(8,128)(2,1)} %get-tuple-element.32.refs_2_.refs_3_) | copy-start | bytes 14155780
  106.5 1.4 copy-start.9
  107.9 20.0 %collective-permute-start.5 = (bf16[512,1536]{1,0:T(8,128)(2,1)}, bf16[512,1536]{1,0:T(8,128)(2,1)}, u32[]{:S(2)}, u32[]{:S(2)}) collective-permute-start(bf16[512,1536]{1,0:T(8,128)(2,1)} %get-tuple-element.41), channel_id=1, source_target_pairs={{0,1},{1,0},{2,3},{3,2},{4,5},{5,4},{6,7},{7,6},{8,9},{9,8},{10,11... | collective-permute-start | bytes 4718600 | tf_op jit(solution)/shard_map/ppermute | solution.py:534
  110.7 12.7 %all-to-all-start.5 = ((bf16[4,32,1024]{2,1,0:T(8,128)(2,1)}), bf16[4,32,1024]{2,1,0:T(8,128)(2,1)S(1)}, u32[]{:S(2)}, u32[]{:S(2)}) async-start(bf16[4,32,1024]{2,1,0:T(8,128)(2,1)} %bitcast.14), calls=%async_computation.5 | async-start | bytes 524288 | tf_op jit(solution)/shard_map/all_to_all | solution.py:547
  123.4 23.0 %all-to-all-start = ((bf16[4,128,1536]{2,1,0:T(8,128)(2,1)}), bf16[4,128,1536]{2,1,0:T(8,128)(2,1)}, u32[]{:S(2)}, u32[]{:S(2)}) async-start(bf16[4,128,1536]{2,1,0:T(8,128)(2,1)} %bitcast.9), calls=%async_computation | async-start | bytes 3145728 | tf_op jit(solution)/shard_map/all_to_all | solution.py:543
  146.4 4.5 %copy-start.7 = (bf16[768,1536]{1,0:T(8,128)(2,1)S(1)}, bf16[768,1536]{1,0:T(8,128)(2,1)}, u32[]{:S(2)}) copy-start(bf16[768,1536]{1,0:T(8,128)(2,1)} %copy-done.6) | copy-start | bytes 7077892
  146.4 23.3 %all-to-all-start.2 = ((bf16[4,128,1536]{2,1,0:T(8,128)(2,1)}), bf16[4,128,1536]{2,1,0:T(8,128)(2,1)}, u32[]{:S(2)}, u32[]{:S(2)}) async-start(bf16[4,128,1536]{2,1,0:T(8,128)(2,1)} %bitcast.11), calls=%async_computation.2 | async-start | bytes 3145728 | tf_op jit(solution)/shard_map/all_to_all | solution.py:543
  150.9 2.8 %copy-start = (bf16[1024,3072]{1,0:T(8,128)(2,1)S(1)}, bf16[1024,3072]{1,0:T(8,128)(2,1)}, u32[]{:S(2)}) copy-start(bf16[1024,3072]{1,0:T(8,128)(2,1)} %refs_4_.1) | copy-start | bytes 18874372
  153.7 1.7 copy-start.10
  161.6 11.8 %copy-start.1 = (bf16[224,384]{1,0:T(8,128)(2,1)S(1)}, bf16[224,384]{1,0:T(8,128)(2,1)}, u32[]{:S(2)}) copy-start(bf16[224,384]{1,0:T(8,128)(2,1)} %constant.57.clone.refs_10_) | copy-start | bytes 516100
  161.6 11.8 %copy-start.2 = (bf16[64,384]{1,0:T(8,128)(2,1)S(1)}, bf16[64,384]{1,0:T(8,128)(2,1)}, u32[]{:S(2)}) copy-start(bf16[64,384]{1,0:T(8,128)(2,1)} %constant.58.clone.refs_11_) | copy-start | bytes 147460
  161.7 11.8 %copy-start.3 = (bf16[96,192]{1,0:T(8,128)(2,1)S(1)}, bf16[96,192]{1,0:T(8,128)(2,1)}, u32[]{:S(2)}) copy-start(bf16[96,192]{1,0:T(8,128)(2,1)} %constant.59.clone.refs_12_) | copy-start | bytes 110596
  161.7 11.8 %copy-start.5 = (bf16[192,1024]{1,0:T(8,128)(2,1)S(1)}, bf16[192,1024]{1,0:T(8,128)(2,1)}, u32[]{:S(2)}) copy-start(bf16[192,1024]{1,0:T(8,128)(2,1)} %get-tuple-element.47.refs_9_.merged) | copy-start | bytes 1179652
  161.7 11.8 %copy-start.22 = (f32[768,128]{1,0:T(8,128)S(1)}, f32[768,128]{1,0:T(8,128)}, u32[]{:S(2)}) copy-start(f32[768,128]{1,0:T(8,128)} %get-tuple-element.45.refs_7_) | copy-start | bytes 1179652
  169.8 29.4 %all-to-all-start.1 = ((bf16[4,32,1536]{2,1,0:T(8,128)(2,1)}), bf16[4,32,1536]{2,1,0:T(8,128)(2,1)S(1)}, u32[]{:S(2)}, u32[]{:S(2)}) async-start(bf16[4,32,1536]{2,1,0:T(8,128)(2,1)} %bitcast.10), calls=%async_computation.1 | async-start | bytes 786432 | tf_op jit(solution)/shard_map/all_to_all | solution.py:547
  173.5 1.7 copy-start.8
  175.1 1.7 copy-start.11
  190.7 15.6 %collective-permute-start.7 = (bf16[208,1024]{1,0:T(8,128)(2,1)S(1)}, bf16[208,1024]{1,0:T(8,128)(2,1)S(1)}, u32[]{:S(2)}, u32[]{:S(2)}) collective-permute-start(bf16[208,1024]{1,0:T(8,128)(2,1)S(1)} %get-tuple-element.50), channel_id=1, source_target_pairs={{0,24},{1,25},{2,26},{3,27},{4,28},{5,29},{6,30},{7,31},{8,0},{9,1... | collective-permute-start | bytes 1277960 | tf_op jit(solution)/shard_map/ppermute | solution.py:517
  194.5 11.7 %collective-permute-start.6 = (bf16[128,1024]{1,0:T(8,128)(2,1)S(1)}, bf16[128,1024]{1,0:T(8,128)(2,1)S(1)}, u32[]{:S(2)}, u32[]{:S(2)}) collective-permute-start(bf16[128,1024]{1,0:T(8,128)(2,1)S(1)} %get-tuple-element.49), channel_id=1, source_target_pairs={{0,7},{1,0},{2,1},{3,2},{4,3},{5,4},{6,5},{7,6},{8,15},{9,8},{10,9... | collective-permute-start | bytes 786440 | tf_op jit(solution)/shard_map/ppermute | solution.py:517
  194.5 11.7 %collective-permute-start.8 = (bf16[48,1024]{1,0:T(8,128)(2,1)S(1)}, bf16[48,1024]{1,0:T(8,128)(2,1)S(1)}, u32[]{:S(2)}, u32[]{:S(2)}) collective-permute-start(bf16[48,1024]{1,0:T(8,128)(2,1)S(1)} %get-tuple-element.51), channel_id=1, source_target_pairs={{0,31},{1,24},{2,25},{3,26},{4,27},{5,28},{6,29},{7,30},{8,7},{9,0... | collective-permute-start | bytes 294920 | tf_op jit(solution)/shard_map/ppermute | solution.py:517
  199.2 14.7 %all-to-all-start.3 = ((bf16[4,32,1536]{2,1,0:T(8,128)(2,1)}), bf16[4,32,1536]{2,1,0:T(8,128)(2,1)S(1)}, u32[]{:S(2)}, u32[]{:S(2)}) async-start(bf16[4,32,1536]{2,1,0:T(8,128)(2,1)} %bitcast.12), calls=%async_computation.3 | async-start | bytes 786432 | tf_op jit(solution)/shard_map/all_to_all | solution.py:547
  (14 other events, 14.9 us)

commit v6 on v5

--- a/solution.py
+++ b/solution.py
@@ -120,7 +120,7 @@
 
 
 def forward_kernel(
-    owner, edge, core, tokens, merged_grad, side, above, corner, order, group,
+    edge, owner, tokens, merged_grad, side, above, corner, order, group, rowmap,
     wqkv_h, wout_h, wm_h,
     normed_h, normt_h, proj_h, dmr_h, dmm_h, grad_h, rstd, merged, out_mine, out_theirs,
     wqkv, wout, wm, source, xw, normed, normt, proj, mixture, inverse, subs, dsubs, cotangent,
@@ -132,7 +132,7 @@
     per_row = windows // 2
     quarter = places // 4
     groups = count // 4
-    devices = len(owner)
+    devices = owner.shape[0]
     block = channels // devices
 
     loads = [
@@ -282,36 +282,41 @@
     stores[5].start()
 
     def turn(field, out):
-        @pl.loop(0, channels // TILE)
-        def _(n):
-            rows = aligned(n * TILE, TILE)
-            turned[rows] = field[:, rows].T
-
-        for d in range(devices):
-            out[d * block:(d + 1) * block] = turned[owner[d] * block:(owner[d] + 1) * block]
+        if block % 16:
+            @pl.loop(0, channels // TILE)
+            def _(n):
+                rows = aligned(n * TILE, TILE)
+                spot = lax.broadcasted_iota(jnp.int32, (TILE, channels), 1)
+                pick = jnp.where(spot == rowmap[rows], 1.0, 0.0).astype(BF16)
+                out[rows] = dot(pick, field[...], NT).astype(BF16)
+        else:
+            @pl.loop(0, channels // TILE)
+            def _(n):
+                rows = aligned(n * TILE, TILE)
+                turned[rows] = field[:, rows].T
+
+            for d in range(devices):
+                out[d * block:(d + 1) * block] = turned[aligned(owner[d] * block, block)]
 
     turn(normed, normt)
     stores[2].start()
     mixt = wqkv.at[:, :count]
     turn(mixture, mixt)
-    own = aligned(core[0] * (channels // 2), channels // 2)
-    other = aligned((1 - core[0]) * (channels // 2), channels // 2)
+    part = channels // 2
 
     @pl.loop(0, channels // TILE)
     def _(n):
         columns = aligned(n * TILE, TILE)
-        out_mine[:, columns] = dot(mixt[own], grad[:, columns]).astype(BF16)
-        out_theirs[:, columns] = dot(mixt[other], grad[:, columns]).astype(BF16)
+        out_mine[:, columns] = dot(mixt[:part], grad[:, columns]).astype(BF16)
+        out_theirs[:, columns] = dot(mixt[part:], grad[:, columns]).astype(BF16)
 
     for store in stores:
         store.wait()
 
 
-def backward_kernel(
-    index, waits, *refs,
-):
-    (edge, core, proj_h, dmr_h, dmm_h, normt_h, pgrad_h, mine_h, theirs_h,
-     held, normt, pgrad, mine, theirs, in_sem, sem, out_sem) = refs[waits:]
+def backward_kernel(index, *refs):
+    (edge, proj_h, dmr_h, dmm_h, normt_h, pgrad_h, mine_h, theirs_h,
+     held, normt, pgrad, mine, theirs, in_sem, sem, out_sem) = refs
     _, count, width = held.shape
     channels = normt.shape[0]
     half = channels // 2
@@ -344,8 +349,6 @@
     turned_load = pltpu.make_async_copy(normt_h, normt, sem.at[0])
     turned_load.start()
     edge_bias = region_bias(places, edge[0] == 1)
-    own = aligned(core[0] * half, half)
-    other = aligned((1 - core[0]) * half, half)
 
     @pl.loop(0, steps)
     def _(g):
@@ -392,8 +395,8 @@
 
         for i in range(3):
             columns = aligned(i * width + g * TILE, TILE)
-            mine[:, columns] = dot(normt[own], pgrad[:, columns]).astype(BF16)
-            theirs[:, columns] = dot(normt[other], pgrad[:, columns]).astype(BF16)
+            mine[:, columns] = dot(normt[:half], pgrad[:, columns]).astype(BF16)
+            theirs[:, columns] = dot(normt[half:], pgrad[:, columns]).astype(BF16)
         for store in stores(g):
             store.start()
 
@@ -434,10 +437,10 @@
         ngrad[:, rows] = dot(pgrad[...], wqkv[rows], NT).astype(BF16)
 
 
-def input_last_kernel(waits, *refs):
+def input_last_kernel(*refs):
     (pg0, pg1, wqkv_h, nfirst_h, normed_h, rstd_h, grad_h, merged,
      pick_first, pick_last, pick_groups, full, side, below, corner,
-     pgrad, wqkv, ngrad, normed, rstd, grad, sem, more_sem) = refs[waits:]
+     pgrad, wqkv, ngrad, normed, rstd, grad, sem, more_sem) = refs
     count, channels = ngrad.shape
     half = channels // 2
     loads, tiles = projection_loads([pg0, pg1], wqkv_h, pgrad, wqkv, sem, half)
@@ -522,34 +525,99 @@
     return [sent(side, sizes, 0, step), sent(lines, sizes, step, 0), sent(corner, sizes, step, step)]
 
 
+def bit_list(count):
+    return [1 << i for i in range(count.bit_length() - 1)]
+
+
 def device_rows(channels, sizes):
     n_lat, n_lon = sizes
-    place = np.arange(n_lat * n_lon)
-    chips = n_lon // 2
-    return place % n_lat * n_lon + place // n_lat % chips * 2 + place // (n_lat * chips)
-
-
-def core_step(theirs, sizes):
-    n_lat, n_lon = sizes
-    return lax.ppermute(theirs, ("lat", "lon"), [(i, i ^ 1) for i in range(n_lat * n_lon)])
-
-
-def core_sum(mine, arrived):
-    return (mine.astype(F32) + arrived.astype(F32)).astype(BF16)
-
-
-def layer_step(total, sizes):
-    cores = [list(range(c, sizes[1], 2)) for c in range(2)]
-    return lax.all_to_all(total, "lon", 0, 0, axis_index_groups=cores, tiled=True)
-
-
-def column_step(total, sizes):
-    return lax.all_to_all(total, "lat", 0, 0, tiled=True)
-
-
-def block_sum(blocks, count, dtype=BF16):
-    blocks = blocks.reshape(count, blocks.shape[0] // count, blocks.shape[1]).astype(F32)
-    return jnp.sum(blocks, axis=0).astype(dtype)
+    devices = n_lat * n_lon
+    rows = channels // devices
+    place = np.arange(devices)
+    partner = np.zeros_like(place)
+    for i, bit in enumerate(bit_list(devices)):
+        partner |= np.where(place & (devices >> (i + 1)), bit, 0)
+    me = (lax.axis_index("lat") * n_lon + lax.axis_index("lon")).astype(jnp.int32)
+    owner = jnp.bitwise_xor(jnp.asarray(partner, jnp.int32), me)
+    rowmap = owner[:, None] * rows + jnp.arange(rows, dtype=jnp.int32)[None, :]
+    return owner, rowmap.reshape(channels, 1)
+
+
+def exchange(block, sizes, bit):
+    devices = sizes[0] * sizes[1]
+    return lax.ppermute(block, ("lat", "lon"), [(i, i ^ bit) for i in range(devices)])
+
+
+def added(a, b, zero, dtype=BF16):
+    return (a.astype(F32) + b.astype(F32) + zero).astype(dtype)
+
+
+class Sum:
+    def __init__(self, mine, theirs, sizes):
+        self.sizes, self.mine, self.theirs, self.zero = sizes, mine, theirs, 0.0
+        self.bits = bit_list(sizes[0] * sizes[1])[1:]
+        layer = bit_list(sizes[1])[1:]
+        self.turns = [layer, layer[1:] + layer[:1]]
+        self.column = [sizes[1] * b for b in bit_list(sizes[0])]
+
+    def send_core(self):
+        self.arrived = exchange(self.theirs, self.sizes, 1)
+
+    def split(self, parts):
+        self.kept, given = [], []
+        for i, part in enumerate(parts):
+            axis = self.bits_of[i].index(self.turns[i][0])
+            self.kept.append(lax.index_in_dim(part, 0, axis, keepdims=False))
+            given.append(lax.index_in_dim(part, 1, axis, keepdims=False))
+        return given
+
+    def send(self, given):
+        self.arrived = []
+        for i, block in enumerate(given):
+            bit = self.turns[i][0]
+            self.arrived.append(exchange(block, self.sizes, bit))
+            self.turns[i] = self.turns[i][1:]
+            self.bits_of[i] = [b for b in self.bits_of[i] if b != bit]
+
+    def first(self):
+        total = added(self.mine, self.arrived, self.zero)
+        columns = total.shape[1] // 2
+        rows = total.shape[0] >> len(self.bits)
+        self.bits_of = [list(self.bits), list(self.bits)]
+        return self.split([
+            total[:, i * columns:(i + 1) * columns].reshape([2] * len(self.bits) + [rows, columns])
+            for i in range(2)
+        ])
+
+    def next(self):
+        parts = [added(k, a, self.zero) for k, a in zip(self.kept, self.arrived)]
+        if not self.turns[0]:
+            parts = [jnp.concatenate(parts, axis=-1)]
+            self.turns, self.bits_of = [self.column], [self.bits_of[0]]
+        return self.split(parts)
+
+    def rest(self):
+        while self.turns[0] or len(self.turns) > 1:
+            self.send(self.next())
+        return added(self.kept[0], self.arrived[0], self.zero, F32)
+
+
+def tied_call(kernel, after, operands, in_specs, out_shape, out_specs, **rest):
+    waits = len(after)
+    reads = waits + len(operands)
+
+    def body(*refs):
+        refs[reads][...] = jnp.zeros_like(refs[reads])
+        kernel(*refs[waits:reads], *refs[reads + 1:])
+
+    zero, *out = pl.pallas_call(
+        body,
+        out_shape=[jax.ShapeDtypeStruct((8, LANES), F32)] + out_shape,
+        in_specs=[pl.BlockSpec(memory_space=pl.ANY)] * waits + in_specs,
+        out_specs=[pl.BlockSpec(memory_space=pltpu.VMEM)] + out_specs,
+        **rest,
+    )(*after, *operands)
+    return zero[0, 0], out
 
 
 def shards(sizes, tokens, qkv_weight, out_weight, merge_weight, merged_grad):
@@ -562,7 +630,6 @@
     vmem = pl.BlockSpec(memory_space=pltpu.VMEM)
     smem = pl.BlockSpec(memory_space=pltpu.SMEM)
     hbm = pl.BlockSpec(memory_space=pl.ANY)
-    pinned = pl.BlockSpec(memory_space=pltpu.HBM)
 
     def shape(*extent, dtype=BF16):
         return jax.ShapeDtypeStruct(extent, dtype)
@@ -612,18 +679,17 @@
     order = jnp.concatenate([picks(cells[:half_cells], held_top), picks(cells[half_cells:], held_low)])
     group = picks(grps, g_own + sum(g_strips, []))
     edge = (lax.axis_index("lat") == 0).astype(jnp.int32).reshape(1)
-    core = (lax.axis_index("lon") % 2).astype(jnp.int32).reshape(1)
-    owner = tuple(int(d) for d in device_rows(channels, sizes))
+    owner, rowmap = device_rows(channels, sizes)
 
     wide = shape(count, channels)
     normed, normt, proj, dmr, dmm, grad, rstd, merged, out_mine, out_theirs = pl.pallas_call(
-        functools.partial(forward_kernel, owner),
+        forward_kernel,
         out_shape=[
             wide, shape(channels, count), shape(count, 3 * channels), wide, wide, wide,
             shape(count, LANES, dtype=F32), shape(groups, merged_width),
             shape(half, channels), shape(half, channels),
         ],
-        in_specs=[smem] * 2 + [vmem] * 7 + [hbm] * 3,
+        in_specs=[smem] * 2 + [vmem] * 8 + [hbm] * 3,
         out_specs=[hbm] * 6 + [vmem] * 4,
         scratch_shapes=[
             pltpu.VMEM(qkv_weight.shape, BF16),
@@ -646,8 +712,8 @@
             pltpu.SemaphoreType.DMA((3,)),
             pltpu.SemaphoreType.DMA((6,)),
         ],
-        name="block_forward", **settings(30, 54),
-    )(edge, core, tokens_flat, merged_grad_flat, *strips, order, group,
+        name="block_forward", **settings(30, 58),
+    )(edge, owner, tokens_flat, merged_grad_flat, *strips, order, group, rowmap,
       qkv_weight, out_weight, merge_weight)
 
     halves = 2
@@ -655,10 +721,10 @@
     steps = width // TILE
 
     def backward(index, after):
-        return pl.pallas_call(
-            functools.partial(backward_kernel, index, len(after)),
-            out_shape=[shape(count, 3 * width), shape(half, 3 * width), shape(half, 3 * width)],
-            in_specs=[hbm] * len(after) + [smem] * 2 + [pinned] * 4, out_specs=[hbm] * 3,
+        return tied_call(
+            functools.partial(backward_kernel, index), after,
+            [edge, proj, dmr, dmm, normt], [smem] + [hbm] * 4,
+            [shape(count, 3 * width), shape(half, 3 * width), shape(half, 3 * width)], [hbm] * 3,
             scratch_shapes=[
                 pltpu.VMEM((5, count, width), BF16),
                 pltpu.VMEM((channels, count), BF16),
@@ -669,44 +735,51 @@
                 pltpu.SemaphoreType.DMA((1,)),
                 pltpu.SemaphoreType.DMA((steps, 3, 3)),
             ],
-            name="attention_backward", **settings(15, 30),
-        )(*after, edge, core, proj, dmr, dmm, normt)
-
-    chips, layers = sizes[1] // 2, sizes[0]
-    arrived = core_step(out_theirs, sizes)
-    pg0, mine1, theirs1 = backward(0, [])
-    total0 = core_sum(out_mine, arrived)
-    blocks0 = layer_step(total0, sizes)
-    arrived = core_step(theirs1, sizes)
-    pg1, mine2, theirs2 = backward(1, [total0])
-    total0 = block_sum(blocks0, chips)
-    blocks0 = column_step(total0, sizes)
-    total1 = core_sum(mine1, arrived)
-    blocks1 = layer_step(total1, sizes)
-    arrived = core_step(theirs2, sizes)
+            name="attention_backward", **settings(15, 48),
+        )
+
+    out_sum = Sum(out_mine, out_theirs, sizes)
+    out_sum.send_core()
+    out_sum.zero, (pg0, mine, theirs) = backward(0, [])
+    given = out_sum.first()
+    out_sum.send(given)
+    first_sum = Sum(mine, theirs, sizes)
+    first_sum.send_core()
+    zero, (pg1, mine, theirs) = backward(1, given)
+    first_sum.zero = out_sum.zero = zero
+    after = out_sum.next()
+    out_sum.send(after)
+    given = first_sum.first()
+    first_sum.send(given)
+    last_sum = Sum(mine, theirs, sizes)
+    last_sum.send_core()
+    after = after + given
 
     in_scratch = [
         pltpu.VMEM((count, 3 * channels), BF16),
         pltpu.VMEM((half, 3 * channels), BF16),
     ]
     in_sems = pltpu.SemaphoreType.DMA((3 * halves + half // TILE,))
-    nfirst = pl.pallas_call(
-        input_first_kernel,
-        out_shape=shape(count, half),
-        in_specs=[hbm] * 3, out_specs=vmem,
+    zero, [nfirst] = tied_call(
+        input_first_kernel, after,
+        [pg0, pg1, qkv_weight], [hbm] * 3, [shape(count, half)], [vmem],
         scratch_shapes=in_scratch + [in_sems],
-        name="input_first", **settings(5, 30),
-    )(pg0, pg1, qkv_weight)
-    total2 = core_sum(mine2, arrived)
-    blocks2 = layer_step(total2, sizes)
-    after = [total1, total2]
+        name="input_first", **settings(5, 36),
+    )
+    last_sum.zero = out_sum.zero = zero
+    given = last_sum.first()
+    last_sum.send(given)
+    after = out_sum.next()
+    out_sum.send(after)
+    after = after + given
 
     first_picks = picks(cs.side[:side_cut] + cs.above + cs.corner, cells[:half_cells])
     last_picks = picks(cs.side[side_cut:], cells[half_cells:])
-    full, *strips = pl.pallas_call(
-        functools.partial(input_last_kernel, len(after)),
-        out_shape=[wide] + [shape(*e) for e in extents],
-        in_specs=[hbm] * (len(after) + 7) + [vmem] * 4, out_specs=[vmem] * 4,
+    zero, [full, *strips] = tied_call(
+        input_last_kernel, after,
+        [pg0, pg1, qkv_weight, nfirst, normed, rstd, grad, merged,
+         first_picks, last_picks, picks(sum(g_strips, []), grps)],
+        [hbm] * 7 + [vmem] * 4, [wide] + [shape(*e) for e in extents], [vmem] * 4,
         scratch_shapes=in_scratch + [
             pltpu.VMEM((count, channels), BF16),
             pltpu.VMEM((count, channels), BF16),
@@ -716,14 +789,13 @@
             pltpu.SemaphoreType.DMA((4,)),
         ],
         name="input_last", **settings(9, 36),
-    )(*after, pg0, pg1, qkv_weight, nfirst, normed, rstd, grad, merged,
-      first_picks, last_picks, picks(sum(g_strips, []), grps))
+    )
+    first_sum.zero = last_sum.zero = out_sum.zero = zero
     strips = sent_strips(strips, sizes, -1)
 
-    total1 = block_sum(blocks1, chips)
-    blocks1 = column_step(total1, sizes)
-    total2 = block_sum(blocks2, chips)
-    blocks2 = column_step(total2, sizes)
+    first_part = first_sum.rest()
+    last_part = last_sum.rest()
+    out_weight_grad = out_sum.rest()
 
     got = [Strips.sent(s, *t) for s, t in zip((cs.side, cs.above, cs.corner), to)]
     g_got = sum((Strips.sent(s, *t) for s, t in zip(g_strips, g_to)), [])
@@ -731,7 +803,7 @@
         unpack_kernel,
         out_shape=[wide, shape(groups, merged_width)],
         in_specs=[vmem] * 9, out_specs=[vmem] * 2,
-        name="unpack_strips", **settings(2),
+        name="unpack_strips", **settings(2, 24),
     )(
         full, merged, *strips,
         picks(box(levels, range(SHIFT, 2 * SHIFT), own_cols), cells[:half_cells] + got[0][:side_cut]),
@@ -741,10 +813,9 @@
     )
     merged = merged.reshape(levels, g_cols, g_rows, merged_width).transpose(0, 2, 1, 3)
 
-    out_weight_grad = block_sum(blocks0, layers, F32)
-    parts = [block_sum(blocks1, layers, F32), block_sum(blocks2, layers, F32)]
     qkv_weight_grad = jnp.concatenate(
-        [part[:, i * width:(i + 1) * width] for i in range(3) for part in parts], axis=1
+        [part[:, i * width:(i + 1) * width] for i in range(3) for part in (first_part, last_part)],
+        axis=1,
     )
     return merged, tokens_grad.reshape(tokens.shape), qkv_weight_grad, out_weight_grad
 

time: 216 us -> 193 us (0.89)
  local copies, waits for them, and re-layouts: 28.9 us -> 10.1 us
  starting transfers between devices: 36.2 us -> 28.6 us
  other arithmetic: 16.8 us -> 21.5 us
    ppermute x3 -> x21, waiting for transfers between devices: 0.01 us -> 30.4 us  [exchange(): lax.ppermute(block, ('lat', 'lon'), [(i, i ^ bit) for i in range(devices)])]
    all_to_all x6 -> x0, waiting for transfers between devices: 30 us -> none  [the longest x3 21 us: layer_step(): lax.all_to_all(total, 'lon', 0, 0, axis_index_groups=cores, tiled=True)]
    unnamed x67 -> x55, local copies, waits for them, and re-layouts: 28.9 us -> 4.71 us
    all_to_all x6 -> x0, starting transfers between devices: 23.8 us -> none  [the longest x3 13.3 us: layer_step(): lax.all_to_all(total, 'lon', 0, 0, axis_index_groups=cores, tiled=True)]
    ppermute x3 -> x21, starting transfers between devices: 1.18 us -> 21 us  [exchange(): lax.ppermute(block, ('lat', 'lon'), [(i, i ^ bit) for i in range(devices)])]
    convert_element_type x3 -> x18, other arithmetic: 8.74 us -> 18.1 us  [added(): return (a.astype(F32) + b.astype(F32) + zero).astype(dtype)]
    reduce_sum x6 -> x0, other arithmetic: 8.06 us -> none  [block_sum(): return jnp.sum(blocks, axis=0).astype(dtype)]
    ppermute x6, starting transfers between devices: 11.2 us -> 7.67 us  [sent(): return lax.ppermute(block, ('lat', 'lon'), route)]
  transfers between devices with their start and end apart: 15 -> 27, of which waited for: 6 -> 10; matrix products, arithmetic and copies ran while one was open for 8% -> 13% of each run, Pallas kernels for 22% -> 24%
where the time goes in v6:
time: 193 us
  Pallas kernels  86.3 us (45%)
  waiting for transfers between devices  45 us (23%)
  starting transfers between devices  28.6 us (15%)
  other arithmetic  21.5 us (11%)
  local copies, waits for them, and re-layouts  10.1 us (5%)
    pallas_call x4, Pallas kernels, tied_call(): pl.pallas_call(body, out_shape=[jax.ShapeDtypeStruct((8, LANES), F32)] +...  44.5 us
    pallas_call x1, Pallas kernels, shards(): pl.pallas_call(forward_kernel, out_shape=[wide, shape(channels, count), s...  36.5 us
    ppermute x21, waiting for transfers between devices, exchange(): lax.ppermute(block, ('lat', 'lon'), [(i, i ^ bit) for i in range(devices)])  30.4 us
    ppermute x21, starting transfers between devices, exchange(): lax.ppermute(block, ('lat', 'lon'), [(i, i ^ bit) for i in range(devices)])  21 us
    convert_element_type x18, other arithmetic, added(): return (a.astype(F32) + b.astype(F32) + zero).astype(dtype)  18.1 us
    ppermute x6, waiting for transfers between devices, sent(): return lax.ppermute(block, ('lat', 'lon'), route)  14.7 us
    ppermute x6, starting transfers between devices, sent(): return lax.ppermute(block, ('lat', 'lon'), route)  7.67 us
    unnamed x55, local copies, waits for them, and re-layouts  4.71 us
  transfers between devices with their start and end apart: 27, of which 10 were waited for; matrix products, arithmetic and copies ran while one was open for 13% of the time, Pallas kernels for 24%

profile of v6, /device:TPU:0, one launch (start us, length us, event | category | flops | bytes accessed | tf_op | source)
XLA Modules:
  0.0 192.8 jit_solution(4793982034997927215)
XLA Ops:
  0.6 3.1 %pack_strips.1 = (bf16[128,1024]{1,0:T(8,128)(2,1)}, bf16[208,1024]{1,0:T(8,128)(2,1)}, bf16[48,1024]{1,0:T(8,128)(2,1)}) custom-call(bf16[768,1024]{1,0:T(8,128)(2,1)} %bitcast.157, bf16[192,1024]{1,0:T(8,128)(2,1)} %bitcast.159, bf16[288,768]{1,0:T(8,128)(2,1)} %constant.40.clone.pick_cells, bf16[96,192]{1,0:T(8,128)(2,1)} %constant.41.clone.pick_groups), custom_call_target="tpu_custom_call" | custom-call | flops 10000000000 | bytes 16777216 | tf_op jit(solution)/shard_map/pack_strips/pallas_call | solution.py:671
  3.8 2.5 %collective-permute-start.2 = (bf16[48,1024]{1,0:T(8,128)(2,1)}, bf16[48,1024]{1,0:T(8,128)(2,1)S(1)}, u32[]{:S(2)}, u32[]{:S(2)}) collective-permute-start(bf16[48,1024]{1,0:T(8,128)(2,1)} %get-tuple-element.36), channel_id=1, source_target_pairs={{0,9},{1,10},{2,11},{3,12},{4,13},{5,14},{6,15},{7,8},{8,17},{9,18... | collective-permute-start | bytes 294920 | tf_op jit(solution)/shard_map/ppermute | solution.py:520
  6.2 1.6 collective-permute-start
  7.8 1.6 collective-permute-start.1
  10.1 1.3 add.253.rowmap
  11.4 1.5 collective-permute-done.2.corner
  14.2 7.6 %collective-permute-done.1.above = bf16[208,1024]{1,0:T(8,128)(2,1)S(1)} collective-permute-done((bf16[208,1024]{1,0:T(8,128)(2,1)}, bf16[208,1024]{1,0:T(8,128)(2,1)S(1)}, u32[]{:S(2)}, u32[]{:S(2)}) %collective-permute-start.1) | collective-permute-done | bytes 426016 | tf_op jit(solution)/shard_map/ppermute | solution.py:520
  22.6 36.5 %block_forward.1 = (bf16[768,1024]{1,0:T(8,128)(2,1)}, bf16[1024,768]{1,0:T(8,128)(2,1)}, bf16[768,3072]{1,0:T(8,128)(2,1)}, bf16[768,1024]{1,0:T(8,128)(2,1)}, ...) custom-call(s32[1]{0:T(128)} %bitcast.edge.refs_0_.refs_2_, ...), custom_call_target="tpu_custom_call" | custom-call | flops 299999985664 | bytes 16777216 | tf_op jit(solution)/shard_map/block_forward/pallas_call | solution.py:685
  59.1 1.4 copy-done.14
  60.5 14.2 %attention_backward.2 = (f32[8,128]{1,0:T(8,128)S(1)}, bf16[768,1536]{1,0:T(8,128)(2,1)}, bf16[512,1536]{1,0:T(8,128)(2,1)S(1)}, bf16[512,1536]{1,0:T(8,128)(2,1)}) custom-call(s32[1]{0:T(128)} %bitcast.edge.refs_0_.refs_2_, bf16[768,3072]{1,0:T(8,128)(2,1)} %get-tuple-element.39.refs_1_.refs_3_, bf16[768,1024]{1,0:T(8,128)(2,1)S(1)} %copy-done.14, ...), custom_call_target="tpu_custom_call" | custom-call | flops 149999992832 | bytes 16777216 | tf_op jit(solution)/shard_map/attention_backward/pallas_call | solution.py:613
  75.8 2.3 %add_convert_fusion.2 = bf16[512,1024]{1,0:T(8,128)(2,1)S(1)} fusion(bf16[512,1024]{1,0:T(8,128)(2,1)} %collective-permute-done.3, bf16[512,1024]{1,0:T(8,128)(2,1)S(1)} %copy-done.18, f32[]{:T(128)} %bitcast.5), kind=kLoop, calls=%fused_computation.2 | loop fusion | flops 2621440 | bytes 3145732 | tf_op jit(solution)/shard_map/convert_element_type | solution.py:552
  79.7 1.6 collective-permute-start.6
  81.2 14.0 %attention_backward.3 = (f32[8,128]{1,0:T(8,128)S(1)}, bf16[768,1536]{1,0:T(8,128)(2,1)}, bf16[512,1536]{1,0:T(8,128)(2,1)S(1)}, bf16[512,1536]{1,0:T(8,128)(2,1)S(1)}) custom-call(bf16[2,2,2,32,512]{4,3,2,1,0:T(8,128)(2,1)S(1)} %bitcast.146, bf16[2,2,2,32,512]{4,3,2,1,0:T(8,128)(2,1)} %slice_bitcast_fusion.5.refs_1_, s32[1]{0:T(128)} %bitcast.edge.refs_0_.refs_2_, ...), custom_call_target="tpu_custom_call" | custom-call | flops 149999992832 | bytes 16777216 | tf_op jit(solution)/shard_map/attention_backward/pallas_call | solution.py:613
  96.4 1.7 fusion.9
  98.1 1.5 collective-permute-start.8
  99.6 4.9 %collective-permute-done.4 = bf16[2,2,2,32,512]{4,3,2,1,0:T(8,128)(2,1)S(1)} collective-permute-done((bf16[2,2,2,32,512]{4,3,2,1,0:T(8,128)(2,1)S(1)}, bf16[2,2,2,32,512]{4,3,2,1,0:T(8,128)(2,1)S(1)}, u32[]{:S(2)}, u32[]{:S(2)}) %collective-permute-start.4) | collective-permute-done | bytes 262176 | tf_op jit(solution)/shard_map/ppermute | solution.py:548
  105.5 2.8 %add_convert_fusion.1 = bf16[512,1536]{1,0:T(8,128)(2,1)S(1)} fusion(bf16[512,1536]{1,0:T(8,128)(2,1)} %collective-permute-done.7, bf16[512,1536]{1,0:T(8,128)(2,1)S(1)} %get-tuple-element.45, f32[]{:T(128)} %bitcast.10), kind=kLoop, calls=%fused_computation.1 | loop fusion | flops 3932160 | bytes 4718596 | tf_op jit(solution)/shard_map/convert_element_type | solution.py:552
  108.5 1.9 collective-permute-start.15
  110.8 1.7 copy-done.10
  112.5 6.5 %input_first.1 = (f32[8,128]{1,0:T(8,128)S(1)}, bf16[768,512]{1,0:T(8,128)(2,1)S(1)}) custom-call(bf16[2,2,32,512]{3,2,1,0:T(8,128)(2,1)S(1)} %slice_bitcast_fusion.16.refs_0_, bf16[2,2,32,512]{3,2,1,0:T(8,128)(2,1)S(1)} %slice_bitcast_fusion.15.refs_1_, bf16[2,2,2,32,768]{4,3,2,1,0:T(8,128)(2,1)S(1)} %bitcast.145, ...), custom_call_target="tpu_custom_call" | custom-call | flops 49999998976 | bytes 16777216 | tf_op jit(solution)/shard_map/input_first/pallas_call | solution.py:613
  124.6 9.9 %input_last.1 = (f32[8,128]{1,0:T(8,128)S(1)}, bf16[768,1024]{1,0:T(8,128)(2,1)S(1)}, bf16[128,1024]{1,0:T(8,128)(2,1)S(1)}, bf16[208,1024]{1,0:T(8,128)(2,1)S(1)}, bf16[48,1024]{1,0:T(8,128)(2,1)S(1)}) custom-call(bf16[2,32,1024]{2,1,0:T(8,128)(2,1)S(1)} %fusion.39.refs_0_, bf16[2,2,2,32,768]{4,3,2,1,0:T(8,128)(2,1)S(1)} %bitcast.143, ...), custom_call_target="tpu_custom_call" | custom-call | flops 89999998976 | bytes 16777216 | tf_op jit(solution)/shard_map/input_last/pallas_call | solution.py:613
  135.7 2.7 %collective-permute-start.26 = (bf16[32,1024]{1,0:T(8,128)(2,1)S(1)}, bf16[32,1024]{1,0:T(8,128)(2,1)S(1)}, u32[]{:S(2)}, u32[]{:S(2)}) collective-permute-start(bf16[32,1024]{1,0:T(8,128)(2,1)S(1)} %slice_bitcast_fusion.22), channel_id=1, source_target_pairs={{0,16},{1,17},{2,18},{3,19},{4,20},{5,21},{6,22},{7,23},{8,24},{9,... | collective-permute-start | bytes 196616 | tf_op jit(solution)/shard_map/ppermute | solution.py:548
  140.7 6.1 %collective-permute-done.16 = bf16[2,2,32,768]{3,2,1,0:T(8,128)(2,1)S(1)} collective-permute-done((bf16[2,2,32,768]{3,2,1,0:T(8,128)(2,1)S(1)}, bf16[2,2,32,768]{3,2,1,0:T(8,128)(2,1)S(1)}, u32[]{:S(2)}, u32[]{:S(2)}) %collective-permute-start.16) | collective-permute-done | bytes 196640 | tf_op jit(solution)/shard_map/ppermute | solution.py:548
  147.5 6.4 %collective-permute-done.14 = bf16[2,2,32,768]{3,2,1,0:T(8,128)(2,1)S(1)} collective-permute-done((bf16[2,2,32,768]{3,2,1,0:T(8,128)(2,1)S(1)}, bf16[2,2,32,768]{3,2,1,0:T(8,128)(2,1)S(1)}, u32[]{:S(2)}, u32[]{:S(2)}) %collective-permute-start.14) | collective-permute-done | bytes 196640 | tf_op jit(solution)/shard_map/ppermute | solution.py:548
  158.0 4.1 %collective-permute-done.17 = bf16[2,32,1536]{2,1,0:T(8,128)(2,1)S(1)} collective-permute-done((bf16[2,32,1536]{2,1,0:T(8,128)(2,1)S(1)}, bf16[2,32,1536]{2,1,0:T(8,128)(2,1)S(1)}, u32[]{:S(2)}, u32[]{:S(2)}) %collective-permute-start.17) | collective-permute-done | bytes 196640 | tf_op jit(solution)/shard_map/ppermute | solution.py:548
  162.0 1.3 collective-permute-start.11
  167.8 1.6 collective-permute-start.20
  169.5 4.3 %collective-permute-done.11.below = bf16[208,1024]{1,0:T(8,128)(2,1)S(1)} collective-permute-done((bf16[208,1024]{1,0:T(8,128)(2,1)S(1)}, bf16[208,1024]{1,0:T(8,128)(2,1)S(1)}, u32[]{:S(2)}, u32[]{:S(2)}) %collective-permute-start.11) | collective-permute-done | bytes 426016 | tf_op jit(solution)/shard_map/ppermute | solution.py:520
  173.8 2.1 %unpack_strips.1 = (bf16[768,1024]{1,0:T(8,128)(2,1)}, bf16[192,1024]{1,0:T(8,128)(2,1)}) custom-call(bf16[768,1024]{1,0:T(8,128)(2,1)S(1)} %get-tuple-element.57.full, bf16[192,1024]{1,0:T(8,128)(2,1)S(1)} %copy-done.8, bf16[128,1024]{1,0:T(8,128)(2,1)S(1)} %collective-permute-done.10.side, bf16[208,1024]{1,0:T(8,128)(2,1)S(1)} %collective-permute-done.11.below, ...), custom_call_target="tpu_custom_call" | custom-call | flops 20000000000 | bytes 16777216 | tf_op jit(solution)/shard_map/unpack_strips/pallas_call | solution.py:802
  177.4 2.9 %collective-permute-start.23 = (bf16[2,32,1536]{2,1,0:T(8,128)(2,1)S(1)}, bf16[2,32,1536]{2,1,0:T(8,128)(2,1)S(1)}, u32[]{:S(2)}, u32[]{:S(2)}) collective-permute-start(bf16[2,32,1536]{2,1,0:T(8,128)(2,1)S(1)} %fusion.34), channel_id=1, source_target_pairs={{0,8},{1,9},{2,10},{3,11},{4,12},{5,13},{6,14},{7,15},{8,0},{9,1},... | collective-permute-start | bytes 589832 | tf_op jit(solution)/shard_map/ppermute | solution.py:548
  180.9 4.0 %collective-permute-done.23 = bf16[2,32,1536]{2,1,0:T(8,128)(2,1)S(1)} collective-permute-done((bf16[2,32,1536]{2,1,0:T(8,128)(2,1)S(1)}, bf16[2,32,1536]{2,1,0:T(8,128)(2,1)S(1)}, u32[]{:S(2)}, u32[]{:S(2)}) %collective-permute-start.23) | collective-permute-done | bytes 196640 | tf_op jit(solution)/shard_map/ppermute | solution.py:548
  186.4 4.9 %collective-permute-done.24 = bf16[32,1536]{1,0:T(8,128)(2,1)S(1)} collective-permute-done((bf16[32,1536]{1,0:T(8,128)(2,1)S(1)}, bf16[32,1536]{1,0:T(8,128)(2,1)S(1)}, u32[]{:S(2)}, u32[]{:S(2)}) %collective-permute-start.24) | collective-permute-done | bytes 98336 | tf_op jit(solution)/shard_map/ppermute | solution.py:548
  (134 shorter events, 31.3 us)
Async XLA Ops:
  3.8 9.1 %collective-permute-start.2 = (bf16[48,1024]{1,0:T(8,128)(2,1)}, bf16[48,1024]{1,0:T(8,128)(2,1)S(1)}, u32[]{:S(2)}, u32[]{:S(2)}) collective-permute-start(bf16[48,1024]{1,0:T(8,128)(2,1)} %get-tuple-element.36), channel_id=1, source_target_pairs={{0,9},{1,10},{2,11},{3,12},{4,13},{5,14},{6,15},{7,8},{8,17},{9,18... | collective-permute-start | bytes 294920 | tf_op jit(solution)/shard_map/ppermute | solution.py:520
  6.2 8.0 %collective-permute-start = (bf16[128,1024]{1,0:T(8,128)(2,1)}, bf16[128,1024]{1,0:T(8,128)(2,1)S(1)}, u32[]{:S(2)}, u32[]{:S(2)}) collective-permute-start(bf16[128,1024]{1,0:T(8,128)(2,1)} %get-tuple-element.34), channel_id=1, source_target_pairs={{0,1},{1,2},{2,3},{3,4},{4,5},{5,6},{6,7},{7,0},{8,9},{9,10},{10,1... | collective-permute-start | bytes 786440 | tf_op jit(solution)/shard_map/ppermute | solution.py:520
  7.8 14.0 %collective-permute-start.1 = (bf16[208,1024]{1,0:T(8,128)(2,1)}, bf16[208,1024]{1,0:T(8,128)(2,1)S(1)}, u32[]{:S(2)}, u32[]{:S(2)}) collective-permute-start(bf16[208,1024]{1,0:T(8,128)(2,1)} %get-tuple-element.35), channel_id=1, source_target_pairs={{0,8},{1,9},{2,10},{3,11},{4,12},{5,13},{6,14},{7,15},{8,16},{9,17... | collective-permute-start | bytes 1277960 | tf_op jit(solution)/shard_map/ppermute | solution.py:520
  59.0 16.7 %collective-permute-start.3 = (bf16[512,1024]{1,0:T(8,128)(2,1)}, bf16[512,1024]{1,0:T(8,128)(2,1)}, u32[]{:S(2)}, u32[]{:S(2)}) collective-permute-start(bf16[512,1024]{1,0:T(8,128)(2,1)} %get-tuple-element.38), channel_id=1, source_target_pairs={{0,1},{1,0},{2,3},{3,2},{4,5},{5,4},{6,7},{7,6},{8,9},{9,8},{10,11... | collective-permute-start | bytes 3145736 | tf_op jit(solution)/shard_map/ppermute | solution.py:548
  60.5 15.2 %copy-start.18 = (bf16[512,1024]{1,0:T(8,128)(2,1)S(1)}, bf16[512,1024]{1,0:T(8,128)(2,1)}, u32[]{:S(2)}) copy-start(bf16[512,1024]{1,0:T(8,128)(2,1)} %get-tuple-element.37) | copy-start | bytes 3145732
  75.3 30.3 %collective-permute-start.7 = (bf16[512,1536]{1,0:T(8,128)(2,1)}, bf16[512,1536]{1,0:T(8,128)(2,1)}, u32[]{:S(2)}, u32[]{:S(2)}) collective-permute-start(bf16[512,1536]{1,0:T(8,128)(2,1)} %get-tuple-element.46), channel_id=1, source_target_pairs={{0,1},{1,0},{2,3},{3,2},{4,5},{5,4},{6,7},{7,6},{8,9},{9,8},{10,11... | collective-permute-start | bytes 4718600 | tf_op jit(solution)/shard_map/ppermute | solution.py:548
  79.7 16.8 %collective-permute-start.6 = (bf16[2,2,2,32,512]{4,3,2,1,0:T(8,128)(2,1)}, bf16[2,2,2,32,512]{4,3,2,1,0:T(8,128)(2,1)}, u32[]{:S(2)}, u32[]{:S(2)}) collective-permute-start(bf16[2,2,2,32,512]{4,3,2,1,0:T(8,128)(2,1)} %slice_bitcast_fusion.5.refs_1_), channel_id=1, source_target_pairs={{0,4},{1,5},{2,6},{3,7},{4,0},{5,1},{6,2},{7,3},{8,12},{9,13},{10,... | collective-permute-start | bytes 786440 | tf_op jit(solution)/shard_map/ppermute | solution.py:548
  81.2 15.2 %copy-start.17 = (bf16[512,512]{1,0:T(8,128)(2,1)S(1)}, bf16[512,512]{1,0:T(8,128)(2,1)}, u32[]{:S(2)}) copy-start(bf16[512,512]{1,0:T(8,128)(2,1)} %copy-done.16) | copy-start | bytes 1572868
  81.2 23.3 %copy-start.19 = (bf16[256,512]{1,0:T(8,128)(2,1)S(1)}, bf16[256,512]{1,0:T(8,128)(2,1)}, u32[]{:S(2)}) copy-start(bf16[256,512]{1,0:T(8,128)(2,1)} %get-tuple-element.69) | copy-start | bytes 786436
  95.2 9.3 %collective-permute-start.4 = (bf16[2,2,2,32,512]{4,3,2,1,0:T(8,128)(2,1)S(1)}, bf16[2,2,2,32,512]{4,3,2,1,0:T(8,128)(2,1)S(1)}, u32[]{:S(2)}, u32[]{:S(2)}) collective-permute-start(bf16[2,2,2,32,512]{4,3,2,1,0:T(8,128)(2,1)S(1)} %bitcast.147), channel_id=1, source_target_pairs={{0,2},{1,3},{2,0},{3,1},{4,6},{5,7},{6,4},{7,5},{8,10},{9,11},{10,... | collective-permute-start | bytes 786440 | tf_op jit(solution)/shard_map/ppermute | solution.py:548
  96.4 24.9 %collective-permute-start.9 = (bf16[512,1536]{1,0:T(8,128)(2,1)S(1)}, bf16[512,1536]{1,0:T(8,128)(2,1)S(1)}, u32[]{:S(2)}, u32[]{:S(2)}) collective-permute-start(bf16[512,1536]{1,0:T(8,128)(2,1)S(1)} %get-tuple-element.51), channel_id=1, source_target_pairs={{0,1},{1,0},{2,3},{3,2},{4,5},{5,4},{6,7},{7,6},{8,9},{9,8},{10,11... | collective-permute-start | bytes 4718600 | tf_op jit(solution)/shard_map/ppermute | solution.py:548
  98.1 21.3 %collective-permute-start.8 = (bf16[2,2,32,512]{3,2,1,0:T(8,128)(2,1)S(1)}, bf16[2,2,32,512]{3,2,1,0:T(8,128)(2,1)S(1)}, u32[]{:S(2)}, u32[]{:S(2)}) collective-permute-start(bf16[2,2,32,512]{3,2,1,0:T(8,128)(2,1)S(1)} %slice_bitcast_fusion.15.refs_1_), channel_id=1, source_target_pairs={{0,2},{1,3},{2,0},{3,1},{4,6},{5,7},{6,4},{7,5},{8,10},{9,11},{10,... | collective-permute-start | bytes 393224 | tf_op jit(solution)/shard_map/ppermute | solution.py:548
  105.3 14.9 %collective-permute-start.5 = (bf16[2,2,32,512]{3,2,1,0:T(8,128)(2,1)S(1)}, bf16[2,2,32,512]{3,2,1,0:T(8,128)(2,1)S(1)}, u32[]{:S(2)}, u32[]{:S(2)}) collective-permute-start(bf16[2,2,32,512]{3,2,1,0:T(8,128)(2,1)S(1)} %slice_bitcast_fusion.16.refs_0_), channel_id=1, source_target_pairs={{0,4},{1,5},{2,6},{3,7},{4,0},{5,1},{6,2},{7,3},{8,12},{9,13},{10,... | collective-permute-start | bytes 393224 | tf_op jit(solution)/shard_map/ppermute | solution.py:548
  108.5 29.8 %collective-permute-start.15 = (bf16[2,2,2,32,768]{4,3,2,1,0:T(8,128)(2,1)S(1)}, bf16[2,2,2,32,768]{4,3,2,1,0:T(8,128)(2,1)S(1)}, u32[]{:S(2)}, u32[]{:S(2)}) collective-permute-start(bf16[2,2,2,32,768]{4,3,2,1,0:T(8,128)(2,1)S(1)} %slice_bitcast_fusion.3.refs_3_), channel_id=1, source_target_pairs={{0,4},{1,5},{2,6},{3,7},{4,0},{5,1},{6,2},{7,3},{8,12},{9,13},{10,... | collective-permute-start | bytes 1179656 | tf_op jit(solution)/shard_map/ppermute | solution.py:548
  110.4 28.7 %collective-permute-start.13 = (bf16[2,2,2,32,768]{4,3,2,1,0:T(8,128)(2,1)S(1)}, bf16[2,2,2,32,768]{4,3,2,1,0:T(8,128)(2,1)S(1)}, u32[]{:S(2)}, u32[]{:S(2)}) collective-permute-start(bf16[2,2,2,32,768]{4,3,2,1,0:T(8,128)(2,1)S(1)} %bitcast.144), channel_id=1, source_target_pairs={{0,2},{1,3},{2,0},{3,1},{4,6},{5,7},{6,4},{7,5},{8,10},{9,11},{10,... | collective-permute-start | bytes 1179656 | tf_op jit(solution)/shard_map/ppermute | solution.py:548
  120.9 14.1 %collective-permute-start.25 = (bf16[2,32,1024]{2,1,0:T(8,128)(2,1)S(1)}, bf16[2,32,1024]{2,1,0:T(8,128)(2,1)S(1)}, u32[]{:S(2)}, u32[]{:S(2)}) collective-permute-start(bf16[2,32,1024]{2,1,0:T(8,128)(2,1)S(1)} %fusion.39.refs_0_), channel_id=1, source_target_pairs={{0,8},{1,9},{2,10},{3,11},{4,12},{5,13},{6,14},{7,15},{8,0},{9,1},... | collective-permute-start | bytes 393224 | tf_op jit(solution)/shard_map/ppermute | solution.py:548
  122.9 41.3 %collective-permute-start.21 = (bf16[2,2,2,32,768]{4,3,2,1,0:T(8,128)(2,1)S(1)}, bf16[2,2,2,32,768]{4,3,2,1,0:T(8,128)(2,1)S(1)}, u32[]{:S(2)}, u32[]{:S(2)}) collective-permute-start(bf16[2,2,2,32,768]{4,3,2,1,0:T(8,128)(2,1)S(1)} %slice_bitcast_fusion.2.refs_2_), channel_id=1, source_target_pairs={{0,4},{1,5},{2,6},{3,7},{4,0},{5,1},{6,2},{7,3},{8,12},{9,13},{10,... | collective-permute-start | bytes 1179656 | tf_op jit(solution)/shard_map/ppermute | solution.py:548
  124.1 42.0 %collective-permute-start.19 = (bf16[2,2,2,32,768]{4,3,2,1,0:T(8,128)(2,1)S(1)}, bf16[2,2,2,32,768]{4,3,2,1,0:T(8,128)(2,1)S(1)}, u32[]{:S(2)}, u32[]{:S(2)}) collective-permute-start(bf16[2,2,2,32,768]{4,3,2,1,0:T(8,128)(2,1)S(1)} %bitcast.142), channel_id=1, source_target_pairs={{0,2},{1,3},{2,0},{3,1},{4,6},{5,7},{6,4},{7,5},{8,10},{9,11},{10,... | collective-permute-start | bytes 1179656 | tf_op jit(solution)/shard_map/ppermute | solution.py:548
  135.7 19.6 %collective-permute-start.26 = (bf16[32,1024]{1,0:T(8,128)(2,1)S(1)}, bf16[32,1024]{1,0:T(8,128)(2,1)S(1)}, u32[]{:S(2)}, u32[]{:S(2)}) collective-permute-start(bf16[32,1024]{1,0:T(8,128)(2,1)S(1)} %slice_bitcast_fusion.22), channel_id=1, source_target_pairs={{0,16},{1,17},{2,18},{3,19},{4,20},{5,21},{6,22},{7,23},{8,24},{9,... | collective-permute-start | bytes 196616 | tf_op jit(solution)/shard_map/ppermute | solution.py:548
  138.3 29.5 %collective-permute-start.12 = (bf16[48,1024]{1,0:T(8,128)(2,1)S(1)}, bf16[48,1024]{1,0:T(8,128)(2,1)S(1)}, u32[]{:S(2)}, u32[]{:S(2)}) collective-permute-start(bf16[48,1024]{1,0:T(8,128)(2,1)S(1)} %get-tuple-element.60), channel_id=1, source_target_pairs={{0,31},{1,24},{2,25},{3,26},{4,27},{5,28},{6,29},{7,30},{8,7},{9,0... | collective-permute-start | bytes 294920 | tf_op jit(solution)/shard_map/ppermute | solution.py:520
  139.1 7.6 %collective-permute-start.16 = (bf16[2,2,32,768]{3,2,1,0:T(8,128)(2,1)S(1)}, bf16[2,2,32,768]{3,2,1,0:T(8,128)(2,1)S(1)}, u32[]{:S(2)}, u32[]{:S(2)}) collective-permute-start(bf16[2,2,32,768]{3,2,1,0:T(8,128)(2,1)S(1)} %slice_bitcast_fusion.10), channel_id=1, source_target_pairs={{0,2},{1,3},{2,0},{3,1},{4,6},{5,7},{6,4},{7,5},{8,10},{9,11},{10,... | collective-permute-start | bytes 589832 | tf_op jit(solution)/shard_map/ppermute | solution.py:548
  146.8 7.1 %collective-permute-start.14 = (bf16[2,2,32,768]{3,2,1,0:T(8,128)(2,1)S(1)}, bf16[2,2,32,768]{3,2,1,0:T(8,128)(2,1)S(1)}, u32[]{:S(2)}, u32[]{:S(2)}) collective-permute-start(bf16[2,2,32,768]{3,2,1,0:T(8,128)(2,1)S(1)} %slice_bitcast_fusion.12), channel_id=1, source_target_pairs={{0,4},{1,5},{2,6},{3,7},{4,0},{5,1},{6,2},{7,3},{8,12},{9,13},{10,... | collective-permute-start | bytes 589832 | tf_op jit(solution)/shard_map/ppermute | solution.py:548
  153.9 15.6 %collective-permute-start.10 = (bf16[128,1024]{1,0:T(8,128)(2,1)S(1)}, bf16[128,1024]{1,0:T(8,128)(2,1)S(1)}, u32[]{:S(2)}, u32[]{:S(2)}) collective-permute-start(bf16[128,1024]{1,0:T(8,128)(2,1)S(1)} %get-tuple-element.58), channel_id=1, source_target_pairs={{0,7},{1,0},{2,1},{3,2},{4,3},{5,4},{6,5},{7,6},{8,15},{9,8},{10,9... | collective-permute-start | bytes 786440 | tf_op jit(solution)/shard_map/ppermute | solution.py:520
  155.3 6.7 %collective-permute-start.17 = (bf16[2,32,1536]{2,1,0:T(8,128)(2,1)S(1)}, bf16[2,32,1536]{2,1,0:T(8,128)(2,1)S(1)}, u32[]{:S(2)}, u32[]{:S(2)}) collective-permute-start(bf16[2,32,1536]{2,1,0:T(8,128)(2,1)S(1)} %fusion.35), channel_id=1, source_target_pairs={{0,8},{1,9},{2,10},{3,11},{4,12},{5,13},{6,14},{7,15},{8,0},{9,1},... | collective-permute-start | bytes 589832 | tf_op jit(solution)/shard_map/ppermute | solution.py:548
  162.0 11.7 %collective-permute-start.11 = (bf16[208,1024]{1,0:T(8,128)(2,1)S(1)}, bf16[208,1024]{1,0:T(8,128)(2,1)S(1)}, u32[]{:S(2)}, u32[]{:S(2)}) collective-permute-start(bf16[208,1024]{1,0:T(8,128)(2,1)S(1)} %get-tuple-element.59), channel_id=1, source_target_pairs={{0,24},{1,25},{2,26},{3,27},{4,28},{5,29},{6,30},{7,31},{8,0},{9,1... | collective-permute-start | bytes 1277960 | tf_op jit(solution)/shard_map/ppermute | solution.py:520
  164.1 9.7 %copy-start.1 = (bf16[384,448]{1,0:T(8,128)(2,1)S(1)}, bf16[384,448]{1,0:T(8,128)(2,1)}, u32[]{:S(2)}) copy-start(bf16[384,448]{1,0:T(8,128)(2,1)} %constant.50.clone.pick_middle) | copy-start | bytes 1032196
  164.1 9.6 %copy-start.2 = (bf16[192,416]{1,0:T(8,128)(2,1)S(1)}, bf16[192,416]{1,0:T(8,128)(2,1)}, u32[]{:S(2)}) copy-start(bf16[192,416]{1,0:T(8,128)(2,1)} %constant.49.clone.pick_top) | copy-start | bytes 479236
  164.1 16.1 %collective-permute-start.18 = (bf16[32,1536]{1,0:T(8,128)(2,1)S(1)}, bf16[32,1536]{1,0:T(8,128)(2,1)S(1)}, u32[]{:S(2)}, u32[]{:S(2)}) collective-permute-start(bf16[32,1536]{1,0:T(8,128)(2,1)S(1)} %slice_bitcast_fusion.20), channel_id=1, source_target_pairs={{0,16},{1,17},{2,18},{3,19},{4,20},{5,21},{6,22},{7,23},{8,24},{9,... | collective-permute-start | bytes 294920 | tf_op jit(solution)/shard_map/ppermute | solution.py:548
  166.1 9.8 %collective-permute-start.22 = (bf16[2,2,32,768]{3,2,1,0:T(8,128)(2,1)S(1)}, bf16[2,2,32,768]{3,2,1,0:T(8,128)(2,1)S(1)}, u32[]{:S(2)}, u32[]{:S(2)}) collective-permute-start(bf16[2,2,32,768]{3,2,1,0:T(8,128)(2,1)S(1)} %slice_bitcast_fusion.6), channel_id=1, source_target_pairs={{0,2},{1,3},{2,0},{3,1},{4,6},{5,7},{6,4},{7,5},{8,10},{9,11},{10,... | collective-permute-start | bytes 589832 | tf_op jit(solution)/shard_map/ppermute | solution.py:548
  167.8 8.8 %collective-permute-start.20 = (bf16[2,2,32,768]{3,2,1,0:T(8,128)(2,1)S(1)}, bf16[2,2,32,768]{3,2,1,0:T(8,128)(2,1)S(1)}, u32[]{:S(2)}, u32[]{:S(2)}) collective-permute-start(bf16[2,2,32,768]{3,2,1,0:T(8,128)(2,1)S(1)} %slice_bitcast_fusion.8), channel_id=1, source_target_pairs={{0,4},{1,5},{2,6},{3,7},{4,0},{5,1},{6,2},{7,3},{8,12},{9,13},{10,... | collective-permute-start | bytes 589832 | tf_op jit(solution)/shard_map/ppermute | solution.py:548
  177.4 7.6 %collective-permute-start.23 = (bf16[2,32,1536]{2,1,0:T(8,128)(2,1)S(1)}, bf16[2,32,1536]{2,1,0:T(8,128)(2,1)S(1)}, u32[]{:S(2)}, u32[]{:S(2)}) collective-permute-start(bf16[2,32,1536]{2,1,0:T(8,128)(2,1)S(1)} %fusion.34), channel_id=1, source_target_pairs={{0,8},{1,9},{2,10},{3,11},{4,12},{5,13},{6,14},{7,15},{8,0},{9,1},... | collective-permute-start | bytes 589832 | tf_op jit(solution)/shard_map/ppermute | solution.py:548
  185.7 5.6 %collective-permute-start.24 = (bf16[32,1536]{1,0:T(8,128)(2,1)S(1)}, bf16[32,1536]{1,0:T(8,128)(2,1)S(1)}, u32[]{:S(2)}, u32[]{:S(2)}) collective-permute-start(bf16[32,1536]{1,0:T(8,128)(2,1)S(1)} %slice_bitcast_fusion.18), channel_id=1, source_target_pairs={{0,16},{1,17},{2,18},{3,19},{4,20},{5,21},{6,22},{7,23},{8,24},{9,... | collective-permute-start | bytes 294920 | tf_op jit(solution)/shard_map/ppermute | solution.py:548
  (20 other events, 78.6 us)

commit v7 on v6

--- a/solution.py
+++ b/solution.py
@@ -427,28 +427,15 @@
     return loads, tiles
 
 
-def input_first_kernel(pg0, pg1, wqkv_h, ngrad, pgrad, wqkv, sem):
-    loads, tiles = projection_loads([pg0, pg1], wqkv_h, pgrad, wqkv, sem, 0)
-    for load in loads:
-        load.wait()
-    for n, load in enumerate(tiles):
-        load.wait()
-        rows = pl.ds(n * TILE, TILE)
-        ngrad[:, rows] = dot(pgrad[...], wqkv[rows], NT).astype(BF16)
-
-
-def input_last_kernel(*refs):
-    (pg0, pg1, wqkv_h, nfirst_h, normed_h, rstd_h, grad_h, merged,
+def input_kernel(*refs):
+    (pg0, pg1, wqkv_h, normed_h, rstd_h, grad_h, merged,
      pick_first, pick_last, pick_groups, full, side, below, corner,
      pgrad, wqkv, ngrad, normed, rstd, grad, sem, more_sem) = refs
     count, channels = ngrad.shape
-    half = channels // 2
-    loads, tiles = projection_loads([pg0, pg1], wqkv_h, pgrad, wqkv, sem, half)
+    loads, tiles = projection_loads([pg0, pg1], wqkv_h, pgrad, wqkv, sem, 0)
     more = [
         pltpu.make_async_copy(src, dst, more_sem.at[i])
-        for i, (src, dst) in enumerate(
-            [(nfirst_h, ngrad.at[:, pl.ds(0, half)]), (normed_h, normed), (rstd_h, rstd), (grad_h, grad)]
-        )
+        for i, (src, dst) in enumerate([(normed_h, normed), (rstd_h, rstd), (grad_h, grad)])
     ]
     for load in more:
         load.start()
@@ -456,7 +443,7 @@
         load.wait()
     for n, load in enumerate(tiles):
         load.wait()
-        ngrad[:, pl.ds(half + n * TILE, TILE)] = dot(
+        ngrad[:, pl.ds(n * TILE, TILE)] = dot(
             pgrad[...], wqkv[pl.ds(n * TILE, TILE)], NT
         ).astype(BF16)
     for load in more:
@@ -525,99 +512,82 @@
     return [sent(side, sizes, 0, step), sent(lines, sizes, step, 0), sent(corner, sizes, step, step)]
 
 
-def bit_list(count):
-    return [1 << i for i in range(count.bit_length() - 1)]
-
-
 def device_rows(channels, sizes):
     n_lat, n_lon = sizes
     devices = n_lat * n_lon
     rows = channels // devices
     place = np.arange(devices)
-    partner = np.zeros_like(place)
-    for i, bit in enumerate(bit_list(devices)):
-        partner |= np.where(place & (devices >> (i + 1)), bit, 0)
-    me = (lax.axis_index("lat") * n_lon + lax.axis_index("lon")).astype(jnp.int32)
-    owner = jnp.bitwise_xor(jnp.asarray(partner, jnp.int32), me)
+    lon = 2 * (place // n_lat % (n_lon // 2)) + place // (devices // 2)
+    lat = place % n_lat
+    owner = (
+        jnp.bitwise_xor(lax.axis_index("lat").astype(jnp.int32), jnp.asarray(lat, jnp.int32)) * n_lon
+        + jnp.bitwise_xor(lax.axis_index("lon").astype(jnp.int32), jnp.asarray(lon, jnp.int32))
+    )
     rowmap = owner[:, None] * rows + jnp.arange(rows, dtype=jnp.int32)[None, :]
     return owner, rowmap.reshape(channels, 1)
 
 
-def exchange(block, sizes, bit):
-    devices = sizes[0] * sizes[1]
-    return lax.ppermute(block, ("lat", "lon"), [(i, i ^ bit) for i in range(devices)])
-
-
-def added(a, b, zero, dtype=BF16):
-    return (a.astype(F32) + b.astype(F32) + zero).astype(dtype)
-
-
-class Sum:
-    def __init__(self, mine, theirs, sizes):
-        self.sizes, self.mine, self.theirs, self.zero = sizes, mine, theirs, 0.0
-        self.bits = bit_list(sizes[0] * sizes[1])[1:]
-        layer = bit_list(sizes[1])[1:]
-        self.turns = [layer, layer[1:] + layer[:1]]
-        self.column = [sizes[1] * b for b in bit_list(sizes[0])]
-
-    def send_core(self):
-        self.arrived = exchange(self.theirs, self.sizes, 1)
-
-    def split(self, parts):
-        self.kept, given = [], []
-        for i, part in enumerate(parts):
-            axis = self.bits_of[i].index(self.turns[i][0])
-            self.kept.append(lax.index_in_dim(part, 0, axis, keepdims=False))
-            given.append(lax.index_in_dim(part, 1, axis, keepdims=False))
-        return given
-
-    def send(self, given):
-        self.arrived = []
-        for i, block in enumerate(given):
-            bit = self.turns[i][0]
-            self.arrived.append(exchange(block, self.sizes, bit))
-            self.turns[i] = self.turns[i][1:]
-            self.bits_of[i] = [b for b in self.bits_of[i] if b != bit]
-
-    def first(self):
-        total = added(self.mine, self.arrived, self.zero)
-        columns = total.shape[1] // 2
-        rows = total.shape[0] >> len(self.bits)
-        self.bits_of = [list(self.bits), list(self.bits)]
-        return self.split([
-            total[:, i * columns:(i + 1) * columns].reshape([2] * len(self.bits) + [rows, columns])
-            for i in range(2)
-        ])
-
-    def next(self):
-        parts = [added(k, a, self.zero) for k, a in zip(self.kept, self.arrived)]
-        if not self.turns[0]:
-            parts = [jnp.concatenate(parts, axis=-1)]
-            self.turns, self.bits_of = [self.column], [self.bits_of[0]]
-        return self.split(parts)
-
-    def rest(self):
-        while self.turns[0] or len(self.turns) > 1:
-            self.send(self.next())
-        return added(self.kept[0], self.arrived[0], self.zero, F32)
+def exchange(block, sizes, lat_bits, lon_bits):
+    n_lat, n_lon = sizes
+    route = [
+        (a * n_lon + b, (a ^ lat_bits) * n_lon + (b ^ lon_bits))
+        for a in range(n_lat) for b in range(n_lon)
+    ]
+    return lax.ppermute(block, ("lat", "lon"), route)
+
+
+def core_step(theirs, sizes):
+    return exchange(theirs, sizes, 0, 1)
+
+
+def layer_blocks(mine, arrived, sizes):
+    blocks = sizes[1] // 2
+    rows = mine.shape[0] // blocks
+    total = [
+        (mine[i * rows:(i + 1) * rows].astype(F32) + arrived[i * rows:(i + 1) * rows].astype(F32))
+        for i in range(blocks)
+    ]
+    return [total[0]] + [t.astype(BF16) for t in total[1:]]
+
+
+def layer_step(blocks, sizes):
+    return [exchange(b, sizes, 0, 2 * i) for i, b in enumerate(blocks) if i]
+
+
+def column_blocks(kept, arrived, sizes):
+    total = kept
+    for block in arrived:
+        total = total + block.astype(F32)
+    rows = total.shape[0] // sizes[0]
+    blocks = [total[i * rows:(i + 1) * rows] for i in range(sizes[0])]
+    return [blocks[0]] + [b.astype(BF16) for b in blocks[1:]]
+
+
+def column_step(blocks, sizes):
+    return [exchange(b, sizes, i, 0) for i, b in enumerate(blocks) if i]
+
+
+def behind(values, marker):
+    *values, _ = lax.optimization_barrier((*values, marker))
+    return values
+
+
+def finished(kept, arrived):
+    for block in arrived:
+        kept = kept + block.astype(F32)
+    return kept
 
 
 def tied_call(kernel, after, operands, in_specs, out_shape, out_specs, **rest):
     waits = len(after)
-    reads = waits + len(operands)
 
     def body(*refs):
-        refs[reads][...] = jnp.zeros_like(refs[reads])
-        kernel(*refs[waits:reads], *refs[reads + 1:])
-
-    zero, *out = pl.pallas_call(
-        body,
-        out_shape=[jax.ShapeDtypeStruct((8, LANES), F32)] + out_shape,
-        in_specs=[pl.BlockSpec(memory_space=pl.ANY)] * waits + in_specs,
-        out_specs=[pl.BlockSpec(memory_space=pltpu.VMEM)] + out_specs,
-        **rest,
+        kernel(*refs[waits:])
+
+    return pl.pallas_call(
+        body, out_shape=out_shape,
+        in_specs=[pl.BlockSpec(memory_space=pl.ANY)] * waits + in_specs, out_specs=out_specs, **rest,
     )(*after, *operands)
-    return zero[0, 0], out
 
 
 def shards(sizes, tokens, qkv_weight, out_weight, merge_weight, merged_grad):
@@ -738,83 +708,70 @@
             name="attention_backward", **settings(15, 48),
         )
 
-    out_sum = Sum(out_mine, out_theirs, sizes)
-    out_sum.send_core()
-    out_sum.zero, (pg0, mine, theirs) = backward(0, [])
-    given = out_sum.first()
-    out_sum.send(given)
-    first_sum = Sum(mine, theirs, sizes)
-    first_sum.send_core()
-    zero, (pg1, mine, theirs) = backward(1, given)
-    first_sum.zero = out_sum.zero = zero
-    after = out_sum.next()
-    out_sum.send(after)
-    given = first_sum.first()
-    first_sum.send(given)
-    last_sum = Sum(mine, theirs, sizes)
-    last_sum.send_core()
-    after = after + given
-
-    in_scratch = [
-        pltpu.VMEM((count, 3 * channels), BF16),
-        pltpu.VMEM((half, 3 * channels), BF16),
-    ]
-    in_sems = pltpu.SemaphoreType.DMA((3 * halves + half // TILE,))
-    zero, [nfirst] = tied_call(
-        input_first_kernel, after,
-        [pg0, pg1, qkv_weight], [hbm] * 3, [shape(count, half)], [vmem],
-        scratch_shapes=in_scratch + [in_sems],
-        name="input_first", **settings(5, 36),
-    )
-    last_sum.zero = out_sum.zero = zero
-    given = last_sum.first()
-    last_sum.send(given)
-    after = out_sum.next()
-    out_sum.send(after)
-    after = after + given
+    arrived = core_step(out_theirs, sizes)
+    pg0, mine1, theirs1 = backward(0, [])
+    out_mine, arrived = behind([out_mine, arrived], pg0)
+    layer0 = layer_blocks(out_mine, arrived, sizes)
+    arrived0 = layer_step(layer0, sizes)
+    arrived = core_step(theirs1, sizes)
+    pg1, mine2, theirs2 = backward(1, layer0[1:])
+    mine1, arrived, *arrived0 = behind([mine1, arrived] + arrived0, pg1)
+    layer1 = layer_blocks(mine1, arrived, sizes)
+    arrived1 = layer_step(layer1, sizes)
+    arrived = core_step(theirs2, sizes)
 
     first_picks = picks(cs.side[:side_cut] + cs.above + cs.corner, cells[:half_cells])
     last_picks = picks(cs.side[side_cut:], cells[half_cells:])
-    zero, [full, *strips] = tied_call(
-        input_last_kernel, after,
-        [pg0, pg1, qkv_weight, nfirst, normed, rstd, grad, merged,
+    full, *strips = tied_call(
+        input_kernel, layer1[1:],
+        [pg0, pg1, qkv_weight, normed, rstd, grad, merged,
          first_picks, last_picks, picks(sum(g_strips, []), grps)],
-        [hbm] * 7 + [vmem] * 4, [wide] + [shape(*e) for e in extents], [vmem] * 4,
-        scratch_shapes=in_scratch + [
+        [hbm] * 6 + [vmem] * 4, [wide] + [shape(*e) for e in extents], [vmem] * 4,
+        scratch_shapes=[
+            pltpu.VMEM((count, 3 * channels), BF16),
+            pltpu.VMEM(qkv_weight.shape, BF16),
             pltpu.VMEM((count, channels), BF16),
             pltpu.VMEM((count, channels), BF16),
             pltpu.VMEM((count, LANES), F32),
             pltpu.VMEM((count, channels), BF16),
-            in_sems,
-            pltpu.SemaphoreType.DMA((4,)),
+            pltpu.SemaphoreType.DMA((3 * halves + channels // TILE,)),
+            pltpu.SemaphoreType.DMA((3,)),
         ],
-        name="input_last", **settings(9, 36),
+        name="input_backward", **settings(13, 40),
     )
-    first_sum.zero = last_sum.zero = out_sum.zero = zero
+    mine2, arrived = behind([mine2, arrived], full)
+    layer2 = layer_blocks(mine2, arrived, sizes)
+    arrived2 = layer_step(layer2, sizes)
+    arrived1 = behind(arrived1, layer2[1])
     strips = sent_strips(strips, sizes, -1)
 
-    first_part = first_sum.rest()
-    last_part = last_sum.rest()
-    out_weight_grad = out_sum.rest()
+    kept = jnp.concatenate([layer0[0], layer1[0]], axis=1)
+    joined = [jnp.concatenate(pair, axis=1) for pair in zip(arrived0, arrived1)]
+    column1 = column_blocks(kept, joined, sizes)
+    column2 = column_blocks(layer2[0], arrived2, sizes)
+    part1 = finished(column1[0], column_step(column1, sizes))
+    part2 = finished(column2[0], column_step(column2, sizes))
+    out_weight_grad = part1[:, :channels]
+    part1 = part1[:, channels:]
 
     got = [Strips.sent(s, *t) for s, t in zip((cs.side, cs.above, cs.corner), to)]
     g_got = sum((Strips.sent(s, *t) for s, t in zip(g_strips, g_to)), [])
-    tokens_grad, merged = pl.pallas_call(
-        unpack_kernel,
-        out_shape=[wide, shape(groups, merged_width)],
-        in_specs=[vmem] * 9, out_specs=[vmem] * 2,
+    tokens_grad, merged = tied_call(
+        unpack_kernel, layer2[1:] + column1[1:],
+        [
+            full, merged, *strips,
+            picks(box(levels, range(SHIFT, 2 * SHIFT), own_cols), cells[:half_cells] + got[0][:side_cut]),
+            picks(box(levels, range(2 * SHIFT, lat_rows), own_cols), cells[half_cells:] + got[0][side_cut:]),
+            picks(box(levels, range(lat_rows, lat_rows + SHIFT), own_cols), got[1] + got[2]),
+            picks(g_own, grps + g_got),
+        ],
+        [vmem] * 9, [wide, shape(groups, merged_width)], [vmem] * 2,
         name="unpack_strips", **settings(2, 24),
-    )(
-        full, merged, *strips,
-        picks(box(levels, range(SHIFT, 2 * SHIFT), own_cols), cells[:half_cells] + got[0][:side_cut]),
-        picks(box(levels, range(2 * SHIFT, lat_rows), own_cols), cells[half_cells:] + got[0][side_cut:]),
-        picks(box(levels, range(lat_rows, lat_rows + SHIFT), own_cols), got[1] + got[2]),
-        picks(g_own, grps + g_got),
     )
     merged = merged.reshape(levels, g_cols, g_rows, merged_width).transpose(0, 2, 1, 3)
 
     qkv_weight_grad = jnp.concatenate(
-        [part[:, i * width:(i + 1) * width] for i in range(3) for part in (first_part, last_part)],
+        [part[:, i * width:(i + 1) * width] for i in range(3) for part in (part1, part2)],
         axis=1,
     )
     return merged, tokens_grad.reshape(tokens.shape), qkv_weight_grad, out_weight_grad

time: 193 us -> 169 us (0.88)
  other arithmetic: 21.5 us -> 7.3 us
  waiting for transfers between devices: 45 us -> 33.5 us
  starting transfers between devices: 28.6 us -> 33.1 us
    convert_element_type x18 -> x1, other arithmetic: 18.1 us -> 0.31 us  [layer_blocks(): return [total[0]] + [t.astype(BF16) for t in total[1:]]]
    ppermute x21 -> x18, waiting for transfers between devices: 30.4 us -> 14.1 us  [exchange(): return lax.ppermute(block, ('lat', 'lon'), route)]
    ppermute x6, waiting for transfers between devices: 14.7 us -> 19.4 us  [sent(): return lax.ppermute(block, ('lat', 'lon'), route)]
    slice x10 -> x3, local copies, waits for them, and re-layouts: 3.13 us -> 0.72 us  [the longest x1 0.66 us: shards(): out_weight_grad = part1[:, :channels]]
    ppermute x21 -> x18, starting transfers between devices: 21 us -> 23.3 us  [exchange(): return lax.ppermute(block, ('lat', 'lon'), route)]
    ppermute x6, starting transfers between devices: 7.67 us -> 9.73 us  [sent(): return lax.ppermute(block, ('lat', 'lon'), route)]
    add x3 -> x4, other arithmetic: 2.67 us -> 4.62 us  [the longest x2 4.5 us: layer_blocks(): mine[i * rows:(i + 1) * rows].astype(F32)]
    unnamed x55 -> x51, local copies, waits for them, and re-layouts: 4.71 us -> 6.29 us
  transfers between devices with their start and end apart: 27 -> 24, of which waited for: 10 -> 9; matrix products, arithmetic and copies ran while one was open for 13% -> 5% of each run, Pallas kernels for 24% -> 27%
where the time goes in v7:
time: 169 us; the launch traced here: 168 us
  Pallas kernels  85 us (50%)
  waiting for transfers between devices  33.5 us (20%)
  starting transfers between devices  33.1 us (20%)
  local copies, waits for them, and re-layouts  8.37 us (5%)
  other arithmetic  7.3 us (4%)
    pallas_call x4, Pallas kernels, tied_call(): pl.pallas_call(body, out_shape=out_shape, in_specs=[pl.BlockSpec(memory_s...  45.4 us
    pallas_call x1, Pallas kernels, shards(): pl.pallas_call(forward_kernel, out_shape=[wide, shape(channels, count), s...  36.5 us
    ppermute x18, starting transfers between devices, exchange(): return lax.ppermute(block, ('lat', 'lon'), route)  23.3 us
    ppermute x6, waiting for transfers between devices, sent(): return lax.ppermute(block, ('lat', 'lon'), route)  19.4 us
    ppermute x18, waiting for transfers between devices, exchange(): return lax.ppermute(block, ('lat', 'lon'), route)  14.1 us
    ppermute x6, starting transfers between devices, sent(): return lax.ppermute(block, ('lat', 'lon'), route)  9.73 us
    unnamed x51, local copies, waits for them, and re-layouts  6.29 us
    add x2, other arithmetic, layer_blocks(): mine[i * rows:(i + 1) * rows].astype(F32)  4.5 us
  transfers between devices with their start and end apart: 24, of which 9 were waited for; matrix products, arithmetic and copies ran while one was open for 5% of the time, Pallas kernels for 27%

profile of v7, /device:TPU:0, one launch (start us, length us, event | category | flops | bytes accessed | tf_op | source)
XLA Modules:
  0.0 168.2 jit_solution(9843182329041293004)
XLA Ops:
  0.7 3.1 %pack_strips.1 = (bf16[128,1024]{1,0:T(8,128)(2,1)}, bf16[208,1024]{1,0:T(8,128)(2,1)}, bf16[48,1024]{1,0:T(8,128)(2,1)}) custom-call(bf16[768,1024]{1,0:T(8,128)(2,1)} %bitcast.9, bf16[192,1024]{1,0:T(8,128)(2,1)} %bitcast.11, bf16[288,768]{1,0:T(8,128)(2,1)} %constant.42.clone.pick_cells, bf16[96,192]{1,0:T(8,128)(2,1)} %constant.43.clone.pick_groups), custom_call_target="tpu_custom_call" | custom-call | flops 10000000000 | bytes 16777216 | tf_op jit(solution)/shard_map/pack_strips/pallas_call | solution.py:641
  3.8 2.5 %collective-permute-start.2 = (bf16[48,1024]{1,0:T(8,128)(2,1)}, bf16[48,1024]{1,0:T(8,128)(2,1)S(1)}, u32[]{:S(2)}, u32[]{:S(2)}) collective-permute-start(bf16[48,1024]{1,0:T(8,128)(2,1)} %get-tuple-element.43), channel_id=1, source_target_pairs={{0,9},{1,10},{2,11},{3,12},{4,13},{5,14},{6,15},{7,8},{8,17},{9,18... | collective-permute-start | bytes 294920 | tf_op jit(solution)/shard_map/ppermute | solution.py:507
  6.3 1.6 collective-permute-start
  7.9 1.6 collective-permute-start.1
  10.1 1.4 add.127.rowmap
  11.4 1.5 collective-permute-done.2.corner
  12.9 1.3 collective-permute-done.side
  14.2 7.6 %collective-permute-done.1.above = bf16[208,1024]{1,0:T(8,128)(2,1)S(1)} collective-permute-done((bf16[208,1024]{1,0:T(8,128)(2,1)}, bf16[208,1024]{1,0:T(8,128)(2,1)S(1)}, u32[]{:S(2)}, u32[]{:S(2)}) %collective-permute-start.1) | collective-permute-done | bytes 426016 | tf_op jit(solution)/shard_map/ppermute | solution.py:507
  22.6 36.5 %block_forward.1 = (bf16[768,1024]{1,0:T(8,128)(2,1)}, bf16[1024,768]{1,0:T(8,128)(2,1)}, bf16[768,3072]{1,0:T(8,128)(2,1)}, bf16[768,1024]{1,0:T(8,128)(2,1)}, ...) custom-call(s32[1]{0:T(128)} %bitcast.edge.refs_0_.refs_3_, ...), custom_call_target="tpu_custom_call" | custom-call | flops 299999985664 | bytes 16777216 | tf_op jit(solution)/shard_map/block_forward/pallas_call | solution.py:655
  59.2 1.4 copy-done.12
  60.6 14.2 %attention_backward.2 = (bf16[768,1536]{1,0:T(8,128)(2,1)}, bf16[512,1536]{1,0:T(8,128)(2,1)S(1)}, bf16[512,1536]{1,0:T(8,128)(2,1)}) custom-call(s32[1]{0:T(128)} %bitcast.edge.refs_0_.refs_3_, bf16[768,3072]{1,0:T(8,128)(2,1)} %get-tuple-element.46.refs_1_.refs_4_, bf16[768,1024]{1,0:T(8,128)(2,1)S(1)} %copy-done.12, ...), custom_call_target="tpu_custom_call" | custom-call | flops 149999992832 | bytes 16777216 | tf_op jit(solution)/shard_map/attention_backward/pallas_call | solution.py:587
  75.3 2.6 %convert_add_fusion.2 = (f32[128,1024]{1,0:T(8,128)}, bf16[128,1024]{1,0:T(8,128)(2,1)}, bf16[128,1024]{1,0:T(8,128)(2,1)}, bf16[128,1024]{1,0:T(8,128)(2,1)}) fusion(bf16[512,1024]{1,0:T(8,128)(2,1)} %collective-permute-done.3, bf16[512,1024]{1,0:T(8,128)(2,1)S(1)} %copy-done.16), kind=kLoop, calls=%fused_computation.11 | loop fusion | flops 1966080 | bytes 3407872 | tf_op jit(solution)/shard_map/add | solution.py:547
  78.0 1.6 collective-permute-start.8
  79.5 1.4 collective-permute-start.7
  81.4 14.0 %attention_backward.3 = (bf16[768,1536]{1,0:T(8,128)(2,1)}, bf16[512,1536]{1,0:T(8,128)(2,1)S(1)}, bf16[512,1536]{1,0:T(8,128)(2,1)S(1)}) custom-call(bf16[128,1024]{1,0:T(8,128)(2,1)} %get-tuple-element.94.refs_0_, bf16[128,1024]{1,0:T(8,128)(2,1)} %get-tuple-element.93.refs_1_, bf16[128,1024]{1,0:T(8,128)(2,1)} %get-tuple-element.92.refs_2_, ...), custom_call_target="tpu_custom_call" | custom-call | flops 149999992832 | bytes 16777216 | tf_op jit(solution)/shard_map/attention_backward/pallas_call | solution.py:587
  95.6 1.9 %convert_add_fusion.1 = (f32[128,1536]{1,0:T(8,128)S(1)}, bf16[128,1536]{1,0:T(8,128)(2,1)S(1)}, bf16[128,1536]{1,0:T(8,128)(2,1)S(1)}, bf16[128,1536]{1,0:T(8,128)(2,1)S(1)}) fusion(bf16[512,1536]{1,0:T(8,128)(2,1)} %collective-permute-done.5, bf16[512,1536]{1,0:T(8,128)(2,1)S(1)} %get-tuple-element.58), kind=kLoop, calls=%fused_computation.4 | loop fusion | flops 2949120 | bytes 5111808 | tf_op jit(solution)/shard_map/add | solution.py:547
  97.5 1.7 collective-permute-start.11
  99.1 1.4 collective-permute-start.10
  101.1 1.7 copy-done.9
  102.8 1.4 copy-done.11
  104.2 15.1 %input_backward.1 = (bf16[768,1024]{1,0:T(8,128)(2,1)S(1)}, bf16[128,1024]{1,0:T(8,128)(2,1)S(1)}, bf16[208,1024]{1,0:T(8,128)(2,1)S(1)}, bf16[48,1024]{1,0:T(8,128)(2,1)S(1)}) custom-call(bf16[128,1536]{1,0:T(8,128)(2,1)S(1)} %get-tuple-element.87.refs_0_, bf16[128,1536]{1,0:T(8,128)(2,1)S(1)} %get-tuple-element.86.refs_1_, ...), custom_call_target="tpu_custom_call" | custom-call | flops 130000003072 | bytes 16777216 | tf_op jit(solution)/shard_map/input_backward/pallas_call | solution.py:587
  119.3 2.5 %collective-permute-start.14 = (bf16[48,1024]{1,0:T(8,128)(2,1)S(1)}, bf16[48,1024]{1,0:T(8,128)(2,1)S(1)}, u32[]{:S(2)}, u32[]{:S(2)}) collective-permute-start(bf16[48,1024]{1,0:T(8,128)(2,1)S(1)} %get-tuple-element.75), channel_id=1, source_target_pairs={{0,31},{1,24},{2,25},{3,26},{4,27},{5,28},{6,29},{7,30},{8,7},{9,0... | collective-permute-start | bytes 294920 | tf_op jit(solution)/shard_map/ppermute | solution.py:507
  123.9 1.5 fusion.7
  126.0 2.4 %collective-permute-start.16 = (bf16[32,2560]{1,0:T(8,128)(2,1)S(1)}, bf16[32,2560]{1,0:T(8,128)(2,1)S(1)}, u32[]{:S(2)}, u32[]{:S(2)}) collective-permute-start(bf16[32,2560]{1,0:T(8,128)(2,1)S(1)} %get-tuple-element.96.refs_4_), channel_id=1, source_target_pairs={{0,16},{1,17},{2,18},{3,19},{4,20},{5,21},{6,22},{7,23},{8,24},{9,... | collective-permute-start | bytes 491528 | tf_op jit(solution)/shard_map/ppermute | solution.py:536
  128.4 1.5 collective-permute-start.15
  130.5 9.0 %collective-permute-done.13.refs_9_ = bf16[208,1024]{1,0:T(8,128)(2,1)S(1)} collective-permute-done((bf16[208,1024]{1,0:T(8,128)(2,1)S(1)}, bf16[208,1024]{1,0:T(8,128)(2,1)S(1)}, u32[]{:S(2)}, u32[]{:S(2)}) %collective-permute-start.13) | collective-permute-done | bytes 426016 | tf_op jit(solution)/shard_map/ppermute | solution.py:507
  139.8 2.2 %unpack_strips.1 = (bf16[768,1024]{1,0:T(8,128)(2,1)}, bf16[192,1024]{1,0:T(8,128)(2,1)}) custom-call(bf16[128,1536]{1,0:T(8,128)(2,1)S(1)} %get-tuple-element.90.refs_0_, bf16[128,1536]{1,0:T(8,128)(2,1)S(1)} %get-tuple-element.89.refs_1_, bf16[128,1536]{1,0:T(8,128)(2,1)S(1)} %get-tuple-element.88.refs_2_, bf16[32,2560]{1,0:T(8,128)(2,1)S(1)} %get-tuple-element.97.refs_3_, ...), custom_call_target="tpu_custom_call" | custom-call | flops 20000000000 | bytes 16777216 | tf_op jit(solution)/shard_map/unpack_strips/pallas_call | solution.py:587
  142.5 5.2 %collective-permute-done.16 = bf16[32,2560]{1,0:T(8,128)(2,1)S(1)} collective-permute-done((bf16[32,2560]{1,0:T(8,128)(2,1)S(1)}, bf16[32,2560]{1,0:T(8,128)(2,1)S(1)}, u32[]{:S(2)}, u32[]{:S(2)}) %collective-permute-start.16) | collective-permute-done | bytes 163872 | tf_op jit(solution)/shard_map/ppermute | solution.py:536
  150.1 6.4 %collective-permute-start.21 = (bf16[32,1536]{1,0:T(8,128)(2,1)S(1)}, bf16[32,1536]{1,0:T(8,128)(2,1)S(1)}, u32[]{:S(2)}, u32[]{:S(2)}) collective-permute-start(bf16[32,1536]{1,0:T(8,128)(2,1)S(1)} %get-tuple-element.98), channel_id=1, source_target_pairs={{0,8},{1,9},{2,10},{3,11},{4,12},{5,13},{6,14},{7,15},{8,0},{9,1},... | collective-permute-start | bytes 294920 | tf_op jit(solution)/shard_map/ppermute | solution.py:536
  156.5 3.4 %collective-permute-start.23 = (bf16[32,1536]{1,0:T(8,128)(2,1)S(1)}, bf16[32,1536]{1,0:T(8,128)(2,1)S(1)}, u32[]{:S(2)}, u32[]{:S(2)}) collective-permute-start(bf16[32,1536]{1,0:T(8,128)(2,1)S(1)} %get-tuple-element.99), channel_id=1, source_target_pairs={{0,24},{1,25},{2,26},{3,27},{4,28},{5,29},{6,30},{7,31},{8,16},{9,... | collective-permute-start | bytes 294920 | tf_op jit(solution)/shard_map/ppermute | solution.py:536
  160.5 4.2 %collective-permute-done.23 = bf16[32,1536]{1,0:T(8,128)(2,1)S(1)} collective-permute-done((bf16[32,1536]{1,0:T(8,128)(2,1)S(1)}, bf16[32,1536]{1,0:T(8,128)(2,1)S(1)}, u32[]{:S(2)}, u32[]{:S(2)}) %collective-permute-start.23) | collective-permute-done | bytes 98336 | tf_op jit(solution)/shard_map/ppermute | solution.py:536
  164.7 2.6 %collective-permute-done.22 = bf16[32,1536]{1,0:T(8,128)(2,1)S(1)} collective-permute-done((bf16[32,1536]{1,0:T(8,128)(2,1)S(1)}, bf16[32,1536]{1,0:T(8,128)(2,1)S(1)}, u32[]{:S(2)}, u32[]{:S(2)}) %collective-permute-start.22) | collective-permute-done | bytes 98336 | tf_op jit(solution)/shard_map/ppermute | solution.py:536
  (87 shorter events, 11.0 us)
Async XLA Ops:
  0.6 8.8 %copy-start.18 = (s32[32]{0:T(128)S(1)}, s32[32]{0:T(128)}, u32[]{:S(2)}) copy-start(s32[32]{0:T(128)} %constant.48.clone) | copy-start | bytes 388
  0.6 8.8 %copy-start.19 = (s32[32]{0:T(128)S(1)}, s32[32]{0:T(128)}, u32[]{:S(2)}) copy-start(s32[32]{0:T(128)} %constant.47.clone) | copy-start | bytes 388
  3.8 9.1 %collective-permute-start.2 = (bf16[48,1024]{1,0:T(8,128)(2,1)}, bf16[48,1024]{1,0:T(8,128)(2,1)S(1)}, u32[]{:S(2)}, u32[]{:S(2)}) collective-permute-start(bf16[48,1024]{1,0:T(8,128)(2,1)} %get-tuple-element.43), channel_id=1, source_target_pairs={{0,9},{1,10},{2,11},{3,12},{4,13},{5,14},{6,15},{7,8},{8,17},{9,18... | collective-permute-start | bytes 294920 | tf_op jit(solution)/shard_map/ppermute | solution.py:507
  6.3 8.0 %collective-permute-start = (bf16[128,1024]{1,0:T(8,128)(2,1)}, bf16[128,1024]{1,0:T(8,128)(2,1)S(1)}, u32[]{:S(2)}, u32[]{:S(2)}) collective-permute-start(bf16[128,1024]{1,0:T(8,128)(2,1)} %get-tuple-element.41), channel_id=1, source_target_pairs={{0,1},{1,2},{2,3},{3,4},{4,5},{5,6},{6,7},{7,0},{8,9},{9,10},{10,1... | collective-permute-start | bytes 786440 | tf_op jit(solution)/shard_map/ppermute | solution.py:507
  7.9 14.0 %collective-permute-start.1 = (bf16[208,1024]{1,0:T(8,128)(2,1)}, bf16[208,1024]{1,0:T(8,128)(2,1)S(1)}, u32[]{:S(2)}, u32[]{:S(2)}) collective-permute-start(bf16[208,1024]{1,0:T(8,128)(2,1)} %get-tuple-element.42), channel_id=1, source_target_pairs={{0,8},{1,9},{2,10},{3,11},{4,12},{5,13},{6,14},{7,15},{8,16},{9,17... | collective-permute-start | bytes 1277960 | tf_op jit(solution)/shard_map/ppermute | solution.py:507
  12.9 8.9 %copy-start.22 = (bf16[48,1024]{1,0:T(8,128)(2,1)}, bf16[48,1024]{1,0:T(8,128)(2,1)S(1)}, u32[]{:S(2)}) copy-start(bf16[48,1024]{1,0:T(8,128)(2,1)S(1)} %collective-permute-done.2.corner) | copy-start | bytes 294916
  59.1 16.2 %collective-permute-start.3 = (bf16[512,1024]{1,0:T(8,128)(2,1)}, bf16[512,1024]{1,0:T(8,128)(2,1)}, u32[]{:S(2)}, u32[]{:S(2)}) collective-permute-start(bf16[512,1024]{1,0:T(8,128)(2,1)} %get-tuple-element.45), channel_id=1, source_target_pairs={{0,1},{1,0},{2,3},{3,2},{4,5},{5,4},{6,7},{7,6},{8,9},{9,8},{10,11... | collective-permute-start | bytes 3145736 | tf_op jit(solution)/shard_map/ppermute | solution.py:536
  60.6 14.8 %copy-start.16 = (bf16[512,1024]{1,0:T(8,128)(2,1)S(1)}, bf16[512,1024]{1,0:T(8,128)(2,1)}, u32[]{:S(2)}) copy-start(bf16[512,1024]{1,0:T(8,128)(2,1)} %get-tuple-element.51) | copy-start | bytes 3145732
  74.8 20.8 %collective-permute-start.5 = (bf16[512,1536]{1,0:T(8,128)(2,1)}, bf16[512,1536]{1,0:T(8,128)(2,1)}, u32[]{:S(2)}, u32[]{:S(2)}) collective-permute-start(bf16[512,1536]{1,0:T(8,128)(2,1)} %get-tuple-element.56), channel_id=1, source_target_pairs={{0,1},{1,0},{2,3},{3,2},{4,5},{5,4},{6,7},{7,6},{8,9},{9,8},{10,11... | collective-permute-start | bytes 4718600 | tf_op jit(solution)/shard_map/ppermute | solution.py:536
  78.0 17.5 %collective-permute-start.8 = (bf16[128,1024]{1,0:T(8,128)(2,1)}, bf16[128,1024]{1,0:T(8,128)(2,1)}, u32[]{:S(2)}, u32[]{:S(2)}) collective-permute-start(bf16[128,1024]{1,0:T(8,128)(2,1)} %get-tuple-element.92.refs_2_), channel_id=1, source_target_pairs={{0,6},{1,7},{2,4},{3,5},{4,2},{5,3},{6,0},{7,1},{8,14},{9,15},{10,... | collective-permute-start | bytes 786440 | tf_op jit(solution)/shard_map/ppermute | solution.py:536
  79.5 16.0 %collective-permute-start.7 = (bf16[128,1024]{1,0:T(8,128)(2,1)}, bf16[128,1024]{1,0:T(8,128)(2,1)}, u32[]{:S(2)}, u32[]{:S(2)}) collective-permute-start(bf16[128,1024]{1,0:T(8,128)(2,1)} %get-tuple-element.93.refs_1_), channel_id=1, source_target_pairs={{0,4},{1,5},{2,6},{3,7},{4,0},{5,1},{6,2},{7,3},{8,12},{9,13},{10,... | collective-permute-start | bytes 786440 | tf_op jit(solution)/shard_map/ppermute | solution.py:536
  80.9 14.6 %collective-permute-start.6 = (bf16[128,1024]{1,0:T(8,128)(2,1)}, bf16[128,1024]{1,0:T(8,128)(2,1)}, u32[]{:S(2)}, u32[]{:S(2)}) collective-permute-start(bf16[128,1024]{1,0:T(8,128)(2,1)} %get-tuple-element.94.refs_0_), channel_id=1, source_target_pairs={{0,2},{1,3},{2,0},{3,1},{4,6},{5,7},{6,4},{7,5},{8,10},{9,11},{10,... | collective-permute-start | bytes 786440 | tf_op jit(solution)/shard_map/ppermute | solution.py:536
  95.4 26.4 %collective-permute-start.4 = (bf16[512,1536]{1,0:T(8,128)(2,1)S(1)}, bf16[512,1536]{1,0:T(8,128)(2,1)S(1)}, u32[]{:S(2)}, u32[]{:S(2)}) collective-permute-start(bf16[512,1536]{1,0:T(8,128)(2,1)S(1)} %get-tuple-element.54), channel_id=1, source_target_pairs={{0,1},{1,0},{2,3},{3,2},{4,5},{5,4},{6,7},{7,6},{8,9},{9,8},{10,11... | collective-permute-start | bytes 4718600 | tf_op jit(solution)/shard_map/ppermute | solution.py:536
  97.5 25.7 %collective-permute-start.11 = (bf16[128,1536]{1,0:T(8,128)(2,1)S(1)}, bf16[128,1536]{1,0:T(8,128)(2,1)S(1)}, u32[]{:S(2)}, u32[]{:S(2)}) collective-permute-start(bf16[128,1536]{1,0:T(8,128)(2,1)S(1)} %get-tuple-element.85.refs_2_), channel_id=1, source_target_pairs={{0,6},{1,7},{2,4},{3,5},{4,2},{5,3},{6,0},{7,1},{8,14},{9,15},{10,... | collective-permute-start | bytes 1179656 | tf_op jit(solution)/shard_map/ppermute | solution.py:536
  99.1 24.5 %collective-permute-start.10 = (bf16[128,1536]{1,0:T(8,128)(2,1)S(1)}, bf16[128,1536]{1,0:T(8,128)(2,1)S(1)}, u32[]{:S(2)}, u32[]{:S(2)}) collective-permute-start(bf16[128,1536]{1,0:T(8,128)(2,1)S(1)} %get-tuple-element.86.refs_1_), channel_id=1, source_target_pairs={{0,4},{1,5},{2,6},{3,7},{4,0},{5,1},{6,2},{7,3},{8,12},{9,13},{10,... | collective-permute-start | bytes 1179656 | tf_op jit(solution)/shard_map/ppermute | solution.py:536
  100.5 23.2 %collective-permute-start.9 = (bf16[128,1536]{1,0:T(8,128)(2,1)S(1)}, bf16[128,1536]{1,0:T(8,128)(2,1)S(1)}, u32[]{:S(2)}, u32[]{:S(2)}) collective-permute-start(bf16[128,1536]{1,0:T(8,128)(2,1)S(1)} %get-tuple-element.87.refs_0_), channel_id=1, source_target_pairs={{0,2},{1,3},{2,0},{3,1},{4,6},{5,7},{6,4},{7,5},{8,10},{9,11},{10,... | collective-permute-start | bytes 1179656 | tf_op jit(solution)/shard_map/ppermute | solution.py:536
  119.3 9.1 %collective-permute-start.14 = (bf16[48,1024]{1,0:T(8,128)(2,1)S(1)}, bf16[48,1024]{1,0:T(8,128)(2,1)S(1)}, u32[]{:S(2)}, u32[]{:S(2)}) collective-permute-start(bf16[48,1024]{1,0:T(8,128)(2,1)S(1)} %get-tuple-element.75), channel_id=1, source_target_pairs={{0,31},{1,24},{2,25},{3,26},{4,27},{5,28},{6,29},{7,30},{8,7},{9,0... | collective-permute-start | bytes 294920 | tf_op jit(solution)/shard_map/ppermute | solution.py:507
  121.8 8.1 %collective-permute-start.12 = (bf16[128,1024]{1,0:T(8,128)(2,1)S(1)}, bf16[128,1024]{1,0:T(8,128)(2,1)S(1)}, u32[]{:S(2)}, u32[]{:S(2)}) collective-permute-start(bf16[128,1024]{1,0:T(8,128)(2,1)S(1)} %get-tuple-element.73), channel_id=1, source_target_pairs={{0,7},{1,0},{2,1},{3,2},{4,3},{5,4},{6,5},{7,6},{8,15},{9,8},{10,9... | collective-permute-start | bytes 786440 | tf_op jit(solution)/shard_map/ppermute | solution.py:507
  123.2 16.3 %collective-permute-start.13 = (bf16[208,1024]{1,0:T(8,128)(2,1)S(1)}, bf16[208,1024]{1,0:T(8,128)(2,1)S(1)}, u32[]{:S(2)}, u32[]{:S(2)}) collective-permute-start(bf16[208,1024]{1,0:T(8,128)(2,1)S(1)} %get-tuple-element.74), channel_id=1, source_target_pairs={{0,24},{1,25},{2,26},{3,27},{4,28},{5,29},{6,30},{7,31},{8,0},{9,1... | collective-permute-start | bytes 1277960 | tf_op jit(solution)/shard_map/ppermute | solution.py:507
  123.9 15.9 %copy-start = (bf16[384,448]{1,0:T(8,128)(2,1)S(1)}, bf16[384,448]{1,0:T(8,128)(2,1)}, u32[]{:S(2)}) copy-start(bf16[384,448]{1,0:T(8,128)(2,1)} %constant.53.clone.refs_12_) | copy-start | bytes 1032196
  123.9 15.9 %copy-start.1 = (bf16[192,416]{1,0:T(8,128)(2,1)S(1)}, bf16[192,416]{1,0:T(8,128)(2,1)}, u32[]{:S(2)}) copy-start(bf16[192,416]{1,0:T(8,128)(2,1)} %constant.52.clone.refs_11_) | copy-start | bytes 479236
  123.9 15.9 %copy-start.3 = (bf16[192,288]{1,0:T(8,128)(2,1)S(1)}, bf16[192,288]{1,0:T(8,128)(2,1)}, u32[]{:S(2)}) copy-start(bf16[192,288]{1,0:T(8,128)(2,1)} %constant.55.clone.refs_14_) | copy-start | bytes 331780
  123.9 15.9 %copy-start.4 = (bf16[192,192]{1,0:T(8,128)(2,1)S(1)}, bf16[192,192]{1,0:T(8,128)(2,1)}, u32[]{:S(2)}) copy-start(bf16[192,192]{1,0:T(8,128)(2,1)} %constant.54.clone.refs_13_) | copy-start | bytes 221188
  125.5 16.5 %collective-permute-start.17 = (bf16[32,2560]{1,0:T(8,128)(2,1)S(1)}, bf16[32,2560]{1,0:T(8,128)(2,1)S(1)}, u32[]{:S(2)}, u32[]{:S(2)}) collective-permute-start(bf16[32,2560]{1,0:T(8,128)(2,1)S(1)} %get-tuple-element.95.refs_5_), channel_id=1, source_target_pairs={{0,24},{1,25},{2,26},{3,27},{4,28},{5,29},{6,30},{7,31},{8,16},{9,... | collective-permute-start | bytes 491528 | tf_op jit(solution)/shard_map/ppermute | solution.py:536
  126.0 21.7 %collective-permute-start.16 = (bf16[32,2560]{1,0:T(8,128)(2,1)S(1)}, bf16[32,2560]{1,0:T(8,128)(2,1)S(1)}, u32[]{:S(2)}, u32[]{:S(2)}) collective-permute-start(bf16[32,2560]{1,0:T(8,128)(2,1)S(1)} %get-tuple-element.96.refs_4_), channel_id=1, source_target_pairs={{0,16},{1,17},{2,18},{3,19},{4,20},{5,21},{6,22},{7,23},{8,24},{9,... | collective-permute-start | bytes 491528 | tf_op jit(solution)/shard_map/ppermute | solution.py:536
  128.4 19.3 %collective-permute-start.15 = (bf16[32,2560]{1,0:T(8,128)(2,1)S(1)}, bf16[32,2560]{1,0:T(8,128)(2,1)S(1)}, u32[]{:S(2)}, u32[]{:S(2)}) collective-permute-start(bf16[32,2560]{1,0:T(8,128)(2,1)S(1)} %get-tuple-element.97.refs_3_), channel_id=1, source_target_pairs={{0,8},{1,9},{2,10},{3,11},{4,12},{5,13},{6,14},{7,15},{8,0},{9,1},... | collective-permute-start | bytes 491528 | tf_op jit(solution)/shard_map/ppermute | solution.py:536
  129.9 17.9 %collective-permute-start.20 = (bf16[128,1536]{1,0:T(8,128)(2,1)S(1)}, bf16[128,1536]{1,0:T(8,128)(2,1)S(1)}, u32[]{:S(2)}, u32[]{:S(2)}) collective-permute-start(bf16[128,1536]{1,0:T(8,128)(2,1)S(1)} %get-tuple-element.88.refs_2_), channel_id=1, source_target_pairs={{0,6},{1,7},{2,4},{3,5},{4,2},{5,3},{6,0},{7,1},{8,14},{9,15},{10,... | collective-permute-start | bytes 1179656 | tf_op jit(solution)/shard_map/ppermute | solution.py:536
  139.5 9.4 %collective-permute-start.19 = (bf16[128,1536]{1,0:T(8,128)(2,1)S(1)}, bf16[128,1536]{1,0:T(8,128)(2,1)S(1)}, u32[]{:S(2)}, u32[]{:S(2)}) collective-permute-start(bf16[128,1536]{1,0:T(8,128)(2,1)S(1)} %get-tuple-element.89.refs_1_), channel_id=1, source_target_pairs={{0,4},{1,5},{2,6},{3,7},{4,0},{5,1},{6,2},{7,3},{8,12},{9,13},{10,... | collective-permute-start | bytes 1179656 | tf_op jit(solution)/shard_map/ppermute | solution.py:536
  142.0 7.8 %collective-permute-start.18 = (bf16[128,1536]{1,0:T(8,128)(2,1)S(1)}, bf16[128,1536]{1,0:T(8,128)(2,1)S(1)}, u32[]{:S(2)}, u32[]{:S(2)}) collective-permute-start(bf16[128,1536]{1,0:T(8,128)(2,1)S(1)} %get-tuple-element.90.refs_0_), channel_id=1, source_target_pairs={{0,2},{1,3},{2,0},{3,1},{4,6},{5,7},{6,4},{7,5},{8,10},{9,11},{10,... | collective-permute-start | bytes 1179656 | tf_op jit(solution)/shard_map/ppermute | solution.py:536
  150.1 10.5 %collective-permute-start.21 = (bf16[32,1536]{1,0:T(8,128)(2,1)S(1)}, bf16[32,1536]{1,0:T(8,128)(2,1)S(1)}, u32[]{:S(2)}, u32[]{:S(2)}) collective-permute-start(bf16[32,1536]{1,0:T(8,128)(2,1)S(1)} %get-tuple-element.98), channel_id=1, source_target_pairs={{0,8},{1,9},{2,10},{3,11},{4,12},{5,13},{6,14},{7,15},{8,0},{9,1},... | collective-permute-start | bytes 294920 | tf_op jit(solution)/shard_map/ppermute | solution.py:536
  156.5 8.3 %collective-permute-start.23 = (bf16[32,1536]{1,0:T(8,128)(2,1)S(1)}, bf16[32,1536]{1,0:T(8,128)(2,1)S(1)}, u32[]{:S(2)}, u32[]{:S(2)}) collective-permute-start(bf16[32,1536]{1,0:T(8,128)(2,1)S(1)} %get-tuple-element.99), channel_id=1, source_target_pairs={{0,24},{1,25},{2,26},{3,27},{4,28},{5,29},{6,30},{7,31},{8,16},{9,... | collective-permute-start | bytes 294920 | tf_op jit(solution)/shard_map/ppermute | solution.py:536
  159.8 7.5 %collective-permute-start.22 = (bf16[32,1536]{1,0:T(8,128)(2,1)S(1)}, bf16[32,1536]{1,0:T(8,128)(2,1)S(1)}, u32[]{:S(2)}, u32[]{:S(2)}) collective-permute-start(bf16[32,1536]{1,0:T(8,128)(2,1)S(1)} %get-tuple-element.100), channel_id=1, source_target_pairs={{0,16},{1,17},{2,18},{3,19},{4,20},{5,21},{6,22},{7,23},{8,24},{9,... | collective-permute-start | bytes 294920 | tf_op jit(solution)/shard_map/ppermute | solution.py:536
  (15 other events, 59.2 us)

commit v8 on v7

--- a/solution.py
+++ b/solution.py
@@ -119,9 +119,77 @@
     return list(zip(cells, groups))
 
 
+def normalized_window(x, rows, xw, normed, rstd):
+    xw[rows] = x.astype(BF16)
+    center = jnp.mean(x, axis=1, keepdims=True)
+    moved = x - center
+    scale = lax.rsqrt(jnp.mean(moved * moved, axis=1, keepdims=True) + EPSILON)
+    rstd[rows] = jnp.broadcast_to(scale, (x.shape[0], LANES))
+    normed[rows] = (moved * scale).astype(BF16)
+
+
+def attended(proj, rows, lanes, masks, factor, bias, mixture, inverse):
+    places = masks[0].shape[0]
+    q, k, v = (proj[rows, at] for at in lanes)
+    scores = dot(q, jnp.concatenate([k * m for m in masks], axis=0), NT)
+    parts = []
+    for h in range(4):
+        part = scores[:, h * places:(h + 1) * places] * factor
+        if bias is not None:
+            part = part + bias
+        part = part - jnp.max(part, axis=1, keepdims=True)
+        parts.append(jnp.exp2(part).astype(BF16))
+    values = jnp.concatenate([jnp.concatenate([v * m, m], axis=1) for m in masks], axis=0)
+    summed = dot(jnp.concatenate(parts, axis=1), values)
+    inv = 1.0 / summed[:, LANES:]
+    inverse[rows, lanes[0]] = inv
+    mixture[rows, lanes[0]] = (summed[:, :LANES] * inv).astype(BF16)
+
+
+def inner_kernel(
+    tokens, order, wqkv_h, xw, normed, rstd, mixture, inverse, proj, wqkv, in_sem,
+):
+    count, channels = xw.shape
+    places = 2 * WIN * WIN
+    tiles = wqkv.shape[1] // TILE
+
+    def load(n):
+        columns = aligned(n * TILE, TILE)
+        return pltpu.make_async_copy(wqkv_h.at[:, columns], wqkv.at[:, columns], in_sem.at[n])
+
+    for n in range(tiles):
+        load(n).start()
+    half = tokens.shape[0] // 2
+    line = half // (2 * WIN)
+    cut = SHIFT * line
+    source = jnp.concatenate(
+        [tokens[cut:cut + WIN * line], tokens[half + cut:half + cut + WIN * line]], axis=0
+    )
+    for w in range(count // places):
+        rows = slice(w * places, (w + 1) * places)
+        normalized_window(dot(order[rows, :source.shape[0]], source), rows, xw, normed, rstd)
+
+    @pl.loop(0, tiles)
+    def _(n):
+        load(n).wait()
+        columns = aligned(n * TILE, TILE)
+        proj[:, columns] = dot(normed[...], wqkv[:, columns]).astype(BF16)
+
+    masks = head_masks()
+    factor = score_scale(channels)
+
+    @pl.loop(0, channels // LANES // 2)
+    def _(g):
+        for i in range(2):
+            lanes = [aligned(j * channels + (2 * g + i) * LANES, LANES) for j in range(3)]
+            for w in range(count // places):
+                rows = slice(w * places, (w + 1) * places)
+                attended(proj, rows, lanes, masks, factor, None, mixture, inverse)
+
+
 def forward_kernel(
     edge, owner, tokens, merged_grad, side, above, corner, order, group, rowmap,
-    wqkv_h, wout_h, wm_h,
+    wqkv_h, wout_h, wm_h, xw_h, normed_in, rstd_h, mixture_h, inverse_h, proj_in,
     normed_h, normt_h, proj_h, dmr_h, dmm_h, grad_h, rstd, merged, out_mine, out_theirs,
     wqkv, wout, wm, source, xw, normed, normt, proj, mixture, inverse, subs, dsubs, cotangent,
     grad, dmr, dmm, turned, in_sem, out_sem,
@@ -139,7 +207,15 @@
         pltpu.make_async_copy(src, dst, in_sem.at[i])
         for i, (src, dst) in enumerate([(wqkv_h, wqkv), (wout_h, wout), (wm_h, wm)])
     ]
-    for load in loads:
+    outer = count - xw_h.shape[0]
+    ready = [
+        pltpu.make_async_copy(src, dst.at[pl.ds(outer, count - outer)], in_sem.at[3 + i])
+        for i, (src, dst) in enumerate(
+            [(xw_h, xw), (normed_in, normed), (rstd_h, rstd), (mixture_h, mixture),
+             (inverse_h, inverse), (proj_in, proj)]
+        )
+    ]
+    for load in loads + ready:
         load.start()
     stores = [
         pltpu.make_async_copy(src, dst, out_sem.at[i])
@@ -166,25 +242,22 @@
         if at < source.shape[1]:
             source[wi, at:] = jnp.zeros((source.shape[1] - at, channels), BF16)
 
-    @pl.loop(0, windows)
+    @pl.loop(0, outer // places)
     def _(w):
         rows = aligned(w * places, places)
-        x = dot(order[rows], source[w // per_row])
-        xw[rows] = x.astype(BF16)
-        center = jnp.mean(x, axis=1, keepdims=True)
-        moved = x - center
-        scale = lax.rsqrt(jnp.mean(moved * moved, axis=1, keepdims=True) + EPSILON)
-        rstd[rows] = jnp.broadcast_to(scale, (places, LANES))
-        normed[rows] = (moved * scale).astype(BF16)
-
-    stores[0].start()
+        normalized_window(dot(order[rows], source[w // per_row]), rows, xw, normed, rstd)
+
     loads[0].wait()
+    outer_rows = slice(0, outer)
 
     @pl.loop(0, wqkv.shape[1] // TILE)
     def _(n):
         columns = aligned(n * TILE, TILE)
-        proj[:, columns] = dot(normed[...], wqkv[:, columns]).astype(BF16)
-
+        proj[outer_rows, columns] = dot(normed[outer_rows], wqkv[:, columns]).astype(BF16)
+
+    for load in ready:
+        load.wait()
+    stores[0].start()
     stores[1].start()
 
     masks = head_masks()
@@ -201,27 +274,11 @@
 
     @pl.loop(0, steps)
     def _(g):
-        lanes = aligned(g * LANES, LANES)
-        key_lanes = aligned(channels + g * LANES, LANES)
-        value_lanes = aligned(2 * channels + g * LANES, LANES)
-        for w in range(windows):
+        lanes = [aligned(i * channels + g * LANES, LANES) for i in range(3)]
+        for w in range(outer // places):
             rows = slice(w * places, (w + 1) * places)
-            q, k, v = proj[rows, lanes], proj[rows, key_lanes], proj[rows, value_lanes]
-            scores = dot(q, jnp.concatenate([k * m for m in masks], axis=0), NT)
-            parts = []
-            for h in range(4):
-                part = scores[:, h * places:(h + 1) * places] * factor
-                if w < per_row:
-                    part = part + edge_bias
-                part = part - jnp.max(part, axis=1, keepdims=True)
-                parts.append(jnp.exp2(part).astype(BF16))
-            values = jnp.concatenate(
-                [jnp.concatenate([v * m, m], axis=1) for m in masks], axis=0
-            )
-            summed = dot(jnp.concatenate(parts, axis=1), values)
-            inv = 1.0 / summed[:, LANES:]
-            inverse[rows, lanes] = inv
-            mixture[rows, lanes] = (summed[:, :LANES] * inv).astype(BF16)
+            bias = edge_bias if w < per_row else None
+            attended(proj, rows, lanes, masks, factor, bias, mixture, inverse)
         for i in range(per_step):
             at = aligned((g * per_step + i) * TILE, TILE)
             dsubs[:, at] = dot(cotangent[...], wm[at], NT).astype(BF16)
@@ -567,6 +624,10 @@
     return [exchange(b, sizes, i, 0) for i, b in enumerate(blocks) if i]
 
 
+def pinned(value):
+    return pltpu.with_memory_space_constraint(value, pltpu.HBM)
+
+
 def behind(values, marker):
     *values, _ = lax.optimization_barrier((*values, marker))
     return values
@@ -638,13 +699,13 @@
     tokens_flat = tokens.reshape(count, channels)
     merged_grad_flat = merged_grad.transpose(0, 2, 1, 3).reshape(groups, merged_width)
     extents = [(n + g, channels) for n, g in strip_rows(None, None)]
-    strips = pl.pallas_call(
+    packed = pl.pallas_call(
         pack_kernel,
         out_shape=[shape(*e) for e in extents],
         in_specs=[vmem] * 4, out_specs=[vmem] * 3,
-        name="pack_strips", **settings(1),
-    )(tokens_flat, merged_grad_flat, picks(sent_cells, own), picks(sent_groups, g_own))
-    strips = sent_strips(strips, sizes, 1)
+        name="pack_strips", **settings(1, 24),
+    )(pinned(tokens_flat), pinned(merged_grad_flat), picks(sent_cells, own), picks(sent_groups, g_own))
+    strips = sent_strips(packed, sizes, 1)
 
     order = jnp.concatenate([picks(cells[:half_cells], held_top), picks(cells[half_cells:], held_low)])
     group = picks(grps, g_own + sum(g_strips, []))
@@ -652,6 +713,20 @@
     owner, rowmap = device_rows(channels, sizes)
 
     wide = shape(count, channels)
+    inner = 2 * 2 * WIN * WIN
+    ready = tied_call(
+        inner_kernel, packed,
+        [pinned(tokens_flat), order[count - inner:], pinned(qkv_weight)],
+        [vmem] * 2 + [hbm],
+        [shape(inner, channels), shape(inner, channels), shape(inner, LANES, dtype=F32),
+         shape(inner, channels), shape(inner, channels, dtype=F32), shape(inner, 3 * channels)],
+        [vmem] * 6,
+        scratch_shapes=[
+            pltpu.VMEM(qkv_weight.shape, BF16),
+            pltpu.SemaphoreType.DMA((3 * channels // TILE,)),
+        ],
+        name="inner_windows", **settings(9, 36),
+    )
     normed, normt, proj, dmr, dmm, grad, rstd, merged, out_mine, out_theirs = pl.pallas_call(
         forward_kernel,
         out_shape=[
@@ -659,7 +734,7 @@
             shape(count, LANES, dtype=F32), shape(groups, merged_width),
             shape(half, channels), shape(half, channels),
         ],
-        in_specs=[smem] * 2 + [vmem] * 8 + [hbm] * 3,
+        in_specs=[smem] * 2 + [vmem] * 8 + [hbm] * 9,
         out_specs=[hbm] * 6 + [vmem] * 4,
         scratch_shapes=[
             pltpu.VMEM(qkv_weight.shape, BF16),
@@ -679,12 +754,12 @@
             pltpu.VMEM((count, channels), BF16),
             pltpu.VMEM((count, channels), BF16),
             pltpu.VMEM((channels, count), BF16),
-            pltpu.SemaphoreType.DMA((3,)),
+            pltpu.SemaphoreType.DMA((9,)),
             pltpu.SemaphoreType.DMA((6,)),
         ],
         name="block_forward", **settings(30, 58),
     )(edge, owner, tokens_flat, merged_grad_flat, *strips, order, group, rowmap,
-      qkv_weight, out_weight, merge_weight)
+      qkv_weight, out_weight, merge_weight, *ready)
 
     halves = 2
     width = channels // halves
@@ -693,7 +768,7 @@
     def backward(index, after):
         return tied_call(
             functools.partial(backward_kernel, index), after,
-            [edge, proj, dmr, dmm, normt], [smem] + [hbm] * 4,
+            [edge, pinned(proj), pinned(dmr), pinned(dmm), pinned(normt)], [smem] + [hbm] * 4,
             [shape(count, 3 * width), shape(half, 3 * width), shape(half, 3 * width)], [hbm] * 3,
             scratch_shapes=[
                 pltpu.VMEM((5, count, width), BF16),
@@ -705,7 +780,7 @@
                 pltpu.SemaphoreType.DMA((1,)),
                 pltpu.SemaphoreType.DMA((steps, 3, 3)),
             ],
-            name="attention_backward", **settings(15, 48),
+            name="attention_backward", **settings(15, 32),
         )
 
     arrived = core_step(out_theirs, sizes)
@@ -724,7 +799,7 @@
     last_picks = picks(cs.side[side_cut:], cells[half_cells:])
     full, *strips = tied_call(
         input_kernel, layer1[1:],
-        [pg0, pg1, qkv_weight, normed, rstd, grad, merged,
+        [pg0, pg1, qkv_weight, pinned(normed), pinned(rstd), pinned(grad), merged,
          first_picks, last_picks, picks(sum(g_strips, []), grps)],
         [hbm] * 6 + [vmem] * 4, [wide] + [shape(*e) for e in extents], [vmem] * 4,
         scratch_shapes=[
@@ -742,18 +817,12 @@
     mine2, arrived = behind([mine2, arrived], full)
     layer2 = layer_blocks(mine2, arrived, sizes)
     arrived2 = layer_step(layer2, sizes)
+    strips = sent_strips(strips, sizes, -1)
+
     arrived1 = behind(arrived1, layer2[1])
-    strips = sent_strips(strips, sizes, -1)
-
     kept = jnp.concatenate([layer0[0], layer1[0]], axis=1)
     joined = [jnp.concatenate(pair, axis=1) for pair in zip(arrived0, arrived1)]
     column1 = column_blocks(kept, joined, sizes)
-    column2 = column_blocks(layer2[0], arrived2, sizes)
-    part1 = finished(column1[0], column_step(column1, sizes))
-    part2 = finished(column2[0], column_step(column2, sizes))
-    out_weight_grad = part1[:, :channels]
-    part1 = part1[:, channels:]
-
     got = [Strips.sent(s, *t) for s, t in zip((cs.side, cs.above, cs.corner), to)]
     g_got = sum((Strips.sent(s, *t) for s, t in zip(g_strips, g_to)), [])
     tokens_grad, merged = tied_call(
@@ -766,8 +835,16 @@
             picks(g_own, grps + g_got),
         ],
         [vmem] * 9, [wide, shape(groups, merged_width)], [vmem] * 2,
-        name="unpack_strips", **settings(2, 24),
+        name="unpack_strips", **settings(20, 24),
     )
+    arrived2 = behind(arrived2, tokens_grad)
+    column1[-1:] = behind(column1[-1:], tokens_grad)
+    column2 = column_blocks(layer2[0], arrived2, sizes)
+    part1 = finished(column1[0], column_step(column1, sizes))
+    part2 = finished(column2[0], column_step(column2, sizes))
+    out_weight_grad = part1[:, :channels]
+    part1 = part1[:, channels:]
+
     merged = merged.reshape(levels, g_cols, g_rows, merged_width).transpose(0, 2, 1, 3)
 
     qkv_weight_grad = jnp.concatenate(

time: 169 us -> 173 us (1.024)
  Pallas kernels: 85 us -> 89.3 us
  waiting for transfers between devices: 33.5 us -> 29.7 us
  other arithmetic: 7.3 us -> 10.7 us
  starting transfers between devices: 33.1 us -> 30.3 us
  local copies, waits for them, and re-layouts: 8.37 us -> 11.1 us
    ppermute x6, waiting for transfers between devices: 19.4 us -> 8.16 us  [sent(): return lax.ppermute(block, ('lat', 'lon'), route)]
    pallas_call x4 -> x5, Pallas kernels: 45.4 us -> 53.9 us  [tied_call(): pl.pallas_call(body, out_shape=out_shape, in_specs=[pl.BlockSpec(memory_s...]
    ppermute x18, waiting for transfers between devices: 14.1 us -> 21.6 us  [exchange(): return lax.ppermute(block, ('lat', 'lon'), route)]
    pallas_call x1, Pallas kernels: 36.5 us -> 33.2 us  [shards(): pl.pallas_call(forward_kernel, out_shape=[wide, shape(channels, count), s...]
    unnamed x51 -> x59, local copies, waits for them, and re-layouts: 6.29 us -> 9.01 us
    ppermute x18, starting transfers between devices: 23.3 us -> 20.8 us  [exchange(): return lax.ppermute(block, ('lat', 'lon'), route)]
    another operation x2, other arithmetic: 1.77 us -> 3.94 us
  transfers between devices with their start and end apart: 24 -> 24, of which waited for: 9 -> 8; matrix products, arithmetic and copies ran while one was open for 5% -> 7% of each run, Pallas kernels for 27% -> 30%
where the time goes in v8:
time: 173 us; the launch traced here: 172 us
  Pallas kernels  89.3 us (52%)
  starting transfers between devices  30.3 us (18%)
  waiting for transfers between devices  29.7 us (17%)
  local copies, waits for them, and re-layouts  11.1 us (6%)
  other arithmetic  10.7 us (6%)
    pallas_call x5, Pallas kernels, tied_call(): pl.pallas_call(body, out_shape=out_shape, in_specs=[pl.BlockSpec(memory_s...  53.9 us
    pallas_call x1, Pallas kernels, shards(): pl.pallas_call(forward_kernel, out_shape=[wide, shape(channels, count), s...  33.2 us
    ppermute x18, waiting for transfers between devices, exchange(): return lax.ppermute(block, ('lat', 'lon'), route)  21.6 us
    ppermute x18, starting transfers between devices, exchange(): return lax.ppermute(block, ('lat', 'lon'), route)  20.8 us
    ppermute x6, starting transfers between devices, sent(): return lax.ppermute(block, ('lat', 'lon'), route)  9.53 us
    unnamed x59, local copies, waits for them, and re-layouts  9.01 us
    ppermute x6, waiting for transfers between devices, sent(): return lax.ppermute(block, ('lat', 'lon'), route)  8.16 us
    add x2, other arithmetic, layer_blocks(): mine[i * rows:(i + 1) * rows].astype(F32)  4.74 us
  transfers between devices with their start and end apart: 24, of which 8 were waited for; matrix products, arithmetic and copies ran while one was open for 7% of the time, Pallas kernels for 30%

profile of v8, /device:TPU:0, one launch (start us, length us, event | category | flops | bytes accessed | tf_op | source)
XLA Modules:
  0.0 172.1 jit_solution(7198277614065579429)
XLA Ops:
  2.4 2.2 %pack_strips.1 = (bf16[128,1024]{1,0:T(8,128)(2,1)S(1)}, bf16[208,1024]{1,0:T(8,128)(2,1)S(1)}, bf16[48,1024]{1,0:T(8,128)(2,1)S(1)}) custom-call(bf16[768,1024]{1,0:T(8,128)(2,1)} %bitcast.9, bf16[192,1024]{1,0:T(8,128)(2,1)} %bitcast.12, bf16[288,768]{1,0:T(8,128)(2,1)S(1)} %copy-done.1, bf16[96,192]{1,0:T(8,128)(2,1)S(1)} %copy-done.10), custom_call_target="tpu_custom_call" | custom-call | flops 10000000000 | bytes 16777216 | tf_op jit(solution)/shard_map/pack_strips/pallas_call | solution.py:702
  4.6 2.5 %collective-permute-start.2 = (bf16[48,1024]{1,0:T(8,128)(2,1)S(1)}, bf16[48,1024]{1,0:T(8,128)(2,1)S(1)}, u32[]{:S(2)}, u32[]{:S(2)}) collective-permute-start(bf16[48,1024]{1,0:T(8,128)(2,1)S(1)} %get-tuple-element.53.refs_2_), channel_id=1, source_target_pairs={{0,9},{1,10},{2,11},{3,12},{4,13},{5,14},{6,15},{7,8},{8,17},{9,18... | collective-permute-start | bytes 294920 | tf_op jit(solution)/shard_map/ppermute | solution.py:564
  7.2 1.6 collective-permute-start
  8.8 1.6 collective-permute-start.1
  10.3 9.0 %inner_windows.1 = (bf16[256,1024]{1,0:T(8,128)(2,1)S(1)}, bf16[256,1024]{1,0:T(8,128)(2,1)S(1)}, f32[256,128]{1,0:T(8,128)S(1)}, bf16[256,1024]{1,0:T(8,128)(2,...) custom-call(bf16[128,1024]{1,0:T(8,128)(2,1)S(1)} %get-tuple-element.51.refs_0_, ...), custom_call_target="tpu_custom_call" | custom-call | flops 89999998976 | bytes 16777216 | tf_op jit(solution)/shard_map/inner_windows/pallas_call | solution.py:648
  27.5 33.2 %block_forward.1 = (bf16[768,1024]{1,0:T(8,128)(2,1)}, bf16[1024,768]{1,0:T(8,128)(2,1)}, bf16[768,3072]{1,0:T(8,128)(2,1)}, bf16[768,1024]{1,0:T(8,128)(2,1)}, ...) custom-call(s32[1]{0:T(128)} %bitcast.edge.refs_0_.refs_3_, ...), custom_call_target="tpu_custom_call" | custom-call | flops 299999985664 | bytes 16777216 | tf_op jit(solution)/shard_map/block_forward/pallas_call | solution.py:730
  60.8 14.1 %attention_backward.2 = (bf16[768,1536]{1,0:T(8,128)(2,1)S(1)}, bf16[512,1536]{1,0:T(8,128)(2,1)S(1)}, bf16[512,1536]{1,0:T(8,128)(2,1)}) custom-call(s32[1]{0:T(128)} %bitcast.edge.refs_0_.refs_3_, bf16[768,3072]{1,0:T(8,128)(2,1)} %get-tuple-element.62.refs_1_.refs_4_, bf16[768,1024]{1,0:T(8,128)(2,1)} %get-tuple-element.63.refs_2_.refs_5_, ...), custom_call_target="tpu_custom_call" | custom-call | flops 149999992832 | bytes 16777216 | tf_op jit(solution)/shard_map/attention_backward/pallas_call | solution.py:648
  75.4 2.5 %convert_add_fusion.2 = (f32[128,1024]{1,0:T(8,128)}, bf16[128,1024]{1,0:T(8,128)(2,1)}, bf16[128,1024]{1,0:T(8,128)(2,1)}, bf16[128,1024]{1,0:T(8,128)(2,1)}) fusion(bf16[512,1024]{1,0:T(8,128)(2,1)} %collective-permute-done.3, bf16[512,1024]{1,0:T(8,128)(2,1)S(1)} %copy-done.20), kind=kLoop, calls=%fused_computation.11 | loop fusion | flops 1966080 | bytes 3407872 | tf_op jit(solution)/shard_map/add | solution.py:604
  77.9 1.4 collective-permute-start.8
  79.4 1.5 collective-permute-start.7
  81.4 13.4 %attention_backward.3 = (bf16[768,1536]{1,0:T(8,128)(2,1)S(1)}, bf16[512,1536]{1,0:T(8,128)(2,1)S(1)}, bf16[512,1536]{1,0:T(8,128)(2,1)S(1)}) custom-call(bf16[128,1024]{1,0:T(8,128)(2,1)} %get-tuple-element.114.refs_0_, bf16[128,1024]{1,0:T(8,128)(2,1)} %get-tuple-element.113.refs_1_, bf16[128,1024]{1,0:T(8,128)(2,1)} %get-tuple-element.112.refs_2_, ...), custom_call_target="tpu_custom_call" | custom-call | flops 149999992832 | bytes 16777216 | tf_op jit(solution)/shard_map/attention_backward/pallas_call | solution.py:648
  95.0 2.2 %convert_add_fusion.1 = (f32[128,1536]{1,0:T(8,128)S(1)}, bf16[128,1536]{1,0:T(8,128)(2,1)S(1)}, bf16[128,1536]{1,0:T(8,128)(2,1)S(1)}, bf16[128,1536]{1,0:T(8,128)(2,1)S(1)}) fusion(bf16[512,1536]{1,0:T(8,128)(2,1)} %collective-permute-done.5, bf16[512,1536]{1,0:T(8,128)(2,1)S(1)} %get-tuple-element.74), kind=kLoop, calls=%fused_computation.4 | loop fusion | flops 2949120 | bytes 5111808 | tf_op jit(solution)/shard_map/add | solution.py:604
  97.2 1.5 collective-permute-start.11
  98.7 1.5 collective-permute-start.10
  100.8 15.3 %input_backward.1 = (bf16[768,1024]{1,0:T(8,128)(2,1)S(1)}, bf16[128,1024]{1,0:T(8,128)(2,1)S(1)}, bf16[208,1024]{1,0:T(8,128)(2,1)S(1)}, bf16[48,1024]{1,0:T(8,128)(2,1)S(1)}) custom-call(bf16[128,1536]{1,0:T(8,128)(2,1)S(1)} %get-tuple-element.107.refs_0_, bf16[128,1536]{1,0:T(8,128)(2,1)S(1)} %get-tuple-element.106.refs_1_, ...), custom_call_target="tpu_custom_call" | custom-call | flops 130000003072 | bytes 16777216 | tf_op jit(solution)/shard_map/input_backward/pallas_call | solution.py:648
  116.1 2.0 %collective-permute-start.14 = (bf16[48,1024]{1,0:T(8,128)(2,1)S(1)}, bf16[48,1024]{1,0:T(8,128)(2,1)S(1)}, u32[]{:S(2)}, u32[]{:S(2)}) collective-permute-start(bf16[48,1024]{1,0:T(8,128)(2,1)S(1)} %get-tuple-element.91), channel_id=1, source_target_pairs={{0,31},{1,24},{2,25},{3,26},{4,27},{5,28},{6,29},{7,30},{8,7},{9,0... | collective-permute-start | bytes 294920 | tf_op jit(solution)/shard_map/ppermute | solution.py:564
  118.1 1.5 collective-permute-start.12
  120.6 2.6 %fusion.7 = (bf16[128,2560]{1,0:T(8,128)(2,1)S(1)}, f32[128,2560]{1,0:T(8,128)}) fusion(bf16[128,1536]{1,0:T(8,128)(2,1)S(1)} %collective-permute-done.11, bf16[128,1024]{1,0:T(8,128)(2,1)} %collective-permute-done.8, bf16[128,1536]{1,0:T(8,128)(2,1)S(1)} %collective-permute-done.10, bf16[128,1024]{1,0:T(8,128)(2,1)} %collective-permute-done.7, ...), kind=kLoop, calls=%fused_computation.31 | loop fusion | flops 5570560 | bytes 5242880 | tf_op jit(solution)/shard_map/convert.6
  123.4 7.9 %collective-permute-done.13.refs_9_ = bf16[208,1024]{1,0:T(8,128)(2,1)S(1)} collective-permute-done((bf16[208,1024]{1,0:T(8,128)(2,1)S(1)}, bf16[208,1024]{1,0:T(8,128)(2,1)S(1)}, u32[]{:S(2)}, u32[]{:S(2)}) %collective-permute-start.13) | collective-permute-done | bytes 426016 | tf_op jit(solution)/shard_map/ppermute | solution.py:564
  131.4 2.1 %unpack_strips.1 = (bf16[768,1024]{1,0:T(8,128)(2,1)}, bf16[192,1024]{1,0:T(8,128)(2,1)}) custom-call(bf16[128,1536]{1,0:T(8,128)(2,1)S(1)} %get-tuple-element.110.refs_0_, bf16[128,1536]{1,0:T(8,128)(2,1)S(1)} %get-tuple-element.109.refs_1_, bf16[128,1536]{1,0:T(8,128)(2,1)S(1)} %get-tuple-element.108.refs_2_, ...), custom_call_target="tpu_custom_call" | custom-call | flops 199999995904 | bytes 16777216 | tf_op jit(solution)/shard_map/unpack_strips/pallas_call | solution.py:648
  133.5 3.0 %collective-permute-start.17 = (bf16[32,2560]{1,0:T(8,128)(2,1)S(1)}, bf16[32,2560]{1,0:T(8,128)(2,1)S(1)}, u32[]{:S(2)}, u32[]{:S(2)}) collective-permute-start(bf16[32,2560]{1,0:T(8,128)(2,1)S(1)} %get-tuple-element.94.refs_5_), channel_id=1, source_target_pairs={{0,24},{1,25},{2,26},{3,27},{4,28},{5,29},{6,30},{7,31},{8,16},{9,... | collective-permute-start | bytes 491528 | tf_op jit(solution)/shard_map/ppermute | solution.py:593
  137.9 1.4 collective-permute-start.20
  139.4 1.5 collective-permute-start.19
  140.9 1.6 collective-permute-done.17
  142.5 1.5 collective-permute-start.18
  144.0 5.8 %collective-permute-done.16 = bf16[32,2560]{1,0:T(8,128)(2,1)S(1)} collective-permute-done((bf16[32,2560]{1,0:T(8,128)(2,1)S(1)}, bf16[32,2560]{1,0:T(8,128)(2,1)S(1)}, u32[]{:S(2)}, u32[]{:S(2)}) %collective-permute-start.16) | collective-permute-done | bytes 163872 | tf_op jit(solution)/shard_map/ppermute | solution.py:593
  150.9 5.8 %collective-permute-done.19 = bf16[128,1536]{1,0:T(8,128)(2,1)S(1)} collective-permute-done((bf16[128,1536]{1,0:T(8,128)(2,1)S(1)}, bf16[128,1536]{1,0:T(8,128)(2,1)S(1)}, u32[]{:S(2)}, u32[]{:S(2)}) %collective-permute-start.19) | collective-permute-done | bytes 393248 | tf_op jit(solution)/shard_map/ppermute | solution.py:593
  156.6 1.4 fusion.6
  158.0 1.5 collective-permute-start.21
  159.6 2.4 %collective-permute-start.23 = (bf16[32,1536]{1,0:T(8,128)(2,1)S(1)}, bf16[32,1536]{1,0:T(8,128)(2,1)S(1)}, u32[]{:S(2)}, u32[]{:S(2)}) collective-permute-start(bf16[32,1536]{1,0:T(8,128)(2,1)S(1)} %get-tuple-element.119), channel_id=1, source_target_pairs={{0,24},{1,25},{2,26},{3,27},{4,28},{5,29},{6,30},{7,31},{8,16},{9,... | collective-permute-start | bytes 294920 | tf_op jit(solution)/shard_map/ppermute | solution.py:593
  162.9 4.9 %collective-permute-done.23 = bf16[32,1536]{1,0:T(8,128)(2,1)S(1)} collective-permute-done((bf16[32,1536]{1,0:T(8,128)(2,1)S(1)}, bf16[32,1536]{1,0:T(8,128)(2,1)S(1)}, u32[]{:S(2)}, u32[]{:S(2)}) %collective-permute-start.23) | collective-permute-done | bytes 98336 | tf_op jit(solution)/shard_map/ppermute | solution.py:593
  167.7 3.5 %collective-permute-done.22 = bf16[32,1536]{1,0:T(8,128)(2,1)S(1)} collective-permute-done((bf16[32,1536]{1,0:T(8,128)(2,1)S(1)}, bf16[32,1536]{1,0:T(8,128)(2,1)S(1)}, u32[]{:S(2)}, u32[]{:S(2)}) %collective-permute-start.22) | collective-permute-done | bytes 98336 | tf_op jit(solution)/shard_map/ppermute | solution.py:593
  (96 shorter events, 17.3 us)
Async XLA Ops:
  4.6 21.9 %collective-permute-start.2 = (bf16[48,1024]{1,0:T(8,128)(2,1)S(1)}, bf16[48,1024]{1,0:T(8,128)(2,1)S(1)}, u32[]{:S(2)}, u32[]{:S(2)}) collective-permute-start(bf16[48,1024]{1,0:T(8,128)(2,1)S(1)} %get-tuple-element.53.refs_2_), channel_id=1, source_target_pairs={{0,9},{1,10},{2,11},{3,12},{4,13},{5,14},{6,15},{7,8},{8,17},{9,18... | collective-permute-start | bytes 294920 | tf_op jit(solution)/shard_map/ppermute | solution.py:564
  7.2 19.4 %collective-permute-start = (bf16[128,1024]{1,0:T(8,128)(2,1)S(1)}, bf16[128,1024]{1,0:T(8,128)(2,1)S(1)}, u32[]{:S(2)}, u32[]{:S(2)}) collective-permute-start(bf16[128,1024]{1,0:T(8,128)(2,1)S(1)} %get-tuple-element.51.refs_0_), channel_id=1, source_target_pairs={{0,1},{1,2},{2,3},{3,4},{4,5},{5,6},{6,7},{7,0},{8,9},{9,10},{10,1... | collective-permute-start | bytes 786440 | tf_op jit(solution)/shard_map/ppermute | solution.py:564
  8.8 17.8 %collective-permute-start.1 = (bf16[208,1024]{1,0:T(8,128)(2,1)S(1)}, bf16[208,1024]{1,0:T(8,128)(2,1)S(1)}, u32[]{:S(2)}, u32[]{:S(2)}) collective-permute-start(bf16[208,1024]{1,0:T(8,128)(2,1)S(1)} %get-tuple-element.52.refs_1_), channel_id=1, source_target_pairs={{0,8},{1,9},{2,10},{3,11},{4,12},{5,13},{6,14},{7,15},{8,16},{9,17... | collective-permute-start | bytes 1277960 | tf_op jit(solution)/shard_map/ppermute | solution.py:564
  10.3 14.2 %copy-start.22 = (s32[32]{0:T(128)S(1)}, s32[32]{0:T(128)}, u32[]{:S(2)}) copy-start(s32[32]{0:T(128)} %constant.48.clone) | copy-start | bytes 388
  10.3 14.2 %copy-start.23 = (s32[32]{0:T(128)S(1)}, s32[32]{0:T(128)}, u32[]{:S(2)}) copy-start(s32[32]{0:T(128)} %constant.47.clone) | copy-start | bytes 388
  60.7 14.8 %collective-permute-start.3 = (bf16[512,1024]{1,0:T(8,128)(2,1)}, bf16[512,1024]{1,0:T(8,128)(2,1)}, u32[]{:S(2)}, u32[]{:S(2)}) collective-permute-start(bf16[512,1024]{1,0:T(8,128)(2,1)} %get-tuple-element.61), channel_id=1, source_target_pairs={{0,1},{1,0},{2,3},{3,2},{4,5},{5,4},{6,7},{7,6},{8,9},{9,8},{10,11... | collective-permute-start | bytes 3145736 | tf_op jit(solution)/shard_map/ppermute | solution.py:593
  60.7 14.7 %copy-start.20 = (bf16[512,1024]{1,0:T(8,128)(2,1)S(1)}, bf16[512,1024]{1,0:T(8,128)(2,1)}, u32[]{:S(2)}) copy-start(bf16[512,1024]{1,0:T(8,128)(2,1)} %get-tuple-element.67) | copy-start | bytes 3145732
  74.9 20.1 %collective-permute-start.5 = (bf16[512,1536]{1,0:T(8,128)(2,1)}, bf16[512,1536]{1,0:T(8,128)(2,1)}, u32[]{:S(2)}, u32[]{:S(2)}) collective-permute-start(bf16[512,1536]{1,0:T(8,128)(2,1)} %get-tuple-element.72), channel_id=1, source_target_pairs={{0,1},{1,0},{2,3},{3,2},{4,5},{5,4},{6,7},{7,6},{8,9},{9,8},{10,11... | collective-permute-start | bytes 4718600 | tf_op jit(solution)/shard_map/ppermute | solution.py:593
  77.9 17.0 %collective-permute-start.8 = (bf16[128,1024]{1,0:T(8,128)(2,1)}, bf16[128,1024]{1,0:T(8,128)(2,1)}, u32[]{:S(2)}, u32[]{:S(2)}) collective-permute-start(bf16[128,1024]{1,0:T(8,128)(2,1)} %get-tuple-element.112.refs_2_), channel_id=1, source_target_pairs={{0,6},{1,7},{2,4},{3,5},{4,2},{5,3},{6,0},{7,1},{8,14},{9,15},{10,... | collective-permute-start | bytes 786440 | tf_op jit(solution)/shard_map/ppermute | solution.py:593
  79.4 15.5 %collective-permute-start.7 = (bf16[128,1024]{1,0:T(8,128)(2,1)}, bf16[128,1024]{1,0:T(8,128)(2,1)}, u32[]{:S(2)}, u32[]{:S(2)}) collective-permute-start(bf16[128,1024]{1,0:T(8,128)(2,1)} %get-tuple-element.113.refs_1_), channel_id=1, source_target_pairs={{0,4},{1,5},{2,6},{3,7},{4,0},{5,1},{6,2},{7,3},{8,12},{9,13},{10,... | collective-permute-start | bytes 786440 | tf_op jit(solution)/shard_map/ppermute | solution.py:593
  80.9 14.0 %collective-permute-start.6 = (bf16[128,1024]{1,0:T(8,128)(2,1)}, bf16[128,1024]{1,0:T(8,128)(2,1)}, u32[]{:S(2)}, u32[]{:S(2)}) collective-permute-start(bf16[128,1024]{1,0:T(8,128)(2,1)} %get-tuple-element.114.refs_0_), channel_id=1, source_target_pairs={{0,2},{1,3},{2,0},{3,1},{4,6},{5,7},{6,4},{7,5},{8,10},{9,11},{10,... | collective-permute-start | bytes 786440 | tf_op jit(solution)/shard_map/ppermute | solution.py:593
  94.8 24.8 %copy-start = (bf16[512,1536]{1,0:T(8,128)(2,1)}, bf16[512,1536]{1,0:T(8,128)(2,1)S(1)}, u32[]{:S(2)}) copy-start(bf16[512,1536]{1,0:T(8,128)(2,1)S(1)} %get-tuple-element.81) | copy-start | bytes 4718596
  94.8 23.3 %collective-permute-start.4 = (bf16[512,1536]{1,0:T(8,128)(2,1)S(1)}, bf16[512,1536]{1,0:T(8,128)(2,1)S(1)}, u32[]{:S(2)}, u32[]{:S(2)}) collective-permute-start(bf16[512,1536]{1,0:T(8,128)(2,1)S(1)} %get-tuple-element.70), channel_id=1, source_target_pairs={{0,1},{1,0},{2,3},{3,2},{4,5},{5,4},{6,7},{7,6},{8,9},{9,8},{10,11... | collective-permute-start | bytes 4718600 | tf_op jit(solution)/shard_map/ppermute | solution.py:593
  97.2 22.7 %collective-permute-start.11 = (bf16[128,1536]{1,0:T(8,128)(2,1)S(1)}, bf16[128,1536]{1,0:T(8,128)(2,1)S(1)}, u32[]{:S(2)}, u32[]{:S(2)}) collective-permute-start(bf16[128,1536]{1,0:T(8,128)(2,1)S(1)} %get-tuple-element.105.refs_2_), channel_id=1, source_target_pairs={{0,6},{1,7},{2,4},{3,5},{4,2},{5,3},{6,0},{7,1},{8,14},{9,15},{10,... | collective-permute-start | bytes 1179656 | tf_op jit(solution)/shard_map/ppermute | solution.py:593
  98.7 21.6 %collective-permute-start.10 = (bf16[128,1536]{1,0:T(8,128)(2,1)S(1)}, bf16[128,1536]{1,0:T(8,128)(2,1)S(1)}, u32[]{:S(2)}, u32[]{:S(2)}) collective-permute-start(bf16[128,1536]{1,0:T(8,128)(2,1)S(1)} %get-tuple-element.106.refs_1_), channel_id=1, source_target_pairs={{0,4},{1,5},{2,6},{3,7},{4,0},{5,1},{6,2},{7,3},{8,12},{9,13},{10,... | collective-permute-start | bytes 1179656 | tf_op jit(solution)/shard_map/ppermute | solution.py:593
  100.2 20.1 %collective-permute-start.9 = (bf16[128,1536]{1,0:T(8,128)(2,1)S(1)}, bf16[128,1536]{1,0:T(8,128)(2,1)S(1)}, u32[]{:S(2)}, u32[]{:S(2)}) collective-permute-start(bf16[128,1536]{1,0:T(8,128)(2,1)S(1)} %get-tuple-element.107.refs_0_), channel_id=1, source_target_pairs={{0,2},{1,3},{2,0},{3,1},{4,6},{5,7},{6,4},{7,5},{8,10},{9,11},{10,... | collective-permute-start | bytes 1179656 | tf_op jit(solution)/shard_map/ppermute | solution.py:593
  116.1 7.1 %collective-permute-start.14 = (bf16[48,1024]{1,0:T(8,128)(2,1)S(1)}, bf16[48,1024]{1,0:T(8,128)(2,1)S(1)}, u32[]{:S(2)}, u32[]{:S(2)}) collective-permute-start(bf16[48,1024]{1,0:T(8,128)(2,1)S(1)} %get-tuple-element.91), channel_id=1, source_target_pairs={{0,31},{1,24},{2,25},{3,26},{4,27},{5,28},{6,29},{7,30},{8,7},{9,0... | collective-permute-start | bytes 294920 | tf_op jit(solution)/shard_map/ppermute | solution.py:564
  118.1 5.4 %collective-permute-start.12 = (bf16[128,1024]{1,0:T(8,128)(2,1)S(1)}, bf16[128,1024]{1,0:T(8,128)(2,1)S(1)}, u32[]{:S(2)}, u32[]{:S(2)}) collective-permute-start(bf16[128,1024]{1,0:T(8,128)(2,1)S(1)} %get-tuple-element.89), channel_id=1, source_target_pairs={{0,7},{1,0},{2,1},{3,2},{4,3},{5,4},{6,5},{7,6},{8,15},{9,8},{10,9... | collective-permute-start | bytes 786440 | tf_op jit(solution)/shard_map/ppermute | solution.py:564
  119.9 11.5 %collective-permute-start.13 = (bf16[208,1024]{1,0:T(8,128)(2,1)S(1)}, bf16[208,1024]{1,0:T(8,128)(2,1)S(1)}, u32[]{:S(2)}, u32[]{:S(2)}) collective-permute-start(bf16[208,1024]{1,0:T(8,128)(2,1)S(1)} %get-tuple-element.90), channel_id=1, source_target_pairs={{0,24},{1,25},{2,26},{3,27},{4,28},{5,29},{6,30},{7,31},{8,0},{9,1... | collective-permute-start | bytes 1277960 | tf_op jit(solution)/shard_map/ppermute | solution.py:564
  120.6 10.8 %copy-start.2 = (bf16[384,448]{1,0:T(8,128)(2,1)S(1)}, bf16[384,448]{1,0:T(8,128)(2,1)}, u32[]{:S(2)}) copy-start(bf16[384,448]{1,0:T(8,128)(2,1)} %constant.53.clone.refs_12_) | copy-start | bytes 1032196
  120.6 10.8 %copy-start.4 = (bf16[192,416]{1,0:T(8,128)(2,1)S(1)}, bf16[192,416]{1,0:T(8,128)(2,1)}, u32[]{:S(2)}) copy-start(bf16[192,416]{1,0:T(8,128)(2,1)} %constant.52.clone.refs_11_) | copy-start | bytes 479236
  120.6 10.8 %copy-start.6 = (bf16[192,288]{1,0:T(8,128)(2,1)S(1)}, bf16[192,288]{1,0:T(8,128)(2,1)}, u32[]{:S(2)}) copy-start(bf16[192,288]{1,0:T(8,128)(2,1)} %constant.55.clone.refs_14_) | copy-start | bytes 331780
  120.6 10.8 %copy-start.7 = (bf16[192,192]{1,0:T(8,128)(2,1)S(1)}, bf16[192,192]{1,0:T(8,128)(2,1)}, u32[]{:S(2)}) copy-start(bf16[192,192]{1,0:T(8,128)(2,1)} %constant.54.clone.refs_13_) | copy-start | bytes 221188
  133.5 9.0 %collective-permute-start.17 = (bf16[32,2560]{1,0:T(8,128)(2,1)S(1)}, bf16[32,2560]{1,0:T(8,128)(2,1)S(1)}, u32[]{:S(2)}, u32[]{:S(2)}) collective-permute-start(bf16[32,2560]{1,0:T(8,128)(2,1)S(1)} %get-tuple-element.94.refs_5_), channel_id=1, source_target_pairs={{0,24},{1,25},{2,26},{3,27},{4,28},{5,29},{6,30},{7,31},{8,16},{9,... | collective-permute-start | bytes 491528 | tf_op jit(solution)/shard_map/ppermute | solution.py:593
  136.6 13.2 %collective-permute-start.16 = (bf16[32,2560]{1,0:T(8,128)(2,1)S(1)}, bf16[32,2560]{1,0:T(8,128)(2,1)S(1)}, u32[]{:S(2)}, u32[]{:S(2)}) collective-permute-start(bf16[32,2560]{1,0:T(8,128)(2,1)S(1)} %get-tuple-element.116.refs_4_), channel_id=1, source_target_pairs={{0,16},{1,17},{2,18},{3,19},{4,20},{5,21},{6,22},{7,23},{8,24},{9,... | collective-permute-start | bytes 491528 | tf_op jit(solution)/shard_map/ppermute | solution.py:593
  136.6 13.2 %collective-permute-start.15 = (bf16[32,2560]{1,0:T(8,128)(2,1)S(1)}, bf16[32,2560]{1,0:T(8,128)(2,1)S(1)}, u32[]{:S(2)}, u32[]{:S(2)}) collective-permute-start(bf16[32,2560]{1,0:T(8,128)(2,1)S(1)} %get-tuple-element.117.refs_3_), channel_id=1, source_target_pairs={{0,8},{1,9},{2,10},{3,11},{4,12},{5,13},{6,14},{7,15},{8,0},{9,1},... | collective-permute-start | bytes 491528 | tf_op jit(solution)/shard_map/ppermute | solution.py:593
  137.9 13.0 %collective-permute-start.20 = (bf16[128,1536]{1,0:T(8,128)(2,1)S(1)}, bf16[128,1536]{1,0:T(8,128)(2,1)S(1)}, u32[]{:S(2)}, u32[]{:S(2)}) collective-permute-start(bf16[128,1536]{1,0:T(8,128)(2,1)S(1)} %get-tuple-element.108.refs_2_), channel_id=1, source_target_pairs={{0,6},{1,7},{2,4},{3,5},{4,2},{5,3},{6,0},{7,1},{8,14},{9,15},{10,... | collective-permute-start | bytes 1179656 | tf_op jit(solution)/shard_map/ppermute | solution.py:593
  139.4 17.3 %collective-permute-start.19 = (bf16[128,1536]{1,0:T(8,128)(2,1)S(1)}, bf16[128,1536]{1,0:T(8,128)(2,1)S(1)}, u32[]{:S(2)}, u32[]{:S(2)}) collective-permute-start(bf16[128,1536]{1,0:T(8,128)(2,1)S(1)} %get-tuple-element.109.refs_1_), channel_id=1, source_target_pairs={{0,4},{1,5},{2,6},{3,7},{4,0},{5,1},{6,2},{7,3},{8,12},{9,13},{10,... | collective-permute-start | bytes 1179656 | tf_op jit(solution)/shard_map/ppermute | solution.py:593
  142.5 14.1 %collective-permute-start.18 = (bf16[128,1536]{1,0:T(8,128)(2,1)S(1)}, bf16[128,1536]{1,0:T(8,128)(2,1)S(1)}, u32[]{:S(2)}, u32[]{:S(2)}) collective-permute-start(bf16[128,1536]{1,0:T(8,128)(2,1)S(1)} %get-tuple-element.110.refs_0_), channel_id=1, source_target_pairs={{0,2},{1,3},{2,0},{3,1},{4,6},{5,7},{6,4},{7,5},{8,10},{9,11},{10,... | collective-permute-start | bytes 1179656 | tf_op jit(solution)/shard_map/ppermute | solution.py:593
  158.0 4.8 %collective-permute-start.21 = (bf16[32,1536]{1,0:T(8,128)(2,1)S(1)}, bf16[32,1536]{1,0:T(8,128)(2,1)S(1)}, u32[]{:S(2)}, u32[]{:S(2)}) collective-permute-start(bf16[32,1536]{1,0:T(8,128)(2,1)S(1)} %get-tuple-element.118), channel_id=1, source_target_pairs={{0,8},{1,9},{2,10},{3,11},{4,12},{5,13},{6,14},{7,15},{8,0},{9,1},... | collective-permute-start | bytes 294920 | tf_op jit(solution)/shard_map/ppermute | solution.py:593
  159.6 8.2 %collective-permute-start.23 = (bf16[32,1536]{1,0:T(8,128)(2,1)S(1)}, bf16[32,1536]{1,0:T(8,128)(2,1)S(1)}, u32[]{:S(2)}, u32[]{:S(2)}) collective-permute-start(bf16[32,1536]{1,0:T(8,128)(2,1)S(1)} %get-tuple-element.119), channel_id=1, source_target_pairs={{0,24},{1,25},{2,26},{3,27},{4,28},{5,29},{6,30},{7,31},{8,16},{9,... | collective-permute-start | bytes 294920 | tf_op jit(solution)/shard_map/ppermute | solution.py:593
  161.9 9.3 %collective-permute-start.22 = (bf16[32,1536]{1,0:T(8,128)(2,1)S(1)}, bf16[32,1536]{1,0:T(8,128)(2,1)S(1)}, u32[]{:S(2)}, u32[]{:S(2)}) collective-permute-start(bf16[32,1536]{1,0:T(8,128)(2,1)S(1)} %get-tuple-element.120), channel_id=1, source_target_pairs={{0,16},{1,17},{2,18},{3,19},{4,20},{5,21},{6,22},{7,23},{8,24},{9,... | collective-permute-start | bytes 294920 | tf_op jit(solution)/shard_map/ppermute | solution.py:593
  (19 other events, 44.1 us)

commit v9 on v8

--- a/solution.py
+++ b/solution.py
@@ -165,9 +165,10 @@
     source = jnp.concatenate(
         [tokens[cut:cut + WIN * line], tokens[half + cut:half + cut + WIN * line]], axis=0
     )
+    x = dot(order[:, :source.shape[0]], source)
     for w in range(count // places):
         rows = slice(w * places, (w + 1) * places)
-        normalized_window(dot(order[rows, :source.shape[0]], source), rows, xw, normed, rstd)
+        normalized_window(x[rows], rows, xw, normed, rstd)
 
     @pl.loop(0, tiles)
     def _(n):
@@ -191,8 +192,8 @@
     edge, owner, tokens, merged_grad, side, above, corner, order, group, rowmap,
     wqkv_h, wout_h, wm_h, xw_h, normed_in, rstd_h, mixture_h, inverse_h, proj_in,
     normed_h, normt_h, proj_h, dmr_h, dmm_h, grad_h, rstd, merged, out_mine, out_theirs,
-    wqkv, wout, wm, source, xw, normed, normt, proj, mixture, inverse, subs, dsubs, cotangent,
-    grad, dmr, dmm, turned, in_sem, out_sem,
+    wqkv, wout, wm, source, xw, normed, proj, mixture, inverse, subs, dsubs, cotangent,
+    grad, dmr, dmm, in_sem, out_sem,
 ):
     count, channels = xw.shape
     places = 2 * WIN * WIN
@@ -220,7 +221,7 @@
     stores = [
         pltpu.make_async_copy(src, dst, out_sem.at[i])
         for i, (src, dst) in enumerate(
-            [(normed, normed_h), (proj, proj_h), (normt, normt_h),
+            [(normed, normed_h), (proj, proj_h), (wqkv.at[:, pl.ds(count, count)], normt_h),
              (grad, grad_h), (dmr, dmr_h), (dmm, dmm_h)]
         )
     ]
@@ -242,10 +243,12 @@
         if at < source.shape[1]:
             source[wi, at:] = jnp.zeros((source.shape[1] - at, channels), BF16)
 
-    @pl.loop(0, outer // places)
-    def _(w):
-        rows = aligned(w * places, places)
-        normalized_window(dot(order[rows], source[w // per_row]), rows, xw, normed, rstd)
+    for wi in range(2):
+        first, last = wi * per_row, min((wi + 1) * per_row, outer // places)
+        x = dot(order[first * places:last * places], source[wi])
+        for w in range(first, last):
+            rows = slice(w * places, (w + 1) * places)
+            normalized_window(x[(w - first) * places:(w - first + 1) * places], rows, xw, normed, rstd)
 
     loads[0].wait()
     outer_rows = slice(0, outer)
@@ -355,9 +358,9 @@
             for d in range(devices):
                 out[d * block:(d + 1) * block] = turned[aligned(owner[d] * block, block)]
 
+    turned, normt, mixt = (wqkv.at[:, pl.ds(i * count, count)] for i in range(3))
     turn(normed, normt)
     stores[2].start()
-    mixt = wqkv.at[:, :count]
     turn(mixture, mixt)
     part = channels // 2
 
@@ -633,6 +636,13 @@
     return values
 
 
+def column_halves(total, sizes, bit):
+    blocks = sizes[0] // (2 * bit)
+    pairs = total.reshape(blocks, 2, total.shape[0] // (2 * blocks), total.shape[1])
+    kept, given = pairs[:, 0], pairs[:, 1]
+    return [x.reshape(-1, total.shape[1]) for x in (kept, given.astype(BF16))]
+
+
 def finished(kept, arrived):
     for block in arrived:
         kept = kept + block.astype(F32)
@@ -703,7 +713,7 @@
         pack_kernel,
         out_shape=[shape(*e) for e in extents],
         in_specs=[vmem] * 4, out_specs=[vmem] * 3,
-        name="pack_strips", **settings(1, 24),
+        name="pack_strips", **settings(1),
     )(pinned(tokens_flat), pinned(merged_grad_flat), picks(sent_cells, own), picks(sent_groups, g_own))
     strips = sent_strips(packed, sizes, 1)
 
@@ -711,6 +721,8 @@
     group = picks(grps, g_own + sum(g_strips, []))
     edge = (lax.axis_index("lat") == 0).astype(jnp.int32).reshape(1)
     owner, rowmap = device_rows(channels, sizes)
+    if channels // (sizes[0] * sizes[1]) % 16 == 0:
+        rowmap = jnp.zeros((8, 1), jnp.int32)
 
     wide = shape(count, channels)
     inner = 2 * 2 * WIN * WIN
@@ -725,7 +737,7 @@
             pltpu.VMEM(qkv_weight.shape, BF16),
             pltpu.SemaphoreType.DMA((3 * channels // TILE,)),
         ],
-        name="inner_windows", **settings(9, 36),
+        name="inner_windows", **settings(9),
     )
     normed, normt, proj, dmr, dmm, grad, rstd, merged, out_mine, out_theirs = pl.pallas_call(
         forward_kernel,
@@ -743,7 +755,6 @@
             pltpu.VMEM((2, depth, channels), BF16),
             pltpu.VMEM((count, channels), BF16),
             pltpu.VMEM((count, channels), BF16),
-            pltpu.VMEM((channels, count), BF16),
             pltpu.VMEM((count, 3 * channels), BF16),
             pltpu.VMEM((count, channels), BF16),
             pltpu.VMEM((count, channels), F32),
@@ -753,11 +764,10 @@
             pltpu.VMEM((count, channels), BF16),
             pltpu.VMEM((count, channels), BF16),
             pltpu.VMEM((count, channels), BF16),
-            pltpu.VMEM((channels, count), BF16),
             pltpu.SemaphoreType.DMA((9,)),
             pltpu.SemaphoreType.DMA((6,)),
         ],
-        name="block_forward", **settings(30, 58),
+        name="block_forward", **settings(30, 55),
     )(edge, owner, tokens_flat, merged_grad_flat, *strips, order, group, rowmap,
       qkv_weight, out_weight, merge_weight, *ready)
 
@@ -793,12 +803,15 @@
     mine1, arrived, *arrived0 = behind([mine1, arrived] + arrived0, pg1)
     layer1 = layer_blocks(mine1, arrived, sizes)
     arrived1 = layer_step(layer1, sizes)
+    theirs2, = behind([theirs2], arrived0)
     arrived = core_step(theirs2, sizes)
+    layer2 = layer_blocks(mine2, arrived, sizes)
+    arrived2 = layer_step(layer2, sizes)
 
     first_picks = picks(cs.side[:side_cut] + cs.above + cs.corner, cells[:half_cells])
     last_picks = picks(cs.side[side_cut:], cells[half_cells:])
     full, *strips = tied_call(
-        input_kernel, layer1[1:],
+        input_kernel, layer1[1:] + layer2[1:],
         [pg0, pg1, qkv_weight, pinned(normed), pinned(rstd), pinned(grad), merged,
          first_picks, last_picks, picks(sum(g_strips, []), grps)],
         [hbm] * 6 + [vmem] * 4, [wide] + [shape(*e) for e in extents], [vmem] * 4,
@@ -814,19 +827,28 @@
         ],
         name="input_backward", **settings(13, 40),
     )
-    mine2, arrived = behind([mine2, arrived], full)
-    layer2 = layer_blocks(mine2, arrived, sizes)
-    arrived2 = layer_step(layer2, sizes)
-    strips = sent_strips(strips, sizes, -1)
-
-    arrived1 = behind(arrived1, layer2[1])
-    kept = jnp.concatenate([layer0[0], layer1[0]], axis=1)
-    joined = [jnp.concatenate(pair, axis=1) for pair in zip(arrived0, arrived1)]
-    column1 = column_blocks(kept, joined, sizes)
+    arrived1 = behind(arrived1, full)
+    strips = sent_strips(behind(strips, arrived1), sizes, -1)
+
+    total1 = jnp.concatenate([layer0[0], layer1[0]], axis=1)
+    for pair in zip(arrived0, arrived1):
+        total1 = total1 + jnp.concatenate(pair, axis=1).astype(F32)
+    kept1, given1 = column_halves(total1, sizes, 1)
+    got1 = exchange(given1, sizes, 1, 0)
+
+    part1 = kept1 + got1.astype(F32)
+    bit = 2
+    while bit < sizes[0]:
+        kept1, given1 = column_halves(part1, sizes, bit)
+        part1 = kept1 + exchange(given1, sizes, bit, 0).astype(F32)
+        bit *= 2
+    column2 = column_blocks(layer2[0], arrived2, sizes)
+    got2 = column_step(column2, sizes)
+
     got = [Strips.sent(s, *t) for s, t in zip((cs.side, cs.above, cs.corner), to)]
     g_got = sum((Strips.sent(s, *t) for s, t in zip(g_strips, g_to)), [])
     tokens_grad, merged = tied_call(
-        unpack_kernel, layer2[1:] + column1[1:],
+        unpack_kernel, column2[1:] + [given1],
         [
             full, merged, *strips,
             picks(box(levels, range(SHIFT, 2 * SHIFT), own_cols), cells[:half_cells] + got[0][:side_cut]),
@@ -837,11 +859,7 @@
         [vmem] * 9, [wide, shape(groups, merged_width)], [vmem] * 2,
         name="unpack_strips", **settings(20, 24),
     )
-    arrived2 = behind(arrived2, tokens_grad)
-    column1[-1:] = behind(column1[-1:], tokens_grad)
-    column2 = column_blocks(layer2[0], arrived2, sizes)
-    part1 = finished(column1[0], column_step(column1, sizes))
-    part2 = finished(column2[0], column_step(column2, sizes))
+    part2 = finished(column2[0], behind(got2, tokens_grad))
     out_weight_grad = part1[:, :channels]
     part1 = part1[:, channels:]
 

time: 173 us -> 156 us (0.902)
  waiting for transfers between devices: 29.7 us -> 23 us
  local copies, waits for them, and re-layouts: 11.1 us -> 4.81 us
  starting transfers between devices: 30.3 us -> 25.8 us
  Pallas kernels: 89.3 us -> 91.6 us
    unnamed x59 -> x41, local copies, waits for them, and re-layouts: 9.01 us -> 1.97 us
    ppermute x6, waiting for transfers between devices: 8.16 us -> 1.44 us  [sent(): return lax.ppermute(block, ('lat', 'lon'), route)]
    ppermute x18 -> x17, starting transfers between devices: 20.8 us -> 17.5 us  [exchange(): return lax.ppermute(block, ('lat', 'lon'), route)]
    add x1 -> x4, other arithmetic: 0.07 us -> 2.91 us  [the longest x1 1.42 us: shards(): total1 = total1 + jnp.concatenate(pair, axis=1).astype(F32)]
    another operation x2 -> x1, other arithmetic: 3.94 us -> 1.19 us
    add x2 -> x1, other arithmetic: 4.74 us -> 2.49 us  [layer_blocks(): mine[i * rows:(i + 1) * rows].astype(F32)]
    ppermute x18 -> x17, waiting for transfers between devices: 21.6 us -> 21.6 us  [exchange(): return lax.ppermute(block, ('lat', 'lon'), route)]
  transfers between devices with their start and end apart: 24 -> 23, of which waited for: 8 -> 8; matrix products, arithmetic and copies ran while one was open for 7% -> 6% of each run, Pallas kernels for 30% -> 35%
where the time goes in v9:
time: 156 us
  Pallas kernels  91.6 us (59%)
  starting transfers between devices  25.8 us (17%)
  waiting for transfers between devices  23 us (15%)
  other arithmetic  9.73 us (6%)
  local copies, waits for them, and re-layouts  4.81 us (3%)
    pallas_call x5, Pallas kernels, tied_call(): pl.pallas_call(body, out_shape=out_shape, in_specs=[pl.BlockSpec(memory_s...  55.3 us
    pallas_call x1, Pallas kernels, shards(): pl.pallas_call(forward_kernel, out_shape=[wide, shape(channels, count), s...  33.1 us
    ppermute x17, waiting for transfers between devices, exchange(): return lax.ppermute(block, ('lat', 'lon'), route)  21.6 us
    ppermute x17, starting transfers between devices, exchange(): return lax.ppermute(block, ('lat', 'lon'), route)  17.5 us
    ppermute x6, starting transfers between devices, sent(): return lax.ppermute(block, ('lat', 'lon'), route)  8.28 us
    pallas_call x1, Pallas kernels, shards(): pl.pallas_call(pack_kernel, out_shape=[shape(*e) for e in extents], in_sp...  3.14 us
  transfers between devices with their start and end apart: 23, of which 8 were waited for; matrix products, arithmetic and copies ran while one was open for 6% of the time, Pallas kernels for 35%

profile of v9, /device:TPU:0, one launch (start us, length us, event | category | flops | bytes accessed | tf_op | source)
XLA Modules:
  0.0 155.9 jit_solution(6700132098296075308)
XLA Ops:
  0.6 3.1 %pack_strips.1 = (bf16[128,1024]{1,0:T(8,128)(2,1)}, bf16[208,1024]{1,0:T(8,128)(2,1)}, bf16[48,1024]{1,0:T(8,128)(2,1)}) custom-call(bf16[768,1024]{1,0:T(8,128)(2,1)} %bitcast.35, bf16[192,1024]{1,0:T(8,128)(2,1)} %bitcast.38, bf16[288,768]{1,0:T(8,128)(2,1)} %constant.41.clone.pick_cells, bf16[96,192]{1,0:T(8,128)(2,1)} %constant.42.clone.pick_groups), custom_call_target="tpu_custom_call" | custom-call | flops 10000000000 | bytes 16777216 | tf_op jit(solution)/shard_map/pack_strips/pallas_call | solution.py:712
  3.8 2.5 %collective-permute-start.2 = (bf16[48,1024]{1,0:T(8,128)(2,1)}, bf16[48,1024]{1,0:T(8,128)(2,1)S(1)}, u32[]{:S(2)}, u32[]{:S(2)}) collective-permute-start(bf16[48,1024]{1,0:T(8,128)(2,1)} %get-tuple-element.54.refs_2_), channel_id=1, source_target_pairs={{0,9},{1,10},{2,11},{3,12},{4,13},{5,14},{6,15},{7,8},{8,17},{9,18... | collective-permute-start | bytes 294920 | tf_op jit(solution)/shard_map/ppermute | solution.py:567
  6.2 1.6 %collective-permute-start = (bf16[128,1024]{1,0:T(8,128)(2,1)}, bf16[128,1024]{1,0:T(8,128)(2,1)S(1)}, u32[]{:S(2)}, u32[]{:S(2)}) collective-permute-start(bf16[128,1024]{1,0:T(8,128)(2,1)} %get-tuple-element.52.refs_0_), channel_id=1, source_target_pairs={{0,1},{1,2},{2,3},{3,4},{4,5},{5,6},{6,7},{7,0},{8,9},{9,10},{10,1... | collective-permute-start | bytes 786440 | tf_op jit(solution)/shard_map/ppermute | solution.py:567
  7.8 1.6 %collective-permute-start.1 = (bf16[208,1024]{1,0:T(8,128)(2,1)}, bf16[208,1024]{1,0:T(8,128)(2,1)S(1)}, u32[]{:S(2)}, u32[]{:S(2)}) collective-permute-start(bf16[208,1024]{1,0:T(8,128)(2,1)} %get-tuple-element.53.refs_1_), channel_id=1, source_target_pairs={{0,8},{1,9},{2,10},{3,11},{4,12},{5,13},{6,14},{7,15},{8,16},{9,17... | collective-permute-start | bytes 1277960 | tf_op jit(solution)/shard_map/ppermute | solution.py:567
  9.4 10.4 %inner_windows.1 = (bf16[256,1024]{1,0:T(8,128)(2,1)}, bf16[256,1024]{1,0:T(8,128)(2,1)}, f32[256,128]{1,0:T(8,128)}, bf16[256,1024]{1,0:T(8,128)(2,1)}, f32[256,1024]{1,0:T(8,128)}, /*index=5*/bf16[256,3072]{1,0:T(8,128)(2,1)}) custom-call(bf16[128,1024]{1,0:T(8,128)(2,1)} %get-tuple-element.52.refs_0_, bf16[208,1024]{1,0:T(8,128)(2,1)} %get-tuple-element.53.refs_1_, ...), custom_call_target="tpu_custom_call" | custom-call | flops 89999998976 | bytes 16777216 | tf_op jit(solution)/shard_map/inner_windows/pallas_call | solution.py:658
  20.4 1.4 collective-permute-done.1.above
  22.6 33.1 %block_forward.1 = (bf16[768,1024]{1,0:T(8,128)(2,1)}, bf16[1024,768]{1,0:T(8,128)(2,1)}, bf16[768,3072]{1,0:T(8,128)(2,1)}, bf16[768,1024]{1,0:T(8,128)(2,1)}, ...) custom-call(s32[1]{0:T(128)} %bitcast.edge.refs_0_.refs_3_, ...), custom_call_target="tpu_custom_call" | custom-call | flops 299999985664 | bytes 16777216 | tf_op jit(solution)/shard_map/block_forward/pallas_call | solution.py:742
  55.8 14.1 %attention_backward.2 = (bf16[768,1536]{1,0:T(8,128)(2,1)S(1)}, bf16[512,1536]{1,0:T(8,128)(2,1)S(1)}, bf16[512,1536]{1,0:T(8,128)(2,1)}) custom-call(s32[1]{0:T(128)} %bitcast.edge.refs_0_.refs_3_, bf16[768,3072]{1,0:T(8,128)(2,1)} %get-tuple-element.63.refs_1_.refs_4_, bf16[768,1024]{1,0:T(8,128)(2,1)} %get-tuple-element.64.refs_2_.refs_5_, ...), custom_call_target="tpu_custom_call" | custom-call | flops 149999992832 | bytes 16777216 | tf_op jit(solution)/shard_map/attention_backward/pallas_call | solution.py:658
  70.5 2.5 %convert_add_fusion.2 = (f32[128,1024]{1,0:T(8,128)}, bf16[128,1024]{1,0:T(8,128)(2,1)}, bf16[128,1024]{1,0:T(8,128)(2,1)}, bf16[128,1024]{1,0:T(8,128)(2,1)}) fusion(bf16[512,1024]{1,0:T(8,128)(2,1)} %collective-permute-done.3, bf16[512,1024]{1,0:T(8,128)(2,1)S(1)} %copy-done.11), kind=kLoop, calls=%fused_computation.13 | loop fusion | flops 1966080 | bytes 3407872 | tf_op jit(solution)/shard_map/add | solution.py:607
  73.0 1.6 %collective-permute-start.7 = (bf16[128,1024]{1,0:T(8,128)(2,1)}, bf16[128,1024]{1,0:T(8,128)(2,1)}, u32[]{:S(2)}, u32[]{:S(2)}) collective-permute-start(bf16[128,1024]{1,0:T(8,128)(2,1)} %get-tuple-element.110.refs_2_), channel_id=1, source_target_pairs={{0,6},{1,7},{2,4},{3,5},{4,2},{5,3},{6,0},{7,1},{8,14},{9,15},{10,... | collective-permute-start | bytes 786440 | tf_op jit(solution)/shard_map/ppermute | solution.py:596
  74.5 1.4 collective-permute-start.6
  76.4 13.4 %attention_backward.3 = (bf16[768,1536]{1,0:T(8,128)(2,1)S(1)}, bf16[512,1536]{1,0:T(8,128)(2,1)S(1)}, bf16[512,1536]{1,0:T(8,128)(2,1)S(1)}) custom-call(bf16[128,1024]{1,0:T(8,128)(2,1)} %get-tuple-element.112.refs_0_, bf16[128,1024]{1,0:T(8,128)(2,1)} %get-tuple-element.111.refs_1_, bf16[128,1024]{1,0:T(8,128)(2,1)} %get-tuple-element.110.refs_2_, ...), custom_call_target="tpu_custom_call" | custom-call | flops 149999992832 | bytes 16777216 | tf_op jit(solution)/shard_map/attention_backward/pallas_call | solution.py:658
  89.9 1.7 %add_convert_fusion = (bf16[128,1536]{1,0:T(8,128)(2,1)S(1)}, bf16[128,1536]{1,0:T(8,128)(2,1)S(1)}, bf16[128,1536]{1,0:T(8,128)(2,1)S(1)}, f32[128,1536]{1,0:T(8,128)S(1)}) fusion(bf16[512,1536]{1,0:T(8,128)(2,1)} %collective-permute-done.4, bf16[512,1536]{1,0:T(8,128)(2,1)S(1)} %get-tuple-element.79), kind=kLoop, calls=%fused_computation.3 | loop fusion | flops 2949120 | bytes 5111808 | tf_op jit(solution)/shard_map/convert_element_type | solution.py:610
  91.7 1.6 %collective-permute-start.14 = (bf16[128,1536]{1,0:T(8,128)(2,1)S(1)}, bf16[128,1536]{1,0:T(8,128)(2,1)S(1)}, u32[]{:S(2)}, u32[]{:S(2)}) collective-permute-start(bf16[128,1536]{1,0:T(8,128)(2,1)S(1)} %get-tuple-element.102.refs_2_), channel_id=1, source_target_pairs={{0,6},{1,7},{2,4},{3,5},{4,2},{5,3},{6,0},{7,1},{8,14},{9,15},{10,... | collective-permute-start | bytes 1179656 | tf_op jit(solution)/shard_map/ppermute | solution.py:596
  93.3 1.4 collective-permute-start.13
  96.4 15.3 %input_backward.1 = (bf16[768,1024]{1,0:T(8,128)(2,1)S(1)}, bf16[128,1024]{1,0:T(8,128)(2,1)S(1)}, bf16[208,1024]{1,0:T(8,128)(2,1)S(1)}, bf16[48,1024]{1,0:T(8,128)(2,1)S(1)}) custom-call(bf16[128,1536]{1,0:T(8,128)(2,1)S(1)} %get-tuple-element.104.refs_0_, bf16[128,1536]{1,0:T(8,128)(2,1)S(1)} %get-tuple-element.103.refs_1_, ...), custom_call_target="tpu_custom_call" | custom-call | flops 130000003072 | bytes 16777216 | tf_op jit(solution)/shard_map/input_backward/pallas_call | solution.py:658
  112.7 1.4 fusion.1
  114.6 1.5 collective-permute-start.9
  116.0 1.5 collective-permute-start.11
  119.0 5.8 %collective-permute-done.15 = bf16[64,2560]{1,0:T(8,128)(2,1)S(1)} collective-permute-done((bf16[64,2560]{1,0:T(8,128)(2,1)S(1)}, bf16[64,2560]{1,0:T(8,128)(2,1)S(1)}, u32[]{:S(2)}, u32[]{:S(2)}) %collective-permute-start.15) | collective-permute-done | bytes 327712 | tf_op jit(solution)/shard_map/ppermute | solution.py:596
  125.8 1.9 %collective-permute-done.9 = bf16[128,1536]{1,0:T(8,128)(2,1)S(1)} collective-permute-done((bf16[128,1536]{1,0:T(8,128)(2,1)S(1)}, bf16[128,1536]{1,0:T(8,128)(2,1)S(1)}, u32[]{:S(2)}, u32[]{:S(2)}) %collective-permute-start.9) | collective-permute-done | bytes 393248 | tf_op jit(solution)/shard_map/ppermute | solution.py:596
  127.7 1.7 %collective-permute-start.17 = (bf16[208,1024]{1,0:T(8,128)(2,1)S(1)}, bf16[208,1024]{1,0:T(8,128)(2,1)S(1)}, u32[]{:S(2)}, u32[]{:S(2)}) collective-permute-start(bf16[208,1024]{1,0:T(8,128)(2,1)S(1)} %get-tuple-element.93), channel_id=1, source_target_pairs={{0,24},{1,25},{2,26},{3,27},{4,28},{5,29},{6,30},{7,31},{8,0},{9,1... | collective-permute-start | bytes 1277960 | tf_op jit(solution)/shard_map/ppermute | solution.py:567
  129.4 6.4 %collective-permute-done.11 = bf16[128,1536]{1,0:T(8,128)(2,1)S(1)} collective-permute-done((bf16[128,1536]{1,0:T(8,128)(2,1)S(1)}, bf16[128,1536]{1,0:T(8,128)(2,1)S(1)}, u32[]{:S(2)}, u32[]{:S(2)}) %collective-permute-start.11) | collective-permute-done | bytes 393248 | tf_op jit(solution)/shard_map/ppermute | solution.py:596
  135.9 1.5 collective-permute-start.19
  137.3 1.2 fusion.6
  139.2 2.6 %collective-permute-start.22 = (bf16[32,1536]{1,0:T(8,128)(2,1)}, bf16[32,1536]{1,0:T(8,128)(2,1)}, u32[]{:S(2)}, u32[]{:S(2)}) collective-permute-start(bf16[32,1536]{1,0:T(8,128)(2,1)} %get-tuple-element.113.refs_2_), channel_id=1, source_target_pairs={{0,24},{1,25},{2,26},{3,27},{4,28},{5,29},{6,30},{7,31},{8,16},{9,... | collective-permute-start | bytes 294920 | tf_op jit(solution)/shard_map/ppermute | solution.py:596
  141.9 1.7 %collective-permute-start.20 = (bf16[32,1536]{1,0:T(8,128)(2,1)}, bf16[32,1536]{1,0:T(8,128)(2,1)}, u32[]{:S(2)}, u32[]{:S(2)}) collective-permute-start(bf16[32,1536]{1,0:T(8,128)(2,1)} %get-tuple-element.115.refs_0_), channel_id=1, source_target_pairs={{0,8},{1,9},{2,10},{3,11},{4,12},{5,13},{6,14},{7,15},{8,0},{9,1},... | collective-permute-start | bytes 294920 | tf_op jit(solution)/shard_map/ppermute | solution.py:596
  143.7 2.2 %unpack_strips.1 = (bf16[768,1024]{1,0:T(8,128)(2,1)}, bf16[192,1024]{1,0:T(8,128)(2,1)}) custom-call(bf16[32,1536]{1,0:T(8,128)(2,1)} %get-tuple-element.115.refs_0_, bf16[32,1536]{1,0:T(8,128)(2,1)} %get-tuple-element.114.refs_1_, bf16[32,1536]{1,0:T(8,128)(2,1)} %get-tuple-element.113.refs_2_, bf16[32,2560]{1,0:T(8,128)(2,1)} %fusion.5.refs_3_, ...), custom_call_target="tpu_custom_call" | custom-call | flops 199999995904 | bytes 16777216 | tf_op jit(solution)/shard_map/unpack_strips/pallas_call | solution.py:658
  145.8 5.2 %collective-permute-done.19 = bf16[32,2560]{1,0:T(8,128)(2,1)} collective-permute-done((bf16[32,2560]{1,0:T(8,128)(2,1)}, bf16[32,2560]{1,0:T(8,128)(2,1)}, u32[]{:S(2)}, u32[]{:S(2)}) %collective-permute-start.19) | collective-permute-done | bytes 163872 | tf_op jit(solution)/shard_map/ppermute | solution.py:596
  151.0 0.9 fusion.2
  152.7 1.3 collective-permute-done.21
  153.9 1.1 fusion.4
  (78 shorter events, 10.3 us)
Async XLA Ops:
  3.8 16.6 %collective-permute-start.2 = (bf16[48,1024]{1,0:T(8,128)(2,1)}, bf16[48,1024]{1,0:T(8,128)(2,1)S(1)}, u32[]{:S(2)}, u32[]{:S(2)}) collective-permute-start(bf16[48,1024]{1,0:T(8,128)(2,1)} %get-tuple-element.54.refs_2_), channel_id=1, source_target_pairs={{0,9},{1,10},{2,11},{3,12},{4,13},{5,14},{6,15},{7,8},{8,17},{9,18... | collective-permute-start | bytes 294920 | tf_op jit(solution)/shard_map/ppermute | solution.py:567
  6.2 14.1 %collective-permute-start = (bf16[128,1024]{1,0:T(8,128)(2,1)}, bf16[128,1024]{1,0:T(8,128)(2,1)S(1)}, u32[]{:S(2)}, u32[]{:S(2)}) collective-permute-start(bf16[128,1024]{1,0:T(8,128)(2,1)} %get-tuple-element.52.refs_0_), channel_id=1, source_target_pairs={{0,1},{1,2},{2,3},{3,4},{4,5},{5,6},{6,7},{7,0},{8,9},{9,10},{10,1... | collective-permute-start | bytes 786440 | tf_op jit(solution)/shard_map/ppermute | solution.py:567
  7.8 12.0 %copy-start.13 = (s32[32]{0:T(128)S(1)}, s32[32]{0:T(128)}, u32[]{:S(2)}) copy-start(s32[32]{0:T(128)} %constant.47.clone) | copy-start | bytes 388
  7.8 12.0 %copy-start.14 = (s32[32]{0:T(128)S(1)}, s32[32]{0:T(128)}, u32[]{:S(2)}) copy-start(s32[32]{0:T(128)} %constant.46.clone) | copy-start | bytes 388
  7.8 14.0 %collective-permute-start.1 = (bf16[208,1024]{1,0:T(8,128)(2,1)}, bf16[208,1024]{1,0:T(8,128)(2,1)S(1)}, u32[]{:S(2)}, u32[]{:S(2)}) collective-permute-start(bf16[208,1024]{1,0:T(8,128)(2,1)} %get-tuple-element.53.refs_1_), channel_id=1, source_target_pairs={{0,8},{1,9},{2,10},{3,11},{4,12},{5,13},{6,14},{7,15},{8,16},{9,17... | collective-permute-start | bytes 1277960 | tf_op jit(solution)/shard_map/ppermute | solution.py:567
  55.7 14.8 %collective-permute-start.3 = (bf16[512,1024]{1,0:T(8,128)(2,1)}, bf16[512,1024]{1,0:T(8,128)(2,1)}, u32[]{:S(2)}, u32[]{:S(2)}) collective-permute-start(bf16[512,1024]{1,0:T(8,128)(2,1)} %get-tuple-element.62), channel_id=1, source_target_pairs={{0,1},{1,0},{2,3},{3,2},{4,5},{5,4},{6,7},{7,6},{8,9},{9,8},{10,11... | collective-permute-start | bytes 3145736 | tf_op jit(solution)/shard_map/ppermute | solution.py:596
  55.8 14.7 %copy-start.11 = (bf16[512,1024]{1,0:T(8,128)(2,1)S(1)}, bf16[512,1024]{1,0:T(8,128)(2,1)}, u32[]{:S(2)}) copy-start(bf16[512,1024]{1,0:T(8,128)(2,1)} %get-tuple-element.68) | copy-start | bytes 3145732
  69.9 19.9 %collective-permute-start.4 = (bf16[512,1536]{1,0:T(8,128)(2,1)}, bf16[512,1536]{1,0:T(8,128)(2,1)}, u32[]{:S(2)}, u32[]{:S(2)}) collective-permute-start(bf16[512,1536]{1,0:T(8,128)(2,1)} %get-tuple-element.73), channel_id=1, source_target_pairs={{0,1},{1,0},{2,3},{3,2},{4,5},{5,4},{6,7},{7,6},{8,9},{9,8},{10,11... | collective-permute-start | bytes 4718600 | tf_op jit(solution)/shard_map/ppermute | solution.py:596
  73.0 16.9 %collective-permute-start.7 = (bf16[128,1024]{1,0:T(8,128)(2,1)}, bf16[128,1024]{1,0:T(8,128)(2,1)}, u32[]{:S(2)}, u32[]{:S(2)}) collective-permute-start(bf16[128,1024]{1,0:T(8,128)(2,1)} %get-tuple-element.110.refs_2_), channel_id=1, source_target_pairs={{0,6},{1,7},{2,4},{3,5},{4,2},{5,3},{6,0},{7,1},{8,14},{9,15},{10,... | collective-permute-start | bytes 786440 | tf_op jit(solution)/shard_map/ppermute | solution.py:596
  74.5 15.3 %collective-permute-start.6 = (bf16[128,1024]{1,0:T(8,128)(2,1)}, bf16[128,1024]{1,0:T(8,128)(2,1)}, u32[]{:S(2)}, u32[]{:S(2)}) collective-permute-start(bf16[128,1024]{1,0:T(8,128)(2,1)} %get-tuple-element.111.refs_1_), channel_id=1, source_target_pairs={{0,4},{1,5},{2,6},{3,7},{4,0},{5,1},{6,2},{7,3},{8,12},{9,13},{10,... | collective-permute-start | bytes 786440 | tf_op jit(solution)/shard_map/ppermute | solution.py:596
  75.9 13.9 %collective-permute-start.5 = (bf16[128,1024]{1,0:T(8,128)(2,1)}, bf16[128,1024]{1,0:T(8,128)(2,1)}, u32[]{:S(2)}, u32[]{:S(2)}) collective-permute-start(bf16[128,1024]{1,0:T(8,128)(2,1)} %get-tuple-element.112.refs_0_), channel_id=1, source_target_pairs={{0,2},{1,3},{2,0},{3,1},{4,6},{5,7},{6,4},{7,5},{8,10},{9,11},{10,... | collective-permute-start | bytes 786440 | tf_op jit(solution)/shard_map/ppermute | solution.py:596
  89.9 5.4 %collective-permute-start.8 = (bf16[512,1536]{1,0:T(8,128)(2,1)S(1)}, bf16[512,1536]{1,0:T(8,128)(2,1)S(1)}, u32[]{:S(2)}, u32[]{:S(2)}) collective-permute-start(bf16[512,1536]{1,0:T(8,128)(2,1)S(1)} %get-tuple-element.78), channel_id=1, source_target_pairs={{0,1},{1,0},{2,3},{3,2},{4,5},{5,4},{6,7},{7,6},{8,9},{9,8},{10,11... | collective-permute-start | bytes 4718600 | tf_op jit(solution)/shard_map/ppermute | solution.py:596
  91.7 20.0 %collective-permute-start.14 = (bf16[128,1536]{1,0:T(8,128)(2,1)S(1)}, bf16[128,1536]{1,0:T(8,128)(2,1)S(1)}, u32[]{:S(2)}, u32[]{:S(2)}) collective-permute-start(bf16[128,1536]{1,0:T(8,128)(2,1)S(1)} %get-tuple-element.102.refs_2_), channel_id=1, source_target_pairs={{0,6},{1,7},{2,4},{3,5},{4,2},{5,3},{6,0},{7,1},{8,14},{9,15},{10,... | collective-permute-start | bytes 1179656 | tf_op jit(solution)/shard_map/ppermute | solution.py:596
  93.3 19.3 %collective-permute-start.13 = (bf16[128,1536]{1,0:T(8,128)(2,1)S(1)}, bf16[128,1536]{1,0:T(8,128)(2,1)S(1)}, u32[]{:S(2)}, u32[]{:S(2)}) collective-permute-start(bf16[128,1536]{1,0:T(8,128)(2,1)S(1)} %get-tuple-element.103.refs_1_), channel_id=1, source_target_pairs={{0,4},{1,5},{2,6},{3,7},{4,0},{5,1},{6,2},{7,3},{8,12},{9,13},{10,... | collective-permute-start | bytes 1179656 | tf_op jit(solution)/shard_map/ppermute | solution.py:596
  94.7 18.0 %collective-permute-start.12 = (bf16[128,1536]{1,0:T(8,128)(2,1)S(1)}, bf16[128,1536]{1,0:T(8,128)(2,1)S(1)}, u32[]{:S(2)}, u32[]{:S(2)}) collective-permute-start(bf16[128,1536]{1,0:T(8,128)(2,1)S(1)} %get-tuple-element.104.refs_0_), channel_id=1, source_target_pairs={{0,2},{1,3},{2,0},{3,1},{4,6},{5,7},{6,4},{7,5},{8,10},{9,11},{10,... | collective-permute-start | bytes 1179656 | tf_op jit(solution)/shard_map/ppermute | solution.py:596
  96.4 16.3 %copy-start.8 = (f32[128,1024]{1,0:T(8,128)S(1)}, f32[128,1024]{1,0:T(8,128)}, u32[]{:S(2)}) copy-start(f32[128,1024]{1,0:T(8,128)} %get-tuple-element.109) | copy-start | bytes 1572868
  114.1 10.7 %collective-permute-start.15 = (bf16[64,2560]{1,0:T(8,128)(2,1)S(1)}, bf16[64,2560]{1,0:T(8,128)(2,1)S(1)}, u32[]{:S(2)}, u32[]{:S(2)}) collective-permute-start(bf16[64,2560]{1,0:T(8,128)(2,1)S(1)} %bitcast.34), channel_id=1, source_target_pairs={{0,8},{1,9},{2,10},{3,11},{4,12},{5,13},{6,14},{7,15},{8,0},{9,1},... | collective-permute-start | bytes 983048 | tf_op jit(solution)/shard_map/ppermute | solution.py:596
  114.6 13.1 %collective-permute-start.9 = (bf16[128,1536]{1,0:T(8,128)(2,1)S(1)}, bf16[128,1536]{1,0:T(8,128)(2,1)S(1)}, u32[]{:S(2)}, u32[]{:S(2)}) collective-permute-start(bf16[128,1536]{1,0:T(8,128)(2,1)S(1)} %get-tuple-element.106.refs_3_), channel_id=1, source_target_pairs={{0,2},{1,3},{2,0},{3,1},{4,6},{5,7},{6,4},{7,5},{8,10},{9,11},{10,... | collective-permute-start | bytes 1179656 | tf_op jit(solution)/shard_map/ppermute | solution.py:596
  116.0 19.8 %collective-permute-start.11 = (bf16[128,1536]{1,0:T(8,128)(2,1)S(1)}, bf16[128,1536]{1,0:T(8,128)(2,1)S(1)}, u32[]{:S(2)}, u32[]{:S(2)}) collective-permute-start(bf16[128,1536]{1,0:T(8,128)(2,1)S(1)} %get-tuple-element.107.refs_5_), channel_id=1, source_target_pairs={{0,6},{1,7},{2,4},{3,5},{4,2},{5,3},{6,0},{7,1},{8,14},{9,15},{10,... | collective-permute-start | bytes 1179656 | tf_op jit(solution)/shard_map/ppermute | solution.py:596
  117.5 19.8 %collective-permute-start.10 = (bf16[128,1536]{1,0:T(8,128)(2,1)S(1)}, bf16[128,1536]{1,0:T(8,128)(2,1)S(1)}, u32[]{:S(2)}, u32[]{:S(2)}) collective-permute-start(bf16[128,1536]{1,0:T(8,128)(2,1)S(1)} %get-tuple-element.108.refs_4_), channel_id=1, source_target_pairs={{0,4},{1,5},{2,6},{3,7},{4,0},{5,1},{6,2},{7,3},{8,12},{9,13},{10,... | collective-permute-start | bytes 1179656 | tf_op jit(solution)/shard_map/ppermute | solution.py:596
  118.1 23.8 %collective-permute-start.18 = (bf16[48,1024]{1,0:T(8,128)(2,1)S(1)}, bf16[48,1024]{1,0:T(8,128)(2,1)S(1)}, u32[]{:S(2)}, u32[]{:S(2)}) collective-permute-start(bf16[48,1024]{1,0:T(8,128)(2,1)S(1)} %get-tuple-element.94), channel_id=1, source_target_pairs={{0,31},{1,24},{2,25},{3,26},{4,27},{5,28},{6,29},{7,30},{8,7},{9,0... | collective-permute-start | bytes 294920 | tf_op jit(solution)/shard_map/ppermute | solution.py:567
  124.8 17.1 %collective-permute-start.16 = (bf16[128,1024]{1,0:T(8,128)(2,1)S(1)}, bf16[128,1024]{1,0:T(8,128)(2,1)S(1)}, u32[]{:S(2)}, u32[]{:S(2)}) collective-permute-start(bf16[128,1024]{1,0:T(8,128)(2,1)S(1)} %get-tuple-element.92), channel_id=1, source_target_pairs={{0,7},{1,0},{2,1},{3,2},{4,3},{5,4},{6,5},{7,6},{8,15},{9,8},{10,9... | collective-permute-start | bytes 786440 | tf_op jit(solution)/shard_map/ppermute | solution.py:567
  125.8 17.9 %copy-start = (bf16[384,448]{1,0:T(8,128)(2,1)S(1)}, bf16[384,448]{1,0:T(8,128)(2,1)}, u32[]{:S(2)}) copy-start(bf16[384,448]{1,0:T(8,128)(2,1)} %constant.52.clone.refs_10_) | copy-start | bytes 1032196
  125.8 17.9 %copy-start.1 = (bf16[192,416]{1,0:T(8,128)(2,1)S(1)}, bf16[192,416]{1,0:T(8,128)(2,1)}, u32[]{:S(2)}) copy-start(bf16[192,416]{1,0:T(8,128)(2,1)} %constant.51.clone.refs_9_) | copy-start | bytes 479236
  125.8 17.9 %copy-start.3 = (bf16[192,288]{1,0:T(8,128)(2,1)S(1)}, bf16[192,288]{1,0:T(8,128)(2,1)}, u32[]{:S(2)}) copy-start(bf16[192,288]{1,0:T(8,128)(2,1)} %constant.54.clone.refs_12_) | copy-start | bytes 331780
  125.8 17.9 %copy-start.4 = (bf16[192,192]{1,0:T(8,128)(2,1)S(1)}, bf16[192,192]{1,0:T(8,128)(2,1)}, u32[]{:S(2)}) copy-start(bf16[192,192]{1,0:T(8,128)(2,1)} %constant.53.clone.refs_11_) | copy-start | bytes 221188
  127.7 15.9 %collective-permute-start.17 = (bf16[208,1024]{1,0:T(8,128)(2,1)S(1)}, bf16[208,1024]{1,0:T(8,128)(2,1)S(1)}, u32[]{:S(2)}, u32[]{:S(2)}) collective-permute-start(bf16[208,1024]{1,0:T(8,128)(2,1)S(1)} %get-tuple-element.93), channel_id=1, source_target_pairs={{0,24},{1,25},{2,26},{3,27},{4,28},{5,29},{6,30},{7,31},{8,0},{9,1... | collective-permute-start | bytes 1277960 | tf_op jit(solution)/shard_map/ppermute | solution.py:567
  135.9 15.2 %collective-permute-start.19 = (bf16[32,2560]{1,0:T(8,128)(2,1)}, bf16[32,2560]{1,0:T(8,128)(2,1)}, u32[]{:S(2)}, u32[]{:S(2)}) collective-permute-start(bf16[32,2560]{1,0:T(8,128)(2,1)} %fusion.5.refs_3_), channel_id=1, source_target_pairs={{0,16},{1,17},{2,18},{3,19},{4,20},{5,21},{6,22},{7,23},{8,24},{9,... | collective-permute-start | bytes 491528 | tf_op jit(solution)/shard_map/ppermute | solution.py:596
  139.2 13.4 %collective-permute-start.22 = (bf16[32,1536]{1,0:T(8,128)(2,1)}, bf16[32,1536]{1,0:T(8,128)(2,1)}, u32[]{:S(2)}, u32[]{:S(2)}) collective-permute-start(bf16[32,1536]{1,0:T(8,128)(2,1)} %get-tuple-element.113.refs_2_), channel_id=1, source_target_pairs={{0,24},{1,25},{2,26},{3,27},{4,28},{5,29},{6,30},{7,31},{8,16},{9,... | collective-permute-start | bytes 294920 | tf_op jit(solution)/shard_map/ppermute | solution.py:596
  141.9 12.1 %collective-permute-start.21 = (bf16[32,1536]{1,0:T(8,128)(2,1)}, bf16[32,1536]{1,0:T(8,128)(2,1)}, u32[]{:S(2)}, u32[]{:S(2)}) collective-permute-start(bf16[32,1536]{1,0:T(8,128)(2,1)} %get-tuple-element.114.refs_1_), channel_id=1, source_target_pairs={{0,16},{1,17},{2,18},{3,19},{4,20},{5,21},{6,22},{7,23},{8,24},{9,... | collective-permute-start | bytes 294920 | tf_op jit(solution)/shard_map/ppermute | solution.py:596
  141.9 12.0 %collective-permute-start.20 = (bf16[32,1536]{1,0:T(8,128)(2,1)}, bf16[32,1536]{1,0:T(8,128)(2,1)}, u32[]{:S(2)}, u32[]{:S(2)}) collective-permute-start(bf16[32,1536]{1,0:T(8,128)(2,1)} %get-tuple-element.115.refs_0_), channel_id=1, source_target_pairs={{0,8},{1,9},{2,10},{3,11},{4,12},{5,13},{6,14},{7,15},{8,0},{9,1},... | collective-permute-start | bytes 294920 | tf_op jit(solution)/shard_map/ppermute | solution.py:596
  143.7 7.4 %copy-start.10 = (f32[64,2560]{1,0:T(8,128)S(1)}, f32[64,2560]{1,0:T(8,128)}, u32[]{:S(2)}) copy-start(f32[64,2560]{1,0:T(8,128)} %copy-done.9) | copy-start | bytes 1966084
  (9 other events, 10.4 us)

commit v10 on v9

--- a/solution.py
+++ b/solution.py
@@ -119,13 +119,23 @@
     return list(zip(cells, groups))
 
 
-def normalized_window(x, rows, xw, normed, rstd):
-    xw[rows] = x.astype(BF16)
-    center = jnp.mean(x, axis=1, keepdims=True)
-    moved = x - center
-    scale = lax.rsqrt(jnp.mean(moved * moved, axis=1, keepdims=True) + EPSILON)
-    rstd[rows] = jnp.broadcast_to(scale, (x.shape[0], LANES))
-    normed[rows] = (moved * scale).astype(BF16)
+def by_rows(count, step, body):
+    @pl.loop(0, count // step)
+    def _(i):
+        body(aligned(i * step, step))
+
+
+def normalize_rows(count, raw, xw, normed, rstd):
+    def block(rows):
+        x = raw[rows]
+        xw[rows] = x.astype(BF16)
+        center = jnp.mean(x, axis=1, keepdims=True)
+        moved = x - center
+        scale = lax.rsqrt(jnp.mean(moved * moved, axis=1, keepdims=True) + EPSILON)
+        rstd[rows] = jnp.broadcast_to(scale, (x.shape[0], LANES))
+        normed[rows] = (moved * scale).astype(BF16)
+
+    by_rows(count, 32, block)
 
 
 def attended(proj, rows, lanes, masks, factor, bias, mixture, inverse):
@@ -147,7 +157,7 @@
 
 
 def inner_kernel(
-    tokens, order, wqkv_h, xw, normed, rstd, mixture, inverse, proj, wqkv, in_sem,
+    tokens, order, wqkv_h, xw, normed, rstd, mixture, inverse, proj, wqkv, raw, in_sem,
 ):
     count, channels = xw.shape
     places = 2 * WIN * WIN
@@ -165,10 +175,8 @@
     source = jnp.concatenate(
         [tokens[cut:cut + WIN * line], tokens[half + cut:half + cut + WIN * line]], axis=0
     )
-    x = dot(order[:, :source.shape[0]], source)
-    for w in range(count // places):
-        rows = slice(w * places, (w + 1) * places)
-        normalized_window(x[rows], rows, xw, normed, rstd)
+    raw[...] = dot(order[:, :source.shape[0]], source)
+    normalize_rows(count, raw, xw, normed, rstd)
 
     @pl.loop(0, tiles)
     def _(n):
@@ -245,10 +253,10 @@
 
     for wi in range(2):
         first, last = wi * per_row, min((wi + 1) * per_row, outer // places)
-        x = dot(order[first * places:last * places], source[wi])
-        for w in range(first, last):
-            rows = slice(w * places, (w + 1) * places)
-            normalized_window(x[(w - first) * places:(w - first + 1) * places], rows, xw, normed, rstd)
+        inverse[first * places:last * places] = dot(
+            order[first * places:last * places], source[wi]
+        )
+    normalize_rows(outer, inverse, xw, normed, rstd)
 
     loads[0].wait()
     outer_rows = slice(0, outer)
@@ -296,48 +304,52 @@
         for w in range(windows):
             for s in range(4):
                 at = w * places + s * quarter
-                subs[s, w * quarter:(w + 1) * quarter, columns] = out[at:at + quarter]
-
-    total = jnp.zeros((groups, 1), F32)
-    for s in range(4):
-        total += jnp.sum(subs[s].astype(F32), axis=1, keepdims=True)
-    center = total / (4 * channels)
-    total = jnp.zeros((groups, 1), F32)
-    for s in range(4):
-        moved = subs[s].astype(F32) - center
-        total += jnp.sum(moved * moved, axis=1, keepdims=True)
-    scale = lax.rsqrt(total / (4 * channels) + EPSILON)
-    result = jnp.zeros((groups, wm.shape[1]), F32)
-    for s in range(4):
-        unit = ((subs[s].astype(F32) - center) * scale).astype(BF16)
-        result += dot(unit, wm[s * channels:(s + 1) * channels])
-    merged[...] = result.astype(BF16)
-
-    mean_g = jnp.zeros((groups, 1), F32)
-    mean_gx = jnp.zeros((groups, 1), F32)
-    for s in range(4):
-        d = dsubs[:, s * channels:(s + 1) * channels].astype(F32)
-        mean_g += jnp.sum(d, axis=1, keepdims=True)
-        mean_gx += jnp.sum(d * ((subs[s].astype(F32) - center) * scale), axis=1, keepdims=True)
-    mean_g = mean_g / (4 * channels)
-    mean_gx = mean_gx / (4 * channels)
-    for s in range(4):
-        unit = (subs[s].astype(F32) - center) * scale
-        d = dsubs[:, s * channels:(s + 1) * channels].astype(F32)
-        d = (scale * (d - mean_g - unit * mean_gx)).astype(BF16)
-        for w in range(windows):
+                spot = aligned(s * channels + n * TILE, TILE)
+                subs[w * quarter:(w + 1) * quarter, spot] = out[at:at + quarter]
+
+    depth = 4 * channels
+
+    def merging(rows):
+        values = [subs[rows, s * channels:(s + 1) * channels].astype(F32) for s in range(4)]
+        center = sum(jnp.sum(v, axis=1, keepdims=True) for v in values) / depth
+        values = [v - center for v in values]
+        spread = sum(jnp.sum(v * v, axis=1, keepdims=True) for v in values) / depth
+        scale = lax.rsqrt(spread + EPSILON)
+        values = [v * scale for v in values]
+        for s in range(4):
+            subs[rows, s * channels:(s + 1) * channels] = values[s].astype(BF16)
+        slopes = [dsubs[rows, s * channels:(s + 1) * channels].astype(F32) for s in range(4)]
+        mean_g = sum(jnp.sum(d, axis=1, keepdims=True) for d in slopes) / depth
+        mean_gx = sum(jnp.sum(d * v, axis=1, keepdims=True) for d, v in zip(slopes, values)) / depth
+        for s in range(4):
+            d = scale * (slopes[s] - mean_g - values[s] * mean_gx)
+            dsubs[rows, s * channels:(s + 1) * channels] = d.astype(BF16)
+
+    by_rows(groups, 16, merging)
+    for w in range(windows):
+        for s in range(4):
             at = w * places + s * quarter
-            grad[at:at + quarter] = d[w * quarter:(w + 1) * quarter]
+            grad[at:at + quarter] = dsubs[
+                w * quarter:(w + 1) * quarter, s * channels:(s + 1) * channels
+            ]
     stores[3].start()
 
     @pl.loop(0, channels // TILE)
     def _(n):
         columns = aligned(n * TILE, TILE)
-        d = dot(grad[...], wout[columns], NT).astype(BF16).astype(F32)
-        d = d * inverse[:, columns]
-        dmr[:, columns] = d.astype(BF16)
-        dmm[:, columns] = (-d * mixture[:, columns].astype(F32)).astype(BF16)
-
+        dmr[:, columns] = dot(grad[...], wout[columns], NT).astype(BF16)
+
+    @pl.loop(0, wm.shape[1] // TILE)
+    def _(n):
+        columns = aligned(n * TILE, TILE)
+        merged[:, columns] = dot(subs[...], wm[:, columns]).astype(BF16)
+
+    def scaled(rows):
+        d = dmr[rows].astype(F32) * inverse[rows]
+        dmr[rows] = d.astype(BF16)
+        dmm[rows] = (-d * mixture[rows].astype(F32)).astype(BF16)
+
+    by_rows(count, 32, scaled)
     stores[4].start()
     stores[5].start()
 
@@ -510,15 +522,15 @@
         load.wait()
     places = 2 * WIN * WIN
 
-    @pl.loop(0, count // places)
-    def _(w):
-        rows = aligned(w * places, places)
+    def block(rows):
         d = ngrad[rows].astype(F32)
         unit = normed[rows].astype(F32)
         mean_d = jnp.mean(d, axis=1, keepdims=True)
         mean_dx = jnp.mean(d * unit, axis=1, keepdims=True)
         part = rstd[rows, :1] * (d - mean_d - unit * mean_dx)
         full[rows] = (part.astype(BF16).astype(F32) + grad[rows].astype(F32)).astype(BF16)
+
+    by_rows(count, 32, block)
 
     (n_side, g_side), (n_above, g_above), (n_corner, g_corner) = strip_rows(None, None)
     side_cut = 2 * SHIFT * SHIFT
@@ -735,6 +747,7 @@
         [vmem] * 6,
         scratch_shapes=[
             pltpu.VMEM(qkv_weight.shape, BF16),
+            pltpu.VMEM((inner, channels), F32),
             pltpu.SemaphoreType.DMA((3 * channels // TILE,)),
         ],
         name="inner_windows", **settings(9),
@@ -758,7 +771,7 @@
             pltpu.VMEM((count, 3 * channels), BF16),
             pltpu.VMEM((count, channels), BF16),
             pltpu.VMEM((count, channels), F32),
-            pltpu.VMEM((4, groups, channels), BF16),
+            pltpu.VMEM((groups, 4 * channels), BF16),
             pltpu.VMEM((groups, 4 * channels), BF16),
             pltpu.VMEM((groups, merged_width), BF16),
             pltpu.VMEM((count, channels), BF16),
@@ -828,7 +841,9 @@
         name="input_backward", **settings(13, 40),
     )
     arrived1 = behind(arrived1, full)
-    strips = sent_strips(behind(strips, arrived1), sizes, -1)
+    early = [arrived2[0], arrived2[2]]
+    strips = sent_strips(behind(strips, (arrived1, early)), sizes, -1)
+    arrived1 = behind(arrived1, early)
 
     total1 = jnp.concatenate([layer0[0], layer1[0]], axis=1)
     for pair in zip(arrived0, arrived1):
@@ -837,12 +852,15 @@
     got1 = exchange(given1, sizes, 1, 0)
 
     part1 = kept1 + got1.astype(F32)
+    column2 = column_blocks(layer2[0], arrived2, sizes)
     bit = 2
-    while bit < sizes[0]:
+    while 2 * bit < sizes[0]:
         kept1, given1 = column_halves(part1, sizes, bit)
         part1 = kept1 + exchange(given1, sizes, bit, 0).astype(F32)
         bit *= 2
-    column2 = column_blocks(layer2[0], arrived2, sizes)
+    kept1, last1 = column_halves(part1, sizes, bit)
+    last_columns = last1.shape[1]
+    column2[bit] = jnp.concatenate([last1, column2[bit]], axis=1)
     got2 = column_step(column2, sizes)
 
     got = [Strips.sent(s, *t) for s, t in zip((cs.side, cs.above, cs.corner), to)]
@@ -859,7 +877,10 @@
         [vmem] * 9, [wide, shape(groups, merged_width)], [vmem] * 2,
         name="unpack_strips", **settings(20, 24),
     )
-    part2 = finished(column2[0], behind(got2, tokens_grad))
+    got2 = behind(got2, tokens_grad)
+    part1 = kept1 + got2[bit - 1][:, :last_columns].astype(F32)
+    got2[bit - 1] = got2[bit - 1][:, last_columns:]
+    part2 = finished(column2[0], got2)
     out_weight_grad = part1[:, :channels]
     part1 = part1[:, channels:]
 

time: 156 us -> 177 us (1.13)
  waiting for transfers between devices: 23 us -> 38.9 us
  Pallas kernels: 91.6 us -> 98.1 us
  starting transfers between devices: 25.8 us -> 23.5 us
  other arithmetic: 9.73 us -> 11.7 us
    ppermute x6, waiting for transfers between devices: 1.44 us -> 10.4 us  [sent(): return lax.ppermute(block, ('lat', 'lon'), route)]
    ppermute x17 -> x16, waiting for transfers between devices: 21.6 us -> 28.5 us  [exchange(): return lax.ppermute(block, ('lat', 'lon'), route)]
    pallas_call x1, Pallas kernels: 33.1 us -> 37.5 us  [shards(): pl.pallas_call(forward_kernel, out_shape=[wide, shape(channels, count), s...]
    ppermute x17 -> x16, starting transfers between devices: 17.5 us -> 13.4 us  [exchange(): return lax.ppermute(block, ('lat', 'lon'), route)]
    pallas_call x5, Pallas kernels: 55.3 us -> 57.5 us  [tied_call(): pl.pallas_call(body, out_shape=out_shape, in_specs=[pl.BlockSpec(memory_s...]
    concatenate x0 -> x2, other arithmetic: none -> 1.92 us  [the longest x1 1.13 us: shards(): total1 = total1 + jnp.concatenate(pair, axis=1).astype(F32)]
    ppermute x6, starting transfers between devices: 8.28 us -> 10.1 us  [sent(): return lax.ppermute(block, ('lat', 'lon'), route)]
  transfers between devices with their start and end apart: 23 -> 22, of which waited for: 8 -> 6; matrix products, arithmetic and copies ran while one was open for 6% -> 6% of each run, Pallas kernels for 35% -> 33%
where the time goes in v10:
time: 177 us; the launch traced here: 176 us
  Pallas kernels  98.1 us (55%)
  waiting for transfers between devices  38.9 us (22%)
  starting transfers between devices  23.5 us (13%)
  other arithmetic  11.7 us (7%)
  local copies, waits for them, and re-layouts  3.08 us (2%)
    pallas_call x5, Pallas kernels, tied_call(): pl.pallas_call(body, out_shape=out_shape, in_specs=[pl.BlockSpec(memory_s...  57.5 us
    pallas_call x1, Pallas kernels, shards(): pl.pallas_call(forward_kernel, out_shape=[wide, shape(channels, count), s...  37.5 us
    ppermute x16, waiting for transfers between devices, exchange(): return lax.ppermute(block, ('lat', 'lon'), route)  28.5 us
    ppermute x16, starting transfers between devices, exchange(): return lax.ppermute(block, ('lat', 'lon'), route)  13.4 us
    ppermute x6, waiting for transfers between devices, sent(): return lax.ppermute(block, ('lat', 'lon'), route)  10.4 us
    ppermute x6, starting transfers between devices, sent(): return lax.ppermute(block, ('lat', 'lon'), route)  10.1 us
  transfers between devices with their start and end apart: 22, of which 6 were waited for; matrix products, arithmetic and copies ran while one was open for 6% of the time, Pallas kernels for 33%

profile of v10, /device:TPU:0, one launch (start us, length us, event | category | flops | bytes accessed | tf_op | source)
XLA Modules:
  0.0 176.3 jit_solution(811082731402588737)
XLA Ops:
  0.6 3.1 %pack_strips.1 = (bf16[128,1024]{1,0:T(8,128)(2,1)}, bf16[208,1024]{1,0:T(8,128)(2,1)}, bf16[48,1024]{1,0:T(8,128)(2,1)}) custom-call(bf16[768,1024]{1,0:T(8,128)(2,1)} %bitcast.36, bf16[192,1024]{1,0:T(8,128)(2,1)} %bitcast.39, bf16[288,768]{1,0:T(8,128)(2,1)} %constant.41.clone.pick_cells, bf16[96,192]{1,0:T(8,128)(2,1)} %constant.42.clone.pick_groups), custom_call_target="tpu_custom_call" | custom-call | flops 10000000000 | bytes 16777216 | tf_op jit(solution)/shard_map/pack_strips/pallas_call | solution.py:724
  3.8 2.5 %collective-permute-start.2 = (bf16[48,1024]{1,0:T(8,128)(2,1)}, bf16[48,1024]{1,0:T(8,128)(2,1)S(1)}, u32[]{:S(2)}, u32[]{:S(2)}) collective-permute-start(bf16[48,1024]{1,0:T(8,128)(2,1)} %get-tuple-element.57.refs_2_), channel_id=1, source_target_pairs={{0,9},{1,10},{2,11},{3,12},{4,13},{5,14},{6,15},{7,8},{8,17},{9,18... | collective-permute-start | bytes 294920 | tf_op jit(solution)/shard_map/ppermute | solution.py:579
  6.2 1.6 collective-permute-start
  7.8 1.6 collective-permute-start.1
  9.4 11.3 %inner_windows.1 = (bf16[256,1024]{1,0:T(8,128)(2,1)}, bf16[256,1024]{1,0:T(8,128)(2,1)}, f32[256,128]{1,0:T(8,128)}, bf16[256,1024]{1,0:T(8,128)(2,1)}, f32[256,1024]{1,0:T(8,128)}, /*index=5*/bf16[256,3072]{1,0:T(8,128)(2,1)}) custom-call(bf16[128,1024]{1,0:T(8,128)(2,1)} %get-tuple-element.55.refs_0_, bf16[208,1024]{1,0:T(8,128)(2,1)} %get-tuple-element.56.refs_1_, ...), custom_call_target="tpu_custom_call" | custom-call | flops 89999998976 | bytes 16777216 | tf_op jit(solution)/shard_map/inner_windows/pallas_call | solution.py:670
  22.6 37.5 %block_forward.1 = (bf16[768,1024]{1,0:T(8,128)(2,1)}, bf16[1024,768]{1,0:T(8,128)(2,1)}, bf16[768,3072]{1,0:T(8,128)(2,1)}, bf16[768,1024]{1,0:T(8,128)(2,1)}, ...) custom-call(s32[1]{0:T(128)} %bitcast.edge.refs_0_.refs_3_, ...), custom_call_target="tpu_custom_call" | custom-call | flops 299999985664 | bytes 16777216 | tf_op jit(solution)/shard_map/block_forward/pallas_call | solution.py:755
  60.2 14.1 %attention_backward.2 = (bf16[768,1536]{1,0:T(8,128)(2,1)S(1)}, bf16[512,1536]{1,0:T(8,128)(2,1)S(1)}, bf16[512,1536]{1,0:T(8,128)(2,1)}) custom-call(s32[1]{0:T(128)} %bitcast.edge.refs_0_.refs_3_, bf16[768,3072]{1,0:T(8,128)(2,1)} %get-tuple-element.66.refs_1_.refs_4_, bf16[768,1024]{1,0:T(8,128)(2,1)} %get-tuple-element.67.refs_2_.refs_5_, ...), custom_call_target="tpu_custom_call" | custom-call | flops 149999992832 | bytes 16777216 | tf_op jit(solution)/shard_map/attention_backward/pallas_call | solution.py:670
  74.9 2.5 %convert_add_fusion.2 = (f32[128,1024]{1,0:T(8,128)}, bf16[128,1024]{1,0:T(8,128)(2,1)}, bf16[128,1024]{1,0:T(8,128)(2,1)}, bf16[128,1024]{1,0:T(8,128)(2,1)}) fusion(bf16[512,1024]{1,0:T(8,128)(2,1)} %collective-permute-done.3, bf16[512,1024]{1,0:T(8,128)(2,1)S(1)} %copy-done.10), kind=kLoop, calls=%fused_computation.17 | loop fusion | flops 1966080 | bytes 3407872 | tf_op jit(solution)/shard_map/add | solution.py:619
  77.4 1.6 collective-permute-start.7
  79.0 1.3 collective-permute-start.6
  80.9 13.4 %attention_backward.3 = (bf16[768,1536]{1,0:T(8,128)(2,1)S(1)}, bf16[512,1536]{1,0:T(8,128)(2,1)S(1)}, bf16[512,1536]{1,0:T(8,128)(2,1)S(1)}) custom-call(bf16[128,1024]{1,0:T(8,128)(2,1)} %get-tuple-element.118.refs_0_, bf16[128,1024]{1,0:T(8,128)(2,1)} %get-tuple-element.117.refs_1_, bf16[128,1024]{1,0:T(8,128)(2,1)} %get-tuple-element.116.refs_2_, ...), custom_call_target="tpu_custom_call" | custom-call | flops 149999992832 | bytes 16777216 | tf_op jit(solution)/shard_map/attention_backward/pallas_call | solution.py:670
  94.4 1.7 add_convert_fusion
  96.1 1.7 collective-permute-start.14
  97.7 1.3 collective-permute-start.13
  100.0 1.5 collective-permute-start.9
  101.5 1.5 collective-permute-start.11
  103.0 16.5 %input_backward.1 = (bf16[768,1024]{1,0:T(8,128)(2,1)S(1)}, bf16[128,1024]{1,0:T(8,128)(2,1)S(1)}, bf16[208,1024]{1,0:T(8,128)(2,1)S(1)}, bf16[48,1024]{1,0:T(8,128)(2,1)S(1)}) custom-call(bf16[128,1536]{1,0:T(8,128)(2,1)S(1)} %get-tuple-element.110.refs_0_, bf16[128,1536]{1,0:T(8,128)(2,1)S(1)} %get-tuple-element.109.refs_1_, ...), custom_call_target="tpu_custom_call" | custom-call | flops 130000003072 | bytes 16777216 | tf_op jit(solution)/shard_map/input_backward/pallas_call | solution.py:670
  120.2 5.7 %collective-permute-done.9 = bf16[128,1536]{1,0:T(8,128)(2,1)S(1)} collective-permute-done((bf16[128,1536]{1,0:T(8,128)(2,1)S(1)}, bf16[128,1536]{1,0:T(8,128)(2,1)S(1)}, u32[]{:S(2)}, u32[]{:S(2)}) %collective-permute-start.9) | collective-permute-done | bytes 393248 | tf_op jit(solution)/shard_map/ppermute | solution.py:608
  125.9 8.1 %collective-permute-done.11 = bf16[128,1536]{1,0:T(8,128)(2,1)S(1)} collective-permute-done((bf16[128,1536]{1,0:T(8,128)(2,1)S(1)}, bf16[128,1536]{1,0:T(8,128)(2,1)S(1)}, u32[]{:S(2)}, u32[]{:S(2)}) %collective-permute-start.11) | collective-permute-done | bytes 393248 | tf_op jit(solution)/shard_map/ppermute | solution.py:608
  134.0 1.1 pad_maximum_fusion.1
  135.1 1.3 fusion.1
  136.5 2.5 %collective-permute-start.18 = (bf16[48,1024]{1,0:T(8,128)(2,1)S(1)}, bf16[48,1024]{1,0:T(8,128)(2,1)S(1)}, u32[]{:S(2)}, u32[]{:S(2)}) collective-permute-start(bf16[48,1024]{1,0:T(8,128)(2,1)S(1)} %get-tuple-element.100), channel_id=1, source_target_pairs={{0,31},{1,24},{2,25},{3,26},{4,27},{5,28},{6,29},{7,30},{8,7},{9,0... | collective-permute-start | bytes 294920 | tf_op jit(solution)/shard_map/ppermute | solution.py:579
  139.0 1.0 collective-permute-start.16
  140.1 1.2 fusion.6
  142.0 1.8 %collective-permute-start.21 = (bf16[32,1536]{1,0:T(8,128)(2,1)}, bf16[32,1536]{1,0:T(8,128)(2,1)}, u32[]{:S(2)}, u32[]{:S(2)}) collective-permute-start(bf16[32,1536]{1,0:T(8,128)(2,1)} %get-tuple-element.119.refs_2_), channel_id=1, source_target_pairs={{0,24},{1,25},{2,26},{3,27},{4,28},{5,29},{6,30},{7,31},{8,16},{9,... | collective-permute-start | bytes 294920 | tf_op jit(solution)/shard_map/ppermute | solution.py:608
  144.0 8.8 %collective-permute-done.15 = bf16[64,2560]{1,0:T(8,128)(2,1)S(1)} collective-permute-done((bf16[64,2560]{1,0:T(8,128)(2,1)S(1)}, bf16[64,2560]{1,0:T(8,128)(2,1)S(1)}, u32[]{:S(2)}, u32[]{:S(2)}) %collective-permute-start.15) | collective-permute-done | bytes 327712 | tf_op jit(solution)/shard_map/ppermute | solution.py:608
  152.8 0.9 collective-permute-start.17
  154.6 10.0 %collective-permute-done.17.refs_7_ = bf16[208,1024]{1,0:T(8,128)(2,1)S(1)} collective-permute-done((bf16[208,1024]{1,0:T(8,128)(2,1)S(1)}, bf16[208,1024]{1,0:T(8,128)(2,1)S(1)}, u32[]{:S(2)}, u32[]{:S(2)}) %collective-permute-start.17) | collective-permute-done | bytes 426016 | tf_op jit(solution)/shard_map/ppermute | solution.py:579
  164.7 2.1 %unpack_strips.1 = (bf16[768,1024]{1,0:T(8,128)(2,1)}, bf16[192,1024]{1,0:T(8,128)(2,1)}) custom-call(bf16[32,1536]{1,0:T(8,128)(2,1)} %get-tuple-element.121.refs_0_, bf16[32,4096]{1,0:T(8,128)(2,1)} %pad_maximum_fusion.4.refs_1_, bf16[32,1536]{1,0:T(8,128)(2,1)} %get-tuple-element.119.refs_2_, bf16[64,2560]{1,0:T(8,128)(2,1)S(1)} %bitcast.28, ...), custom_call_target="tpu_custom_call" | custom-call | flops 199999995904 | bytes 16777216 | tf_op jit(solution)/shard_map/unpack_strips/pallas_call | solution.py:670
  166.8 5.8 %collective-permute-done.20 = bf16[32,4096]{1,0:T(8,128)(2,1)} collective-permute-done((bf16[32,4096]{1,0:T(8,128)(2,1)}, bf16[32,4096]{1,0:T(8,128)(2,1)}, u32[]{:S(2)}, u32[]{:S(2)}) %collective-permute-start.20) | collective-permute-done | bytes 262176 | tf_op jit(solution)/shard_map/ppermute | solution.py:608
  172.6 1.0 fusion.2
  174.3 1.1 fusion.4
  (76 shorter events, 7.8 us)
Async XLA Ops:
  3.8 17.6 %collective-permute-start.2 = (bf16[48,1024]{1,0:T(8,128)(2,1)}, bf16[48,1024]{1,0:T(8,128)(2,1)S(1)}, u32[]{:S(2)}, u32[]{:S(2)}) collective-permute-start(bf16[48,1024]{1,0:T(8,128)(2,1)} %get-tuple-element.57.refs_2_), channel_id=1, source_target_pairs={{0,9},{1,10},{2,11},{3,12},{4,13},{5,14},{6,15},{7,8},{8,17},{9,18... | collective-permute-start | bytes 294920 | tf_op jit(solution)/shard_map/ppermute | solution.py:579
  6.2 15.2 %collective-permute-start = (bf16[128,1024]{1,0:T(8,128)(2,1)}, bf16[128,1024]{1,0:T(8,128)(2,1)S(1)}, u32[]{:S(2)}, u32[]{:S(2)}) collective-permute-start(bf16[128,1024]{1,0:T(8,128)(2,1)} %get-tuple-element.55.refs_0_), channel_id=1, source_target_pairs={{0,1},{1,2},{2,3},{3,4},{4,5},{5,6},{6,7},{7,0},{8,9},{9,10},{10,1... | collective-permute-start | bytes 786440 | tf_op jit(solution)/shard_map/ppermute | solution.py:579
  7.8 12.9 %copy-start.12 = (s32[32]{0:T(128)S(1)}, s32[32]{0:T(128)}, u32[]{:S(2)}) copy-start(s32[32]{0:T(128)} %constant.47.clone) | copy-start | bytes 388
  7.8 12.9 %copy-start.13 = (s32[32]{0:T(128)S(1)}, s32[32]{0:T(128)}, u32[]{:S(2)}) copy-start(s32[32]{0:T(128)} %constant.46.clone) | copy-start | bytes 388
  7.8 14.0 %collective-permute-start.1 = (bf16[208,1024]{1,0:T(8,128)(2,1)}, bf16[208,1024]{1,0:T(8,128)(2,1)S(1)}, u32[]{:S(2)}, u32[]{:S(2)}) collective-permute-start(bf16[208,1024]{1,0:T(8,128)(2,1)} %get-tuple-element.56.refs_1_), channel_id=1, source_target_pairs={{0,8},{1,9},{2,10},{3,11},{4,12},{5,13},{6,14},{7,15},{8,16},{9,17... | collective-permute-start | bytes 1277960 | tf_op jit(solution)/shard_map/ppermute | solution.py:579
  60.1 14.8 %collective-permute-start.3 = (bf16[512,1024]{1,0:T(8,128)(2,1)}, bf16[512,1024]{1,0:T(8,128)(2,1)}, u32[]{:S(2)}, u32[]{:S(2)}) collective-permute-start(bf16[512,1024]{1,0:T(8,128)(2,1)} %get-tuple-element.65), channel_id=1, source_target_pairs={{0,1},{1,0},{2,3},{3,2},{4,5},{5,4},{6,7},{7,6},{8,9},{9,8},{10,11... | collective-permute-start | bytes 3145736 | tf_op jit(solution)/shard_map/ppermute | solution.py:608
  60.2 14.7 %copy-start.10 = (bf16[512,1024]{1,0:T(8,128)(2,1)S(1)}, bf16[512,1024]{1,0:T(8,128)(2,1)}, u32[]{:S(2)}) copy-start(bf16[512,1024]{1,0:T(8,128)(2,1)} %get-tuple-element.71) | copy-start | bytes 3145732
  74.3 20.0 %collective-permute-start.4 = (bf16[512,1536]{1,0:T(8,128)(2,1)}, bf16[512,1536]{1,0:T(8,128)(2,1)}, u32[]{:S(2)}, u32[]{:S(2)}) collective-permute-start(bf16[512,1536]{1,0:T(8,128)(2,1)} %get-tuple-element.76), channel_id=1, source_target_pairs={{0,1},{1,0},{2,3},{3,2},{4,5},{5,4},{6,7},{7,6},{8,9},{9,8},{10,11... | collective-permute-start | bytes 4718600 | tf_op jit(solution)/shard_map/ppermute | solution.py:608
  77.4 16.9 %collective-permute-start.7 = (bf16[128,1024]{1,0:T(8,128)(2,1)}, bf16[128,1024]{1,0:T(8,128)(2,1)}, u32[]{:S(2)}, u32[]{:S(2)}) collective-permute-start(bf16[128,1024]{1,0:T(8,128)(2,1)} %get-tuple-element.116.refs_2_), channel_id=1, source_target_pairs={{0,6},{1,7},{2,4},{3,5},{4,2},{5,3},{6,0},{7,1},{8,14},{9,15},{10,... | collective-permute-start | bytes 786440 | tf_op jit(solution)/shard_map/ppermute | solution.py:608
  79.0 15.3 %collective-permute-start.6 = (bf16[128,1024]{1,0:T(8,128)(2,1)}, bf16[128,1024]{1,0:T(8,128)(2,1)}, u32[]{:S(2)}, u32[]{:S(2)}) collective-permute-start(bf16[128,1024]{1,0:T(8,128)(2,1)} %get-tuple-element.117.refs_1_), channel_id=1, source_target_pairs={{0,4},{1,5},{2,6},{3,7},{4,0},{5,1},{6,2},{7,3},{8,12},{9,13},{10,... | collective-permute-start | bytes 786440 | tf_op jit(solution)/shard_map/ppermute | solution.py:608
  80.3 13.9 %collective-permute-start.5 = (bf16[128,1024]{1,0:T(8,128)(2,1)}, bf16[128,1024]{1,0:T(8,128)(2,1)}, u32[]{:S(2)}, u32[]{:S(2)}) collective-permute-start(bf16[128,1024]{1,0:T(8,128)(2,1)} %get-tuple-element.118.refs_0_), channel_id=1, source_target_pairs={{0,2},{1,3},{2,0},{3,1},{4,6},{5,7},{6,4},{7,5},{8,10},{9,11},{10,... | collective-permute-start | bytes 786440 | tf_op jit(solution)/shard_map/ppermute | solution.py:608
  94.3 5.4 %collective-permute-start.8 = (bf16[512,1536]{1,0:T(8,128)(2,1)S(1)}, bf16[512,1536]{1,0:T(8,128)(2,1)S(1)}, u32[]{:S(2)}, u32[]{:S(2)}) collective-permute-start(bf16[512,1536]{1,0:T(8,128)(2,1)S(1)} %get-tuple-element.81), channel_id=1, source_target_pairs={{0,1},{1,0},{2,3},{3,2},{4,5},{5,4},{6,7},{7,6},{8,9},{9,8},{10,11... | collective-permute-start | bytes 4718600 | tf_op jit(solution)/shard_map/ppermute | solution.py:608
  96.1 23.5 %collective-permute-start.14 = (bf16[128,1536]{1,0:T(8,128)(2,1)S(1)}, bf16[128,1536]{1,0:T(8,128)(2,1)S(1)}, u32[]{:S(2)}, u32[]{:S(2)}) collective-permute-start(bf16[128,1536]{1,0:T(8,128)(2,1)S(1)} %get-tuple-element.108.refs_2_), channel_id=1, source_target_pairs={{0,6},{1,7},{2,4},{3,5},{4,2},{5,3},{6,0},{7,1},{8,14},{9,15},{10,... | collective-permute-start | bytes 1179656 | tf_op jit(solution)/shard_map/ppermute | solution.py:608
  97.7 22.4 %collective-permute-start.13 = (bf16[128,1536]{1,0:T(8,128)(2,1)S(1)}, bf16[128,1536]{1,0:T(8,128)(2,1)S(1)}, u32[]{:S(2)}, u32[]{:S(2)}) collective-permute-start(bf16[128,1536]{1,0:T(8,128)(2,1)S(1)} %get-tuple-element.109.refs_1_), channel_id=1, source_target_pairs={{0,4},{1,5},{2,6},{3,7},{4,0},{5,1},{6,2},{7,3},{8,12},{9,13},{10,... | collective-permute-start | bytes 1179656 | tf_op jit(solution)/shard_map/ppermute | solution.py:608
  99.1 21.1 %collective-permute-start.12 = (bf16[128,1536]{1,0:T(8,128)(2,1)S(1)}, bf16[128,1536]{1,0:T(8,128)(2,1)S(1)}, u32[]{:S(2)}, u32[]{:S(2)}) collective-permute-start(bf16[128,1536]{1,0:T(8,128)(2,1)S(1)} %get-tuple-element.110.refs_0_), channel_id=1, source_target_pairs={{0,2},{1,3},{2,0},{3,1},{4,6},{5,7},{6,4},{7,5},{8,10},{9,11},{10,... | collective-permute-start | bytes 1179656 | tf_op jit(solution)/shard_map/ppermute | solution.py:608
  99.7 3.4 %copy-start.6 = (bf16[64,384]{1,0:T(8,128)(2,1)S(1)}, bf16[64,384]{1,0:T(8,128)(2,1)}, u32[]{:S(2)}) copy-start(bf16[64,384]{1,0:T(8,128)(2,1)} %constant.49.clone.refs_14_) | copy-start | bytes 147460
  100.0 25.9 %collective-permute-start.9 = (bf16[128,1536]{1,0:T(8,128)(2,1)S(1)}, bf16[128,1536]{1,0:T(8,128)(2,1)S(1)}, u32[]{:S(2)}, u32[]{:S(2)}) collective-permute-start(bf16[128,1536]{1,0:T(8,128)(2,1)S(1)} %get-tuple-element.112.refs_3_), channel_id=1, source_target_pairs={{0,2},{1,3},{2,0},{3,1},{4,6},{5,7},{6,4},{7,5},{8,10},{9,11},{10,... | collective-permute-start | bytes 1179656 | tf_op jit(solution)/shard_map/ppermute | solution.py:608
  101.5 32.5 %collective-permute-start.11 = (bf16[128,1536]{1,0:T(8,128)(2,1)S(1)}, bf16[128,1536]{1,0:T(8,128)(2,1)S(1)}, u32[]{:S(2)}, u32[]{:S(2)}) collective-permute-start(bf16[128,1536]{1,0:T(8,128)(2,1)S(1)} %get-tuple-element.113.refs_5_), channel_id=1, source_target_pairs={{0,6},{1,7},{2,4},{3,5},{4,2},{5,3},{6,0},{7,1},{8,14},{9,15},{10,... | collective-permute-start | bytes 1179656 | tf_op jit(solution)/shard_map/ppermute | solution.py:608
  119.5 15.6 %copy-start.8 = (f32[128,1024]{1,0:T(8,128)S(1)}, f32[128,1024]{1,0:T(8,128)}, u32[]{:S(2)}) copy-start(f32[128,1024]{1,0:T(8,128)} %get-tuple-element.115) | copy-start | bytes 1572868
  119.6 20.5 %collective-permute-start.10 = (bf16[128,1536]{1,0:T(8,128)(2,1)S(1)}, bf16[128,1536]{1,0:T(8,128)(2,1)S(1)}, u32[]{:S(2)}, u32[]{:S(2)}) collective-permute-start(bf16[128,1536]{1,0:T(8,128)(2,1)S(1)} %get-tuple-element.114.refs_4_), channel_id=1, source_target_pairs={{0,4},{1,5},{2,6},{3,7},{4,0},{5,1},{6,2},{7,3},{8,12},{9,13},{10,... | collective-permute-start | bytes 1179656 | tf_op jit(solution)/shard_map/ppermute | solution.py:608
  136.5 18.1 %collective-permute-start.18 = (bf16[48,1024]{1,0:T(8,128)(2,1)S(1)}, bf16[48,1024]{1,0:T(8,128)(2,1)S(1)}, u32[]{:S(2)}, u32[]{:S(2)}) collective-permute-start(bf16[48,1024]{1,0:T(8,128)(2,1)S(1)} %get-tuple-element.100), channel_id=1, source_target_pairs={{0,31},{1,24},{2,25},{3,26},{4,27},{5,28},{6,29},{7,30},{8,7},{9,0... | collective-permute-start | bytes 294920 | tf_op jit(solution)/shard_map/ppermute | solution.py:579
  139.0 15.6 %collective-permute-start.16 = (bf16[128,1024]{1,0:T(8,128)(2,1)S(1)}, bf16[128,1024]{1,0:T(8,128)(2,1)S(1)}, u32[]{:S(2)}, u32[]{:S(2)}) collective-permute-start(bf16[128,1024]{1,0:T(8,128)(2,1)S(1)} %get-tuple-element.98), channel_id=1, source_target_pairs={{0,7},{1,0},{2,1},{3,2},{4,3},{5,4},{6,5},{7,6},{8,15},{9,8},{10,9... | collective-permute-start | bytes 786440 | tf_op jit(solution)/shard_map/ppermute | solution.py:579
  140.1 12.8 %collective-permute-start.15 = (bf16[64,2560]{1,0:T(8,128)(2,1)S(1)}, bf16[64,2560]{1,0:T(8,128)(2,1)S(1)}, u32[]{:S(2)}, u32[]{:S(2)}) collective-permute-start(bf16[64,2560]{1,0:T(8,128)(2,1)S(1)} %bitcast.27), channel_id=1, source_target_pairs={{0,8},{1,9},{2,10},{3,11},{4,12},{5,13},{6,14},{7,15},{8,0},{9,1},... | collective-permute-start | bytes 983048 | tf_op jit(solution)/shard_map/ppermute | solution.py:608
  141.3 23.4 %copy-start = (bf16[384,448]{1,0:T(8,128)(2,1)S(1)}, bf16[384,448]{1,0:T(8,128)(2,1)}, u32[]{:S(2)}) copy-start(bf16[384,448]{1,0:T(8,128)(2,1)} %constant.52.clone.refs_10_) | copy-start | bytes 1032196
  141.3 23.4 %copy-start.1 = (bf16[192,416]{1,0:T(8,128)(2,1)S(1)}, bf16[192,416]{1,0:T(8,128)(2,1)}, u32[]{:S(2)}) copy-start(bf16[192,416]{1,0:T(8,128)(2,1)} %constant.51.clone.refs_9_) | copy-start | bytes 479236
  141.3 23.4 %copy-start.3 = (bf16[192,288]{1,0:T(8,128)(2,1)S(1)}, bf16[192,288]{1,0:T(8,128)(2,1)}, u32[]{:S(2)}) copy-start(bf16[192,288]{1,0:T(8,128)(2,1)} %constant.54.clone.refs_12_) | copy-start | bytes 331780
  141.3 23.4 %copy-start.4 = (bf16[192,192]{1,0:T(8,128)(2,1)S(1)}, bf16[192,192]{1,0:T(8,128)(2,1)}, u32[]{:S(2)}) copy-start(bf16[192,192]{1,0:T(8,128)(2,1)} %constant.53.clone.refs_11_) | copy-start | bytes 221188
  142.0 24.9 %collective-permute-start.21 = (bf16[32,1536]{1,0:T(8,128)(2,1)}, bf16[32,1536]{1,0:T(8,128)(2,1)}, u32[]{:S(2)}, u32[]{:S(2)}) collective-permute-start(bf16[32,1536]{1,0:T(8,128)(2,1)} %get-tuple-element.119.refs_2_), channel_id=1, source_target_pairs={{0,24},{1,25},{2,26},{3,27},{4,28},{5,29},{6,30},{7,31},{8,16},{9,... | collective-permute-start | bytes 294920 | tf_op jit(solution)/shard_map/ppermute | solution.py:608
  143.8 23.0 %collective-permute-start.19 = (bf16[32,1536]{1,0:T(8,128)(2,1)}, bf16[32,1536]{1,0:T(8,128)(2,1)}, u32[]{:S(2)}, u32[]{:S(2)}) collective-permute-start(bf16[32,1536]{1,0:T(8,128)(2,1)} %get-tuple-element.121.refs_0_), channel_id=1, source_target_pairs={{0,8},{1,9},{2,10},{3,11},{4,12},{5,13},{6,14},{7,15},{8,0},{9,1},... | collective-permute-start | bytes 294920 | tf_op jit(solution)/shard_map/ppermute | solution.py:608
  152.8 11.8 %collective-permute-start.17 = (bf16[208,1024]{1,0:T(8,128)(2,1)S(1)}, bf16[208,1024]{1,0:T(8,128)(2,1)S(1)}, u32[]{:S(2)}, u32[]{:S(2)}) collective-permute-start(bf16[208,1024]{1,0:T(8,128)(2,1)S(1)} %get-tuple-element.99), channel_id=1, source_target_pairs={{0,24},{1,25},{2,26},{3,27},{4,28},{5,29},{6,30},{7,31},{8,0},{9,1... | collective-permute-start | bytes 1277960 | tf_op jit(solution)/shard_map/ppermute | solution.py:579
  153.8 13.0 %copy-start.9 = (f32[64,2560]{1,0:T(8,128)}, f32[64,2560]{1,0:T(8,128)S(1)}, u32[]{:S(2)}) copy-start(f32[64,2560]{1,0:T(8,128)S(1)} %bitcast_add_fusion) | copy-start | bytes 1966084
  154.6 18.0 %collective-permute-start.20 = (bf16[32,4096]{1,0:T(8,128)(2,1)}, bf16[32,4096]{1,0:T(8,128)(2,1)}, u32[]{:S(2)}, u32[]{:S(2)}) collective-permute-start(bf16[32,4096]{1,0:T(8,128)(2,1)} %pad_maximum_fusion.4.refs_1_), channel_id=1, source_target_pairs={{0,16},{1,17},{2,18},{3,19},{4,20},{5,21},{6,22},{7,23},{8,24},{9,... | collective-permute-start | bytes 786440 | tf_op jit(solution)/shard_map/ppermute | solution.py:608
  (7 other events, 13.7 us)

commit v11 on v9

--- a/solution.py
+++ b/solution.py
@@ -14,6 +14,7 @@
 LANES = 128
 HALF = SHIFT // 2
 TILE = 256
+WIDE = 512
 EPSILON = 1e-05
 MIB = 1 << 20
 
@@ -151,10 +152,10 @@
 ):
     count, channels = xw.shape
     places = 2 * WIN * WIN
-    tiles = wqkv.shape[1] // TILE
+    tiles = wqkv.shape[1] // WIDE
 
     def load(n):
-        columns = aligned(n * TILE, TILE)
+        columns = aligned(n * WIDE, WIDE)
         return pltpu.make_async_copy(wqkv_h.at[:, columns], wqkv.at[:, columns], in_sem.at[n])
 
     for n in range(tiles):
@@ -173,7 +174,7 @@
     @pl.loop(0, tiles)
     def _(n):
         load(n).wait()
-        columns = aligned(n * TILE, TILE)
+        columns = aligned(n * WIDE, WIDE)
         proj[:, columns] = dot(normed[...], wqkv[:, columns]).astype(BF16)
 
     masks = head_masks()
@@ -253,9 +254,9 @@
     loads[0].wait()
     outer_rows = slice(0, outer)
 
-    @pl.loop(0, wqkv.shape[1] // TILE)
+    @pl.loop(0, wqkv.shape[1] // WIDE)
     def _(n):
-        columns = aligned(n * TILE, TILE)
+        columns = aligned(n * WIDE, WIDE)
         proj[outer_rows, columns] = dot(normed[outer_rows], wqkv[:, columns]).astype(BF16)
 
     for load in ready:
@@ -288,9 +289,9 @@
 
     loads[1].wait()
 
-    @pl.loop(0, channels // TILE)
+    @pl.loop(0, channels // WIDE)
     def _(n):
-        columns = aligned(n * TILE, TILE)
+        columns = aligned(n * WIDE, WIDE)
         out = dot(mixture[...], wout[:, columns]) + xw[:, columns].astype(F32)
         out = out.astype(BF16)
         for w in range(windows):
@@ -330,9 +331,9 @@
             grad[at:at + quarter] = d[w * quarter:(w + 1) * quarter]
     stores[3].start()
 
-    @pl.loop(0, channels // TILE)
+    @pl.loop(0, channels // WIDE)
     def _(n):
-        columns = aligned(n * TILE, TILE)
+        columns = aligned(n * WIDE, WIDE)
         d = dot(grad[...], wout[columns], NT).astype(BF16).astype(F32)
         d = d * inverse[:, columns]
         dmr[:, columns] = d.astype(BF16)
@@ -350,9 +351,9 @@
                 pick = jnp.where(spot == rowmap[rows], 1.0, 0.0).astype(BF16)
                 out[rows] = dot(pick, field[...], NT).astype(BF16)
         else:
-            @pl.loop(0, channels // TILE)
+            @pl.loop(0, channels // WIDE)
             def _(n):
-                rows = aligned(n * TILE, TILE)
+                rows = aligned(n * WIDE, WIDE)
                 turned[rows] = field[:, rows].T
 
             for d in range(devices):
@@ -364,11 +365,12 @@
     turn(mixture, mixt)
     part = channels // 2
 
-    @pl.loop(0, channels // TILE)
+    @pl.loop(0, channels // WIDE)
     def _(n):
-        columns = aligned(n * TILE, TILE)
-        out_mine[:, columns] = dot(mixt[:part], grad[:, columns]).astype(BF16)
-        out_theirs[:, columns] = dot(mixt[part:], grad[:, columns]).astype(BF16)
+        columns = aligned(n * WIDE, WIDE)
+        terms = dot(mixt[...], grad[:, columns]).astype(BF16)
+        out_mine[:, columns] = terms[:part]
+        out_theirs[:, columns] = terms[part:]
 
     for store in stores:
         store.wait()
@@ -455,8 +457,9 @@
 
         for i in range(3):
             columns = aligned(i * width + g * TILE, TILE)
-            mine[:, columns] = dot(normt[:half], pgrad[:, columns]).astype(BF16)
-            theirs[:, columns] = dot(normt[half:], pgrad[:, columns]).astype(BF16)
+            terms = dot(normt[...], pgrad[:, columns]).astype(BF16)
+            mine[:, columns] = terms[:half]
+            theirs[:, columns] = terms[half:]
         for store in stores(g):
             store.start()
 
@@ -501,11 +504,14 @@
         load.start()
     for load in loads:
         load.wait()
-    for n, load in enumerate(tiles):
+    for load in tiles:
         load.wait()
-        ngrad[:, pl.ds(n * TILE, TILE)] = dot(
-            pgrad[...], wqkv[pl.ds(n * TILE, TILE)], NT
-        ).astype(BF16)
+
+    @pl.loop(0, channels // WIDE)
+    def _(n):
+        rows = aligned(n * WIDE, WIDE)
+        ngrad[:, rows] = dot(pgrad[...], wqkv[rows], NT).astype(BF16)
+
     for load in more:
         load.wait()
     places = 2 * WIN * WIN
@@ -532,6 +538,22 @@
     side[n_side:] = groups[:g_side]
     below[n_above:] = groups[g_side:g_side + g_above]
     corner[n_corner:] = groups[g_side + g_above:]
+
+
+def end_kernel(bit, kept1, kept2, *refs):
+    arrived, (qkv, out) = refs[:-2], refs[-2:]
+    channels = out.shape[1]
+    columns = kept1.shape[1]
+    first = kept1[...] + arrived[bit - 1][:, :columns].astype(F32)
+    last = kept2[...]
+    for i, block in enumerate(arrived):
+        last += (block[:, columns:] if i == bit - 1 else block[...]).astype(F32)
+    out[...] = first[:, :channels]
+    width = channels // 2
+    for i in range(3):
+        at = i * channels
+        qkv[:, at:at + width] = first[:, channels + i * width:channels + (i + 1) * width]
+        qkv[:, at + width:at + channels] = last[:, i * width:(i + 1) * width]
 
 
 def unpack_kernel(full, merged, side, below, corner, pick_top, pick_middle, pick_bottom,
@@ -837,12 +859,14 @@
     got1 = exchange(given1, sizes, 1, 0)
 
     part1 = kept1 + got1.astype(F32)
+    column2 = column_blocks(layer2[0], arrived2, sizes)
     bit = 2
-    while bit < sizes[0]:
+    while 2 * bit < sizes[0]:
         kept1, given1 = column_halves(part1, sizes, bit)
         part1 = kept1 + exchange(given1, sizes, bit, 0).astype(F32)
         bit *= 2
-    column2 = column_blocks(layer2[0], arrived2, sizes)
+    kept1, last1 = column_halves(part1, sizes, bit)
+    column2[bit] = jnp.concatenate([last1, column2[bit]], axis=1)
     got2 = column_step(column2, sizes)
 
     got = [Strips.sent(s, *t) for s, t in zip((cs.side, cs.above, cs.corner), to)]
@@ -859,16 +883,16 @@
         [vmem] * 9, [wide, shape(groups, merged_width)], [vmem] * 2,
         name="unpack_strips", **settings(20, 24),
     )
-    part2 = finished(column2[0], behind(got2, tokens_grad))
-    out_weight_grad = part1[:, :channels]
-    part1 = part1[:, channels:]
-
+    got2 = behind(got2, tokens_grad)
+    qkv_weight_grad, out_weight_grad = pl.pallas_call(
+        functools.partial(end_kernel, bit),
+        out_shape=[
+            shape(kept1.shape[0], 3 * channels, dtype=F32), shape(kept1.shape[0], channels, dtype=F32),
+        ],
+        in_specs=[vmem] * (2 + len(got2)), out_specs=[vmem] * 2,
+        name="end_sums", **settings(1, 16),
+    )(kept1, column2[0], *got2)
     merged = merged.reshape(levels, g_cols, g_rows, merged_width).transpose(0, 2, 1, 3)
-
-    qkv_weight_grad = jnp.concatenate(
-        [part[:, i * width:(i + 1) * width] for i in range(3) for part in (part1, part2)],
-        axis=1,
-    )
     return merged, tokens_grad.reshape(tokens.shape), qkv_weight_grad, out_weight_grad
 
 

time: 156 us -> 156 us (level)
  waiting for transfers between devices: 23 us -> 32.2 us
  Pallas kernels: 91.6 us -> 87.1 us
  local copies, waits for them, and re-layouts: 4.81 us -> 2.47 us
    ppermute x17 -> x16, waiting for transfers between devices: 21.6 us -> 29.8 us  [exchange(): return lax.ppermute(block, ('lat', 'lon'), route)]
    pallas_call x5, Pallas kernels: 55.3 us -> 51.3 us  [tied_call(): pl.pallas_call(body, out_shape=out_shape, in_specs=[pl.BlockSpec(memory_s...]
    pallas_call x1, Pallas kernels: 33.1 us -> 30.8 us  [shards(): pl.pallas_call(forward_kernel, out_shape=[wide, shape(channels, count), s...]
    add x2 -> x0, other arithmetic: 2.07 us -> none  [the longest x1 1.12 us: finished(): kept = kept + block.astype(F32)]
    concatenate x0 -> x2, other arithmetic: none -> 1.85 us  [the longest x1 1.13 us: shards(): total1 = total1 + jnp.concatenate(pair, axis=1).astype(F32)]
    pallas_call x0 -> x1, Pallas kernels: none -> 1.83 us  [shards(): pl.pallas_call(functools.partial(end_kernel, bit), out_shape=[shape(kept1...]
    ppermute x17 -> x16, starting transfers between devices: 17.5 us -> 15.8 us  [exchange(): return lax.ppermute(block, ('lat', 'lon'), route)]
  transfers between devices with their start and end apart: 23 -> 22, of which waited for: 8 -> 9; matrix products, arithmetic and copies ran while one was open for 6% -> 4% of each run, Pallas kernels for 35% -> 33%
where the time goes in v11:
time: 156 us
  Pallas kernels  87.1 us (56%)
  waiting for transfers between devices  32.2 us (21%)
  starting transfers between devices  24.5 us (16%)
  other arithmetic  8.54 us (5%)
  local copies, waits for them, and re-layouts  2.47 us (2%)
    pallas_call x5, Pallas kernels, tied_call(): pl.pallas_call(body, out_shape=out_shape, in_specs=[pl.BlockSpec(memory_s...  51.3 us
    pallas_call x1, Pallas kernels, shards(): pl.pallas_call(forward_kernel, out_shape=[wide, shape(channels, count), s...  30.8 us
    ppermute x16, waiting for transfers between devices, exchange(): return lax.ppermute(block, ('lat', 'lon'), route)  29.8 us
    ppermute x16, starting transfers between devices, exchange(): return lax.ppermute(block, ('lat', 'lon'), route)  15.8 us
    ppermute x6, starting transfers between devices, sent(): return lax.ppermute(block, ('lat', 'lon'), route)  8.71 us
    pallas_call x1, Pallas kernels, shards(): pl.pallas_call(pack_kernel, out_shape=[shape(*e) for e in extents], in_sp...  3.14 us
  transfers between devices with their start and end apart: 22, of which 9 were waited for; matrix products, arithmetic and copies ran while one was open for 4% of the time, Pallas kernels for 33%

profile of v11, /device:TPU:0, one launch (start us, length us, event | category | flops | bytes accessed | tf_op | source)
XLA Modules:
  0.0 155.8 jit_solution(11392896392246170787)
XLA Ops:
  0.6 3.1 %pack_strips.1 = (bf16[128,1024]{1,0:T(8,128)(2,1)}, bf16[208,1024]{1,0:T(8,128)(2,1)}, bf16[48,1024]{1,0:T(8,128)(2,1)}) custom-call(bf16[768,1024]{1,0:T(8,128)(2,1)} %bitcast.34, bf16[192,1024]{1,0:T(8,128)(2,1)} %bitcast.37, bf16[288,768]{1,0:T(8,128)(2,1)} %constant.41.clone.pick_cells, bf16[96,192]{1,0:T(8,128)(2,1)} %constant.42.clone.pick_groups), custom_call_target="tpu_custom_call" | custom-call | flops 10000000000 | bytes 16777216 | tf_op jit(solution)/shard_map/pack_strips/pallas_call | solution.py:734
  3.8 2.5 %collective-permute-start.2 = (bf16[48,1024]{1,0:T(8,128)(2,1)}, bf16[48,1024]{1,0:T(8,128)(2,1)S(1)}, u32[]{:S(2)}, u32[]{:S(2)}) collective-permute-start(bf16[48,1024]{1,0:T(8,128)(2,1)} %get-tuple-element.56.refs_2_), channel_id=1, source_target_pairs={{0,9},{1,10},{2,11},{3,12},{4,13},{5,14},{6,15},{7,8},{8,17},{9,18... | collective-permute-start | bytes 294920 | tf_op jit(solution)/shard_map/ppermute | solution.py:589
  6.2 1.6 %collective-permute-start = (bf16[128,1024]{1,0:T(8,128)(2,1)}, bf16[128,1024]{1,0:T(8,128)(2,1)S(1)}, u32[]{:S(2)}, u32[]{:S(2)}) collective-permute-start(bf16[128,1024]{1,0:T(8,128)(2,1)} %get-tuple-element.54.refs_0_), channel_id=1, source_target_pairs={{0,1},{1,2},{2,3},{3,4},{4,5},{5,6},{6,7},{7,0},{8,9},{9,10},{10,1... | collective-permute-start | bytes 786440 | tf_op jit(solution)/shard_map/ppermute | solution.py:589
  7.8 1.6 %collective-permute-start.1 = (bf16[208,1024]{1,0:T(8,128)(2,1)}, bf16[208,1024]{1,0:T(8,128)(2,1)S(1)}, u32[]{:S(2)}, u32[]{:S(2)}) collective-permute-start(bf16[208,1024]{1,0:T(8,128)(2,1)} %get-tuple-element.55.refs_1_), channel_id=1, source_target_pairs={{0,8},{1,9},{2,10},{3,11},{4,12},{5,13},{6,14},{7,15},{8,16},{9,17... | collective-permute-start | bytes 1277960 | tf_op jit(solution)/shard_map/ppermute | solution.py:589
  9.4 9.4 %inner_windows.1 = (bf16[256,1024]{1,0:T(8,128)(2,1)}, bf16[256,1024]{1,0:T(8,128)(2,1)}, f32[256,128]{1,0:T(8,128)}, bf16[256,1024]{1,0:T(8,128)(2,1)}, f32[256,1024]{1,0:T(8,128)}, /*index=5*/bf16[256,3072]{1,0:T(8,128)(2,1)}) custom-call(bf16[128,1024]{1,0:T(8,128)(2,1)} %get-tuple-element.54.refs_0_, bf16[208,1024]{1,0:T(8,128)(2,1)} %get-tuple-element.55.refs_1_, ...), custom_call_target="tpu_custom_call" | custom-call | flops 89999998976 | bytes 16777216 | tf_op jit(solution)/shard_map/inner_windows/pallas_call | solution.py:680
  19.5 2.3 %collective-permute-done.1.above = bf16[208,1024]{1,0:T(8,128)(2,1)S(1)} collective-permute-done((bf16[208,1024]{1,0:T(8,128)(2,1)}, bf16[208,1024]{1,0:T(8,128)(2,1)S(1)}, u32[]{:S(2)}, u32[]{:S(2)}) %collective-permute-start.1) | collective-permute-done | bytes 426016 | tf_op jit(solution)/shard_map/ppermute | solution.py:589
  22.6 30.8 %block_forward.1 = (bf16[768,1024]{1,0:T(8,128)(2,1)}, bf16[1024,768]{1,0:T(8,128)(2,1)}, bf16[768,3072]{1,0:T(8,128)(2,1)}, bf16[768,1024]{1,0:T(8,128)(2,1)}, ...) custom-call(s32[1]{0:T(128)} %bitcast.edge.refs_0_.refs_3_, ...), custom_call_target="tpu_custom_call" | custom-call | flops 299999985664 | bytes 16777216 | tf_op jit(solution)/shard_map/block_forward/pallas_call | solution.py:764
  53.5 14.2 %attention_backward.2 = (bf16[768,1536]{1,0:T(8,128)(2,1)S(1)}, bf16[512,1536]{1,0:T(8,128)(2,1)S(1)}, bf16[512,1536]{1,0:T(8,128)(2,1)}) custom-call(s32[1]{0:T(128)} %bitcast.edge.refs_0_.refs_3_, bf16[768,3072]{1,0:T(8,128)(2,1)} %get-tuple-element.65.refs_1_.refs_4_, bf16[768,1024]{1,0:T(8,128)(2,1)} %get-tuple-element.66.refs_2_.refs_5_, ...), custom_call_target="tpu_custom_call" | custom-call | flops 149999992832 | bytes 16777216 | tf_op jit(solution)/shard_map/attention_backward/pallas_call | solution.py:680
  68.3 2.5 %convert_add_fusion.2 = (f32[128,1024]{1,0:T(8,128)}, bf16[128,1024]{1,0:T(8,128)(2,1)}, bf16[128,1024]{1,0:T(8,128)(2,1)}, bf16[128,1024]{1,0:T(8,128)(2,1)}) fusion(bf16[512,1024]{1,0:T(8,128)(2,1)} %collective-permute-done.3, bf16[512,1024]{1,0:T(8,128)(2,1)S(1)} %copy-done.9), kind=kLoop, calls=%fused_computation.17 | loop fusion | flops 1966080 | bytes 3407872 | tf_op jit(solution)/shard_map/add | solution.py:629
  70.8 1.6 %collective-permute-start.7 = (bf16[128,1024]{1,0:T(8,128)(2,1)}, bf16[128,1024]{1,0:T(8,128)(2,1)}, u32[]{:S(2)}, u32[]{:S(2)}) collective-permute-start(bf16[128,1024]{1,0:T(8,128)(2,1)} %get-tuple-element.114.refs_2_), channel_id=1, source_target_pairs={{0,6},{1,7},{2,4},{3,5},{4,2},{5,3},{6,0},{7,1},{8,14},{9,15},{10,... | collective-permute-start | bytes 786440 | tf_op jit(solution)/shard_map/ppermute | solution.py:618
  72.4 1.4 collective-permute-start.6
  74.3 13.4 %attention_backward.3 = (bf16[768,1536]{1,0:T(8,128)(2,1)S(1)}, bf16[512,1536]{1,0:T(8,128)(2,1)S(1)}, bf16[512,1536]{1,0:T(8,128)(2,1)S(1)}) custom-call(bf16[128,1024]{1,0:T(8,128)(2,1)} %get-tuple-element.116.refs_0_, bf16[128,1024]{1,0:T(8,128)(2,1)} %get-tuple-element.115.refs_1_, bf16[128,1024]{1,0:T(8,128)(2,1)} %get-tuple-element.114.refs_2_, ...), custom_call_target="tpu_custom_call" | custom-call | flops 149999992832 | bytes 16777216 | tf_op jit(solution)/shard_map/attention_backward/pallas_call | solution.py:680
  87.9 1.7 %add_convert_fusion = (bf16[128,1536]{1,0:T(8,128)(2,1)S(1)}, bf16[128,1536]{1,0:T(8,128)(2,1)S(1)}, bf16[128,1536]{1,0:T(8,128)(2,1)S(1)}, f32[128,1536]{1,0:T(8,128)S(1)}) fusion(bf16[512,1536]{1,0:T(8,128)(2,1)} %collective-permute-done.4, bf16[512,1536]{1,0:T(8,128)(2,1)S(1)} %get-tuple-element.81), kind=kLoop, calls=%fused_computation.4 | loop fusion | flops 2949120 | bytes 5111808 | tf_op jit(solution)/shard_map/convert_element_type | solution.py:632
  89.6 1.7 %collective-permute-start.14 = (bf16[128,1536]{1,0:T(8,128)(2,1)S(1)}, bf16[128,1536]{1,0:T(8,128)(2,1)S(1)}, u32[]{:S(2)}, u32[]{:S(2)}) collective-permute-start(bf16[128,1536]{1,0:T(8,128)(2,1)S(1)} %get-tuple-element.106.refs_2_), channel_id=1, source_target_pairs={{0,6},{1,7},{2,4},{3,5},{4,2},{5,3},{6,0},{7,1},{8,14},{9,15},{10,... | collective-permute-start | bytes 1179656 | tf_op jit(solution)/shard_map/ppermute | solution.py:618
  91.2 1.4 collective-permute-start.13
  94.3 12.1 %input_backward.1 = (bf16[768,1024]{1,0:T(8,128)(2,1)S(1)}, bf16[128,1024]{1,0:T(8,128)(2,1)S(1)}, bf16[208,1024]{1,0:T(8,128)(2,1)S(1)}, bf16[48,1024]{1,0:T(8,128)(2,1)S(1)}) custom-call(bf16[128,1536]{1,0:T(8,128)(2,1)S(1)} %get-tuple-element.108.refs_0_, bf16[128,1536]{1,0:T(8,128)(2,1)S(1)} %get-tuple-element.107.refs_1_, ...), custom_call_target="tpu_custom_call" | custom-call | flops 130000003072 | bytes 16777216 | tf_op jit(solution)/shard_map/input_backward/pallas_call | solution.py:680
  106.4 4.1 %collective-permute-done.13 = bf16[128,1536]{1,0:T(8,128)(2,1)S(1)} collective-permute-done((bf16[128,1536]{1,0:T(8,128)(2,1)S(1)}, bf16[128,1536]{1,0:T(8,128)(2,1)S(1)}, u32[]{:S(2)}, u32[]{:S(2)}) %collective-permute-start.13) | collective-permute-done | bytes 393248 | tf_op jit(solution)/shard_map/ppermute | solution.py:618
  110.6 1.1 pad_maximum_fusion.1
  111.7 1.2 fusion.1
  113.1 1.5 collective-permute-start.9
  114.6 1.5 collective-permute-start.11
  116.7 1.1 collective-permute-start.18
  117.8 5.9 %collective-permute-done.15 = bf16[64,2560]{1,0:T(8,128)(2,1)S(1)} collective-permute-done((bf16[64,2560]{1,0:T(8,128)(2,1)S(1)}, bf16[64,2560]{1,0:T(8,128)(2,1)S(1)}, u32[]{:S(2)}, u32[]{:S(2)}) %collective-permute-start.15) | collective-permute-done | bytes 327712 | tf_op jit(solution)/shard_map/ppermute | solution.py:618
  123.9 2.3 %collective-permute-done.9 = bf16[128,1536]{1,0:T(8,128)(2,1)S(1)} collective-permute-done((bf16[128,1536]{1,0:T(8,128)(2,1)S(1)}, bf16[128,1536]{1,0:T(8,128)(2,1)S(1)}, u32[]{:S(2)}, u32[]{:S(2)}) %collective-permute-start.9) | collective-permute-done | bytes 393248 | tf_op jit(solution)/shard_map/ppermute | solution.py:618
  126.2 2.0 %collective-permute-start.17 = (bf16[208,1024]{1,0:T(8,128)(2,1)S(1)}, bf16[208,1024]{1,0:T(8,128)(2,1)S(1)}, u32[]{:S(2)}, u32[]{:S(2)}) collective-permute-start(bf16[208,1024]{1,0:T(8,128)(2,1)S(1)} %get-tuple-element.95), channel_id=1, source_target_pairs={{0,24},{1,25},{2,26},{3,27},{4,28},{5,29},{6,30},{7,31},{8,0},{9,1... | collective-permute-start | bytes 1277960 | tf_op jit(solution)/shard_map/ppermute | solution.py:589
  128.2 6.5 %collective-permute-done.11 = bf16[128,1536]{1,0:T(8,128)(2,1)S(1)} collective-permute-done((bf16[128,1536]{1,0:T(8,128)(2,1)S(1)}, bf16[128,1536]{1,0:T(8,128)(2,1)S(1)}, u32[]{:S(2)}, u32[]{:S(2)}) %collective-permute-start.11) | collective-permute-done | bytes 393248 | tf_op jit(solution)/shard_map/ppermute | solution.py:618
  136.0 1.6 %collective-permute-start.21 = (bf16[32,1536]{1,0:T(8,128)(2,1)}, bf16[32,1536]{1,0:T(8,128)(2,1)}, u32[]{:S(2)}, u32[]{:S(2)}) collective-permute-start(bf16[32,1536]{1,0:T(8,128)(2,1)} %get-tuple-element.117.refs_2_), channel_id=1, source_target_pairs={{0,24},{1,25},{2,26},{3,27},{4,28},{5,29},{6,30},{7,31},{8,16},{9,... | collective-permute-start | bytes 294920 | tf_op jit(solution)/shard_map/ppermute | solution.py:618
  137.9 0.7 pad_maximum_fusion.4.refs_1_
  138.7 2.5 %collective-permute-start.20 = (bf16[32,4096]{1,0:T(8,128)(2,1)}, bf16[32,4096]{1,0:T(8,128)(2,1)}, u32[]{:S(2)}, u32[]{:S(2)}) collective-permute-start(bf16[32,4096]{1,0:T(8,128)(2,1)} %pad_maximum_fusion.4.refs_1_), channel_id=1, source_target_pairs={{0,16},{1,17},{2,18},{3,19},{4,20},{5,21},{6,22},{7,23},{8,24},{9,... | collective-permute-start | bytes 786440 | tf_op jit(solution)/shard_map/ppermute | solution.py:618
  141.2 2.2 %unpack_strips.1 = (bf16[768,1024]{1,0:T(8,128)(2,1)}, bf16[192,1024]{1,0:T(8,128)(2,1)}) custom-call(bf16[32,1536]{1,0:T(8,128)(2,1)} %get-tuple-element.119.refs_0_, bf16[32,4096]{1,0:T(8,128)(2,1)} %pad_maximum_fusion.4.refs_1_, bf16[32,1536]{1,0:T(8,128)(2,1)} %get-tuple-element.117.refs_2_, bf16[64,2560]{1,0:T(8,128)(2,1)S(1)} %bitcast.26, ...), custom_call_target="tpu_custom_call" | custom-call | flops 199999995904 | bytes 16777216 | tf_op jit(solution)/shard_map/unpack_strips/pallas_call | solution.py:680
  143.9 10.1 %collective-permute-done.20.refs_1_ = bf16[32,4096]{1,0:T(8,128)(2,1)} collective-permute-done((bf16[32,4096]{1,0:T(8,128)(2,1)}, bf16[32,4096]{1,0:T(8,128)(2,1)}, u32[]{:S(2)}, u32[]{:S(2)}) %collective-permute-start.20) | collective-permute-done | bytes 262176 | tf_op jit(solution)/shard_map/ppermute | solution.py:618
  154.0 1.8 %end_sums.1 = (f32[32,3072]{1,0:T(8,128)}, f32[32,1024]{1,0:T(8,128)}) custom-call(f32[32,2560]{1,0:T(8,128)S(1)} %slice_bitcast_fusion.kept1, f32[32,1536]{1,0:T(8,128)S(1)} %slice.148.kept2, bf16[32,1536]{1,0:T(8,128)(2,1)} %collective-permute-done.19.refs_0_, bf16[32,4096]{1,0:T(8,128)(2,1)} %collective-permute-done.20.refs_1_, ...), custom_call_target="tpu_custom_call" | custom-call | flops 10000000000 | bytes 16777216 | tf_op jit(solution)/shard_map/end_sums/pallas_call | solution.py:887
  (66 shorter events, 7.3 us)
Async XLA Ops:
  3.8 15.7 %collective-permute-start.2 = (bf16[48,1024]{1,0:T(8,128)(2,1)}, bf16[48,1024]{1,0:T(8,128)(2,1)S(1)}, u32[]{:S(2)}, u32[]{:S(2)}) collective-permute-start(bf16[48,1024]{1,0:T(8,128)(2,1)} %get-tuple-element.56.refs_2_), channel_id=1, source_target_pairs={{0,9},{1,10},{2,11},{3,12},{4,13},{5,14},{6,15},{7,8},{8,17},{9,18... | collective-permute-start | bytes 294920 | tf_op jit(solution)/shard_map/ppermute | solution.py:589
  6.2 13.2 %collective-permute-start = (bf16[128,1024]{1,0:T(8,128)(2,1)}, bf16[128,1024]{1,0:T(8,128)(2,1)S(1)}, u32[]{:S(2)}, u32[]{:S(2)}) collective-permute-start(bf16[128,1024]{1,0:T(8,128)(2,1)} %get-tuple-element.54.refs_0_), channel_id=1, source_target_pairs={{0,1},{1,2},{2,3},{3,4},{4,5},{5,6},{6,7},{7,0},{8,9},{9,10},{10,1... | collective-permute-start | bytes 786440 | tf_op jit(solution)/shard_map/ppermute | solution.py:589
  7.8 11.0 %copy-start.10 = (s32[32]{0:T(128)S(1)}, s32[32]{0:T(128)}, u32[]{:S(2)}) copy-start(s32[32]{0:T(128)} %constant.47.clone) | copy-start | bytes 388
  7.8 11.0 %copy-start.11 = (s32[32]{0:T(128)S(1)}, s32[32]{0:T(128)}, u32[]{:S(2)}) copy-start(s32[32]{0:T(128)} %constant.46.clone) | copy-start | bytes 388
  7.8 14.0 %collective-permute-start.1 = (bf16[208,1024]{1,0:T(8,128)(2,1)}, bf16[208,1024]{1,0:T(8,128)(2,1)S(1)}, u32[]{:S(2)}, u32[]{:S(2)}) collective-permute-start(bf16[208,1024]{1,0:T(8,128)(2,1)} %get-tuple-element.55.refs_1_), channel_id=1, source_target_pairs={{0,8},{1,9},{2,10},{3,11},{4,12},{5,13},{6,14},{7,15},{8,16},{9,17... | collective-permute-start | bytes 1277960 | tf_op jit(solution)/shard_map/ppermute | solution.py:589
  19.4 3.0 %copy-start.14 = (bf16[48,1024]{1,0:T(8,128)(2,1)}, bf16[48,1024]{1,0:T(8,128)(2,1)S(1)}, u32[]{:S(2)}) copy-start(bf16[48,1024]{1,0:T(8,128)(2,1)S(1)} %collective-permute-done.2.corner) | copy-start | bytes 294916
  19.4 3.0 %copy-start.13 = (bf16[128,1024]{1,0:T(8,128)(2,1)}, bf16[128,1024]{1,0:T(8,128)(2,1)S(1)}, u32[]{:S(2)}) copy-start(bf16[128,1024]{1,0:T(8,128)(2,1)S(1)} %collective-permute-done.side) | copy-start | bytes 786436
  53.4 14.8 %collective-permute-start.3 = (bf16[512,1024]{1,0:T(8,128)(2,1)}, bf16[512,1024]{1,0:T(8,128)(2,1)}, u32[]{:S(2)}, u32[]{:S(2)}) collective-permute-start(bf16[512,1024]{1,0:T(8,128)(2,1)} %get-tuple-element.64), channel_id=1, source_target_pairs={{0,1},{1,0},{2,3},{3,2},{4,5},{5,4},{6,7},{7,6},{8,9},{9,8},{10,11... | collective-permute-start | bytes 3145736 | tf_op jit(solution)/shard_map/ppermute | solution.py:618
  53.5 14.8 %copy-start.9 = (bf16[512,1024]{1,0:T(8,128)(2,1)S(1)}, bf16[512,1024]{1,0:T(8,128)(2,1)}, u32[]{:S(2)}) copy-start(bf16[512,1024]{1,0:T(8,128)(2,1)} %get-tuple-element.70) | copy-start | bytes 3145732
  67.7 20.0 %collective-permute-start.4 = (bf16[512,1536]{1,0:T(8,128)(2,1)}, bf16[512,1536]{1,0:T(8,128)(2,1)}, u32[]{:S(2)}, u32[]{:S(2)}) collective-permute-start(bf16[512,1536]{1,0:T(8,128)(2,1)} %get-tuple-element.75), channel_id=1, source_target_pairs={{0,1},{1,0},{2,3},{3,2},{4,5},{5,4},{6,7},{7,6},{8,9},{9,8},{10,11... | collective-permute-start | bytes 4718600 | tf_op jit(solution)/shard_map/ppermute | solution.py:618
  70.8 16.9 %collective-permute-start.7 = (bf16[128,1024]{1,0:T(8,128)(2,1)}, bf16[128,1024]{1,0:T(8,128)(2,1)}, u32[]{:S(2)}, u32[]{:S(2)}) collective-permute-start(bf16[128,1024]{1,0:T(8,128)(2,1)} %get-tuple-element.114.refs_2_), channel_id=1, source_target_pairs={{0,6},{1,7},{2,4},{3,5},{4,2},{5,3},{6,0},{7,1},{8,14},{9,15},{10,... | collective-permute-start | bytes 786440 | tf_op jit(solution)/shard_map/ppermute | solution.py:618
  72.4 15.4 %collective-permute-start.6 = (bf16[128,1024]{1,0:T(8,128)(2,1)}, bf16[128,1024]{1,0:T(8,128)(2,1)}, u32[]{:S(2)}, u32[]{:S(2)}) collective-permute-start(bf16[128,1024]{1,0:T(8,128)(2,1)} %get-tuple-element.115.refs_1_), channel_id=1, source_target_pairs={{0,4},{1,5},{2,6},{3,7},{4,0},{5,1},{6,2},{7,3},{8,12},{9,13},{10,... | collective-permute-start | bytes 786440 | tf_op jit(solution)/shard_map/ppermute | solution.py:618
  73.8 14.0 %collective-permute-start.5 = (bf16[128,1024]{1,0:T(8,128)(2,1)}, bf16[128,1024]{1,0:T(8,128)(2,1)}, u32[]{:S(2)}, u32[]{:S(2)}) collective-permute-start(bf16[128,1024]{1,0:T(8,128)(2,1)} %get-tuple-element.116.refs_0_), channel_id=1, source_target_pairs={{0,2},{1,3},{2,0},{3,1},{4,6},{5,7},{6,4},{7,5},{8,10},{9,11},{10,... | collective-permute-start | bytes 786440 | tf_op jit(solution)/shard_map/ppermute | solution.py:618
  87.8 5.4 %collective-permute-start.8 = (bf16[512,1536]{1,0:T(8,128)(2,1)S(1)}, bf16[512,1536]{1,0:T(8,128)(2,1)S(1)}, u32[]{:S(2)}, u32[]{:S(2)}) collective-permute-start(bf16[512,1536]{1,0:T(8,128)(2,1)S(1)} %get-tuple-element.80), channel_id=1, source_target_pairs={{0,1},{1,0},{2,3},{3,2},{4,5},{5,4},{6,7},{7,6},{8,9},{9,8},{10,11... | collective-permute-start | bytes 4718600 | tf_op jit(solution)/shard_map/ppermute | solution.py:618
  89.6 16.8 %collective-permute-start.14 = (bf16[128,1536]{1,0:T(8,128)(2,1)S(1)}, bf16[128,1536]{1,0:T(8,128)(2,1)S(1)}, u32[]{:S(2)}, u32[]{:S(2)}) collective-permute-start(bf16[128,1536]{1,0:T(8,128)(2,1)S(1)} %get-tuple-element.106.refs_2_), channel_id=1, source_target_pairs={{0,6},{1,7},{2,4},{3,5},{4,2},{5,3},{6,0},{7,1},{8,14},{9,15},{10,... | collective-permute-start | bytes 1179656 | tf_op jit(solution)/shard_map/ppermute | solution.py:618
  91.2 19.2 %collective-permute-start.13 = (bf16[128,1536]{1,0:T(8,128)(2,1)S(1)}, bf16[128,1536]{1,0:T(8,128)(2,1)S(1)}, u32[]{:S(2)}, u32[]{:S(2)}) collective-permute-start(bf16[128,1536]{1,0:T(8,128)(2,1)S(1)} %get-tuple-element.107.refs_1_), channel_id=1, source_target_pairs={{0,4},{1,5},{2,6},{3,7},{4,0},{5,1},{6,2},{7,3},{8,12},{9,13},{10,... | collective-permute-start | bytes 1179656 | tf_op jit(solution)/shard_map/ppermute | solution.py:618
  92.6 18.0 %collective-permute-start.12 = (bf16[128,1536]{1,0:T(8,128)(2,1)S(1)}, bf16[128,1536]{1,0:T(8,128)(2,1)S(1)}, u32[]{:S(2)}, u32[]{:S(2)}) collective-permute-start(bf16[128,1536]{1,0:T(8,128)(2,1)S(1)} %get-tuple-element.108.refs_0_), channel_id=1, source_target_pairs={{0,2},{1,3},{2,0},{3,1},{4,6},{5,7},{6,4},{7,5},{8,10},{9,11},{10,... | collective-permute-start | bytes 1179656 | tf_op jit(solution)/shard_map/ppermute | solution.py:618
  106.4 5.3 %copy-start.8 = (f32[128,1024]{1,0:T(8,128)S(1)}, f32[128,1024]{1,0:T(8,128)}, u32[]{:S(2)}) copy-start(f32[128,1024]{1,0:T(8,128)} %get-tuple-element.113) | copy-start | bytes 1572868
  113.0 10.7 %collective-permute-start.15 = (bf16[64,2560]{1,0:T(8,128)(2,1)S(1)}, bf16[64,2560]{1,0:T(8,128)(2,1)S(1)}, u32[]{:S(2)}, u32[]{:S(2)}) collective-permute-start(bf16[64,2560]{1,0:T(8,128)(2,1)S(1)} %bitcast.25), channel_id=1, source_target_pairs={{0,8},{1,9},{2,10},{3,11},{4,12},{5,13},{6,14},{7,15},{8,0},{9,1},... | collective-permute-start | bytes 983048 | tf_op jit(solution)/shard_map/ppermute | solution.py:618
  113.1 13.1 %collective-permute-start.9 = (bf16[128,1536]{1,0:T(8,128)(2,1)S(1)}, bf16[128,1536]{1,0:T(8,128)(2,1)S(1)}, u32[]{:S(2)}, u32[]{:S(2)}) collective-permute-start(bf16[128,1536]{1,0:T(8,128)(2,1)S(1)} %get-tuple-element.110.refs_3_), channel_id=1, source_target_pairs={{0,2},{1,3},{2,0},{3,1},{4,6},{5,7},{6,4},{7,5},{8,10},{9,11},{10,... | collective-permute-start | bytes 1179656 | tf_op jit(solution)/shard_map/ppermute | solution.py:618
  114.6 20.1 %collective-permute-start.11 = (bf16[128,1536]{1,0:T(8,128)(2,1)S(1)}, bf16[128,1536]{1,0:T(8,128)(2,1)S(1)}, u32[]{:S(2)}, u32[]{:S(2)}) collective-permute-start(bf16[128,1536]{1,0:T(8,128)(2,1)S(1)} %get-tuple-element.111.refs_5_), channel_id=1, source_target_pairs={{0,6},{1,7},{2,4},{3,5},{4,2},{5,3},{6,0},{7,1},{8,14},{9,15},{10,... | collective-permute-start | bytes 1179656 | tf_op jit(solution)/shard_map/ppermute | solution.py:618
  116.1 18.9 %collective-permute-start.10 = (bf16[128,1536]{1,0:T(8,128)(2,1)S(1)}, bf16[128,1536]{1,0:T(8,128)(2,1)S(1)}, u32[]{:S(2)}, u32[]{:S(2)}) collective-permute-start(bf16[128,1536]{1,0:T(8,128)(2,1)S(1)} %get-tuple-element.112.refs_4_), channel_id=1, source_target_pairs={{0,4},{1,5},{2,6},{3,7},{4,0},{5,1},{6,2},{7,3},{8,12},{9,13},{10,... | collective-permute-start | bytes 1179656 | tf_op jit(solution)/shard_map/ppermute | solution.py:618
  116.7 22.0 %collective-permute-start.18 = (bf16[48,1024]{1,0:T(8,128)(2,1)S(1)}, bf16[48,1024]{1,0:T(8,128)(2,1)S(1)}, u32[]{:S(2)}, u32[]{:S(2)}) collective-permute-start(bf16[48,1024]{1,0:T(8,128)(2,1)S(1)} %get-tuple-element.96), channel_id=1, source_target_pairs={{0,31},{1,24},{2,25},{3,26},{4,27},{5,28},{6,29},{7,30},{8,7},{9,0... | collective-permute-start | bytes 294920 | tf_op jit(solution)/shard_map/ppermute | solution.py:589
  123.7 17.5 %collective-permute-start.16 = (bf16[128,1024]{1,0:T(8,128)(2,1)S(1)}, bf16[128,1024]{1,0:T(8,128)(2,1)S(1)}, u32[]{:S(2)}, u32[]{:S(2)}) collective-permute-start(bf16[128,1024]{1,0:T(8,128)(2,1)S(1)} %get-tuple-element.94), channel_id=1, source_target_pairs={{0,7},{1,0},{2,1},{3,2},{4,3},{5,4},{6,5},{7,6},{8,15},{9,8},{10,9... | collective-permute-start | bytes 786440 | tf_op jit(solution)/shard_map/ppermute | solution.py:589
  123.8 17.4 %copy-start = (bf16[384,448]{1,0:T(8,128)(2,1)S(1)}, bf16[384,448]{1,0:T(8,128)(2,1)}, u32[]{:S(2)}) copy-start(bf16[384,448]{1,0:T(8,128)(2,1)} %constant.52.clone.refs_10_) | copy-start | bytes 1032196
  123.8 17.4 %copy-start.1 = (bf16[192,416]{1,0:T(8,128)(2,1)S(1)}, bf16[192,416]{1,0:T(8,128)(2,1)}, u32[]{:S(2)}) copy-start(bf16[192,416]{1,0:T(8,128)(2,1)} %constant.51.clone.refs_9_) | copy-start | bytes 479236
  123.9 17.4 %copy-start.3 = (bf16[192,288]{1,0:T(8,128)(2,1)S(1)}, bf16[192,288]{1,0:T(8,128)(2,1)}, u32[]{:S(2)}) copy-start(bf16[192,288]{1,0:T(8,128)(2,1)} %constant.54.clone.refs_12_) | copy-start | bytes 331780
  123.9 17.4 %copy-start.4 = (bf16[192,192]{1,0:T(8,128)(2,1)S(1)}, bf16[192,192]{1,0:T(8,128)(2,1)}, u32[]{:S(2)}) copy-start(bf16[192,192]{1,0:T(8,128)(2,1)} %constant.53.clone.refs_11_) | copy-start | bytes 221188
  126.2 15.0 %collective-permute-start.17 = (bf16[208,1024]{1,0:T(8,128)(2,1)S(1)}, bf16[208,1024]{1,0:T(8,128)(2,1)S(1)}, u32[]{:S(2)}, u32[]{:S(2)}) collective-permute-start(bf16[208,1024]{1,0:T(8,128)(2,1)S(1)} %get-tuple-element.95), channel_id=1, source_target_pairs={{0,24},{1,25},{2,26},{3,27},{4,28},{5,29},{6,30},{7,31},{8,0},{9,1... | collective-permute-start | bytes 1277960 | tf_op jit(solution)/shard_map/ppermute | solution.py:589
  136.0 7.9 %collective-permute-start.21 = (bf16[32,1536]{1,0:T(8,128)(2,1)}, bf16[32,1536]{1,0:T(8,128)(2,1)}, u32[]{:S(2)}, u32[]{:S(2)}) collective-permute-start(bf16[32,1536]{1,0:T(8,128)(2,1)} %get-tuple-element.117.refs_2_), channel_id=1, source_target_pairs={{0,24},{1,25},{2,26},{3,27},{4,28},{5,29},{6,30},{7,31},{8,16},{9,... | collective-permute-start | bytes 294920 | tf_op jit(solution)/shard_map/ppermute | solution.py:618
  137.6 6.2 %collective-permute-start.19 = (bf16[32,1536]{1,0:T(8,128)(2,1)}, bf16[32,1536]{1,0:T(8,128)(2,1)}, u32[]{:S(2)}, u32[]{:S(2)}) collective-permute-start(bf16[32,1536]{1,0:T(8,128)(2,1)} %get-tuple-element.119.refs_0_), channel_id=1, source_target_pairs={{0,8},{1,9},{2,10},{3,11},{4,12},{5,13},{6,14},{7,15},{8,0},{9,1},... | collective-permute-start | bytes 294920 | tf_op jit(solution)/shard_map/ppermute | solution.py:618
  138.7 15.3 %collective-permute-start.20 = (bf16[32,4096]{1,0:T(8,128)(2,1)}, bf16[32,4096]{1,0:T(8,128)(2,1)}, u32[]{:S(2)}, u32[]{:S(2)}) collective-permute-start(bf16[32,4096]{1,0:T(8,128)(2,1)} %pad_maximum_fusion.4.refs_1_), channel_id=1, source_target_pairs={{0,16},{1,17},{2,18},{3,19},{4,20},{5,21},{6,22},{7,23},{8,24},{9,... | collective-permute-start | bytes 786440 | tf_op jit(solution)/shard_map/ppermute | solution.py:618
  (5 other events, 4.7 us)

commit v12 on v11

--- a/solution.py
+++ b/solution.py
@@ -622,18 +622,47 @@
     return exchange(theirs, sizes, 0, 1)
 
 
-def layer_blocks(mine, arrived, sizes):
-    blocks = sizes[1] // 2
-    rows = mine.shape[0] // blocks
-    total = [
-        (mine[i * rows:(i + 1) * rows].astype(F32) + arrived[i * rows:(i + 1) * rows].astype(F32))
-        for i in range(blocks)
-    ]
-    return [total[0]] + [t.astype(BF16) for t in total[1:]]
-
-
-def layer_step(blocks, sizes):
-    return [exchange(b, sizes, 0, 2 * i) for i, b in enumerate(blocks) if i]
+def core_sum(mine, arrived):
+    return (mine.astype(F32) + arrived.astype(F32)).astype(BF16)
+
+
+class Layer:
+    def __init__(self, total, sizes):
+        self.sizes = sizes
+        chips = sizes[1] // 2
+        bits = [1 << i for i in range(chips.bit_length() - 1)]
+        self.orders = [list(bits), bits[1:] + bits[:1]]
+        self.bits = [bits[::-1], bits[::-1]]
+        columns = total.shape[1] // 2
+        rows = total.shape[0] // chips
+        self.parts = [
+            total[:, i * columns:(i + 1) * columns].reshape([2] * len(bits) + [rows, columns])
+            for i in range(2)
+        ]
+
+    def give(self):
+        self.kept, given = [], []
+        for i, part in enumerate(self.parts):
+            axis = self.bits[i].index(self.orders[i][0])
+            self.kept.append(lax.index_in_dim(part, 0, axis, keepdims=False))
+            given.append(lax.index_in_dim(part, 1, axis, keepdims=False))
+        return given
+
+    def send(self, given):
+        arrived = []
+        for i, block in enumerate(given):
+            bit = self.orders[i].pop(0)
+            self.bits[i] = [b for b in self.bits[i] if b != bit]
+            arrived.append(exchange(block, self.sizes, 0, 2 * bit))
+        return arrived
+
+    def add(self, arrived):
+        self.parts = [core_sum(k, a) for k, a in zip(self.kept, arrived)]
+
+    def finish(self):
+        while self.orders[0]:
+            self.add(self.send(self.give()))
+        return jnp.concatenate(self.parts, axis=-1).astype(F32)
 
 
 def column_blocks(kept, arrived, sizes):
@@ -818,22 +847,27 @@
     arrived = core_step(out_theirs, sizes)
     pg0, mine1, theirs1 = backward(0, [])
     out_mine, arrived = behind([out_mine, arrived], pg0)
-    layer0 = layer_blocks(out_mine, arrived, sizes)
-    arrived0 = layer_step(layer0, sizes)
-    arrived = core_step(theirs1, sizes)
-    pg1, mine2, theirs2 = backward(1, layer0[1:])
-    mine1, arrived, *arrived0 = behind([mine1, arrived] + arrived0, pg1)
-    layer1 = layer_blocks(mine1, arrived, sizes)
-    arrived1 = layer_step(layer1, sizes)
-    theirs2, = behind([theirs2], arrived0)
+    theirs1, = behind([theirs1], arrived)
+    total = core_sum(out_mine, arrived)
+    total1 = core_sum(mine1, core_step(theirs1, sizes))
+    layer1 = Layer(jnp.concatenate([total, total1], axis=1), sizes)
+    given = layer1.give()
+    arrived1 = layer1.send(given)
+    pg1, mine2, theirs2 = backward(1, given)
+    arrived1 = behind(arrived1, pg1)
+    theirs2, = behind([theirs2], arrived1)
     arrived = core_step(theirs2, sizes)
-    layer2 = layer_blocks(mine2, arrived, sizes)
-    arrived2 = layer_step(layer2, sizes)
+    layer1.add(arrived1)
+    given1 = layer1.give()
+    arrived1 = layer1.send(given1)
+    layer2 = Layer(core_sum(mine2, arrived), sizes)
+    given2 = layer2.give()
+    arrived2 = layer2.send(given2)
 
     first_picks = picks(cs.side[:side_cut] + cs.above + cs.corner, cells[:half_cells])
     last_picks = picks(cs.side[side_cut:], cells[half_cells:])
     full, *strips = tied_call(
-        input_kernel, layer1[1:] + layer2[1:],
+        input_kernel, given1 + given2,
         [pg0, pg1, qkv_weight, pinned(normed), pinned(rstd), pinned(grad), merged,
          first_picks, last_picks, picks(sum(g_strips, []), grps)],
         [hbm] * 6 + [vmem] * 4, [wide] + [shape(*e) for e in extents], [vmem] * 4,
@@ -850,16 +884,18 @@
         name="input_backward", **settings(13, 40),
     )
     arrived1 = behind(arrived1, full)
-    strips = sent_strips(behind(strips, arrived1), sizes, -1)
-
-    total1 = jnp.concatenate([layer0[0], layer1[0]], axis=1)
-    for pair in zip(arrived0, arrived1):
-        total1 = total1 + jnp.concatenate(pair, axis=1).astype(F32)
+    arrived2 = behind(arrived2, full)
+    arrived1 = behind(arrived1, arrived2)
+    strips = sent_strips(behind(strips, (arrived1, arrived2)), sizes, -1)
+    layer2.add(arrived2)
+    total2 = layer2.finish()
+    layer1.add(arrived1)
+    total1 = layer1.finish()
     kept1, given1 = column_halves(total1, sizes, 1)
     got1 = exchange(given1, sizes, 1, 0)
 
     part1 = kept1 + got1.astype(F32)
-    column2 = column_blocks(layer2[0], arrived2, sizes)
+    column2 = column_blocks(total2, [], sizes)
     bit = 2
     while 2 * bit < sizes[0]:
         kept1, given1 = column_halves(part1, sizes, bit)

time: 156 us -> 152 us (0.974)
  waiting for transfers between devices: 32.2 us -> 24 us
  starting transfers between devices: 24.5 us -> 28.7 us
    ppermute x16 -> x15, waiting for transfers between devices: 29.8 us -> 18.6 us  [exchange(): return lax.ppermute(block, ('lat', 'lon'), route)]
    add x2 -> x0, other arithmetic: 3.75 us -> none  [the longest x1 2.51 us: layer_blocks(): mine[i * rows:(i + 1) * rows].astype(F32)]
    convert_element_type x2 -> x10, other arithmetic: 2.03 us -> 5.36 us  [core_sum(): return (mine.astype(F32) + arrived.astype(F32)).astype(BF16)]
    ppermute x16 -> x15, starting transfers between devices: 15.8 us -> 18.9 us  [exchange(): return lax.ppermute(block, ('lat', 'lon'), route)]
    ppermute x6, waiting for transfers between devices: 2.36 us -> 5.33 us  [sent(): return lax.ppermute(block, ('lat', 'lon'), route)]
  transfers between devices with their start and end apart: 22 -> 21, of which waited for: 9 -> 9; matrix products, arithmetic and copies ran while one was open for 4% -> 5% of each run, Pallas kernels for 33% -> 34%
where the time goes in v12:
time: 152 us; the launch traced here: 151 us
  Pallas kernels  86.6 us (57%)
  starting transfers between devices  28.7 us (19%)
  waiting for transfers between devices  24 us (16%)
  other arithmetic  7.56 us (5%)
  local copies, waits for them, and re-layouts  3.26 us (2%)
    pallas_call x5, Pallas kernels, tied_call(): pl.pallas_call(body, out_shape=out_shape, in_specs=[pl.BlockSpec(memory_s...  50.8 us
    pallas_call x1, Pallas kernels, shards(): pl.pallas_call(forward_kernel, out_shape=[wide, shape(channels, count), s...  30.9 us
    ppermute x15, starting transfers between devices, exchange(): return lax.ppermute(block, ('lat', 'lon'), route)  18.9 us
    ppermute x15, waiting for transfers between devices, exchange(): return lax.ppermute(block, ('lat', 'lon'), route)  18.6 us
    ppermute x6, starting transfers between devices, sent(): return lax.ppermute(block, ('lat', 'lon'), route)  9.73 us
    convert_element_type x10, other arithmetic, core_sum(): return (mine.astype(F32) + arrived.astype(F32)).astype(BF16)  5.36 us
    ppermute x6, waiting for transfers between devices, sent(): return lax.ppermute(block, ('lat', 'lon'), route)  5.33 us
    pallas_call x1, Pallas kernels, shards(): pl.pallas_call(pack_kernel, out_shape=[shape(*e) for e in extents], in_sp...  3.14 us
  transfers between devices with their start and end apart: 21, of which 9 were waited for; matrix products, arithmetic and copies ran while one was open for 5% of the time, Pallas kernels for 34%

profile of v12, /device:TPU:0, one launch (start us, length us, event | category | flops | bytes accessed | tf_op | source)
XLA Modules:
  0.0 151.1 jit_solution(11676121673817488251)
XLA Ops:
  0.6 3.1 %pack_strips.1 = (bf16[128,1024]{1,0:T(8,128)(2,1)}, bf16[208,1024]{1,0:T(8,128)(2,1)}, bf16[48,1024]{1,0:T(8,128)(2,1)}) custom-call(bf16[768,1024]{1,0:T(8,128)(2,1)} %bitcast.96, bf16[192,1024]{1,0:T(8,128)(2,1)} %bitcast.99, bf16[288,768]{1,0:T(8,128)(2,1)} %constant.41.clone.pick_cells, bf16[96,192]{1,0:T(8,128)(2,1)} %constant.42.clone.pick_groups), custom_call_target="tpu_custom_call" | custom-call | flops 10000000000 | bytes 16777216 | tf_op jit(solution)/shard_map/pack_strips/pallas_call | solution.py:763
  3.8 2.5 %collective-permute-start.2 = (bf16[48,1024]{1,0:T(8,128)(2,1)}, bf16[48,1024]{1,0:T(8,128)(2,1)S(1)}, u32[]{:S(2)}, u32[]{:S(2)}) collective-permute-start(bf16[48,1024]{1,0:T(8,128)(2,1)} %get-tuple-element.57.refs_2_), channel_id=1, source_target_pairs={{0,9},{1,10},{2,11},{3,12},{4,13},{5,14},{6,15},{7,8},{8,17},{9,18... | collective-permute-start | bytes 294920 | tf_op jit(solution)/shard_map/ppermute | solution.py:589
  6.2 1.6 %collective-permute-start = (bf16[128,1024]{1,0:T(8,128)(2,1)}, bf16[128,1024]{1,0:T(8,128)(2,1)S(1)}, u32[]{:S(2)}, u32[]{:S(2)}) collective-permute-start(bf16[128,1024]{1,0:T(8,128)(2,1)} %get-tuple-element.55.refs_0_), channel_id=1, source_target_pairs={{0,1},{1,2},{2,3},{3,4},{4,5},{5,6},{6,7},{7,0},{8,9},{9,10},{10,1... | collective-permute-start | bytes 786440 | tf_op jit(solution)/shard_map/ppermute | solution.py:589
  7.8 1.6 %collective-permute-start.1 = (bf16[208,1024]{1,0:T(8,128)(2,1)}, bf16[208,1024]{1,0:T(8,128)(2,1)S(1)}, u32[]{:S(2)}, u32[]{:S(2)}) collective-permute-start(bf16[208,1024]{1,0:T(8,128)(2,1)} %get-tuple-element.56.refs_1_), channel_id=1, source_target_pairs={{0,8},{1,9},{2,10},{3,11},{4,12},{5,13},{6,14},{7,15},{8,16},{9,17... | collective-permute-start | bytes 1277960 | tf_op jit(solution)/shard_map/ppermute | solution.py:589
  9.4 9.4 %inner_windows.1 = (bf16[256,1024]{1,0:T(8,128)(2,1)}, bf16[256,1024]{1,0:T(8,128)(2,1)}, f32[256,128]{1,0:T(8,128)}, bf16[256,1024]{1,0:T(8,128)(2,1)}, f32[256,1024]{1,0:T(8,128)}, /*index=5*/bf16[256,3072]{1,0:T(8,128)(2,1)}) custom-call(bf16[128,1024]{1,0:T(8,128)(2,1)} %get-tuple-element.55.refs_0_, bf16[208,1024]{1,0:T(8,128)(2,1)} %get-tuple-element.56.refs_1_, ...), custom_call_target="tpu_custom_call" | custom-call | flops 89999998976 | bytes 16777216 | tf_op jit(solution)/shard_map/inner_windows/pallas_call | solution.py:709
  19.5 2.3 %collective-permute-done.1.above = bf16[208,1024]{1,0:T(8,128)(2,1)S(1)} collective-permute-done((bf16[208,1024]{1,0:T(8,128)(2,1)}, bf16[208,1024]{1,0:T(8,128)(2,1)S(1)}, u32[]{:S(2)}, u32[]{:S(2)}) %collective-permute-start.1) | collective-permute-done | bytes 426016 | tf_op jit(solution)/shard_map/ppermute | solution.py:589
  22.6 30.9 %block_forward.1 = (bf16[768,1024]{1,0:T(8,128)(2,1)}, bf16[1024,768]{1,0:T(8,128)(2,1)}, bf16[768,3072]{1,0:T(8,128)(2,1)}, bf16[768,1024]{1,0:T(8,128)(2,1)}, ...) custom-call(s32[1]{0:T(128)} %bitcast.edge.refs_0_.refs_2_, ...), custom_call_target="tpu_custom_call" | custom-call | flops 299999985664 | bytes 16777216 | tf_op jit(solution)/shard_map/block_forward/pallas_call | solution.py:793
  53.6 13.5 %attention_backward.2 = (bf16[768,1536]{1,0:T(8,128)(2,1)S(1)}, bf16[512,1536]{1,0:T(8,128)(2,1)S(1)}, bf16[512,1536]{1,0:T(8,128)(2,1)S(1)}) custom-call(s32[1]{0:T(128)} %bitcast.edge.refs_0_.refs_2_, bf16[768,3072]{1,0:T(8,128)(2,1)} %get-tuple-element.66.refs_1_.refs_3_, bf16[768,1024]{1,0:T(8,128)(2,1)} %get-tuple-element.67.refs_2_.refs_4_, ...), custom_call_target="tpu_custom_call" | custom-call | flops 149999992832 | bytes 16777216 | tf_op jit(solution)/shard_map/attention_backward/pallas_call | solution.py:709
  67.7 1.6 %add_convert_fusion.2 = bf16[512,1024]{1,0:T(8,128)(2,1)S(1)} fusion(bf16[512,1024]{1,0:T(8,128)(2,1)} %collective-permute-done.3, bf16[512,1024]{1,0:T(8,128)(2,1)S(1)} %copy-done.11), kind=kLoop, calls=%fused_computation.2 | loop fusion | flops 2097152 | bytes 3145728 | tf_op jit(solution)/shard_map/convert_element_type | solution.py:626
  69.3 1.4 collective-permute-done.4
  71.1 1.2 fusion.15
  73.4 1.5 %collective-permute-start.5 = (bf16[2,128,1280]{2,1,0:T(8,128)(2,1)}, bf16[2,128,1280]{2,1,0:T(8,128)(2,1)}, u32[]{:S(2)}, u32[]{:S(2)}) collective-permute-start(bf16[2,128,1280]{2,1,0:T(8,128)(2,1)} %slice_bitcast_fusion.1.refs_0_), channel_id=1, source_target_pairs={{0,2},{1,3},{2,0},{3,1},{4,6},{5,7},{6,4},{7,5},{8,10},{9,11},{10,... | collective-permute-start | bytes 1966088 | tf_op jit(solution)/shard_map/ppermute | solution.py:618
  75.5 13.8 %attention_backward.3 = (bf16[768,1536]{1,0:T(8,128)(2,1)S(1)}, bf16[512,1536]{1,0:T(8,128)(2,1)S(1)}, bf16[512,1536]{1,0:T(8,128)(2,1)S(1)}) custom-call(bf16[2,128,1280]{2,1,0:T(8,128)(2,1)} %slice_bitcast_fusion.1.refs_0_, bf16[2,128,1280]{2,1,0:T(8,128)(2,1)} %bitcast.7.refs_1_, s32[1]{0:T(128)} %bitcast.edge.refs_0_.refs_2_, ...), custom_call_target="tpu_custom_call" | custom-call | flops 149999992832 | bytes 16777216 | tf_op jit(solution)/shard_map/attention_backward/pallas_call | solution.py:709
  89.3 1.4 collective-permute-done.5
  90.7 1.2 collective-permute-done.6
  91.9 1.3 fusion.1
  93.9 1.2 fusion
  95.2 1.5 collective-permute-start.13
  98.0 1.4 collective-permute-start.9
  99.4 11.9 %input_backward.1 = (bf16[768,1024]{1,0:T(8,128)(2,1)S(1)}, bf16[128,1024]{1,0:T(8,128)(2,1)S(1)}, bf16[208,1024]{1,0:T(8,128)(2,1)S(1)}, bf16[48,1024]{1,0:T(8,128)(2,1)S(1)}) custom-call(bf16[128,1280]{1,0:T(8,128)(2,1)S(1)} %slice_bitcast_fusion.8.refs_0_, bf16[128,1280]{1,0:T(8,128)(2,1)S(1)} %slice_bitcast_fusion.7.refs_1_, ...), custom_call_target="tpu_custom_call" | custom-call | flops 130000003072 | bytes 16777216 | tf_op jit(solution)/shard_map/input_backward/pallas_call | solution.py:709
  111.3 2.2 %collective-permute-done.8 = bf16[2,128,768]{2,1,0:T(8,128)(2,1)S(1)} collective-permute-done((bf16[2,128,768]{2,1,0:T(8,128)(2,1)S(1)}, bf16[2,128,768]{2,1,0:T(8,128)(2,1)S(1)}, u32[]{:S(2)}, u32[]{:S(2)}) %collective-permute-start.8) | collective-permute-done | bytes 393248 | tf_op jit(solution)/shard_map/ppermute | solution.py:618
  113.9 1.0 collective-permute-start.17
  115.0 1.8 %collective-permute-start.10 = (bf16[128,768]{1,0:T(8,128)(2,1)S(1)}, bf16[128,768]{1,0:T(8,128)(2,1)S(1)}, u32[]{:S(2)}, u32[]{:S(2)}) collective-permute-start(bf16[128,768]{1,0:T(8,128)(2,1)S(1)} %slice_bitcast_fusion.11), channel_id=1, source_target_pairs={{0,4},{1,5},{2,6},{3,7},{4,0},{5,1},{6,2},{7,3},{8,12},{9,13},{10,... | collective-permute-start | bytes 589832 | tf_op jit(solution)/shard_map/ppermute | solution.py:618
  117.1 1.9 %collective-permute-start.15 = (bf16[128,1024]{1,0:T(8,128)(2,1)S(1)}, bf16[128,1024]{1,0:T(8,128)(2,1)S(1)}, u32[]{:S(2)}, u32[]{:S(2)}) collective-permute-start(bf16[128,1024]{1,0:T(8,128)(2,1)S(1)} %get-tuple-element.96), channel_id=1, source_target_pairs={{0,7},{1,0},{2,1},{3,2},{4,3},{5,4},{6,5},{7,6},{8,15},{9,8},{10,9... | collective-permute-start | bytes 786440 | tf_op jit(solution)/shard_map/ppermute | solution.py:589
  119.1 3.4 %collective-permute-done.10 = bf16[128,768]{1,0:T(8,128)(2,1)S(1)} collective-permute-done((bf16[128,768]{1,0:T(8,128)(2,1)S(1)}, bf16[128,768]{1,0:T(8,128)(2,1)S(1)}, u32[]{:S(2)}, u32[]{:S(2)}) %collective-permute-start.10) | collective-permute-done | bytes 196640 | tf_op jit(solution)/shard_map/ppermute | solution.py:618
  122.5 1.2 collective-permute-start.16
  125.4 3.7 %collective-permute-done.14 = bf16[64,2560]{1,0:T(8,128)(2,1)S(1)} collective-permute-done((bf16[64,2560]{1,0:T(8,128)(2,1)S(1)}, bf16[64,2560]{1,0:T(8,128)(2,1)S(1)}, u32[]{:S(2)}, u32[]{:S(2)}) %collective-permute-start.14) | collective-permute-done | bytes 327712 | tf_op jit(solution)/shard_map/ppermute | solution.py:618
  129.1 8.8 %collective-permute-start.20 = (bf16[32,1536]{1,0:T(8,128)(2,1)}, bf16[32,1536]{1,0:T(8,128)(2,1)}, u32[]{:S(2)}, u32[]{:S(2)}) collective-permute-start(bf16[32,1536]{1,0:T(8,128)(2,1)} %get-tuple-element.115.refs_2_), channel_id=1, source_target_pairs={{0,24},{1,25},{2,26},{3,27},{4,28},{5,29},{6,30},{7,31},{8,16},{9,... | collective-permute-start | bytes 294920 | tf_op jit(solution)/shard_map/ppermute | solution.py:618
  138.8 3.0 %collective-permute-done.16.refs_7_ = bf16[208,1024]{1,0:T(8,128)(2,1)S(1)} collective-permute-done((bf16[208,1024]{1,0:T(8,128)(2,1)S(1)}, bf16[208,1024]{1,0:T(8,128)(2,1)S(1)}, u32[]{:S(2)}, u32[]{:S(2)}) %collective-permute-start.16) | collective-permute-done | bytes 426016 | tf_op jit(solution)/shard_map/ppermute | solution.py:589
  141.8 2.2 %unpack_strips.1 = (bf16[768,1024]{1,0:T(8,128)(2,1)}, bf16[192,1024]{1,0:T(8,128)(2,1)}) custom-call(bf16[32,1536]{1,0:T(8,128)(2,1)} %get-tuple-element.113.refs_0_, bf16[32,4096]{1,0:T(8,128)(2,1)} %pad_maximum_fusion.2.refs_1_, bf16[32,1536]{1,0:T(8,128)(2,1)} %get-tuple-element.115.refs_2_, bf16[64,2560]{1,0:T(8,128)(2,1)S(1)} %bitcast.85, ...), custom_call_target="tpu_custom_call" | custom-call | flops 199999995904 | bytes 16777216 | tf_op jit(solution)/shard_map/unpack_strips/pallas_call | solution.py:709
  143.9 5.3 %collective-permute-done.19.refs_1_ = bf16[32,4096]{1,0:T(8,128)(2,1)} collective-permute-done((bf16[32,4096]{1,0:T(8,128)(2,1)}, bf16[32,4096]{1,0:T(8,128)(2,1)}, u32[]{:S(2)}, u32[]{:S(2)}) %collective-permute-start.19) | collective-permute-done | bytes 262176 | tf_op jit(solution)/shard_map/ppermute | solution.py:618
  149.2 1.8 %end_sums.1 = (f32[32,3072]{1,0:T(8,128)}, f32[32,1024]{1,0:T(8,128)}) custom-call(f32[32,2560]{1,0:T(8,128)S(1)} %slice_bitcast_fusion.4.kept1, f32[32,1536]{1,0:T(8,128)S(1)} %get-tuple-element.112.kept2, bf16[32,1536]{1,0:T(8,128)(2,1)} %collective-permute-done.18.refs_0_, bf16[32,4096]{1,0:T(8,128)(2,1)} %collective-permute-done.19.refs_1_, ...), custom_call_target="tpu_custom_call" | custom-call | flops 10000000000 | bytes 16777216 | tf_op jit(solution)/shard_map/end_sums/pallas_call | solution.py:923
  (80 shorter events, 9.5 us)
Async XLA Ops:
  3.8 15.7 %collective-permute-start.2 = (bf16[48,1024]{1,0:T(8,128)(2,1)}, bf16[48,1024]{1,0:T(8,128)(2,1)S(1)}, u32[]{:S(2)}, u32[]{:S(2)}) collective-permute-start(bf16[48,1024]{1,0:T(8,128)(2,1)} %get-tuple-element.57.refs_2_), channel_id=1, source_target_pairs={{0,9},{1,10},{2,11},{3,12},{4,13},{5,14},{6,15},{7,8},{8,17},{9,18... | collective-permute-start | bytes 294920 | tf_op jit(solution)/shard_map/ppermute | solution.py:589
  6.2 13.2 %collective-permute-start = (bf16[128,1024]{1,0:T(8,128)(2,1)}, bf16[128,1024]{1,0:T(8,128)(2,1)S(1)}, u32[]{:S(2)}, u32[]{:S(2)}) collective-permute-start(bf16[128,1024]{1,0:T(8,128)(2,1)} %get-tuple-element.55.refs_0_), channel_id=1, source_target_pairs={{0,1},{1,2},{2,3},{3,4},{4,5},{5,6},{6,7},{7,0},{8,9},{9,10},{10,1... | collective-permute-start | bytes 786440 | tf_op jit(solution)/shard_map/ppermute | solution.py:589
  7.8 11.0 %copy-start.12 = (s32[32]{0:T(128)S(1)}, s32[32]{0:T(128)}, u32[]{:S(2)}) copy-start(s32[32]{0:T(128)} %constant.47.clone) | copy-start | bytes 388
  7.8 11.0 %copy-start.13 = (s32[32]{0:T(128)S(1)}, s32[32]{0:T(128)}, u32[]{:S(2)}) copy-start(s32[32]{0:T(128)} %constant.46.clone) | copy-start | bytes 388
  7.8 14.0 %collective-permute-start.1 = (bf16[208,1024]{1,0:T(8,128)(2,1)}, bf16[208,1024]{1,0:T(8,128)(2,1)S(1)}, u32[]{:S(2)}, u32[]{:S(2)}) collective-permute-start(bf16[208,1024]{1,0:T(8,128)(2,1)} %get-tuple-element.56.refs_1_), channel_id=1, source_target_pairs={{0,8},{1,9},{2,10},{3,11},{4,12},{5,13},{6,14},{7,15},{8,16},{9,17... | collective-permute-start | bytes 1277960 | tf_op jit(solution)/shard_map/ppermute | solution.py:589
  19.4 3.0 %copy-start.16 = (bf16[48,1024]{1,0:T(8,128)(2,1)}, bf16[48,1024]{1,0:T(8,128)(2,1)S(1)}, u32[]{:S(2)}) copy-start(bf16[48,1024]{1,0:T(8,128)(2,1)S(1)} %collective-permute-done.2.corner) | copy-start | bytes 294916
  19.4 3.0 %copy-start.15 = (bf16[128,1024]{1,0:T(8,128)(2,1)}, bf16[128,1024]{1,0:T(8,128)(2,1)S(1)}, u32[]{:S(2)}) copy-start(bf16[128,1024]{1,0:T(8,128)(2,1)S(1)} %collective-permute-done.side) | copy-start | bytes 786436
  53.5 13.6 %collective-permute-start.3 = (bf16[512,1024]{1,0:T(8,128)(2,1)}, bf16[512,1024]{1,0:T(8,128)(2,1)}, u32[]{:S(2)}, u32[]{:S(2)}) collective-permute-start(bf16[512,1024]{1,0:T(8,128)(2,1)} %get-tuple-element.65), channel_id=1, source_target_pairs={{0,1},{1,0},{2,3},{3,2},{4,5},{5,4},{6,7},{7,6},{8,9},{9,8},{10,11... | collective-permute-start | bytes 3145736 | tf_op jit(solution)/shard_map/ppermute | solution.py:618
  53.6 14.1 %copy-start.11 = (bf16[512,1024]{1,0:T(8,128)(2,1)S(1)}, bf16[512,1024]{1,0:T(8,128)(2,1)}, u32[]{:S(2)}) copy-start(bf16[512,1024]{1,0:T(8,128)(2,1)} %get-tuple-element.71) | copy-start | bytes 3145732
  67.1 3.6 %collective-permute-start.4 = (bf16[512,1536]{1,0:T(8,128)(2,1)S(1)}, bf16[512,1536]{1,0:T(8,128)(2,1)S(1)}, u32[]{:S(2)}, u32[]{:S(2)}) collective-permute-start(bf16[512,1536]{1,0:T(8,128)(2,1)S(1)} %get-tuple-element.75), channel_id=1, source_target_pairs={{0,1},{1,0},{2,3},{3,2},{4,5},{5,4},{6,7},{7,6},{8,9},{9,8},{10,11... | collective-permute-start | bytes 4718600 | tf_op jit(solution)/shard_map/ppermute | solution.py:618
  73.4 17.3 %collective-permute-start.5 = (bf16[2,128,1280]{2,1,0:T(8,128)(2,1)}, bf16[2,128,1280]{2,1,0:T(8,128)(2,1)}, u32[]{:S(2)}, u32[]{:S(2)}) collective-permute-start(bf16[2,128,1280]{2,1,0:T(8,128)(2,1)} %slice_bitcast_fusion.1.refs_0_), channel_id=1, source_target_pairs={{0,2},{1,3},{2,0},{3,1},{4,6},{5,7},{6,4},{7,5},{8,10},{9,11},{10,... | collective-permute-start | bytes 1966088 | tf_op jit(solution)/shard_map/ppermute | solution.py:618
  74.9 17.0 %collective-permute-start.6 = (bf16[2,128,1280]{2,1,0:T(8,128)(2,1)}, bf16[2,128,1280]{2,1,0:T(8,128)(2,1)}, u32[]{:S(2)}, u32[]{:S(2)}) collective-permute-start(bf16[2,128,1280]{2,1,0:T(8,128)(2,1)} %bitcast.7.refs_1_), channel_id=1, source_target_pairs={{0,4},{1,5},{2,6},{3,7},{4,0},{5,1},{6,2},{7,3},{8,12},{9,13},{10,... | collective-permute-start | bytes 1966088 | tf_op jit(solution)/shard_map/ppermute | solution.py:618
  75.5 16.4 %copy-start.9 = (bf16[512,1280]{1,0:T(8,128)(2,1)S(1)}, bf16[512,1280]{1,0:T(8,128)(2,1)}, u32[]{:S(2)}) copy-start(bf16[512,1280]{1,0:T(8,128)(2,1)} %copy-done.8) | copy-start | bytes 3932164
  89.3 4.6 %copy-start.10 = (bf16[256,1280]{1,0:T(8,128)(2,1)S(1)}, bf16[256,1280]{1,0:T(8,128)(2,1)}, u32[]{:S(2)}) copy-start(bf16[256,1280]{1,0:T(8,128)(2,1)} %get-tuple-element.108) | copy-start | bytes 1966084
  91.9 4.8 %collective-permute-start.7 = (bf16[512,1536]{1,0:T(8,128)(2,1)S(1)}, bf16[512,1536]{1,0:T(8,128)(2,1)S(1)}, u32[]{:S(2)}, u32[]{:S(2)}) collective-permute-start(bf16[512,1536]{1,0:T(8,128)(2,1)S(1)} %get-tuple-element.81), channel_id=1, source_target_pairs={{0,1},{1,0},{2,3},{3,2},{4,5},{5,4},{6,7},{7,6},{8,9},{9,8},{10,11... | collective-permute-start | bytes 4718600 | tf_op jit(solution)/shard_map/ppermute | solution.py:618
  93.2 18.1 %collective-permute-start.12 = (bf16[128,1280]{1,0:T(8,128)(2,1)S(1)}, bf16[128,1280]{1,0:T(8,128)(2,1)S(1)}, u32[]{:S(2)}, u32[]{:S(2)}) collective-permute-start(bf16[128,1280]{1,0:T(8,128)(2,1)S(1)} %slice_bitcast_fusion.8.refs_0_), channel_id=1, source_target_pairs={{0,4},{1,5},{2,6},{3,7},{4,0},{5,1},{6,2},{7,3},{8,12},{9,13},{10,... | collective-permute-start | bytes 983048 | tf_op jit(solution)/shard_map/ppermute | solution.py:618
  95.2 16.1 %collective-permute-start.13 = (bf16[128,1280]{1,0:T(8,128)(2,1)S(1)}, bf16[128,1280]{1,0:T(8,128)(2,1)S(1)}, u32[]{:S(2)}, u32[]{:S(2)}) collective-permute-start(bf16[128,1280]{1,0:T(8,128)(2,1)S(1)} %slice_bitcast_fusion.7.refs_1_), channel_id=1, source_target_pairs={{0,2},{1,3},{2,0},{3,1},{4,6},{5,7},{6,4},{7,5},{8,10},{9,11},{10,... | collective-permute-start | bytes 983048 | tf_op jit(solution)/shard_map/ppermute | solution.py:618
  97.3 16.3 %collective-permute-start.8 = (bf16[2,128,768]{2,1,0:T(8,128)(2,1)S(1)}, bf16[2,128,768]{2,1,0:T(8,128)(2,1)S(1)}, u32[]{:S(2)}, u32[]{:S(2)}) collective-permute-start(bf16[2,128,768]{2,1,0:T(8,128)(2,1)S(1)} %slice_bitcast_fusion.2.refs_2_), channel_id=1, source_target_pairs={{0,2},{1,3},{2,0},{3,1},{4,6},{5,7},{6,4},{7,5},{8,10},{9,11},{10,... | collective-permute-start | bytes 1179656 | tf_op jit(solution)/shard_map/ppermute | solution.py:618
  98.0 15.6 %collective-permute-start.9 = (bf16[2,128,768]{2,1,0:T(8,128)(2,1)S(1)}, bf16[2,128,768]{2,1,0:T(8,128)(2,1)S(1)}, u32[]{:S(2)}, u32[]{:S(2)}) collective-permute-start(bf16[2,128,768]{2,1,0:T(8,128)(2,1)S(1)} %bitcast.82), channel_id=1, source_target_pairs={{0,4},{1,5},{2,6},{3,7},{4,0},{5,1},{6,2},{7,3},{8,12},{9,13},{10,... | collective-permute-start | bytes 1179656 | tf_op jit(solution)/shard_map/ppermute | solution.py:618
  113.9 24.8 %collective-permute-start.17 = (bf16[48,1024]{1,0:T(8,128)(2,1)S(1)}, bf16[48,1024]{1,0:T(8,128)(2,1)S(1)}, u32[]{:S(2)}, u32[]{:S(2)}) collective-permute-start(bf16[48,1024]{1,0:T(8,128)(2,1)S(1)} %get-tuple-element.98), channel_id=1, source_target_pairs={{0,31},{1,24},{2,25},{3,26},{4,27},{5,28},{6,29},{7,30},{8,7},{9,0... | collective-permute-start | bytes 294920 | tf_op jit(solution)/shard_map/ppermute | solution.py:589
  115.0 7.5 %collective-permute-start.10 = (bf16[128,768]{1,0:T(8,128)(2,1)S(1)}, bf16[128,768]{1,0:T(8,128)(2,1)S(1)}, u32[]{:S(2)}, u32[]{:S(2)}) collective-permute-start(bf16[128,768]{1,0:T(8,128)(2,1)S(1)} %slice_bitcast_fusion.11), channel_id=1, source_target_pairs={{0,4},{1,5},{2,6},{3,7},{4,0},{5,1},{6,2},{7,3},{8,12},{9,13},{10,... | collective-permute-start | bytes 589832 | tf_op jit(solution)/shard_map/ppermute | solution.py:618
  116.7 7.0 %collective-permute-start.11 = (bf16[128,768]{1,0:T(8,128)(2,1)S(1)}, bf16[128,768]{1,0:T(8,128)(2,1)S(1)}, u32[]{:S(2)}, u32[]{:S(2)}) collective-permute-start(bf16[128,768]{1,0:T(8,128)(2,1)S(1)} %slice_bitcast_fusion.9), channel_id=1, source_target_pairs={{0,2},{1,3},{2,0},{3,1},{4,6},{5,7},{6,4},{7,5},{8,10},{9,11},{10,... | collective-permute-start | bytes 589832 | tf_op jit(solution)/shard_map/ppermute | solution.py:618
  117.1 21.7 %collective-permute-start.15 = (bf16[128,1024]{1,0:T(8,128)(2,1)S(1)}, bf16[128,1024]{1,0:T(8,128)(2,1)S(1)}, u32[]{:S(2)}, u32[]{:S(2)}) collective-permute-start(bf16[128,1024]{1,0:T(8,128)(2,1)S(1)} %get-tuple-element.96), channel_id=1, source_target_pairs={{0,7},{1,0},{2,1},{3,2},{4,3},{5,4},{6,5},{7,6},{8,15},{9,8},{10,9... | collective-permute-start | bytes 786440 | tf_op jit(solution)/shard_map/ppermute | solution.py:589
  119.0 10.1 %collective-permute-start.14 = (bf16[64,2560]{1,0:T(8,128)(2,1)S(1)}, bf16[64,2560]{1,0:T(8,128)(2,1)S(1)}, u32[]{:S(2)}, u32[]{:S(2)}) collective-permute-start(bf16[64,2560]{1,0:T(8,128)(2,1)S(1)} %bitcast.84), channel_id=1, source_target_pairs={{0,8},{1,9},{2,10},{3,11},{4,12},{5,13},{6,14},{7,15},{8,0},{9,1},... | collective-permute-start | bytes 983048 | tf_op jit(solution)/shard_map/ppermute | solution.py:618
  122.5 19.3 %collective-permute-start.16 = (bf16[208,1024]{1,0:T(8,128)(2,1)S(1)}, bf16[208,1024]{1,0:T(8,128)(2,1)S(1)}, u32[]{:S(2)}, u32[]{:S(2)}) collective-permute-start(bf16[208,1024]{1,0:T(8,128)(2,1)S(1)} %get-tuple-element.97), channel_id=1, source_target_pairs={{0,24},{1,25},{2,26},{3,27},{4,28},{5,29},{6,30},{7,31},{8,0},{9,1... | collective-permute-start | bytes 1277960 | tf_op jit(solution)/shard_map/ppermute | solution.py:589
  124.5 17.2 %copy-start = (bf16[384,448]{1,0:T(8,128)(2,1)S(1)}, bf16[384,448]{1,0:T(8,128)(2,1)}, u32[]{:S(2)}) copy-start(bf16[384,448]{1,0:T(8,128)(2,1)} %constant.52.clone.refs_10_) | copy-start | bytes 1032196
  124.5 17.2 %copy-start.1 = (bf16[192,416]{1,0:T(8,128)(2,1)S(1)}, bf16[192,416]{1,0:T(8,128)(2,1)}, u32[]{:S(2)}) copy-start(bf16[192,416]{1,0:T(8,128)(2,1)} %constant.51.clone.refs_9_) | copy-start | bytes 479236
  124.5 17.3 %copy-start.3 = (bf16[192,288]{1,0:T(8,128)(2,1)S(1)}, bf16[192,288]{1,0:T(8,128)(2,1)}, u32[]{:S(2)}) copy-start(bf16[192,288]{1,0:T(8,128)(2,1)} %constant.54.clone.refs_12_) | copy-start | bytes 331780
  124.5 17.3 %copy-start.4 = (bf16[192,192]{1,0:T(8,128)(2,1)S(1)}, bf16[192,192]{1,0:T(8,128)(2,1)}, u32[]{:S(2)}) copy-start(bf16[192,192]{1,0:T(8,128)(2,1)} %constant.53.clone.refs_11_) | copy-start | bytes 221188
  124.5 19.4 %collective-permute-start.18 = (bf16[32,1536]{1,0:T(8,128)(2,1)}, bf16[32,1536]{1,0:T(8,128)(2,1)}, u32[]{:S(2)}, u32[]{:S(2)}) collective-permute-start(bf16[32,1536]{1,0:T(8,128)(2,1)} %get-tuple-element.113.refs_0_), channel_id=1, source_target_pairs={{0,8},{1,9},{2,10},{3,11},{4,12},{5,13},{6,14},{7,15},{8,0},{9,1},... | collective-permute-start | bytes 294920 | tf_op jit(solution)/shard_map/ppermute | solution.py:618
  129.1 14.9 %collective-permute-start.20 = (bf16[32,1536]{1,0:T(8,128)(2,1)}, bf16[32,1536]{1,0:T(8,128)(2,1)}, u32[]{:S(2)}, u32[]{:S(2)}) collective-permute-start(bf16[32,1536]{1,0:T(8,128)(2,1)} %get-tuple-element.115.refs_2_), channel_id=1, source_target_pairs={{0,24},{1,25},{2,26},{3,27},{4,28},{5,29},{6,30},{7,31},{8,16},{9,... | collective-permute-start | bytes 294920 | tf_op jit(solution)/shard_map/ppermute | solution.py:618
  138.8 10.5 %collective-permute-start.19 = (bf16[32,4096]{1,0:T(8,128)(2,1)}, bf16[32,4096]{1,0:T(8,128)(2,1)}, u32[]{:S(2)}, u32[]{:S(2)}) collective-permute-start(bf16[32,4096]{1,0:T(8,128)(2,1)} %pad_maximum_fusion.2.refs_1_), channel_id=1, source_target_pairs={{0,16},{1,17},{2,18},{3,19},{4,20},{5,21},{6,22},{7,23},{8,24},{9,... | collective-permute-start | bytes 786440 | tf_op jit(solution)/shard_map/ppermute | solution.py:618
  (6 other events, 12.1 us)

commit v13 on v12

--- a/solution.py
+++ b/solution.py
@@ -15,6 +15,7 @@
 HALF = SHIFT // 2
 TILE = 256
 WIDE = 512
+BROAD = 1024
 EPSILON = 1e-05
 MIB = 1 << 20
 
@@ -152,10 +153,10 @@
 ):
     count, channels = xw.shape
     places = 2 * WIN * WIN
-    tiles = wqkv.shape[1] // WIDE
+    tiles = wqkv.shape[1] // BROAD
 
     def load(n):
-        columns = aligned(n * WIDE, WIDE)
+        columns = aligned(n * BROAD, BROAD)
         return pltpu.make_async_copy(wqkv_h.at[:, columns], wqkv.at[:, columns], in_sem.at[n])
 
     for n in range(tiles):
@@ -174,7 +175,7 @@
     @pl.loop(0, tiles)
     def _(n):
         load(n).wait()
-        columns = aligned(n * WIDE, WIDE)
+        columns = aligned(n * BROAD, BROAD)
         proj[:, columns] = dot(normed[...], wqkv[:, columns]).astype(BF16)
 
     masks = head_masks()
@@ -254,9 +255,9 @@
     loads[0].wait()
     outer_rows = slice(0, outer)
 
-    @pl.loop(0, wqkv.shape[1] // WIDE)
+    @pl.loop(0, wqkv.shape[1] // BROAD)
     def _(n):
-        columns = aligned(n * WIDE, WIDE)
+        columns = aligned(n * BROAD, BROAD)
         proj[outer_rows, columns] = dot(normed[outer_rows], wqkv[:, columns]).astype(BF16)
 
     for load in ready:
@@ -490,30 +491,22 @@
     return loads, tiles
 
 
-def input_kernel(*refs):
-    (pg0, pg1, wqkv_h, normed_h, rstd_h, grad_h, merged,
-     pick_first, pick_last, pick_groups, full, side, below, corner,
-     pgrad, wqkv, ngrad, normed, rstd, grad, sem, more_sem) = refs
+def product_kernel(pg0, pg1, wqkv_h, ngrad, pgrad, wqkv, sem):
+    channels = ngrad.shape[1]
+    loads, tiles = projection_loads([pg0, pg1], wqkv_h, pgrad, wqkv, sem, 0)
+    for load in loads + tiles:
+        load.wait()
+
+    @pl.loop(0, channels // BROAD)
+    def _(n):
+        rows = aligned(n * BROAD, BROAD)
+        ngrad[:, rows] = dot(pgrad[...], wqkv[rows], NT).astype(BF16)
+
+
+def input_kernel(
+    ngrad, normed, rstd, grad, merged, pick_first, pick_last, pick_groups, full, side, below, corner,
+):
     count, channels = ngrad.shape
-    loads, tiles = projection_loads([pg0, pg1], wqkv_h, pgrad, wqkv, sem, 0)
-    more = [
-        pltpu.make_async_copy(src, dst, more_sem.at[i])
-        for i, (src, dst) in enumerate([(normed_h, normed), (rstd_h, rstd), (grad_h, grad)])
-    ]
-    for load in more:
-        load.start()
-    for load in loads:
-        load.wait()
-    for load in tiles:
-        load.wait()
-
-    @pl.loop(0, channels // WIDE)
-    def _(n):
-        rows = aligned(n * WIDE, WIDE)
-        ngrad[:, rows] = dot(pgrad[...], wqkv[rows], NT).astype(BF16)
-
-    for load in more:
-        load.wait()
     places = 2 * WIN * WIN
 
     @pl.loop(0, count // places)
@@ -866,33 +859,32 @@
 
     first_picks = picks(cs.side[:side_cut] + cs.above + cs.corner, cells[:half_cells])
     last_picks = picks(cs.side[side_cut:], cells[half_cells:])
-    full, *strips = tied_call(
-        input_kernel, given1 + given2,
-        [pg0, pg1, qkv_weight, pinned(normed), pinned(rstd), pinned(grad), merged,
-         first_picks, last_picks, picks(sum(g_strips, []), grps)],
-        [hbm] * 6 + [vmem] * 4, [wide] + [shape(*e) for e in extents], [vmem] * 4,
+    [ngrad] = tied_call(
+        product_kernel, given1 + given2,
+        [pg0, pg1, qkv_weight], [hbm] * 3, [wide], [vmem],
         scratch_shapes=[
             pltpu.VMEM((count, 3 * channels), BF16),
             pltpu.VMEM(qkv_weight.shape, BF16),
-            pltpu.VMEM((count, channels), BF16),
-            pltpu.VMEM((count, channels), BF16),
-            pltpu.VMEM((count, LANES), F32),
-            pltpu.VMEM((count, channels), BF16),
             pltpu.SemaphoreType.DMA((3 * halves + channels // TILE,)),
-            pltpu.SemaphoreType.DMA((3,)),
         ],
-        name="input_backward", **settings(13, 40),
+        name="input_product", **settings(8, 36),
     )
-    arrived1 = behind(arrived1, full)
-    arrived2 = behind(arrived2, full)
-    arrived1 = behind(arrived1, arrived2)
-    strips = sent_strips(behind(strips, (arrived1, arrived2)), sizes, -1)
-    layer2.add(arrived2)
-    total2 = layer2.finish()
+    arrived1 = behind(arrived1, ngrad)
     layer1.add(arrived1)
     total1 = layer1.finish()
     kept1, given1 = column_halves(total1, sizes, 1)
     got1 = exchange(given1, sizes, 1, 0)
+    full, *strips = tied_call(
+        input_kernel, [given1],
+        [ngrad, normed, rstd, grad, merged,
+         first_picks, last_picks, picks(sum(g_strips, []), grps)],
+        [vmem] * 8, [wide] + [shape(*e) for e in extents], [vmem] * 4,
+        name="input_backward", **settings(5, 30),
+    )
+    got1, *arrived2 = behind([got1] + arrived2, full)
+    strips = sent_strips(behind(strips, (got1, arrived2)), sizes, -1)
+    layer2.add(arrived2)
+    total2 = layer2.finish()
 
     part1 = kept1 + got1.astype(F32)
     column2 = column_blocks(total2, [], sizes)

time: 152 us -> 149 us (0.980)
  waiting for transfers between devices: 24 us -> 32 us
  starting transfers between devices: 28.7 us -> 21 us
  Pallas kernels: 86.6 us -> 83.1 us
    ppermute x15, waiting for transfers between devices: 18.6 us -> 26.2 us  [exchange(): return lax.ppermute(block, ('lat', 'lon'), route)]
    ppermute x15, starting transfers between devices: 18.9 us -> 12.1 us  [exchange(): return lax.ppermute(block, ('lat', 'lon'), route)]
    pallas_call x5 -> x6, Pallas kernels: 50.8 us -> 47.4 us  [tied_call(): pl.pallas_call(body, out_shape=out_shape, in_specs=[pl.BlockSpec(memory_s...]
  transfers between devices with their start and end apart: 21 -> 21, of which waited for: 9 -> 12; matrix products, arithmetic and copies ran while one was open for 5% -> 5% of each run, Pallas kernels for 34% -> 32%
where the time goes in v13:
time: 149 us
  Pallas kernels  83.1 us (56%)
  waiting for transfers between devices  32 us (21%)
  starting transfers between devices  21 us (14%)
  other arithmetic  8.19 us (5%)
  local copies, waits for them, and re-layouts  3.26 us (2%)
    pallas_call x6, Pallas kernels, tied_call(): pl.pallas_call(body, out_shape=out_shape, in_specs=[pl.BlockSpec(memory_s...  47.4 us
    pallas_call x1, Pallas kernels, shards(): pl.pallas_call(forward_kernel, out_shape=[wide, shape(channels, count), s...  30.7 us
    ppermute x15, waiting for transfers between devices, exchange(): return lax.ppermute(block, ('lat', 'lon'), route)  26.2 us
    ppermute x15, starting transfers between devices, exchange(): return lax.ppermute(block, ('lat', 'lon'), route)  12.1 us
    ppermute x6, starting transfers between devices, sent(): return lax.ppermute(block, ('lat', 'lon'), route)  8.89 us
    convert_element_type x10, other arithmetic, core_sum(): return (mine.astype(F32) + arrived.astype(F32)).astype(BF16)  5.95 us
    ppermute x6, waiting for transfers between devices, sent(): return lax.ppermute(block, ('lat', 'lon'), route)  5.81 us
    pallas_call x1, Pallas kernels, shards(): pl.pallas_call(pack_kernel, out_shape=[shape(*e) for e in extents], in_sp...  3.14 us
  transfers between devices with their start and end apart: 21, of which 12 were waited for; matrix products, arithmetic and copies ran while one was open for 5% of the time, Pallas kernels for 32%

profile of v13, /device:TPU:0, one launch (start us, length us, event | category | flops | bytes accessed | tf_op | source)
XLA Modules:
  0.0 148.6 jit_solution(13588551614959992853)
XLA Ops:
  0.6 3.1 %pack_strips.1 = (bf16[128,1024]{1,0:T(8,128)(2,1)}, bf16[208,1024]{1,0:T(8,128)(2,1)}, bf16[48,1024]{1,0:T(8,128)(2,1)}) custom-call(bf16[768,1024]{1,0:T(8,128)(2,1)} %bitcast.99, bf16[192,1024]{1,0:T(8,128)(2,1)} %bitcast.102, bf16[288,768]{1,0:T(8,128)(2,1)} %constant.41.clone.pick_cells, bf16[96,192]{1,0:T(8,128)(2,1)} %constant.42.clone.pick_groups), custom_call_target="tpu_custom_call" | custom-call | flops 10000000000 | bytes 16777216 | tf_op jit(solution)/shard_map/pack_strips/pallas_call | solution.py:756
  3.8 2.5 %collective-permute-start.2 = (bf16[48,1024]{1,0:T(8,128)(2,1)}, bf16[48,1024]{1,0:T(8,128)(2,1)S(1)}, u32[]{:S(2)}, u32[]{:S(2)}) collective-permute-start(bf16[48,1024]{1,0:T(8,128)(2,1)} %get-tuple-element.56.refs_2_), channel_id=1, source_target_pairs={{0,9},{1,10},{2,11},{3,12},{4,13},{5,14},{6,15},{7,8},{8,17},{9,18... | collective-permute-start | bytes 294920 | tf_op jit(solution)/shard_map/ppermute | solution.py:582
  6.2 1.6 %collective-permute-start = (bf16[128,1024]{1,0:T(8,128)(2,1)}, bf16[128,1024]{1,0:T(8,128)(2,1)S(1)}, u32[]{:S(2)}, u32[]{:S(2)}) collective-permute-start(bf16[128,1024]{1,0:T(8,128)(2,1)} %get-tuple-element.54.refs_0_), channel_id=1, source_target_pairs={{0,1},{1,2},{2,3},{3,4},{4,5},{5,6},{6,7},{7,0},{8,9},{9,10},{10,1... | collective-permute-start | bytes 786440 | tf_op jit(solution)/shard_map/ppermute | solution.py:582
  7.8 1.6 %collective-permute-start.1 = (bf16[208,1024]{1,0:T(8,128)(2,1)}, bf16[208,1024]{1,0:T(8,128)(2,1)S(1)}, u32[]{:S(2)}, u32[]{:S(2)}) collective-permute-start(bf16[208,1024]{1,0:T(8,128)(2,1)} %get-tuple-element.55.refs_1_), channel_id=1, source_target_pairs={{0,8},{1,9},{2,10},{3,11},{4,12},{5,13},{6,14},{7,15},{8,16},{9,17... | collective-permute-start | bytes 1277960 | tf_op jit(solution)/shard_map/ppermute | solution.py:582
  9.4 9.3 %inner_windows.1 = (bf16[256,1024]{1,0:T(8,128)(2,1)}, bf16[256,1024]{1,0:T(8,128)(2,1)}, f32[256,128]{1,0:T(8,128)}, bf16[256,1024]{1,0:T(8,128)(2,1)}, f32[256,1024]{1,0:T(8,128)}, /*index=5*/bf16[256,3072]{1,0:T(8,128)(2,1)}) custom-call(bf16[128,1024]{1,0:T(8,128)(2,1)} %get-tuple-element.54.refs_0_, bf16[208,1024]{1,0:T(8,128)(2,1)} %get-tuple-element.55.refs_1_, ...), custom_call_target="tpu_custom_call" | custom-call | flops 89999998976 | bytes 16777216 | tf_op jit(solution)/shard_map/inner_windows/pallas_call | solution.py:702
  19.3 2.5 %collective-permute-done.1.above = bf16[208,1024]{1,0:T(8,128)(2,1)S(1)} collective-permute-done((bf16[208,1024]{1,0:T(8,128)(2,1)}, bf16[208,1024]{1,0:T(8,128)(2,1)S(1)}, u32[]{:S(2)}, u32[]{:S(2)}) %collective-permute-start.1) | collective-permute-done | bytes 426016 | tf_op jit(solution)/shard_map/ppermute | solution.py:582
  22.6 30.7 %block_forward.1 = (bf16[768,1024]{1,0:T(8,128)(2,1)}, bf16[1024,768]{1,0:T(8,128)(2,1)}, bf16[768,3072]{1,0:T(8,128)(2,1)}, bf16[768,1024]{1,0:T(8,128)(2,1)}, ...) custom-call(s32[1]{0:T(128)} %bitcast.edge.refs_0_.refs_2_, ...), custom_call_target="tpu_custom_call" | custom-call | flops 299999985664 | bytes 16777216 | tf_op jit(solution)/shard_map/block_forward/pallas_call | solution.py:786
  53.4 13.5 %attention_backward.2 = (bf16[768,1536]{1,0:T(8,128)(2,1)S(1)}, bf16[512,1536]{1,0:T(8,128)(2,1)S(1)}, bf16[512,1536]{1,0:T(8,128)(2,1)S(1)}) custom-call(s32[1]{0:T(128)} %bitcast.edge.refs_0_.refs_2_, bf16[768,3072]{1,0:T(8,128)(2,1)} %get-tuple-element.65.refs_1_.refs_3_, bf16[768,1024]{1,0:T(8,128)(2,1)} %get-tuple-element.66.refs_2_.refs_4_, ...), custom_call_target="tpu_custom_call" | custom-call | flops 149999992832 | bytes 16777216 | tf_op jit(solution)/shard_map/attention_backward/pallas_call | solution.py:702
  67.5 1.6 %add_convert_fusion.2 = bf16[512,1024]{1,0:T(8,128)(2,1)S(1)} fusion(bf16[512,1024]{1,0:T(8,128)(2,1)} %collective-permute-done.3, bf16[512,1024]{1,0:T(8,128)(2,1)S(1)} %copy-done.13), kind=kLoop, calls=%fused_computation.2 | loop fusion | flops 2097152 | bytes 3145728 | tf_op jit(solution)/shard_map/convert_element_type | solution.py:619
  69.2 1.4 collective-permute-done.4
  71.0 1.2 fusion.15
  73.2 1.5 %collective-permute-start.5 = (bf16[2,128,1280]{2,1,0:T(8,128)(2,1)}, bf16[2,128,1280]{2,1,0:T(8,128)(2,1)}, u32[]{:S(2)}, u32[]{:S(2)}) collective-permute-start(bf16[2,128,1280]{2,1,0:T(8,128)(2,1)} %slice_bitcast_fusion.1.refs_0_), channel_id=1, source_target_pairs={{0,2},{1,3},{2,0},{3,1},{4,6},{5,7},{6,4},{7,5},{8,10},{9,11},{10,... | collective-permute-start | bytes 1966088 | tf_op jit(solution)/shard_map/ppermute | solution.py:611
  75.4 13.7 %attention_backward.3 = (bf16[768,1536]{1,0:T(8,128)(2,1)S(1)}, bf16[512,1536]{1,0:T(8,128)(2,1)S(1)}, bf16[512,1536]{1,0:T(8,128)(2,1)S(1)}) custom-call(bf16[2,128,1280]{2,1,0:T(8,128)(2,1)} %slice_bitcast_fusion.1.refs_0_, bf16[2,128,1280]{2,1,0:T(8,128)(2,1)} %bitcast.7.refs_1_, s32[1]{0:T(128)} %bitcast.edge.refs_0_.refs_2_, ...), custom_call_target="tpu_custom_call" | custom-call | flops 149999992832 | bytes 16777216 | tf_op jit(solution)/shard_map/attention_backward/pallas_call | solution.py:702
  89.1 1.5 collective-permute-done.5
  90.5 1.2 collective-permute-done.6
  91.8 1.4 fusion.1
  94.0 1.6 %fusion = bf16[2,128,1280]{2,1,0:T(8,128)(2,1)S(1)} fusion(bf16[2,128,1280]{2,1,0:T(8,128)(2,1)S(1)} %bitcast.93, bf16[2,128,1280]{2,1,0:T(8,128)(2,1)} %collective-permute-done.6), kind=kLoop, calls=%fused_computation.5 | loop fusion | flops 1310720 | bytes 1966080 | tf_op jit(solution)/shard_map/convert_element_type | solution.py:619
  95.6 1.1 collective-permute-start.9
  97.3 1.1 collective-permute-start.11
  98.4 6.3 %input_product.1.refs_1_ = bf16[768,1024]{1,0:T(8,128)(2,1)S(1)} custom-call(bf16[128,1280]{1,0:T(8,128)(2,1)S(1)} %slice_bitcast_fusion.7.refs_0_, bf16[128,1280]{1,0:T(8,128)(2,1)S(1)} %slice_bitcast_fusion.6.refs_1_, bf16[2,128,768]{2,1,0:T(8,128)(2,1)S(1)} %slice_bitcast_fusion.2.refs_2_, bf16[2,128,768]{2,1,0:T(8,128)(2,1)S(1)} %bitcast.82, ...), custom_call_target="tpu_custom_call" | custom-call | flops 80000000000 | bytes 16777216 | tf_op jit(solution)/shard_map/input_product/pallas_call | solution.py:702
  106.6 2.5 %input_backward.1 = (bf16[768,1024]{1,0:T(8,128)(2,1)S(1)}, bf16[128,1024]{1,0:T(8,128)(2,1)S(1)}, bf16[208,1024]{1,0:T(8,128)(2,1)S(1)}, bf16[48,1024]{1,0:T(8,128)(2,1)S(1)}) custom-call(bf16[64,2560]{1,0:T(8,128)(2,1)S(1)} %bitcast.85, bf16[768,1024]{1,0:T(8,128)(2,1)S(1)} %input_product.1.refs_1_, bf16[768,1024]{1,0:T(8,128)(2,1)S(1)} %copy-done.7, ...), custom_call_target="tpu_custom_call" | custom-call | flops 49999998976 | bytes 16777216 | tf_op jit(solution)/shard_map/input_backward/pallas_call | solution.py:702
  109.1 6.1 %collective-permute-done.10 = bf16[64,2560]{1,0:T(8,128)(2,1)S(1)} collective-permute-done((bf16[64,2560]{1,0:T(8,128)(2,1)S(1)}, bf16[64,2560]{1,0:T(8,128)(2,1)S(1)}, u32[]{:S(2)}, u32[]{:S(2)}) %collective-permute-start.10) | collective-permute-done | bytes 327712 | tf_op jit(solution)/shard_map/ppermute | solution.py:611
  117.0 1.7 %collective-permute-start.13 = (bf16[128,768]{1,0:T(8,128)(2,1)S(1)}, bf16[128,768]{1,0:T(8,128)(2,1)S(1)}, u32[]{:S(2)}, u32[]{:S(2)}) collective-permute-start(bf16[128,768]{1,0:T(8,128)(2,1)S(1)} %slice_bitcast_fusion.11), channel_id=1, source_target_pairs={{0,4},{1,5},{2,6},{3,7},{4,0},{5,1},{6,2},{7,3},{8,12},{9,13},{10,... | collective-permute-start | bytes 589832 | tf_op jit(solution)/shard_map/ppermute | solution.py:611
  118.8 1.8 %collective-permute-start.15 = (bf16[128,1024]{1,0:T(8,128)(2,1)S(1)}, bf16[128,1024]{1,0:T(8,128)(2,1)S(1)}, u32[]{:S(2)}, u32[]{:S(2)}) collective-permute-start(bf16[128,1024]{1,0:T(8,128)(2,1)S(1)} %get-tuple-element.94), channel_id=1, source_target_pairs={{0,7},{1,0},{2,1},{3,2},{4,3},{5,4},{6,5},{7,6},{8,15},{9,8},{10,9... | collective-permute-start | bytes 786440 | tf_op jit(solution)/shard_map/ppermute | solution.py:582
  121.2 3.6 %collective-permute-done.13 = bf16[128,768]{1,0:T(8,128)(2,1)S(1)} collective-permute-done((bf16[128,768]{1,0:T(8,128)(2,1)S(1)}, bf16[128,768]{1,0:T(8,128)(2,1)S(1)}, u32[]{:S(2)}, u32[]{:S(2)}) %collective-permute-start.13) | collective-permute-done | bytes 196640 | tf_op jit(solution)/shard_map/ppermute | solution.py:611
  126.7 1.7 %collective-permute-start.20 = (bf16[32,1536]{1,0:T(8,128)(2,1)}, bf16[32,1536]{1,0:T(8,128)(2,1)}, u32[]{:S(2)}, u32[]{:S(2)}) collective-permute-start(bf16[32,1536]{1,0:T(8,128)(2,1)} %get-tuple-element.113.refs_2_), channel_id=1, source_target_pairs={{0,24},{1,25},{2,26},{3,27},{4,28},{5,29},{6,30},{7,31},{8,16},{9,... | collective-permute-start | bytes 294920 | tf_op jit(solution)/shard_map/ppermute | solution.py:611
  129.1 1.2 collective-permute-start.19
  130.3 3.3 %collective-permute-done.16.refs_7_ = bf16[208,1024]{1,0:T(8,128)(2,1)S(1)} collective-permute-done((bf16[208,1024]{1,0:T(8,128)(2,1)S(1)}, bf16[208,1024]{1,0:T(8,128)(2,1)S(1)}, u32[]{:S(2)}, u32[]{:S(2)}) %collective-permute-start.16) | collective-permute-done | bytes 426016 | tf_op jit(solution)/shard_map/ppermute | solution.py:582
  133.6 2.1 %unpack_strips.1 = (bf16[768,1024]{1,0:T(8,128)(2,1)}, bf16[192,1024]{1,0:T(8,128)(2,1)}) custom-call(bf16[32,1536]{1,0:T(8,128)(2,1)} %get-tuple-element.111.refs_0_, bf16[32,4096]{1,0:T(8,128)(2,1)} %pad_maximum_fusion.2.refs_1_, bf16[32,1536]{1,0:T(8,128)(2,1)} %get-tuple-element.113.refs_2_, bf16[64,2560]{1,0:T(8,128)(2,1)S(1)} %bitcast.86, ...), custom_call_target="tpu_custom_call" | custom-call | flops 199999995904 | bytes 16777216 | tf_op jit(solution)/shard_map/unpack_strips/pallas_call | solution.py:702
  135.8 1.1 collective-permute-done.20.refs_2_
  136.9 9.9 %collective-permute-done.19.refs_1_ = bf16[32,4096]{1,0:T(8,128)(2,1)} collective-permute-done((bf16[32,4096]{1,0:T(8,128)(2,1)}, bf16[32,4096]{1,0:T(8,128)(2,1)}, u32[]{:S(2)}, u32[]{:S(2)}) %collective-permute-start.19) | collective-permute-done | bytes 262176 | tf_op jit(solution)/shard_map/ppermute | solution.py:611
  146.8 1.8 %end_sums.1 = (f32[32,3072]{1,0:T(8,128)}, f32[32,1024]{1,0:T(8,128)}) custom-call(f32[32,2560]{1,0:T(8,128)S(1)} %slice_bitcast_fusion.4.kept1, f32[32,1536]{1,0:T(8,128)S(1)} %get-tuple-element.110.kept2, bf16[32,1536]{1,0:T(8,128)(2,1)} %collective-permute-done.18.refs_0_, bf16[32,4096]{1,0:T(8,128)(2,1)} %collective-permute-done.19.refs_1_, ...), custom_call_target="tpu_custom_call" | custom-call | flops 10000000000 | bytes 16777216 | tf_op jit(solution)/shard_map/end_sums/pallas_call | solution.py:915
  (90 shorter events, 12.3 us)
Async XLA Ops:
  3.8 15.5 %collective-permute-start.2 = (bf16[48,1024]{1,0:T(8,128)(2,1)}, bf16[48,1024]{1,0:T(8,128)(2,1)S(1)}, u32[]{:S(2)}, u32[]{:S(2)}) collective-permute-start(bf16[48,1024]{1,0:T(8,128)(2,1)} %get-tuple-element.56.refs_2_), channel_id=1, source_target_pairs={{0,9},{1,10},{2,11},{3,12},{4,13},{5,14},{6,15},{7,8},{8,17},{9,18... | collective-permute-start | bytes 294920 | tf_op jit(solution)/shard_map/ppermute | solution.py:582
  6.2 13.0 %collective-permute-start = (bf16[128,1024]{1,0:T(8,128)(2,1)}, bf16[128,1024]{1,0:T(8,128)(2,1)S(1)}, u32[]{:S(2)}, u32[]{:S(2)}) collective-permute-start(bf16[128,1024]{1,0:T(8,128)(2,1)} %get-tuple-element.54.refs_0_), channel_id=1, source_target_pairs={{0,1},{1,2},{2,3},{3,4},{4,5},{5,6},{6,7},{7,0},{8,9},{9,10},{10,1... | collective-permute-start | bytes 786440 | tf_op jit(solution)/shard_map/ppermute | solution.py:582
  7.8 10.9 %copy-start.14 = (s32[32]{0:T(128)S(1)}, s32[32]{0:T(128)}, u32[]{:S(2)}) copy-start(s32[32]{0:T(128)} %constant.47.clone) | copy-start | bytes 388
  7.8 10.9 %copy-start.15 = (s32[32]{0:T(128)S(1)}, s32[32]{0:T(128)}, u32[]{:S(2)}) copy-start(s32[32]{0:T(128)} %constant.46.clone) | copy-start | bytes 388
  7.8 14.0 %collective-permute-start.1 = (bf16[208,1024]{1,0:T(8,128)(2,1)}, bf16[208,1024]{1,0:T(8,128)(2,1)S(1)}, u32[]{:S(2)}, u32[]{:S(2)}) collective-permute-start(bf16[208,1024]{1,0:T(8,128)(2,1)} %get-tuple-element.55.refs_1_), channel_id=1, source_target_pairs={{0,8},{1,9},{2,10},{3,11},{4,12},{5,13},{6,14},{7,15},{8,16},{9,17... | collective-permute-start | bytes 1277960 | tf_op jit(solution)/shard_map/ppermute | solution.py:582
  53.3 13.6 %collective-permute-start.3 = (bf16[512,1024]{1,0:T(8,128)(2,1)}, bf16[512,1024]{1,0:T(8,128)(2,1)}, u32[]{:S(2)}, u32[]{:S(2)}) collective-permute-start(bf16[512,1024]{1,0:T(8,128)(2,1)} %get-tuple-element.64), channel_id=1, source_target_pairs={{0,1},{1,0},{2,3},{3,2},{4,5},{5,4},{6,7},{7,6},{8,9},{9,8},{10,11... | collective-permute-start | bytes 3145736 | tf_op jit(solution)/shard_map/ppermute | solution.py:611
  53.4 14.1 %copy-start.13 = (bf16[512,1024]{1,0:T(8,128)(2,1)S(1)}, bf16[512,1024]{1,0:T(8,128)(2,1)}, u32[]{:S(2)}) copy-start(bf16[512,1024]{1,0:T(8,128)(2,1)} %get-tuple-element.70) | copy-start | bytes 3145732
  67.0 3.6 %collective-permute-start.4 = (bf16[512,1536]{1,0:T(8,128)(2,1)S(1)}, bf16[512,1536]{1,0:T(8,128)(2,1)S(1)}, u32[]{:S(2)}, u32[]{:S(2)}) collective-permute-start(bf16[512,1536]{1,0:T(8,128)(2,1)S(1)} %get-tuple-element.74), channel_id=1, source_target_pairs={{0,1},{1,0},{2,3},{3,2},{4,5},{5,4},{6,7},{7,6},{8,9},{9,8},{10,11... | collective-permute-start | bytes 4718600 | tf_op jit(solution)/shard_map/ppermute | solution.py:611
  72.2 16.8 %copy-start.11 = (bf16[512,1280]{1,0:T(8,128)(2,1)}, bf16[512,1280]{1,0:T(8,128)(2,1)S(1)}, u32[]{:S(2)}) copy-start(bf16[512,1280]{1,0:T(8,128)(2,1)S(1)} %pad_maximum_fusion) | copy-start | bytes 3932164
  73.2 17.3 %collective-permute-start.5 = (bf16[2,128,1280]{2,1,0:T(8,128)(2,1)}, bf16[2,128,1280]{2,1,0:T(8,128)(2,1)}, u32[]{:S(2)}, u32[]{:S(2)}) collective-permute-start(bf16[2,128,1280]{2,1,0:T(8,128)(2,1)} %slice_bitcast_fusion.1.refs_0_), channel_id=1, source_target_pairs={{0,2},{1,3},{2,0},{3,1},{4,6},{5,7},{6,4},{7,5},{8,10},{9,11},{10,... | collective-permute-start | bytes 1966088 | tf_op jit(solution)/shard_map/ppermute | solution.py:611
  74.7 17.0 %collective-permute-start.6 = (bf16[2,128,1280]{2,1,0:T(8,128)(2,1)}, bf16[2,128,1280]{2,1,0:T(8,128)(2,1)}, u32[]{:S(2)}, u32[]{:S(2)}) collective-permute-start(bf16[2,128,1280]{2,1,0:T(8,128)(2,1)} %bitcast.7.refs_1_), channel_id=1, source_target_pairs={{0,4},{1,5},{2,6},{3,7},{4,0},{5,1},{6,2},{7,3},{8,12},{9,13},{10,... | collective-permute-start | bytes 1966088 | tf_op jit(solution)/shard_map/ppermute | solution.py:611
  89.1 4.9 %copy-start.12 = (bf16[256,1280]{1,0:T(8,128)(2,1)S(1)}, bf16[256,1280]{1,0:T(8,128)(2,1)}, u32[]{:S(2)}) copy-start(bf16[256,1280]{1,0:T(8,128)(2,1)} %get-tuple-element.106) | copy-start | bytes 1966084
  91.7 5.0 %collective-permute-start.7 = (bf16[512,1536]{1,0:T(8,128)(2,1)S(1)}, bf16[512,1536]{1,0:T(8,128)(2,1)S(1)}, u32[]{:S(2)}, u32[]{:S(2)}) collective-permute-start(bf16[512,1536]{1,0:T(8,128)(2,1)S(1)} %get-tuple-element.80), channel_id=1, source_target_pairs={{0,1},{1,0},{2,3},{3,2},{4,5},{5,4},{6,7},{7,6},{8,9},{9,8},{10,11... | collective-permute-start | bytes 4718600 | tf_op jit(solution)/shard_map/ppermute | solution.py:611
  93.2 5.2 %slice-start = ((s8[6291456]{0:T(1024)(128)(4,1)}), s8[4194304]{0:T(1024)(128)(4,1)S(1)}, s32[]{:S(2)}) async-start(s8[6291456]{0:T(1024)(128)(4,1)} %bitcast.87), calls=%async_computation | async-start | bytes 8388608
  93.2 12.6 %collective-permute-start.8 = (bf16[128,1280]{1,0:T(8,128)(2,1)S(1)}, bf16[128,1280]{1,0:T(8,128)(2,1)S(1)}, u32[]{:S(2)}, u32[]{:S(2)}) collective-permute-start(bf16[128,1280]{1,0:T(8,128)(2,1)S(1)} %slice_bitcast_fusion.7.refs_0_), channel_id=1, source_target_pairs={{0,4},{1,5},{2,6},{3,7},{4,0},{5,1},{6,2},{7,3},{8,12},{9,13},{10,... | collective-permute-start | bytes 983048 | tf_op jit(solution)/shard_map/ppermute | solution.py:611
  95.6 10.6 %collective-permute-start.9 = (bf16[128,1280]{1,0:T(8,128)(2,1)S(1)}, bf16[128,1280]{1,0:T(8,128)(2,1)S(1)}, u32[]{:S(2)}, u32[]{:S(2)}) collective-permute-start(bf16[128,1280]{1,0:T(8,128)(2,1)S(1)} %slice_bitcast_fusion.6.refs_1_), channel_id=1, source_target_pairs={{0,2},{1,3},{2,0},{3,1},{4,6},{5,7},{6,4},{7,5},{8,10},{9,11},{10,... | collective-permute-start | bytes 983048 | tf_op jit(solution)/shard_map/ppermute | solution.py:611
  97.3 17.9 %collective-permute-start.11 = (bf16[2,128,768]{2,1,0:T(8,128)(2,1)S(1)}, bf16[2,128,768]{2,1,0:T(8,128)(2,1)S(1)}, u32[]{:S(2)}, u32[]{:S(2)}) collective-permute-start(bf16[2,128,768]{2,1,0:T(8,128)(2,1)S(1)} %slice_bitcast_fusion.2.refs_2_), channel_id=1, source_target_pairs={{0,2},{1,3},{2,0},{3,1},{4,6},{5,7},{6,4},{7,5},{8,10},{9,11},{10,... | collective-permute-start | bytes 1179656 | tf_op jit(solution)/shard_map/ppermute | solution.py:611
  98.4 8.2 %copy-start.8 = (bf16[768,1024]{1,0:T(8,128)(2,1)S(1)}, bf16[768,1024]{1,0:T(8,128)(2,1)}, u32[]{:S(2)}) copy-start(bf16[768,1024]{1,0:T(8,128)(2,1)} %get-tuple-element.85.refs_4_) | copy-start | bytes 4718596
  104.8 11.0 %collective-permute-start.12 = (bf16[2,128,768]{2,1,0:T(8,128)(2,1)S(1)}, bf16[2,128,768]{2,1,0:T(8,128)(2,1)S(1)}, u32[]{:S(2)}, u32[]{:S(2)}) collective-permute-start(bf16[2,128,768]{2,1,0:T(8,128)(2,1)S(1)} %bitcast.83), channel_id=1, source_target_pairs={{0,4},{1,5},{2,6},{3,7},{4,0},{5,1},{6,2},{7,3},{8,12},{9,13},{10,... | collective-permute-start | bytes 1179656 | tf_op jit(solution)/shard_map/ppermute | solution.py:611
  106.5 8.7 %collective-permute-start.10 = (bf16[64,2560]{1,0:T(8,128)(2,1)S(1)}, bf16[64,2560]{1,0:T(8,128)(2,1)S(1)}, u32[]{:S(2)}, u32[]{:S(2)}) collective-permute-start(bf16[64,2560]{1,0:T(8,128)(2,1)S(1)} %bitcast.84), channel_id=1, source_target_pairs={{0,8},{1,9},{2,10},{3,11},{4,12},{5,13},{6,14},{7,15},{8,0},{9,1},... | collective-permute-start | bytes 983048 | tf_op jit(solution)/shard_map/ppermute | solution.py:611
  116.1 13.0 %collective-permute-start.17 = (bf16[48,1024]{1,0:T(8,128)(2,1)S(1)}, bf16[48,1024]{1,0:T(8,128)(2,1)S(1)}, u32[]{:S(2)}, u32[]{:S(2)}) collective-permute-start(bf16[48,1024]{1,0:T(8,128)(2,1)S(1)} %get-tuple-element.96), channel_id=1, source_target_pairs={{0,31},{1,24},{2,25},{3,26},{4,27},{5,28},{6,29},{7,30},{8,7},{9,0... | collective-permute-start | bytes 294920 | tf_op jit(solution)/shard_map/ppermute | solution.py:582
  117.0 16.6 %copy-start = (bf16[384,448]{1,0:T(8,128)(2,1)S(1)}, bf16[384,448]{1,0:T(8,128)(2,1)}, u32[]{:S(2)}) copy-start(bf16[384,448]{1,0:T(8,128)(2,1)} %constant.52.clone.refs_10_) | copy-start | bytes 1032196
  117.0 16.6 %copy-start.1 = (bf16[192,416]{1,0:T(8,128)(2,1)S(1)}, bf16[192,416]{1,0:T(8,128)(2,1)}, u32[]{:S(2)}) copy-start(bf16[192,416]{1,0:T(8,128)(2,1)} %constant.51.clone.refs_9_) | copy-start | bytes 479236
  117.0 16.6 %copy-start.3 = (bf16[192,288]{1,0:T(8,128)(2,1)S(1)}, bf16[192,288]{1,0:T(8,128)(2,1)}, u32[]{:S(2)}) copy-start(bf16[192,288]{1,0:T(8,128)(2,1)} %constant.54.clone.refs_12_) | copy-start | bytes 331780
  117.0 16.6 %copy-start.4 = (bf16[192,192]{1,0:T(8,128)(2,1)S(1)}, bf16[192,192]{1,0:T(8,128)(2,1)}, u32[]{:S(2)}) copy-start(bf16[192,192]{1,0:T(8,128)(2,1)} %constant.53.clone.refs_11_) | copy-start | bytes 221188
  117.0 7.8 %collective-permute-start.13 = (bf16[128,768]{1,0:T(8,128)(2,1)S(1)}, bf16[128,768]{1,0:T(8,128)(2,1)S(1)}, u32[]{:S(2)}, u32[]{:S(2)}) collective-permute-start(bf16[128,768]{1,0:T(8,128)(2,1)S(1)} %slice_bitcast_fusion.11), channel_id=1, source_target_pairs={{0,4},{1,5},{2,6},{3,7},{4,0},{5,1},{6,2},{7,3},{8,12},{9,13},{10,... | collective-permute-start | bytes 589832 | tf_op jit(solution)/shard_map/ppermute | solution.py:611
  118.8 6.6 %collective-permute-start.14 = (bf16[128,768]{1,0:T(8,128)(2,1)S(1)}, bf16[128,768]{1,0:T(8,128)(2,1)S(1)}, u32[]{:S(2)}, u32[]{:S(2)}) collective-permute-start(bf16[128,768]{1,0:T(8,128)(2,1)S(1)} %slice_bitcast_fusion.9), channel_id=1, source_target_pairs={{0,2},{1,3},{2,0},{3,1},{4,6},{5,7},{6,4},{7,5},{8,10},{9,11},{10,... | collective-permute-start | bytes 589832 | tf_op jit(solution)/shard_map/ppermute | solution.py:611
  118.8 11.5 %collective-permute-start.15 = (bf16[128,1024]{1,0:T(8,128)(2,1)S(1)}, bf16[128,1024]{1,0:T(8,128)(2,1)S(1)}, u32[]{:S(2)}, u32[]{:S(2)}) collective-permute-start(bf16[128,1024]{1,0:T(8,128)(2,1)S(1)} %get-tuple-element.94), channel_id=1, source_target_pairs={{0,7},{1,0},{2,1},{3,2},{4,3},{5,4},{6,5},{7,6},{8,15},{9,8},{10,9... | collective-permute-start | bytes 786440 | tf_op jit(solution)/shard_map/ppermute | solution.py:582
  120.6 12.9 %collective-permute-start.16 = (bf16[208,1024]{1,0:T(8,128)(2,1)S(1)}, bf16[208,1024]{1,0:T(8,128)(2,1)S(1)}, u32[]{:S(2)}, u32[]{:S(2)}) collective-permute-start(bf16[208,1024]{1,0:T(8,128)(2,1)S(1)} %get-tuple-element.95), channel_id=1, source_target_pairs={{0,24},{1,25},{2,26},{3,27},{4,28},{5,29},{6,30},{7,31},{8,0},{9,1... | collective-permute-start | bytes 1277960 | tf_op jit(solution)/shard_map/ppermute | solution.py:582
  126.1 9.7 %collective-permute-start.18 = (bf16[32,1536]{1,0:T(8,128)(2,1)}, bf16[32,1536]{1,0:T(8,128)(2,1)}, u32[]{:S(2)}, u32[]{:S(2)}) collective-permute-start(bf16[32,1536]{1,0:T(8,128)(2,1)} %get-tuple-element.111.refs_0_), channel_id=1, source_target_pairs={{0,8},{1,9},{2,10},{3,11},{4,12},{5,13},{6,14},{7,15},{8,0},{9,1},... | collective-permute-start | bytes 294920 | tf_op jit(solution)/shard_map/ppermute | solution.py:611
  126.7 10.2 %collective-permute-start.20 = (bf16[32,1536]{1,0:T(8,128)(2,1)}, bf16[32,1536]{1,0:T(8,128)(2,1)}, u32[]{:S(2)}, u32[]{:S(2)}) collective-permute-start(bf16[32,1536]{1,0:T(8,128)(2,1)} %get-tuple-element.113.refs_2_), channel_id=1, source_target_pairs={{0,24},{1,25},{2,26},{3,27},{4,28},{5,29},{6,30},{7,31},{8,16},{9,... | collective-permute-start | bytes 294920 | tf_op jit(solution)/shard_map/ppermute | solution.py:611
  129.1 17.6 %collective-permute-start.19 = (bf16[32,4096]{1,0:T(8,128)(2,1)}, bf16[32,4096]{1,0:T(8,128)(2,1)}, u32[]{:S(2)}, u32[]{:S(2)}) collective-permute-start(bf16[32,4096]{1,0:T(8,128)(2,1)} %pad_maximum_fusion.2.refs_1_), channel_id=1, source_target_pairs={{0,16},{1,17},{2,18},{3,19},{4,20},{5,21},{6,22},{7,23},{8,24},{9,... | collective-permute-start | bytes 786440 | tf_op jit(solution)/shard_map/ppermute | solution.py:611
  (10 other events, 20.2 us)

commit v14 on v13

--- a/solution.py
+++ b/solution.py
@@ -766,7 +766,7 @@
     edge = (lax.axis_index("lat") == 0).astype(jnp.int32).reshape(1)
     owner, rowmap = device_rows(channels, sizes)
     if channels // (sizes[0] * sizes[1]) % 16 == 0:
-        rowmap = jnp.zeros((8, 1), jnp.int32)
+        rowmap = jnp.asarray(np.zeros((8, LANES), np.int32))
 
     wide = shape(count, channels)
     inner = 2 * 2 * WIN * WIN
@@ -882,7 +882,7 @@
         name="input_backward", **settings(5, 30),
     )
     got1, *arrived2 = behind([got1] + arrived2, full)
-    strips = sent_strips(behind(strips, (got1, arrived2)), sizes, -1)
+    strips = sent_strips(strips, sizes, -1)
     layer2.add(arrived2)
     total2 = layer2.finish()
 

time: 149 us -> 144 us (0.966)
  waiting for transfers between devices: 32 us -> 23.7 us
  starting transfers between devices: 21 us -> 24.6 us
    ppermute x15, waiting for transfers between devices: 26.2 us -> 21.2 us  [exchange(): return lax.ppermute(block, ('lat', 'lon'), route)]
    ppermute x6, waiting for transfers between devices: 5.81 us -> 2.53 us  [sent(): return lax.ppermute(block, ('lat', 'lon'), route)]
    ppermute x15, starting transfers between devices: 12.1 us -> 15.4 us  [exchange(): return lax.ppermute(block, ('lat', 'lon'), route)]
  transfers between devices with their start and end apart: 21 -> 21, of which waited for: 12 -> 10; matrix products, arithmetic and copies ran while one was open for 5% -> 6% of each run, Pallas kernels for 32% -> 33%
where the time goes in v14:
time: 144 us
  Pallas kernels  83.1 us (58%)
  starting transfers between devices  24.6 us (17%)
  waiting for transfers between devices  23.7 us (16%)
  other arithmetic  8.19 us (6%)
  local copies, waits for them, and re-layouts  3.26 us (2%)
    pallas_call x6, Pallas kernels, tied_call(): pl.pallas_call(body, out_shape=out_shape, in_specs=[pl.BlockSpec(memory_s...  47.4 us
    pallas_call x1, Pallas kernels, shards(): pl.pallas_call(forward_kernel, out_shape=[wide, shape(channels, count), s...  30.7 us
    ppermute x15, waiting for transfers between devices, exchange(): return lax.ppermute(block, ('lat', 'lon'), route)  21.2 us
    ppermute x15, starting transfers between devices, exchange(): return lax.ppermute(block, ('lat', 'lon'), route)  15.4 us
    ppermute x6, starting transfers between devices, sent(): return lax.ppermute(block, ('lat', 'lon'), route)  9.28 us
    convert_element_type x10, other arithmetic, core_sum(): return (mine.astype(F32) + arrived.astype(F32)).astype(BF16)  5.95 us
    pallas_call x1, Pallas kernels, shards(): pl.pallas_call(pack_kernel, out_shape=[shape(*e) for e in extents], in_sp...  3.14 us
  transfers between devices with their start and end apart: 21, of which 10 were waited for; matrix products, arithmetic and copies ran while one was open for 6% of the time, Pallas kernels for 33%

profile of v14, /device:TPU:0, one launch (start us, length us, event | category | flops | bytes accessed | tf_op | source)
XLA Modules:
  0.0 143.9 jit_solution(2028940436599611841)
XLA Ops:
  0.6 3.1 %pack_strips.1 = (bf16[128,1024]{1,0:T(8,128)(2,1)}, bf16[208,1024]{1,0:T(8,128)(2,1)}, bf16[48,1024]{1,0:T(8,128)(2,1)}) custom-call(bf16[768,1024]{1,0:T(8,128)(2,1)} %bitcast.99, bf16[192,1024]{1,0:T(8,128)(2,1)} %bitcast.102, bf16[288,768]{1,0:T(8,128)(2,1)} %constant.42.clone.pick_cells, bf16[96,192]{1,0:T(8,128)(2,1)} %constant.43.clone.pick_groups), custom_call_target="tpu_custom_call" | custom-call | flops 10000000000 | bytes 16777216 | tf_op jit(solution)/shard_map/pack_strips/pallas_call | solution.py:756
  3.8 2.5 %collective-permute-start.2 = (bf16[48,1024]{1,0:T(8,128)(2,1)}, bf16[48,1024]{1,0:T(8,128)(2,1)S(1)}, u32[]{:S(2)}, u32[]{:S(2)}) collective-permute-start(bf16[48,1024]{1,0:T(8,128)(2,1)} %get-tuple-element.53.refs_2_), channel_id=1, source_target_pairs={{0,9},{1,10},{2,11},{3,12},{4,13},{5,14},{6,15},{7,8},{8,17},{9,18... | collective-permute-start | bytes 294920 | tf_op jit(solution)/shard_map/ppermute | solution.py:582
  6.2 1.6 %collective-permute-start = (bf16[128,1024]{1,0:T(8,128)(2,1)}, bf16[128,1024]{1,0:T(8,128)(2,1)S(1)}, u32[]{:S(2)}, u32[]{:S(2)}) collective-permute-start(bf16[128,1024]{1,0:T(8,128)(2,1)} %get-tuple-element.51.refs_0_), channel_id=1, source_target_pairs={{0,1},{1,2},{2,3},{3,4},{4,5},{5,6},{6,7},{7,0},{8,9},{9,10},{10,1... | collective-permute-start | bytes 786440 | tf_op jit(solution)/shard_map/ppermute | solution.py:582
  7.8 1.6 %collective-permute-start.1 = (bf16[208,1024]{1,0:T(8,128)(2,1)}, bf16[208,1024]{1,0:T(8,128)(2,1)S(1)}, u32[]{:S(2)}, u32[]{:S(2)}) collective-permute-start(bf16[208,1024]{1,0:T(8,128)(2,1)} %get-tuple-element.52.refs_1_), channel_id=1, source_target_pairs={{0,8},{1,9},{2,10},{3,11},{4,12},{5,13},{6,14},{7,15},{8,16},{9,17... | collective-permute-start | bytes 1277960 | tf_op jit(solution)/shard_map/ppermute | solution.py:582
  9.4 9.3 %inner_windows.1 = (bf16[256,1024]{1,0:T(8,128)(2,1)}, bf16[256,1024]{1,0:T(8,128)(2,1)}, f32[256,128]{1,0:T(8,128)}, bf16[256,1024]{1,0:T(8,128)(2,1)}, f32[256,1024]{1,0:T(8,128)}, /*index=5*/bf16[256,3072]{1,0:T(8,128)(2,1)}) custom-call(bf16[128,1024]{1,0:T(8,128)(2,1)} %get-tuple-element.51.refs_0_, bf16[208,1024]{1,0:T(8,128)(2,1)} %get-tuple-element.52.refs_1_, ...), custom_call_target="tpu_custom_call" | custom-call | flops 89999998976 | bytes 16777216 | tf_op jit(solution)/shard_map/inner_windows/pallas_call | solution.py:702
  19.3 2.5 %collective-permute-done.1.above = bf16[208,1024]{1,0:T(8,128)(2,1)S(1)} collective-permute-done((bf16[208,1024]{1,0:T(8,128)(2,1)}, bf16[208,1024]{1,0:T(8,128)(2,1)S(1)}, u32[]{:S(2)}, u32[]{:S(2)}) %collective-permute-start.1) | collective-permute-done | bytes 426016 | tf_op jit(solution)/shard_map/ppermute | solution.py:582
  22.6 30.7 %block_forward.1 = (bf16[768,1024]{1,0:T(8,128)(2,1)}, bf16[1024,768]{1,0:T(8,128)(2,1)}, bf16[768,3072]{1,0:T(8,128)(2,1)}, bf16[768,1024]{1,0:T(8,128)(2,1)}, ...) custom-call(s32[1]{0:T(128)} %bitcast.edge.refs_0_.refs_2_, ...), custom_call_target="tpu_custom_call" | custom-call | flops 299999985664 | bytes 16777216 | tf_op jit(solution)/shard_map/block_forward/pallas_call | solution.py:786
  53.4 13.5 %attention_backward.2 = (bf16[768,1536]{1,0:T(8,128)(2,1)S(1)}, bf16[512,1536]{1,0:T(8,128)(2,1)S(1)}, bf16[512,1536]{1,0:T(8,128)(2,1)S(1)}) custom-call(s32[1]{0:T(128)} %bitcast.edge.refs_0_.refs_2_, bf16[768,3072]{1,0:T(8,128)(2,1)} %get-tuple-element.62.refs_1_.refs_3_, bf16[768,1024]{1,0:T(8,128)(2,1)} %get-tuple-element.63.refs_2_.refs_4_, ...), custom_call_target="tpu_custom_call" | custom-call | flops 149999992832 | bytes 16777216 | tf_op jit(solution)/shard_map/attention_backward/pallas_call | solution.py:702
  67.5 1.6 %add_convert_fusion.2 = bf16[512,1024]{1,0:T(8,128)(2,1)S(1)} fusion(bf16[512,1024]{1,0:T(8,128)(2,1)} %collective-permute-done.3, bf16[512,1024]{1,0:T(8,128)(2,1)S(1)} %copy-done.13), kind=kLoop, calls=%fused_computation.2 | loop fusion | flops 2097152 | bytes 3145728 | tf_op jit(solution)/shard_map/convert_element_type | solution.py:619
  69.2 1.4 collective-permute-done.4
  71.0 1.2 fusion.15
  73.2 1.5 %collective-permute-start.5 = (bf16[2,128,1280]{2,1,0:T(8,128)(2,1)}, bf16[2,128,1280]{2,1,0:T(8,128)(2,1)}, u32[]{:S(2)}, u32[]{:S(2)}) collective-permute-start(bf16[2,128,1280]{2,1,0:T(8,128)(2,1)} %slice_bitcast_fusion.1.refs_0_), channel_id=1, source_target_pairs={{0,2},{1,3},{2,0},{3,1},{4,6},{5,7},{6,4},{7,5},{8,10},{9,11},{10,... | collective-permute-start | bytes 1966088 | tf_op jit(solution)/shard_map/ppermute | solution.py:611
  75.4 13.7 %attention_backward.3 = (bf16[768,1536]{1,0:T(8,128)(2,1)S(1)}, bf16[512,1536]{1,0:T(8,128)(2,1)S(1)}, bf16[512,1536]{1,0:T(8,128)(2,1)S(1)}) custom-call(bf16[2,128,1280]{2,1,0:T(8,128)(2,1)} %slice_bitcast_fusion.1.refs_0_, bf16[2,128,1280]{2,1,0:T(8,128)(2,1)} %bitcast.7.refs_1_, s32[1]{0:T(128)} %bitcast.edge.refs_0_.refs_2_, ...), custom_call_target="tpu_custom_call" | custom-call | flops 149999992832 | bytes 16777216 | tf_op jit(solution)/shard_map/attention_backward/pallas_call | solution.py:702
  89.1 1.5 %collective-permute-done.5 = bf16[2,128,1280]{2,1,0:T(8,128)(2,1)} collective-permute-done((bf16[2,128,1280]{2,1,0:T(8,128)(2,1)}, bf16[2,128,1280]{2,1,0:T(8,128)(2,1)}, u32[]{:S(2)}, u32[]{:S(2)}) %collective-permute-start.5) | collective-permute-done | bytes 655392 | tf_op jit(solution)/shard_map/ppermute | solution.py:611
  90.5 1.2 collective-permute-done.6
  91.8 1.4 fusion.1
  94.0 1.6 %fusion = bf16[2,128,1280]{2,1,0:T(8,128)(2,1)S(1)} fusion(bf16[2,128,1280]{2,1,0:T(8,128)(2,1)S(1)} %bitcast.93, bf16[2,128,1280]{2,1,0:T(8,128)(2,1)} %collective-permute-done.6), kind=kLoop, calls=%fused_computation.5 | loop fusion | flops 1310720 | bytes 1966080 | tf_op jit(solution)/shard_map/convert_element_type | solution.py:619
  95.6 1.1 collective-permute-start.9
  97.3 1.1 collective-permute-start.11
  98.4 6.3 %input_product.1.refs_1_ = bf16[768,1024]{1,0:T(8,128)(2,1)S(1)} custom-call(bf16[128,1280]{1,0:T(8,128)(2,1)S(1)} %slice_bitcast_fusion.7.refs_0_, bf16[128,1280]{1,0:T(8,128)(2,1)S(1)} %slice_bitcast_fusion.6.refs_1_, bf16[2,128,768]{2,1,0:T(8,128)(2,1)S(1)} %slice_bitcast_fusion.2.refs_2_, bf16[2,128,768]{2,1,0:T(8,128)(2,1)S(1)} %bitcast.82, ...), custom_call_target="tpu_custom_call" | custom-call | flops 80000000000 | bytes 16777216 | tf_op jit(solution)/shard_map/input_product/pallas_call | solution.py:702
  106.6 2.5 %input_backward.1 = (bf16[768,1024]{1,0:T(8,128)(2,1)S(1)}, bf16[128,1024]{1,0:T(8,128)(2,1)S(1)}, bf16[208,1024]{1,0:T(8,128)(2,1)S(1)}, bf16[48,1024]{1,0:T(8,128)(2,1)S(1)}) custom-call(bf16[64,2560]{1,0:T(8,128)(2,1)S(1)} %bitcast.85, bf16[768,1024]{1,0:T(8,128)(2,1)S(1)} %input_product.1.refs_1_, bf16[768,1024]{1,0:T(8,128)(2,1)S(1)} %copy-done.7, ...), custom_call_target="tpu_custom_call" | custom-call | flops 49999998976 | bytes 16777216 | tf_op jit(solution)/shard_map/input_backward/pallas_call | solution.py:702
  109.1 1.8 %collective-permute-start.17 = (bf16[48,1024]{1,0:T(8,128)(2,1)S(1)}, bf16[48,1024]{1,0:T(8,128)(2,1)S(1)}, u32[]{:S(2)}, u32[]{:S(2)}) collective-permute-start(bf16[48,1024]{1,0:T(8,128)(2,1)S(1)} %get-tuple-element.90), channel_id=1, source_target_pairs={{0,31},{1,24},{2,25},{3,26},{4,27},{5,28},{6,29},{7,30},{8,7},{9,0... | collective-permute-start | bytes 294920 | tf_op jit(solution)/shard_map/ppermute | solution.py:582
  110.9 1.2 collective-permute-start.15
  112.1 4.4 %collective-permute-done.10 = bf16[64,2560]{1,0:T(8,128)(2,1)S(1)} collective-permute-done((bf16[64,2560]{1,0:T(8,128)(2,1)S(1)}, bf16[64,2560]{1,0:T(8,128)(2,1)S(1)}, u32[]{:S(2)}, u32[]{:S(2)}) %collective-permute-start.10) | collective-permute-done | bytes 327712 | tf_op jit(solution)/shard_map/ppermute | solution.py:611
  117.5 1.5 %collective-permute-start.13 = (bf16[128,768]{1,0:T(8,128)(2,1)S(1)}, bf16[128,768]{1,0:T(8,128)(2,1)S(1)}, u32[]{:S(2)}, u32[]{:S(2)}) collective-permute-start(bf16[128,768]{1,0:T(8,128)(2,1)S(1)} %slice_bitcast_fusion.11), channel_id=1, source_target_pairs={{0,4},{1,5},{2,6},{3,7},{4,0},{5,1},{6,2},{7,3},{8,12},{9,13},{10,... | collective-permute-start | bytes 589832 | tf_op jit(solution)/shard_map/ppermute | solution.py:611
  119.1 3.6 %collective-permute-start.14 = (bf16[128,768]{1,0:T(8,128)(2,1)S(1)}, bf16[128,768]{1,0:T(8,128)(2,1)S(1)}, u32[]{:S(2)}, u32[]{:S(2)}) collective-permute-start(bf16[128,768]{1,0:T(8,128)(2,1)S(1)} %slice_bitcast_fusion.9), channel_id=1, source_target_pairs={{0,2},{1,3},{2,0},{3,1},{4,6},{5,7},{6,4},{7,5},{8,10},{9,11},{10,... | collective-permute-start | bytes 589832 | tf_op jit(solution)/shard_map/ppermute | solution.py:611
  123.3 3.1 %collective-permute-done.14 = bf16[128,768]{1,0:T(8,128)(2,1)S(1)} collective-permute-done((bf16[128,768]{1,0:T(8,128)(2,1)S(1)}, bf16[128,768]{1,0:T(8,128)(2,1)S(1)}, u32[]{:S(2)}, u32[]{:S(2)}) %collective-permute-start.14) | collective-permute-done | bytes 196640 | tf_op jit(solution)/shard_map/ppermute | solution.py:611
  127.1 1.2 collective-permute-start.20
  129.1 2.2 %collective-permute-start.19 = (bf16[32,4096]{1,0:T(8,128)(2,1)}, bf16[32,4096]{1,0:T(8,128)(2,1)}, u32[]{:S(2)}, u32[]{:S(2)}) collective-permute-start(bf16[32,4096]{1,0:T(8,128)(2,1)} %pad_maximum_fusion.2.refs_1_), channel_id=1, source_target_pairs={{0,16},{1,17},{2,18},{3,19},{4,20},{5,21},{6,22},{7,23},{8,24},{9,... | collective-permute-start | bytes 786440 | tf_op jit(solution)/shard_map/ppermute | solution.py:611
  131.4 2.1 %unpack_strips.1 = (bf16[768,1024]{1,0:T(8,128)(2,1)}, bf16[192,1024]{1,0:T(8,128)(2,1)}) custom-call(bf16[32,1536]{1,0:T(8,128)(2,1)} %get-tuple-element.105.refs_0_, bf16[32,4096]{1,0:T(8,128)(2,1)} %pad_maximum_fusion.2.refs_1_, bf16[32,1536]{1,0:T(8,128)(2,1)} %get-tuple-element.107.refs_2_, bf16[64,2560]{1,0:T(8,128)(2,1)S(1)} %bitcast.86, ...), custom_call_target="tpu_custom_call" | custom-call | flops 199999995904 | bytes 16777216 | tf_op jit(solution)/shard_map/unpack_strips/pallas_call | solution.py:702
  133.9 8.2 %collective-permute-done.19.refs_1_ = bf16[32,4096]{1,0:T(8,128)(2,1)} collective-permute-done((bf16[32,4096]{1,0:T(8,128)(2,1)}, bf16[32,4096]{1,0:T(8,128)(2,1)}, u32[]{:S(2)}, u32[]{:S(2)}) %collective-permute-start.19) | collective-permute-done | bytes 262176 | tf_op jit(solution)/shard_map/ppermute | solution.py:611
  142.1 1.8 %end_sums.1 = (f32[32,3072]{1,0:T(8,128)}, f32[32,1024]{1,0:T(8,128)}) custom-call(f32[32,2560]{1,0:T(8,128)S(1)} %slice_bitcast_fusion.4.kept1, f32[32,1536]{1,0:T(8,128)S(1)} %get-tuple-element.104.kept2, bf16[32,1536]{1,0:T(8,128)(2,1)} %collective-permute-done.18.refs_0_, bf16[32,4096]{1,0:T(8,128)(2,1)} %collective-permute-done.19.refs_1_, ...), custom_call_target="tpu_custom_call" | custom-call | flops 10000000000 | bytes 16777216 | tf_op jit(solution)/shard_map/end_sums/pallas_call | solution.py:915
  (90 shorter events, 10.7 us)
Async XLA Ops:
  3.8 15.5 %collective-permute-start.2 = (bf16[48,1024]{1,0:T(8,128)(2,1)}, bf16[48,1024]{1,0:T(8,128)(2,1)S(1)}, u32[]{:S(2)}, u32[]{:S(2)}) collective-permute-start(bf16[48,1024]{1,0:T(8,128)(2,1)} %get-tuple-element.53.refs_2_), channel_id=1, source_target_pairs={{0,9},{1,10},{2,11},{3,12},{4,13},{5,14},{6,15},{7,8},{8,17},{9,18... | collective-permute-start | bytes 294920 | tf_op jit(solution)/shard_map/ppermute | solution.py:582
  6.2 13.0 %collective-permute-start = (bf16[128,1024]{1,0:T(8,128)(2,1)}, bf16[128,1024]{1,0:T(8,128)(2,1)S(1)}, u32[]{:S(2)}, u32[]{:S(2)}) collective-permute-start(bf16[128,1024]{1,0:T(8,128)(2,1)} %get-tuple-element.51.refs_0_), channel_id=1, source_target_pairs={{0,1},{1,2},{2,3},{3,4},{4,5},{5,6},{6,7},{7,0},{8,9},{9,10},{10,1... | collective-permute-start | bytes 786440 | tf_op jit(solution)/shard_map/ppermute | solution.py:582
  7.8 10.9 %copy-start.14 = (s32[32]{0:T(128)S(1)}, s32[32]{0:T(128)}, u32[]{:S(2)}) copy-start(s32[32]{0:T(128)} %constant.48.clone) | copy-start | bytes 388
  7.8 10.9 %copy-start.15 = (s32[32]{0:T(128)S(1)}, s32[32]{0:T(128)}, u32[]{:S(2)}) copy-start(s32[32]{0:T(128)} %constant.47.clone) | copy-start | bytes 388
  7.8 14.0 %collective-permute-start.1 = (bf16[208,1024]{1,0:T(8,128)(2,1)}, bf16[208,1024]{1,0:T(8,128)(2,1)S(1)}, u32[]{:S(2)}, u32[]{:S(2)}) collective-permute-start(bf16[208,1024]{1,0:T(8,128)(2,1)} %get-tuple-element.52.refs_1_), channel_id=1, source_target_pairs={{0,8},{1,9},{2,10},{3,11},{4,12},{5,13},{6,14},{7,15},{8,16},{9,17... | collective-permute-start | bytes 1277960 | tf_op jit(solution)/shard_map/ppermute | solution.py:582
  53.3 13.6 %collective-permute-start.3 = (bf16[512,1024]{1,0:T(8,128)(2,1)}, bf16[512,1024]{1,0:T(8,128)(2,1)}, u32[]{:S(2)}, u32[]{:S(2)}) collective-permute-start(bf16[512,1024]{1,0:T(8,128)(2,1)} %get-tuple-element.61), channel_id=1, source_target_pairs={{0,1},{1,0},{2,3},{3,2},{4,5},{5,4},{6,7},{7,6},{8,9},{9,8},{10,11... | collective-permute-start | bytes 3145736 | tf_op jit(solution)/shard_map/ppermute | solution.py:611
  53.4 14.1 %copy-start.13 = (bf16[512,1024]{1,0:T(8,128)(2,1)S(1)}, bf16[512,1024]{1,0:T(8,128)(2,1)}, u32[]{:S(2)}) copy-start(bf16[512,1024]{1,0:T(8,128)(2,1)} %get-tuple-element.67) | copy-start | bytes 3145732
  67.0 3.6 %collective-permute-start.4 = (bf16[512,1536]{1,0:T(8,128)(2,1)S(1)}, bf16[512,1536]{1,0:T(8,128)(2,1)S(1)}, u32[]{:S(2)}, u32[]{:S(2)}) collective-permute-start(bf16[512,1536]{1,0:T(8,128)(2,1)S(1)} %get-tuple-element.71), channel_id=1, source_target_pairs={{0,1},{1,0},{2,3},{3,2},{4,5},{5,4},{6,7},{7,6},{8,9},{9,8},{10,11... | collective-permute-start | bytes 4718600 | tf_op jit(solution)/shard_map/ppermute | solution.py:611
  72.2 16.8 %copy-start.11 = (bf16[512,1280]{1,0:T(8,128)(2,1)}, bf16[512,1280]{1,0:T(8,128)(2,1)S(1)}, u32[]{:S(2)}) copy-start(bf16[512,1280]{1,0:T(8,128)(2,1)S(1)} %pad_maximum_fusion) | copy-start | bytes 3932164
  73.2 17.3 %collective-permute-start.5 = (bf16[2,128,1280]{2,1,0:T(8,128)(2,1)}, bf16[2,128,1280]{2,1,0:T(8,128)(2,1)}, u32[]{:S(2)}, u32[]{:S(2)}) collective-permute-start(bf16[2,128,1280]{2,1,0:T(8,128)(2,1)} %slice_bitcast_fusion.1.refs_0_), channel_id=1, source_target_pairs={{0,2},{1,3},{2,0},{3,1},{4,6},{5,7},{6,4},{7,5},{8,10},{9,11},{10,... | collective-permute-start | bytes 1966088 | tf_op jit(solution)/shard_map/ppermute | solution.py:611
  74.7 17.0 %collective-permute-start.6 = (bf16[2,128,1280]{2,1,0:T(8,128)(2,1)}, bf16[2,128,1280]{2,1,0:T(8,128)(2,1)}, u32[]{:S(2)}, u32[]{:S(2)}) collective-permute-start(bf16[2,128,1280]{2,1,0:T(8,128)(2,1)} %bitcast.7.refs_1_), channel_id=1, source_target_pairs={{0,4},{1,5},{2,6},{3,7},{4,0},{5,1},{6,2},{7,3},{8,12},{9,13},{10,... | collective-permute-start | bytes 1966088 | tf_op jit(solution)/shard_map/ppermute | solution.py:611
  89.1 4.9 %copy-start.12 = (bf16[256,1280]{1,0:T(8,128)(2,1)S(1)}, bf16[256,1280]{1,0:T(8,128)(2,1)}, u32[]{:S(2)}) copy-start(bf16[256,1280]{1,0:T(8,128)(2,1)} %get-tuple-element.100) | copy-start | bytes 1966084
  91.7 5.0 %collective-permute-start.7 = (bf16[512,1536]{1,0:T(8,128)(2,1)S(1)}, bf16[512,1536]{1,0:T(8,128)(2,1)S(1)}, u32[]{:S(2)}, u32[]{:S(2)}) collective-permute-start(bf16[512,1536]{1,0:T(8,128)(2,1)S(1)} %get-tuple-element.77), channel_id=1, source_target_pairs={{0,1},{1,0},{2,3},{3,2},{4,5},{5,4},{6,7},{7,6},{8,9},{9,8},{10,11... | collective-permute-start | bytes 4718600 | tf_op jit(solution)/shard_map/ppermute | solution.py:611
  93.2 5.2 %slice-start = ((s8[6291456]{0:T(1024)(128)(4,1)}), s8[4194304]{0:T(1024)(128)(4,1)S(1)}, s32[]{:S(2)}) async-start(s8[6291456]{0:T(1024)(128)(4,1)} %bitcast.87), calls=%async_computation | async-start | bytes 8388608
  93.2 12.6 %collective-permute-start.8 = (bf16[128,1280]{1,0:T(8,128)(2,1)S(1)}, bf16[128,1280]{1,0:T(8,128)(2,1)S(1)}, u32[]{:S(2)}, u32[]{:S(2)}) collective-permute-start(bf16[128,1280]{1,0:T(8,128)(2,1)S(1)} %slice_bitcast_fusion.7.refs_0_), channel_id=1, source_target_pairs={{0,4},{1,5},{2,6},{3,7},{4,0},{5,1},{6,2},{7,3},{8,12},{9,13},{10,... | collective-permute-start | bytes 983048 | tf_op jit(solution)/shard_map/ppermute | solution.py:611
  95.6 10.6 %collective-permute-start.9 = (bf16[128,1280]{1,0:T(8,128)(2,1)S(1)}, bf16[128,1280]{1,0:T(8,128)(2,1)S(1)}, u32[]{:S(2)}, u32[]{:S(2)}) collective-permute-start(bf16[128,1280]{1,0:T(8,128)(2,1)S(1)} %slice_bitcast_fusion.6.refs_1_), channel_id=1, source_target_pairs={{0,2},{1,3},{2,0},{3,1},{4,6},{5,7},{6,4},{7,5},{8,10},{9,11},{10,... | collective-permute-start | bytes 983048 | tf_op jit(solution)/shard_map/ppermute | solution.py:611
  97.3 19.9 %collective-permute-start.11 = (bf16[2,128,768]{2,1,0:T(8,128)(2,1)S(1)}, bf16[2,128,768]{2,1,0:T(8,128)(2,1)S(1)}, u32[]{:S(2)}, u32[]{:S(2)}) collective-permute-start(bf16[2,128,768]{2,1,0:T(8,128)(2,1)S(1)} %slice_bitcast_fusion.2.refs_2_), channel_id=1, source_target_pairs={{0,2},{1,3},{2,0},{3,1},{4,6},{5,7},{6,4},{7,5},{8,10},{9,11},{10,... | collective-permute-start | bytes 1179656 | tf_op jit(solution)/shard_map/ppermute | solution.py:611
  98.4 8.2 %copy-start.8 = (bf16[768,1024]{1,0:T(8,128)(2,1)S(1)}, bf16[768,1024]{1,0:T(8,128)(2,1)}, u32[]{:S(2)}) copy-start(bf16[768,1024]{1,0:T(8,128)(2,1)} %get-tuple-element.82.refs_4_) | copy-start | bytes 4718596
  104.8 12.4 %collective-permute-start.12 = (bf16[2,128,768]{2,1,0:T(8,128)(2,1)S(1)}, bf16[2,128,768]{2,1,0:T(8,128)(2,1)S(1)}, u32[]{:S(2)}, u32[]{:S(2)}) collective-permute-start(bf16[2,128,768]{2,1,0:T(8,128)(2,1)S(1)} %bitcast.83), channel_id=1, source_target_pairs={{0,4},{1,5},{2,6},{3,7},{4,0},{5,1},{6,2},{7,3},{8,12},{9,13},{10,... | collective-permute-start | bytes 1179656 | tf_op jit(solution)/shard_map/ppermute | solution.py:611
  106.5 10.1 %collective-permute-start.10 = (bf16[64,2560]{1,0:T(8,128)(2,1)S(1)}, bf16[64,2560]{1,0:T(8,128)(2,1)S(1)}, u32[]{:S(2)}, u32[]{:S(2)}) collective-permute-start(bf16[64,2560]{1,0:T(8,128)(2,1)S(1)} %bitcast.84), channel_id=1, source_target_pairs={{0,8},{1,9},{2,10},{3,11},{4,12},{5,13},{6,14},{7,15},{8,0},{9,1},... | collective-permute-start | bytes 983048 | tf_op jit(solution)/shard_map/ppermute | solution.py:611
  109.1 20.0 %collective-permute-start.17 = (bf16[48,1024]{1,0:T(8,128)(2,1)S(1)}, bf16[48,1024]{1,0:T(8,128)(2,1)S(1)}, u32[]{:S(2)}, u32[]{:S(2)}) collective-permute-start(bf16[48,1024]{1,0:T(8,128)(2,1)S(1)} %get-tuple-element.90), channel_id=1, source_target_pairs={{0,31},{1,24},{2,25},{3,26},{4,27},{5,28},{6,29},{7,30},{8,7},{9,0... | collective-permute-start | bytes 294920 | tf_op jit(solution)/shard_map/ppermute | solution.py:582
  110.9 20.4 %collective-permute-start.15 = (bf16[128,1024]{1,0:T(8,128)(2,1)S(1)}, bf16[128,1024]{1,0:T(8,128)(2,1)S(1)}, u32[]{:S(2)}, u32[]{:S(2)}) collective-permute-start(bf16[128,1024]{1,0:T(8,128)(2,1)S(1)} %get-tuple-element.88), channel_id=1, source_target_pairs={{0,7},{1,0},{2,1},{3,2},{4,3},{5,4},{6,5},{7,6},{8,15},{9,8},{10,9... | collective-permute-start | bytes 786440 | tf_op jit(solution)/shard_map/ppermute | solution.py:582
  116.6 14.8 %collective-permute-start.16 = (bf16[208,1024]{1,0:T(8,128)(2,1)S(1)}, bf16[208,1024]{1,0:T(8,128)(2,1)S(1)}, u32[]{:S(2)}, u32[]{:S(2)}) collective-permute-start(bf16[208,1024]{1,0:T(8,128)(2,1)S(1)} %get-tuple-element.89), channel_id=1, source_target_pairs={{0,24},{1,25},{2,26},{3,27},{4,28},{5,29},{6,30},{7,31},{8,0},{9,1... | collective-permute-start | bytes 1277960 | tf_op jit(solution)/shard_map/ppermute | solution.py:582
  117.5 5.7 %collective-permute-start.13 = (bf16[128,768]{1,0:T(8,128)(2,1)S(1)}, bf16[128,768]{1,0:T(8,128)(2,1)S(1)}, u32[]{:S(2)}, u32[]{:S(2)}) collective-permute-start(bf16[128,768]{1,0:T(8,128)(2,1)S(1)} %slice_bitcast_fusion.11), channel_id=1, source_target_pairs={{0,4},{1,5},{2,6},{3,7},{4,0},{5,1},{6,2},{7,3},{8,12},{9,13},{10,... | collective-permute-start | bytes 589832 | tf_op jit(solution)/shard_map/ppermute | solution.py:611
  119.1 12.3 %copy-start = (bf16[384,448]{1,0:T(8,128)(2,1)S(1)}, bf16[384,448]{1,0:T(8,128)(2,1)}, u32[]{:S(2)}) copy-start(bf16[384,448]{1,0:T(8,128)(2,1)} %constant.54.clone.refs_10_) | copy-start | bytes 1032196
  119.1 12.3 %copy-start.1 = (bf16[192,416]{1,0:T(8,128)(2,1)S(1)}, bf16[192,416]{1,0:T(8,128)(2,1)}, u32[]{:S(2)}) copy-start(bf16[192,416]{1,0:T(8,128)(2,1)} %constant.53.clone.refs_9_) | copy-start | bytes 479236
  119.1 12.3 %copy-start.3 = (bf16[192,288]{1,0:T(8,128)(2,1)S(1)}, bf16[192,288]{1,0:T(8,128)(2,1)}, u32[]{:S(2)}) copy-start(bf16[192,288]{1,0:T(8,128)(2,1)} %constant.56.clone.refs_12_) | copy-start | bytes 331780
  119.1 12.3 %copy-start.4 = (bf16[192,192]{1,0:T(8,128)(2,1)S(1)}, bf16[192,192]{1,0:T(8,128)(2,1)}, u32[]{:S(2)}) copy-start(bf16[192,192]{1,0:T(8,128)(2,1)} %constant.55.clone.refs_11_) | copy-start | bytes 221188
  119.1 7.2 %collective-permute-start.14 = (bf16[128,768]{1,0:T(8,128)(2,1)S(1)}, bf16[128,768]{1,0:T(8,128)(2,1)S(1)}, u32[]{:S(2)}, u32[]{:S(2)}) collective-permute-start(bf16[128,768]{1,0:T(8,128)(2,1)S(1)} %slice_bitcast_fusion.9), channel_id=1, source_target_pairs={{0,2},{1,3},{2,0},{3,1},{4,6},{5,7},{6,4},{7,5},{8,10},{9,11},{10,... | collective-permute-start | bytes 589832 | tf_op jit(solution)/shard_map/ppermute | solution.py:611
  127.1 6.4 %collective-permute-start.18 = (bf16[32,1536]{1,0:T(8,128)(2,1)}, bf16[32,1536]{1,0:T(8,128)(2,1)}, u32[]{:S(2)}, u32[]{:S(2)}) collective-permute-start(bf16[32,1536]{1,0:T(8,128)(2,1)} %get-tuple-element.105.refs_0_), channel_id=1, source_target_pairs={{0,8},{1,9},{2,10},{3,11},{4,12},{5,13},{6,14},{7,15},{8,0},{9,1},... | collective-permute-start | bytes 294920 | tf_op jit(solution)/shard_map/ppermute | solution.py:611
  127.1 6.8 %collective-permute-start.20 = (bf16[32,1536]{1,0:T(8,128)(2,1)}, bf16[32,1536]{1,0:T(8,128)(2,1)}, u32[]{:S(2)}, u32[]{:S(2)}) collective-permute-start(bf16[32,1536]{1,0:T(8,128)(2,1)} %get-tuple-element.107.refs_2_), channel_id=1, source_target_pairs={{0,24},{1,25},{2,26},{3,27},{4,28},{5,29},{6,30},{7,31},{8,16},{9,... | collective-permute-start | bytes 294920 | tf_op jit(solution)/shard_map/ppermute | solution.py:611
  129.1 13.0 %collective-permute-start.19 = (bf16[32,4096]{1,0:T(8,128)(2,1)}, bf16[32,4096]{1,0:T(8,128)(2,1)}, u32[]{:S(2)}, u32[]{:S(2)}) collective-permute-start(bf16[32,4096]{1,0:T(8,128)(2,1)} %pad_maximum_fusion.2.refs_1_), channel_id=1, source_target_pairs={{0,16},{1,17},{2,18},{3,19},{4,20},{5,21},{6,22},{7,23},{8,24},{9,... | collective-permute-start | bytes 786440 | tf_op jit(solution)/shard_map/ppermute | solution.py:611
  (10 other events, 20.2 us)
